TPU v7x, 32 devices: a whole 2x2x4 slice. The times are simulated.
32 devices in a mesh: grp: 2 (over x), lon: 4 (over y, core), lat: 4 (over z).
Axes of the slice: x: 2, y: 2, z: 4, core: 2. Of those that a mesh axis runs over, the one named last changes fastest.
Arguments:
- fields: bfloat16 [256, 128, 512], P(('grp', 'lat'), 'lon'), parts along dimension 0, may hold values from -6 to 6
- land_mask: int32 [256, 128], P(('grp', 'lat'), 'lon'), parts along dimension 0, may hold values from 0 to 1
- cotangent: bfloat16 [256, 128, 512], P(('grp', 'lat'), 'lon'), parts along dimension 0, may hold values from -6 to 6
- kernel: float32 [7, 7, 512], replicated, may hold values from -0.875 to 0.875
- layer_norm_gain: float32 [512], replicated, may hold values from 0.5 to 1.5
- layer_norm_bias: float32 [512], replicated, may hold values from -3 to 3
- w_in: bfloat16 [512, 2048], replicated, may hold values from -0.25 to 0.25
- b_in: float32 [2048], replicated, may hold values from -3 to 3
- w_out: bfloat16 [2048, 512], replicated, may hold values from -0.125 to 0.125
- b_out: float32 [512], replicated, may hold values from -3 to 3
- layer_scale: float32 [512], replicated, may hold values from 0.3 to 1.5
Outputs:
- mixed: bfloat16 [256, 128, 512], P(('grp', 'lat'), 'lon'), parts along dimension 0
- grad_fields: bfloat16 [256, 128, 512], P(('grp', 'lat'), 'lon'), parts along dimension 0
- grad_kernel: float32 [14, 7, 512], P('grp'), parts along dimension 0
- grad_gain: float32 [1024], P('grp'), parts along dimension 0
- grad_shift: float32 [1024], P('grp'), parts along dimension 0
- grad_w_in: float32 [1024, 2048], P('grp', ('lon', 'lat')), parts along dimension 0
- grad_b_in: float32 [4096], P('grp'), parts along dimension 0
- grad_w_out: float32 [2048, 1024], P(('lon', 'lat'), 'grp'), parts along dimension 1
- grad_b_out: float32 [1024], P('grp'), parts along dimension 0
- grad_scale: float32 [1024], P('grp'), parts along dimension 0
There are 2 independent parts, one for each index of `grp`. A program takes and returns all parts, laid end to end along the dimension named above; an argument that names none is the same for every part. Nothing has to cross between parts.
All inputs are finite; a program needn't handle non-finite values.
Results may differ from a plain program's by a relative error of at most 0.0067.
Values may be sent and summed in bfloat16 or wider, within the bound.
No kernel may reach another device: no remote copies, remote signals or barrier semaphores. Data moves between devices by JAX's collectives and lax.ppermute only.
A program may use at most 128 MiB of HBM per device.

v0:
```python
import jax
import jax.numpy as jnp
from jax import lax
from jax.sharding import PartitionSpec as P


def extended(cells, sides, width, closed):
    for axis, dim in sides:
        count = lax.axis_size(axis)
        ends = count if closed else count - 1
        head = lax.slice_in_dim(cells, 0, width, axis=dim)
        tail = lax.slice_in_dim(cells, cells.shape[dim] - width, cells.shape[dim], axis=dim)
        cells = jnp.concatenate(
            [
                lax.ppermute(tail, axis, [(i, (i + 1) % count) for i in range(ends)]),
                cells,
                lax.ppermute(head, axis, [((i + 1) % count, i) for i in range(ends)]),
            ],
            axis=dim,
        )
    return cells


def depthwise(padded, kernel, tile_rows, tile_cols):
    result = jnp.zeros((tile_rows, tile_cols, padded.shape[2]), jnp.float32)
    for row_off in range(7):
        for col_off in range(7):
            window = padded[row_off : row_off + tile_rows, col_off : col_off + tile_cols].astype(
                jnp.float32
            )
            result = result + kernel[row_off, col_off] * window
    return result


def kernel_grad(padded, convolution_gradient, tile_rows, tile_cols):
    grad_f = convolution_gradient.astype(jnp.float32)
    entries = []
    for row_off in range(7):
        for col_off in range(7):
            window = padded[row_off : row_off + tile_rows, col_off : col_off + tile_cols].astype(
                jnp.float32
            )
            entries.append(jnp.sum(grad_f * window, axis=(0, 1)))
    return jnp.stack(entries).reshape(7, 7, padded.shape[2])


def input_grad(d_padded, kernel, tile_rows, tile_cols):
    result = jnp.zeros((tile_rows, tile_cols, d_padded.shape[2]), jnp.float32)
    for row_off in range(7):
        for col_off in range(7):
            window = d_padded[
                6 - row_off : 6 - row_off + tile_rows, 6 - col_off : 6 - col_off + tile_cols
            ].astype(jnp.float32)
            result = result + kernel[row_off, col_off] * window
    return result


def pointwise(
    conv_rows,
    field_rows,
    mask_rows,
    cot_rows,
    layer_norm_gain,
    layer_norm_bias,
    w_in,
    b_in,
    w_out,
    b_out,
    layer_scale,
):
    average = jnp.mean(conv_rows, axis=-1, keepdims=True)
    mean_centered = conv_rows - average
    variance = jnp.mean(mean_centered * mean_centered, axis=-1, keepdims=True)
    inverse_deviation = lax.rsqrt(variance + 1e-06)
    standardized_input = mean_centered * inverse_deviation
    normalized_input = (standardized_input * layer_norm_gain + layer_norm_bias).astype(jnp.bfloat16)
    pre_act = jnp.dot(normalized_input, w_in, preferred_element_type=jnp.float32) + b_in
    activ = jax.nn.gelu(pre_act).astype(jnp.bfloat16)
    residual_branch = jnp.dot(activ, w_out, preferred_element_type=jnp.float32) + b_out
    ocean_mask = mask_rows.astype(jnp.float32)[:, None]
    mixed = (field_rows.astype(jnp.float32) + ocean_mask * layer_scale * residual_branch).astype(
        jnp.bfloat16
    )
    cotangent_field = cot_rows.astype(jnp.float32)
    branch_field_gradient = ocean_mask * layer_scale * cotangent_field
    d_branch = branch_field_gradient.astype(jnp.bfloat16)
    d_act = jnp.dot(d_branch, w_out.T, preferred_element_type=jnp.float32)
    _, gelu_back = jax.vjp(jax.nn.gelu, pre_act)
    preactivation_gradient = gelu_back(d_act)[0]
    d_pre_b = preactivation_gradient.astype(jnp.bfloat16)
    normalized_gradient = jnp.dot(d_pre_b, w_in.T, preferred_element_type=jnp.float32)
    scaled_branch = normalized_gradient * layer_norm_gain
    convolution_gradient = inverse_deviation * (
        scaled_branch
        - jnp.mean(scaled_branch, axis=-1, keepdims=True)
        - standardized_input * jnp.mean(scaled_branch * standardized_input, axis=-1, keepdims=True)
    )
    partial_totals = (
        jnp.sum(ocean_mask * cotangent_field * residual_branch, axis=0),
        jnp.sum(branch_field_gradient, axis=0),
        jnp.sum(preactivation_gradient, axis=0),
        jnp.sum(normalized_gradient * standardized_input, axis=0),
        jnp.sum(normalized_gradient, axis=0),
    )
    return (
        mixed,
        convolution_gradient.astype(jnp.bfloat16),
        partial_totals,
        activ,
        d_branch,
        normalized_input,
        d_pre_b,
    )


def per_device(
    fields,
    land_mask,
    cotangent,
    kernel,
    layer_norm_gain,
    layer_norm_bias,
    w_in,
    b_in,
    w_out,
    b_out,
    layer_scale,
):
    tile_rows, tile_cols, channels = fields.shape
    cells = tile_rows * tile_cols
    masked = fields * land_mask.astype(jnp.bfloat16)[:, :, None]
    side_ext = extended(masked, (("lon", 1),), 3, True)
    padded = extended(side_ext, (("lat", 0),), 3, False)
    conv = depthwise(padded, kernel, tile_rows, tile_cols).reshape(cells, channels)
    mixed, convolution_gradient, partial_totals, activ, d_branch, normalized_input, d_pre_b = (
        pointwise(
            conv,
            fields.reshape(cells, channels),
            land_mask.reshape(cells),
            cotangent.reshape(cells, channels),
            layer_norm_gain,
            layer_norm_bias,
            w_in,
            b_in,
            w_out,
            b_out,
            layer_scale,
        )
    )
    convolution_gradient = convolution_gradient.reshape(tile_rows, tile_cols, channels)
    d_side = extended(convolution_gradient, (("lon", 1),), 3, True)
    d_padded = extended(d_side, (("lat", 0),), 3, False)
    d_masked = input_grad(d_padded, kernel, tile_rows, tile_cols)
    ocean_mask = land_mask.astype(jnp.float32)[:, :, None]
    grad_fields = (cotangent.astype(jnp.float32) + ocean_mask * d_masked).astype(jnp.bfloat16)
    local_kernel = kernel_grad(padded, convolution_gradient, tile_rows, tile_cols)
    grad_k, grad_sc, grad_bo, grad_bi, grad_ga, grad_sh = lax.psum(
        (
            local_kernel,
            partial_totals[0],
            partial_totals[1],
            partial_totals[2],
            partial_totals[3],
            partial_totals[4],
        ),
        ("lon", "lat"),
    )
    in_term = jnp.dot(normalized_input.T, d_pre_b, preferred_element_type=jnp.float32)
    grad_wo = lax.psum_scatter(
        jnp.dot(activ.T, d_branch, preferred_element_type=jnp.float32),
        ("lon", "lat"),
        scatter_dimension=0,
        tiled=True,
    )
    grad_wi = lax.psum_scatter(in_term, ("lon", "lat"), scatter_dimension=1, tiled=True)
    mixed = mixed.reshape(tile_rows, tile_cols, channels)
    return (
        mixed,
        grad_fields,
        grad_k,
        grad_ga,
        grad_sh,
        grad_wi,
        grad_bi,
        grad_wo,
        grad_bo,
        grad_sc,
    )


def solution(mesh):
    placed = (
        P(("grp", "lat"), "lon", None),
        P(("grp", "lat"), "lon"),
        P(("grp", "lat"), "lon", None),
        P(),
        P(),
        P(),
        P(),
        P(),
        P(),
        P(),
        P(),
    )
    return jax.shard_map(
        per_device,
        mesh=mesh,
        in_specs=placed,
        out_specs=(
            P(("grp", "lat"), "lon", None),
            P(("grp", "lat"), "lon", None),
            P("grp", None, None),
            P("grp"),
            P("grp"),
            P("grp", ("lon", "lat")),
            P("grp"),
            P(("lon", "lat"), "grp"),
            P("grp"),
            P("grp"),
        ),
        check_vma=False,
    )
```

profile of v0, /device:TPU:0, one launch (start us, length us, event | category | flops | bytes accessed | tf_op | source)
XLA Modules:
  0.0 345.8 jit_solution(4636488289154403921)
XLA Ops:
  11.0 2.0 collective-permute-start.1
  17.2 3.5 %collective-permute-start.2 = (bf16[3,38,512]{2,1,0:T(8,128)(2,1)S(1)}, bf16[3,38,512]{2,1,0:T(8,128)(2,1)S(1)}, u32[]{:S(2)}, u32[]{:S(2)}) collective-permute-start(bf16[3,38,512]{2,1,0:T(8,128)(2,1)S(1)} %get-tuple-element.85), channel_id=1, source_target_pairs={{0,1},{1,2},{2,3},{4,5},{5,6},{6,7},{8,9},{9,10},{10,11},{12,13},{... | collective-permute-start | bytes 350216 | tf_op jit(solution)/shard_map/ppermute | solution.py:15
  24.3 4.4 %collective-permute-done.3 = bf16[3,38,512]{2,1,0:T(8,128)(2,1)S(1)} collective-permute-done((bf16[3,38,512]{2,1,0:T(8,128)(2,1)S(1)}, bf16[3,38,512]{2,1,0:T(8,128)(2,1)S(1)}, u32[]{:S(2)}, u32[]{:S(2)}) %collective-permute-start.3) | collective-permute-done | bytes 116768 | tf_op jit(solution)/shard_map/ppermute | solution.py:17
  28.7 2.9 maximum_maximum_fusion
  32.1 16.4 %fusion.148 = (f32[32,32]{1,0:T(8,128)S(1)}, f32[32,32,512]{2,1,0:T(8,128)}) fusion(bf16[35,38,512]{2,1,0:T(8,128)(2,1)S(1)} %get-tuple-element.84, f32[512]{0:T(512)S(1)} %bitcast.282, f32[512]{0:T(512)S(1)} %bitcast.284, f32[512]{0:T(512)S(1)} %bitcast.190, f32[512]{0:T(512)S(1)} %bitcast.192, f32[512]{0:T(512)S(1)} %bitcast.194, f32[512]{0:T(512)S(1)} %bitcast.196, ...), kind=kLoop, calls=%fused_computation.297 | loop fusion | flops 86506496 | bytes 47486976 | tf_op jit(solution)/shard_map/reduce_sum | solution.py:71
  49.9 2.0 multiply_reduce_fusion.2
  53.3 2.0 add_convert_fusion
  55.4 4.2 %multiply_convert_fusion = (bf16[1024,2048]{1,0:T(8,128)(2,1)S(1)}, f32[1024,2048]{1,0:T(8,128)S(1)}) fusion(f32[2048]{0:T(1024)S(1)} %copy-done.153, bf16[1024,512]{1,0:T(8,128)(2,1)S(1)} %add_convert_fusion, bf16[512,2048]{1,0:T(8,128)(2,1)S(1)} %copy-done), kind=kOutput, calls=%fused_computation.58 | convolution fusion | flops 2168455168 | bytes 15736832 | tf_op jit(solution)/shard_map/dot_general | solution.py:77
  59.7 4.3 %fusion.134 = (f32[512]{0:T(512)}, bf16[1024,512]{1,0:T(8,128)(2,1)}, bf16[1024,512]{1,0:T(8,128)(2,1)S(1)}) fusion(bf16[32,32,512]{2,1,0:T(8,128)(2,1)S(1)} %copy-done.12, f32[512]{0:T(512)S(1)} %copy-done.154, f32[1024]{0:T(1024)S(1)} %copy-done.149, f32[512]{0:T(512)S(1)} %copy-done.150, bf16[32,32,512]{2,1,0:T(8,128)(2,1)S(1)} %copy-done.21, ...), kind=kOutput, calls=%fused_computation.241 | convolution fusion | flops 2153774592 | bytes 10496000 | tf_op jit(solution)/shard_map/dot_general | solution.py:79
  64.0 8.6 %fusion.156 = (f32[2048]{0:T(1024)}, bf16[1024,2048]{1,0:T(8,128)(2,1)S(1)}) fusion(f32[1024,2048]{1,0:T(8,128)S(1)} %get-tuple-element.144, f32[2048]{0:T(1024)S(1)} %copy-done.153, bf16[1024,512]{1,0:T(8,128)(2,1)S(1)} %get-tuple-element.87, bf16[2048,512]{1,0:T(8,128)(2,1)S(1)} %copy-done.152), kind=kOutput, calls=%fused_computation.304 | convolution fusion | flops 2193618944 | bytes 15745024 | tf_op jit(solution)/shard_map/dot_general | solution.py:87
  72.6 3.5 %multiply_reduce_fusion = (f32[512]{0:T(512)}, f32[1024]{0:T(1024)S(1)}, f32[1024]{0:T(1024)S(1)}, f32[512]{0:T(512)}, f32[1024,512]{1,0:T(8,128)S(1)}) fusion(f32[32,32,512]{2,1,0:T(8,128)S(1)} %copy-done.5, f32[1024]{0:T(1024)S(1)} %rsqrt.12, f32[1024]{0:T(1024)S(1)} %div.15, f32[512]{0:T(512)S(1)} %copy-done.111, bf16[512,2048]{1,0:T(8,128)(2,1)S(1)} %copy-done, ...), kind=kOutput, calls=%fused_computation.244 | convolution fusion | flops 2152199168 | bytes 10508288 | tf_op jit(solution)/shard_map/dot_general | solution.py:91
  76.2 7.2 %fusion.130 = (f32[512]{0:T(512)}, f32[512]{0:T(512)}, f32[512]{0:T(512)}, f32[512]{0:T(512)}, f32[512]{0:T(512)}, /*index=5*/f32[512]{0:T(512)}, f32[512]{0:T(5...) fusion(bf16[35,38,512]{2,1,0:T(8,128)(2,1)S(1)} %get-tuple-elem, ...), kind=kLoop, calls=%fused_computation.234 | loop fusion | flops 33020928 | bytes 24172544 | tf_op jit(solution)/shard_map/reduce_sum | solution.py:43
  83.4 5.8 %fusion.102 = (f32[512]{0:T(512)}, f32[512]{0:T(512)}, f32[512]{0:T(512)}, f32[512]{0:T(512)}, f32[512]{0:T(512)}, /*index=5*/f32[512]{0:T(512)}, f32[512]{0:T(5...) fusion(bf16[35,38,512]{2,1,0:T(8,128)(2,1)S(1)} %copy-done.2, ...), kind=kLoop, calls=%fused_computation.206 | loop fusion | flops 28826624 | bytes 19959808 | tf_op jit(solution)/shard_map/reduce_sum | solution.py:43
  89.2 2.4 fusion.112
  91.9 2.6 fusion.109
  96.5 6.8 %fusion.157 = f32[2048,512]{1,0:T(8,128)} fusion(bf16[1024,2048]{1,0:T(8,128)(2,1)} %copy-done.155, bf16[1024,512]{1,0:T(8,128)(2,1)} %copy-done.156), kind=kOutput, calls=%fused_computation.305 | convolution fusion | flops 2147483648 | bytes 9437184 | tf_op jit(solution)/shard_map/dot_general | solution.py:170
  104.6 6.6 %fusion.136 = f32[512,2048]{1,0:T(8,128)} fusion(bf16[1024,512]{1,0:T(8,128)(2,1)S(1)} %copy-done.11, bf16[1024,2048]{1,0:T(8,128)(2,1)} %copy-done.9), kind=kOutput, calls=%fused_computation.247 | convolution fusion | flops 2147483648 | bytes 9437184 | tf_op jit(solution)/shard_map/dot_general | solution.py:168
  114.3 2.6 collective-permute-done.4
  119.0 5.2 %collective-permute-start.7 = (bf16[3,38,512]{2,1,0:T(8,128)(2,1)}, bf16[3,38,512]{2,1,0:T(8,128)(2,1)}, u32[]{:S(2)}, u32[]{:S(2)}) collective-permute-start(bf16[3,38,512]{2,1,0:T(8,128)(2,1)} %get-tuple-element.82), channel_id=1, source_target_pairs={{0,1},{1,2},{2,3},{4,5},{5,6},{6,7},{8,9},{9,10},{10,11},{12,13},{... | collective-permute-start | bytes 350216 | tf_op jit(solution)/shard_map/ppermute | solution.py:15
  124.6 60.0 %all-reduce = (f32[512]{0:T(512)}, f32[512]{0:T(512)}, f32[2048]{0:T(1024)}, f32[512]{0:T(512)}, f32[512]{0:T(512)}) all-reduce(f32[512]{0:T(512)} %get-tuple-element.10, f32[512]{0:T(512)} %get-tuple-element.61, f32[2048]{0:T(1024)} %get-tuple-element.146, ...), channel_id=1, replica_groups=mesh['grp'=2,'lon'=4,'lat'=4] {'lon','lat'}, use_global_device_ids=true, to_apply=%region_55.0 | all-reduce | flops 4096 | bytes 32768 | tf_op jit(solution)/shard_map/psum | solution.py:157
  185.0 2.6 pad_maximum_fusion.1
  188.0 16.7 %fusion.131 = bf16[32,32,512]{2,1,0:T(8,128)(2,1)} fusion(bf16[32,32,512]{2,1,0:T(8,128)(2,1)S(1)} %copy-done.14, bf16[32,32,512]{2,1,0:T(8,128)(2,1)S(1)} %bitcast.187, bf16[32,3,512]{2,1,0:T(4,128)(2,1)S(1)} %collective-permute-done.4, bf16[32,3,512]{2,1,0:T(4,128)(2,1)S(1)} %collective-permute-done.5, bf16[35,38,512]{2,1,0:T(8,128)(2,1)S(1)} %get-tuple-element.80, ...), kind=kLoop, calls=%fused_computation.238 | loop fusion | flops 88080384 | bytes 47486976 | tf_op jit(solution)/shard_map/convert_element_type | solution.py:155
  204.7 56.6 %reduce-scatter.5.cloned.1.call-done = f32[128,512]{1,0:T(8,128)} async-done(((f32[2048,512]{1,0:T(8,128)}), f32[128,512]{1,0:T(8,128)}) %reduce-scatter.5.cloned.1.call-update) | async-done | bytes 262160 | tf_op jit(solution)/shard_map/reduce_scatter | solution.py:169
  261.2 76.4 %reduce-scatter.3.cloned.1.call-done = f32[512,128]{1,0:T(8,128)} async-done(((f32[512,2048]{1,0:T(8,128)}), f32[512,128]{1,0:T(8,128)}) %reduce-scatter.3.cloned.1.call-update) | async-done | bytes 262160 | tf_op jit(solution)/shard_map/reduce_scatter | solution.py:175
  (351 shorter events, 24.5 us)
Async XLA Ops:
  7.2 48.1 %copy-start = (bf16[512,2048]{1,0:T(8,128)(2,1)S(1)}, bf16[512,2048]{1,0:T(8,128)(2,1)}, u32[]{:S(2)}) copy-start(bf16[512,2048]{1,0:T(8,128)(2,1)} %param.17) | copy-start | bytes 6291460
  7.2 197.4 %all-reduce.3.cloned.1.call-start = ((), (), s32[]{:S(2)}) async-start(), calls=%async_computation.2 | async-start | bytes 229376 | tf_op jit(solution)/shard_map/psum | solution.py:157
  9.6 14.7 %copy-start.6 = (bf16[32,32,512]{2,1,0:T(8,128)(2,1)}, bf16[32,32,512]{2,1,0:T(8,128)(2,1)S(1)}, u32[]{:S(2)}) copy-start(bf16[32,32,512]{2,1,0:T(8,128)(2,1)S(1)} %broadcast_multiply_fusion) | copy-start | bytes 3145732
  10.5 5.3 %collective-permute-start = (bf16[32,3,512]{2,1,0:T(4,128)(2,1)}, bf16[32,3,512]{2,1,0:T(4,128)(2,1)S(1)}, u32[]{:S(2)}, u32[]{:S(2)}) collective-permute-start(bf16[32,3,512]{2,1,0:T(4,128)(2,1)} %get-tuple-element.90), channel_id=1, source_target_pairs={{0,4},{4,8},{8,12},{12,0},{1,5},{5,9},{9,13},{13,1},{2,6},{6,10},{... | collective-permute-start | bytes 294920 | tf_op jit(solution)/shard_map/ppermute | solution.py:15
  11.0 6.1 %collective-permute-start.1 = (bf16[32,3,512]{2,1,0:T(4,128)(2,1)}, bf16[32,3,512]{2,1,0:T(4,128)(2,1)S(1)}, u32[]{:S(2)}, u32[]{:S(2)}) collective-permute-start(bf16[32,3,512]{2,1,0:T(4,128)(2,1)} %get-tuple-element.91), channel_id=1, source_target_pairs={{4,0},{8,4},{12,8},{0,12},{5,1},{9,5},{13,9},{1,13},{6,2},{10,6},{... | collective-permute-start | bytes 294920 | tf_op jit(solution)/shard_map/ppermute | solution.py:17
  13.6 18.0 %copy-start.23 = (f32[1,1,512]{2,1,0:T(1,128)}, f32[1,1,512]{2,1,0:T(1,128)S(1)}, u32[]{:S(2)}) copy-start(f32[1,1,512]{2,1,0:T(1,128)S(1)} %get-tuple-element.92) | copy-start | bytes 6148
  13.6 18.0 %copy-start.25 = (f32[1,1,512]{2,1,0:T(1,128)}, f32[1,1,512]{2,1,0:T(1,128)S(1)}, u32[]{:S(2)}) copy-start(f32[1,1,512]{2,1,0:T(1,128)S(1)} %get-tuple-element.93) | copy-start | bytes 6148
  17.2 7.1 %collective-permute-start.2 = (bf16[3,38,512]{2,1,0:T(8,128)(2,1)S(1)}, bf16[3,38,512]{2,1,0:T(8,128)(2,1)S(1)}, u32[]{:S(2)}, u32[]{:S(2)}) collective-permute-start(bf16[3,38,512]{2,1,0:T(8,128)(2,1)S(1)} %get-tuple-element.85), channel_id=1, source_target_pairs={{0,1},{1,2},{2,3},{4,5},{5,6},{6,7},{8,9},{9,10},{10,11},{12,13},{... | collective-permute-start | bytes 350216 | tf_op jit(solution)/shard_map/ppermute | solution.py:15
  20.7 7.9 %collective-permute-start.3 = (bf16[3,38,512]{2,1,0:T(8,128)(2,1)S(1)}, bf16[3,38,512]{2,1,0:T(8,128)(2,1)S(1)}, u32[]{:S(2)}, u32[]{:S(2)}) collective-permute-start(bf16[3,38,512]{2,1,0:T(8,128)(2,1)S(1)} %get-tuple-element.86), channel_id=1, source_target_pairs={{1,0},{2,1},{3,2},{5,4},{6,5},{7,6},{9,8},{10,9},{11,10},{13,12},{... | collective-permute-start | bytes 350216 | tf_op jit(solution)/shard_map/ppermute | solution.py:17
  23.0 8.7 %copy-start.99 = (f32[1,1,512]{2,1,0:T(1,128)}, f32[1,1,512]{2,1,0:T(1,128)S(1)}, u32[]{:S(2)}) copy-start(f32[1,1,512]{2,1,0:T(1,128)S(1)} %get-tuple-element.130) | copy-start | bytes 6148
  23.0 8.7 %copy-start.101 = (f32[1,1,512]{2,1,0:T(1,128)}, f32[1,1,512]{2,1,0:T(1,128)S(1)}, u32[]{:S(2)}) copy-start(f32[1,1,512]{2,1,0:T(1,128)S(1)} %get-tuple-element.131) | copy-start | bytes 6148
  23.0 8.7 %copy-start.102 = (f32[1,1,512]{2,1,0:T(1,128)}, f32[1,1,512]{2,1,0:T(1,128)S(1)}, u32[]{:S(2)}) copy-start(f32[1,1,512]{2,1,0:T(1,128)S(1)} %get-tuple-element.132) | copy-start | bytes 6148
  23.0 8.7 %copy-start.103 = (f32[1,1,512]{2,1,0:T(1,128)}, f32[1,1,512]{2,1,0:T(1,128)S(1)}, u32[]{:S(2)}) copy-start(f32[1,1,512]{2,1,0:T(1,128)S(1)} %get-tuple-element.133) | copy-start | bytes 6148
  23.0 8.7 %copy-start.104 = (f32[1,1,512]{2,1,0:T(1,128)}, f32[1,1,512]{2,1,0:T(1,128)S(1)}, u32[]{:S(2)}) copy-start(f32[1,1,512]{2,1,0:T(1,128)S(1)} %get-tuple-element.134) | copy-start | bytes 6148
  23.0 8.7 %copy-start.105 = (f32[1,1,512]{2,1,0:T(1,128)}, f32[1,1,512]{2,1,0:T(1,128)S(1)}, u32[]{:S(2)}) copy-start(f32[1,1,512]{2,1,0:T(1,128)S(1)} %get-tuple-element.135) | copy-start | bytes 6148
  31.6 16.9 %copy-start.1 = (bf16[35,38,512]{2,1,0:T(8,128)(2,1)}, bf16[35,38,512]{2,1,0:T(8,128)(2,1)S(1)}, u32[]{:S(2)}) copy-start(bf16[35,38,512]{2,1,0:T(8,128)(2,1)S(1)} %get-tuple-element.83) | copy-start | bytes 4085764
  96.5 164.7 %reduce-scatter.5.cloned.1.call-start = ((), (), s32[]{:S(2)}) async-start(), calls=%async_computation.4 | async-start | bytes 4456448 | tf_op jit(solution)/shard_map/reduce_scatter | solution.py:169
  103.4 234.3 %reduce-scatter.3.cloned.1.call-start = ((), (), s32[]{:S(2)}) async-start(), calls=%async_computation.3 | async-start | bytes 4456448 | tf_op jit(solution)/shard_map/reduce_scatter | solution.py:175
  111.2 13.1 %copy-start.151 = (f32[512]{0:T(512)S(1)}, f32[512]{0:T(512)}, u32[]{:S(2)}) copy-start(f32[512]{0:T(512)} %param.21) | copy-start | bytes 6148
  111.2 13.0 %copy-start.13 = (bf16[32,32,512]{2,1,0:T(8,128)(2,1)S(1)}, bf16[32,32,512]{2,1,0:T(8,128)(2,1)}, u32[]{:S(2)}) copy-start(bf16[32,32,512]{2,1,0:T(8,128)(2,1)} %param.13) | copy-start | bytes 3145732
  112.5 4.4 %collective-permute-start.4 = (bf16[32,3,512]{2,1,0:T(4,128)(2,1)S(1)}, bf16[32,3,512]{2,1,0:T(4,128)(2,1)S(1)}, u32[]{:S(2)}, u32[]{:S(2)}) collective-permute-start(bf16[32,3,512]{2,1,0:T(4,128)(2,1)S(1)} %get-tuple-element.89), channel_id=1, source_target_pairs={{0,4},{4,8},{8,12},{12,0},{1,5},{5,9},{9,13},{13,1},{2,6},{6,10},{... | collective-permute-start | bytes 294920 | tf_op jit(solution)/shard_map/ppermute | solution.py:15
  112.6 4.4 %collective-permute-start.5 = (bf16[32,3,512]{2,1,0:T(4,128)(2,1)S(1)}, bf16[32,3,512]{2,1,0:T(4,128)(2,1)S(1)}, u32[]{:S(2)}, u32[]{:S(2)}) collective-permute-start(bf16[32,3,512]{2,1,0:T(4,128)(2,1)S(1)} %get-tuple-element.88), channel_id=1, source_target_pairs={{4,0},{8,4},{12,8},{0,12},{5,1},{9,5},{13,9},{1,13},{6,2},{10,6},{... | collective-permute-start | bytes 294920 | tf_op jit(solution)/shard_map/ppermute | solution.py:17
  117.7 67.2 %collective-permute-start.6 = (bf16[3,38,512]{2,1,0:T(8,128)(2,1)}, bf16[3,38,512]{2,1,0:T(8,128)(2,1)S(1)}, u32[]{:S(2)}, u32[]{:S(2)}) collective-permute-start(bf16[3,38,512]{2,1,0:T(8,128)(2,1)} %get-tuple-element.81), channel_id=1, source_target_pairs={{1,0},{2,1},{3,2},{5,4},{6,5},{7,6},{9,8},{10,9},{11,10},{13,12},{... | collective-permute-start | bytes 350216 | tf_op jit(solution)/shard_map/ppermute | solution.py:17
  119.0 65.9 %collective-permute-start.7 = (bf16[3,38,512]{2,1,0:T(8,128)(2,1)}, bf16[3,38,512]{2,1,0:T(8,128)(2,1)}, u32[]{:S(2)}, u32[]{:S(2)}) collective-permute-start(bf16[3,38,512]{2,1,0:T(8,128)(2,1)} %get-tuple-element.82), channel_id=1, source_target_pairs={{0,1},{1,2},{2,3},{4,5},{5,6},{6,7},{8,9},{9,10},{10,11},{12,13},{... | collective-permute-start | bytes 350216 | tf_op jit(solution)/shard_map/ppermute | solution.py:15
  (144 other events, 707.7 us)
Sparse Core Ops, SparseCore 0:
  96.6 85.5 all-reduce.2
  186.6 74.5 reduce-scatter.4
  266.2 71.4 reduce-scatter.2
where the time goes:
time: 346 us
  waiting for transfers between devices  143 us (41%)
  other arithmetic  65.3 us (19%)
  blocking collectives  60 us (17%)
  matrix products  34 us (10%)
  between operations  16.1 us (5%)
  starting transfers between devices  15.8 us (5%)
  local copies, waits for them, and re-layouts  11.5 us (3%)
    reduce_scatter x1, waiting for transfers between devices, per_device(): lax.psum_scatter(in_term, ('lon', 'lat'), scatter_dimension=1, tiled=True)  76.4 us
    psum x1, blocking collectives, per_device(): lax.psum((local_kernel, partial_totals[0], partial_totals[1], partial_tot...  60 us
    reduce_scatter x1, waiting for transfers between devices, per_device(): lax.psum_scatter(jnp.dot(activ.T, d_branch, preferred_element_type=jnp.fl...  56.6 us
    reduce_sum x4, other arithmetic, kernel_grad(): entries.append(jnp.sum(grad_f * window, axis=(0, 1)))  18 us
    convert_element_type x1, other arithmetic, per_device(): (cotangent.astype(jnp.float32) + ocean_mask * d_masked).astype(jnp.bfloat16)  16.7 us
    reduce_sum x1, other arithmetic, pointwise(): average = jnp.mean(conv_rows, axis=-1, keepdims=True)  16.4 us
    ppermute x4, starting transfers between devices, extended(): lax.ppermute(tail, axis, [(i, (i + 1) % count) for i in range(ends)])  9.2 us
    dot_general x1, matrix products, pointwise(): d_act = jnp.dot(d_branch, w_out.T, preferred_element_type=jnp.float32)  8.59 us
  transfers between devices with their start and end apart: 11, of which 7 were waited for; matrix products, arithmetic and copies ran while one was open for 11% of the time, Pallas kernels for 0%

commit v1 on v0

v1 whole, which is shorter than its diff:
```python
import functools
import math

import jax
import jax.numpy as jnp
from jax import lax
from jax.experimental import pallas as pl
from jax.experimental.pallas import tpu as pltpu
from jax.sharding import PartitionSpec as P

F32 = jnp.float32
BF16 = jnp.bfloat16
LANES = 128
SUB = 8
VMEM_LIMIT = 56 * 1024 * 1024


def params():
    return pltpu.CompilerParams(vmem_limit_bytes=VMEM_LIMIT)


def whole_spec(shape):
    zeros = (0,) * len(shape)
    return pl.BlockSpec(shape, lambda *_: zeros)


def shifted(window, row, start, offset):
    return window[row, pl.ds(start + offset, SUB), :]


def band_conv(window, taps, start, rows, pad):
    sums = [None] * rows
    for col_off in range(7):
        weights = [taps(row_off, col_off) for row_off in range(7)]
        for src in range(window.shape[0]):
            hits = [(src - pad - row_off + 3, row_off) for row_off in range(7)]
            hits = [(out, row_off) for out, row_off in hits if 0 <= out < rows]
            if not hits:
                continue
            cells = shifted(window, src, start, 5 + col_off)
            for out, row_off in hits:
                term = weights[row_off] * cells
                sums[out] = term if sums[out] is None else sums[out] + term
    return sums


def conv_inner_kernel(f_ref, m_ref, k_ref, o_ref, window):
    rows, cols, _ = f_ref.shape
    window[:, 8 : 8 + cols, :] = f_ref[...].astype(F32) * m_ref[...]
    for start in range(8, cols - 8, 8):
        sums = band_conv(window, lambda p, q: k_ref[pl.ds(p * 7 + q, 1), :], start, rows, 0)
        for row in range(rows):
            o_ref[row, start - 8 : start, :] = sums[row]


def conv_side_kernel(f_ref, m_ref, k_ref, l_ref, r_ref, o_ref, window):
    rows, cols, _ = f_ref.shape
    window[:, 5:8, :] = l_ref[...].astype(F32)
    window[:, 8 : 8 + cols, :] = f_ref[...].astype(F32) * m_ref[...]
    window[:, 8 + cols : 11 + cols, :] = r_ref[...].astype(F32)
    for at, start in ((0, 0), (8, cols - 8)):
        sums = band_conv(window, lambda p, q: k_ref[pl.ds(p * 7 + q, 1), :], start, rows, 0)
        for row in range(rows):
            o_ref[row, at : at + 8, :] = sums[row]


def by_channels(shape):
    return pl.BlockSpec(shape[:-1] + (LANES,), lambda c: (0,) * (len(shape) - 1) + (c,))


def conv_cost(rows, cols, channels):
    return pl.CostEstimate(
        flops=98 * rows * cols * channels, bytes_accessed=6 * rows * cols * channels, transcendentals=0
    )


def conv_inner(fields, mask_b, taps):
    rows, cols, channels = fields.shape
    return pl.pallas_call(
        conv_inner_kernel,
        grid=(channels // LANES,),
        out_shape=jax.ShapeDtypeStruct((rows, cols - 16, channels), F32),
        in_specs=[by_channels(fields.shape), whole_spec(mask_b.shape), by_channels(taps.shape)],
        out_specs=by_channels((rows, cols - 16, channels)),
        scratch_shapes=[pltpu.VMEM((rows, cols + 16, LANES), F32)],
        compiler_params=params(),
        cost_estimate=conv_cost(rows, cols - 16, channels),
        name="conv_inner",
    )(fields, mask_b, taps)


def conv_side(fields, mask_b, taps, left, right):
    rows, cols, channels = fields.shape
    return pl.pallas_call(
        conv_side_kernel,
        grid=(channels // LANES,),
        out_shape=jax.ShapeDtypeStruct((rows, 16, channels), F32),
        in_specs=[
            by_channels(fields.shape),
            whole_spec(mask_b.shape),
            by_channels(taps.shape),
            by_channels(left.shape),
            by_channels(right.shape),
        ],
        out_specs=by_channels((rows, 16, channels)),
        scratch_shapes=[pltpu.VMEM((rows, cols + 16, LANES), F32)],
        compiler_params=params(),
        cost_estimate=conv_cost(rows, 16, channels),
        name="conv_side",
    )(fields, mask_b, taps, left, right)


def gelu_pair(x):
    root = math.sqrt(2.0 / math.pi)
    square = x * x
    half = 0.5 * jnp.tanh(x * (root + (root * 0.044715) * square)) + 0.5
    value = x * half
    slope = half + 2.0 * value * (1.0 - half) * (root + (3.0 * root * 0.044715) * square)
    return value, slope


def expand_kernel(
    inner_ref, side_ref, top_ref, bot_ref, k_ref, gain_ref, bias_ref, scale_ref, m_ref, cot_ref,
    wi_ref, bi_ref, wo_ref,
    xhat_ref, inv_ref, act_ref, dpre_ref, gwo_ref, gwi_ref, gbi_ref, gbo_ref,
    conv, halo, normed, normed_t, dbr, dbr_t,
):
    rows, cols, channels = conv.shape
    cells = rows * cols

    @pl.when(pl.program_id(0) == 0)
    def _():
        conv[:, 0:8, :] = side_ref[:, 0:8, :]
        conv[:, 8 : cols - 8, :] = inner_ref[...]
        conv[:, cols - 8 : cols, :] = side_ref[:, 8:16, :]
        halo[0:3, 5 : 11 + cols, :] = top_ref[...].astype(F32)
        halo[3:6, 5 : 11 + cols, :] = bot_ref[...].astype(F32)
        for block in range(channels // LANES):
            lanes = slice(block * LANES, (block + 1) * LANES)
            for start in range(0, cols, 8):
                outs = list(range(3)) + list(range(rows - 3, rows))
                sums = {out: conv[out, start : start + 8, lanes] for out in outs}
                for col_off in range(7):
                    for src in range(6):
                        lat = src - 3 if src < 3 else rows + src - 3
                        cell = halo[src, start + 5 + col_off : start + 13 + col_off, lanes]
                        for out in outs:
                            row_off = lat - out + 3
                            if 0 <= row_off < 7:
                                tap = k_ref[row_off * 7 + col_off : row_off * 7 + col_off + 1, lanes]
                                sums[out] = sums[out] + tap * cell
                for out in outs:
                    conv[out, start : start + 8, lanes] = sums[out]
        gbo_ref[...] = jnp.zeros_like(gbo_ref)

        chunk = 128
        chunk_rows = chunk // cols

        def standardize(step, _):
            at = pl.multiple_of(step * chunk, chunk)
            here = pl.ds(at, chunk)
            x = conv[pl.ds(step * chunk_rows, chunk_rows)].reshape(chunk, channels)
            mean = jnp.mean(x, axis=-1, keepdims=True)
            centered = x - mean
            var = jnp.mean(centered * centered, axis=-1, keepdims=True)
            inv = lax.rsqrt(var + 1e-06)
            xhat = centered * inv
            xhat_ref[here, :] = xhat
            inv_ref[here, :] = jnp.broadcast_to(inv, (chunk, LANES))
            scaled = xhat * gain_ref[...] + bias_ref[...]
            normed[here, :] = scaled.astype(BF16)
            normed_t[:, here] = scaled.T.astype(BF16)
            ocean = jnp.concatenate([m_ref[here, :]] * (channels // LANES), axis=1)
            grad = ocean * scale_ref[...] * cot_ref[here, :].astype(F32)
            gbo_ref[...] += jnp.sum(grad, axis=0, keepdims=True)
            dbr[here, :] = grad.astype(BF16)
            dbr_t[:, here] = grad.T.astype(BF16)
            return 0

        lax.fori_loop(0, cells // chunk, standardize, 0)

    part = 256
    total = None
    for at in range(0, cells, part):
        here = slice(at, at + part)
        pre = jnp.dot(normed[here, :], wi_ref[...], preferred_element_type=F32) + bi_ref[...]
        d_act = lax.dot_general(
            dbr[here, :], wo_ref[...], (((1,), (1,)), ((), ())), preferred_element_type=F32
        )
        value, slope = gelu_pair(pre)
        act_ref[here, :] = value.astype(BF16)
        d_pre = d_act * slope
        dpre_ref[here, :] = d_pre.astype(BF16)
        sums = jnp.sum(d_pre, axis=0, keepdims=True)
        total = sums if total is None else total + sums
    gbi_ref[...] = total
    gwo = jnp.dot(dbr_t[...], act_ref[...], preferred_element_type=F32).astype(BF16)
    gwi = jnp.dot(normed_t[...], dpre_ref[...], preferred_element_type=F32).astype(BF16)
    parts, _, width = gwo_ref.shape
    for index in range(parts):
        gwo_ref[index] = gwo[:, index * width : (index + 1) * width]
        gwi_ref[index] = gwi[:, index * width : (index + 1) * width]


def expand(inner, side, top, bot, taps, gain, bias, scale, mask_b, cot, w_in, b_in, w_out, n_lon, n_lat):
    rows, _, channels = inner.shape
    hidden = w_in.shape[1]
    cells, _ = cot.shape
    cols = cells // rows
    block = hidden // n_lon
    split = n_lat if (block // n_lat) % LANES == 0 else 1
    grads = (n_lon, split, channels, block // split)
    grad_spec = pl.BlockSpec((None,) + grads[1:], lambda h: (h, 0, 0, 0))
    out = pl.pallas_call(
        expand_kernel,
        grid=(n_lon,),
        out_shape=[
            jax.ShapeDtypeStruct((cells, channels), F32),
            jax.ShapeDtypeStruct((cells, LANES), F32),
            jax.ShapeDtypeStruct((cells, hidden), BF16),
            jax.ShapeDtypeStruct((cells, hidden), BF16),
            jax.ShapeDtypeStruct(grads, BF16),
            jax.ShapeDtypeStruct(grads, BF16),
            jax.ShapeDtypeStruct((1, hidden), F32),
            jax.ShapeDtypeStruct((1, channels), F32),
        ],
        in_specs=[
            whole_spec(inner.shape),
            whole_spec(side.shape),
            whole_spec(top.shape),
            whole_spec(bot.shape),
            whole_spec(taps.shape),
            whole_spec(gain.shape),
            whole_spec(bias.shape),
            whole_spec(scale.shape),
            whole_spec(mask_b.shape),
            whole_spec(cot.shape),
            pl.BlockSpec((channels, block), lambda h: (0, h)),
            pl.BlockSpec((1, block), lambda h: (0, h)),
            pl.BlockSpec((block, channels), lambda h: (h, 0)),
        ],
        out_specs=[
            whole_spec((cells, channels)),
            whole_spec((cells, LANES)),
            pl.BlockSpec((cells, block), lambda h: (0, h)),
            pl.BlockSpec((cells, block), lambda h: (0, h)),
            grad_spec,
            grad_spec,
            pl.BlockSpec((1, block), lambda h: (0, h)),
            whole_spec((1, channels)),
        ],
        scratch_shapes=[
            pltpu.VMEM((rows, cols, channels), F32),
            pltpu.VMEM((6, cols + 16, channels), F32),
            pltpu.VMEM((cells, channels), BF16),
            pltpu.VMEM((channels, cells), BF16),
            pltpu.VMEM((cells, channels), BF16),
            pltpu.VMEM((channels, cells), BF16),
        ],
        compiler_params=params(),
        cost_estimate=pl.CostEstimate(
            flops=8 * cells * channels * hidden,
            bytes_accessed=20 * cells * channels,
            transcendentals=cells * hidden,
        ),
        name="expand",
    )(inner, side, top, bot, taps, gain, bias, scale, mask_b, cot, w_in, b_in, w_out)
    return out


def project_kernel(
    act_ref, dpre_ref, wo_ref, wi_ref, xhat_ref, inv_ref, f_ref, cot_ref, m_ref, scale_ref, gain_ref, bo_ref,
    mixed_ref, dconv_ref, sums_ref,
):
    channels = xhat_ref.shape[1]

    def wide(ref):
        return jnp.concatenate([ref[...]] * (channels // LANES), axis=1)

    @pl.when(pl.program_id(0) == 0)
    def _():
        sums_ref[...] = jnp.zeros_like(sums_ref)

    branch = jnp.dot(act_ref[...], wo_ref[...], preferred_element_type=F32) + bo_ref[...]
    d_normed = lax.dot_general(
        dpre_ref[...], wi_ref[...], (((1,), (1,)), ((), ())), preferred_element_type=F32
    )
    ocean = wide(m_ref) * branch
    mixed_ref[...] = (f_ref[...].astype(F32) + ocean * scale_ref[...]).astype(BF16)
    xhat = xhat_ref[...]
    normed_term = d_normed * xhat
    sums_ref[0:1, :] += jnp.sum(ocean * cot_ref[...].astype(F32), axis=0, keepdims=True)
    sums_ref[1:2, :] += jnp.sum(normed_term, axis=0, keepdims=True)
    sums_ref[2:3, :] += jnp.sum(d_normed, axis=0, keepdims=True)
    e = d_normed * gain_ref[...]
    m1 = jnp.mean(e, axis=-1, keepdims=True)
    m2 = jnp.mean(normed_term * gain_ref[...], axis=-1, keepdims=True)
    dconv_ref[...] = (wide(inv_ref) * (e - m1 - xhat * m2)).astype(BF16)


def project(act, dpre, w_out, w_in, xhat, inv, fields, cot, mask_b, scale, gain, b_out):
    cells, hidden = act.shape
    channels = w_out.shape[1]
    part = 256

    def rows_of(width):
        return pl.BlockSpec((part, width), lambda i: (i, 0))

    return pl.pallas_call(
        project_kernel,
        grid=(cells // part,),
        out_shape=[
            jax.ShapeDtypeStruct((cells, channels), BF16),
            jax.ShapeDtypeStruct((cells, channels), BF16),
            jax.ShapeDtypeStruct((SUB, channels), F32),
        ],
        in_specs=[
            rows_of(hidden),
            rows_of(hidden),
            whole_spec(w_out.shape),
            whole_spec(w_in.shape),
            rows_of(channels),
            rows_of(LANES),
            rows_of(channels),
            rows_of(channels),
            rows_of(LANES),
            whole_spec(scale.shape),
            whole_spec(gain.shape),
            whole_spec(b_out.shape),
        ],
        out_specs=[rows_of(channels), rows_of(channels), whole_spec((SUB, channels))],
        compiler_params=params(),
        cost_estimate=pl.CostEstimate(
            flops=4 * cells * channels * hidden, bytes_accessed=16 * cells * channels, transcendentals=0
        ),
        name="project",
    )(act, dpre, w_out, w_in, xhat, inv, fields, cot, mask_b, scale, gain, b_out)


def fill_window(window, center, left, right, top, bot):
    rows, cols, _ = center.shape
    window[3 : 3 + rows, 5:8, :] = left[...].astype(F32)
    window[3 : 3 + rows, 8 : 8 + cols, :] = center
    window[3 : 3 + rows, 8 + cols : 11 + cols, :] = right[...].astype(F32)
    window[0:3, 5 : 11 + cols, :] = top[...].astype(F32)
    window[3 + rows : 6 + rows, 5 : 11 + cols, :] = bot[...].astype(F32)


def filter_grad_kernel(f_ref, m_ref, l_ref, r_ref, t_ref, b_ref, d_ref, o_ref, window, grad):
    rows, cols, _ = f_ref.shape
    fill_window(window, f_ref[...].astype(F32) * m_ref[...], l_ref, r_ref, t_ref, b_ref)
    grad[...] = d_ref[...].astype(F32)
    for col_off in range(7):

        def band(index, sums):
            start = pl.multiple_of(index * 8, 8)
            sums = list(sums)
            held = {}
            for src in range(rows + 6):
                if src < rows:
                    held[src] = grad[src, pl.ds(start, SUB), :]
                cells = shifted(window, src, start, 5 + col_off)
                for row_off in range(7):
                    out = src - row_off
                    if 0 <= out < rows:
                        sums[row_off] = sums[row_off] + held[out] * cells
            return tuple(sums)

        start = tuple(jnp.zeros((SUB, LANES), F32) for _ in range(7))
        sums = lax.fori_loop(0, cols // 8, band, start)
        for row_off in range(7):
            at = row_off * 7 + col_off
            o_ref[at : at + 1, :] = jnp.sum(sums[row_off], axis=0, keepdims=True)


def filter_grad(fields, mask_b, left, right, top, bot, d_conv):
    rows, cols, channels = fields.shape
    return pl.pallas_call(
        filter_grad_kernel,
        grid=(channels // LANES,),
        out_shape=jax.ShapeDtypeStruct((49, channels), F32),
        in_specs=[
            by_channels(fields.shape),
            whole_spec(mask_b.shape),
            by_channels(left.shape),
            by_channels(right.shape),
            by_channels(top.shape),
            by_channels(bot.shape),
            by_channels(d_conv.shape),
        ],
        out_specs=by_channels((49, channels)),
        scratch_shapes=[
            pltpu.VMEM((rows + 6, cols + 16, LANES), F32),
            pltpu.VMEM((rows, cols, LANES), F32),
        ],
        compiler_params=params(),
        cost_estimate=conv_cost(rows, cols, channels),
        name="filter_grad",
    )(fields, mask_b, left, right, top, bot, d_conv)


def input_grad_kernel(d_ref, l_ref, r_ref, t_ref, b_ref, k_ref, m_ref, cot_ref, o_ref, window, grad):
    rows, cols, _ = d_ref.shape
    fill_window(window, d_ref[...].astype(F32), l_ref, r_ref, t_ref, b_ref)
    for start in range(0, cols, 8):
        sums = band_conv(window, lambda p, q: k_ref[pl.ds(48 - p * 7 - q, 1), :], start, rows, 3)
        for row in range(rows):
            grad[row, start : start + 8, :] = sums[row]
    o_ref[...] = (cot_ref[...].astype(F32) + m_ref[...] * grad[...]).astype(BF16)


def input_grad(d_conv, left, right, top, bot, taps, mask_b, cot):
    rows, cols, channels = d_conv.shape
    return pl.pallas_call(
        input_grad_kernel,
        grid=(channels // LANES,),
        out_shape=jax.ShapeDtypeStruct((rows, cols, channels), BF16),
        in_specs=[
            by_channels(d_conv.shape),
            by_channels(left.shape),
            by_channels(right.shape),
            by_channels(top.shape),
            by_channels(bot.shape),
            by_channels(taps.shape),
            whole_spec(mask_b.shape),
            by_channels(cot.shape),
        ],
        out_specs=by_channels((rows, cols, channels)),
        scratch_shapes=[
            pltpu.VMEM((rows + 6, cols + 16, LANES), F32),
            pltpu.VMEM((rows, cols, LANES), F32),
        ],
        compiler_params=params(),
        cost_estimate=conv_cost(rows, cols, channels),
        name="input_grad",
    )(d_conv, left, right, top, bot, taps, mask_b, cot)


def swap(values, axis, bit):
    count = lax.axis_size(axis)
    return lax.ppermute(values, axis, [(i, i ^ bit) for i in range(count)])


def bits_of(axis):
    return [1 << k for k in range(int(math.log2(lax.axis_size(axis))))]


def scatter_sum(values):
    for dim, axis in ((0, "lon"), (1, "lat")):
        for bit in bits_of(axis):
            mine = (lax.axis_index(axis) // bit) % 2
            shape = values.shape
            paired = values.reshape(shape[:dim] + (shape[dim] // 2, 2) + shape[dim + 1 :])
            kept = lax.dynamic_index_in_dim(paired, mine, dim + 1, keepdims=False)
            sent = lax.dynamic_index_in_dim(paired, 1 - mine, dim + 1, keepdims=False)
            values = kept.astype(F32) + swap(sent.astype(BF16), axis, bit).astype(F32)
    return values[0, 0]


def total_sum(values):
    for axis in ("lon", "lat"):
        for bit in bits_of(axis):
            values = values + swap(values, axis, bit)
    return values


def side_halo(cells):
    count = lax.axis_size("lon")
    ahead = [(i, (i + 1) % count) for i in range(count)]
    back = [((i + 1) % count, i) for i in range(count)]
    cols = cells.shape[1]
    return (
        lax.ppermute(cells[:, cols - 3 :], "lon", ahead),
        lax.ppermute(cells[:, :3], "lon", back),
    )


def end_halo(cells, left, right):
    count = lax.axis_size("lat")
    ahead = [(i, i + 1) for i in range(count - 1)]
    back = [(i + 1, i) for i in range(count - 1)]
    rows = cells.shape[0]
    tail = jnp.concatenate([left[rows - 3 :], cells[rows - 3 :], right[rows - 3 :]], axis=1)
    head = jnp.concatenate([left[:3], cells[:3], right[:3]], axis=1)
    return lax.ppermute(tail, "lat", ahead), lax.ppermute(head, "lat", back)


def per_device(
    fields,
    land_mask,
    cotangent,
    kernel,
    layer_norm_gain,
    layer_norm_bias,
    w_in,
    b_in,
    w_out,
    b_out,
    layer_scale,
):
    rows, cols, channels = fields.shape
    cells = rows * cols
    hidden = w_in.shape[1]
    n_lon, n_lat = lax.axis_size("lon"), lax.axis_size("lat")
    taps = kernel.reshape(49, channels)
    gain, bias = layer_norm_gain.reshape(1, -1), layer_norm_bias.reshape(1, -1)
    scale = layer_scale.reshape(1, -1)
    mask_b = jnp.broadcast_to(land_mask.astype(F32)[:, :, None], (rows, cols, LANES))
    mask_rows = mask_b.reshape(cells, LANES)
    cot_rows = cotangent.reshape(cells, channels)

    masked = fields * land_mask.astype(BF16)[:, :, None]
    left, right = side_halo(masked)
    inner = conv_inner(fields, mask_b, taps)
    top, bot = end_halo(masked, left, right)
    side = conv_side(fields, mask_b, taps, left, right)
    xhat, inv, act, d_pre, g_wo, g_wi, g_bi, g_bo = expand(
        inner, side, top, bot, taps, gain, bias, scale, mask_rows, cot_rows,
        w_in, b_in.reshape(1, -1), w_out, n_lon, n_lat,
    )
    mixed, d_conv, sums = project(
        act, d_pre, w_out, w_in, xhat, inv, fields.reshape(cells, channels), cot_rows, mask_rows,
        scale, gain, b_out.reshape(1, -1),
    )
    d_conv = d_conv.reshape(rows, cols, channels)
    d_left, d_right = side_halo(d_conv)
    d_top, d_bot = end_halo(d_conv, d_left, d_right)
    g_k = filter_grad(fields, mask_b, left, right, top, bot, d_conv)
    grad_fields = input_grad(d_conv, d_left, d_right, d_top, d_bot, taps, mask_b, cotangent)

    width = hidden // (n_lon * n_lat)

    def owned(grads):
        if grads.shape[1] != n_lat:
            grads = grads.reshape(n_lon, channels, n_lat, width).transpose(0, 2, 1, 3)
        return scatter_sum(grads)

    grad_wo = owned(g_wo).T
    grad_wi = owned(g_wi)
    small = total_sum(
        jnp.concatenate([g_k, sums[:3], g_bo, g_bi.reshape(-1, channels)], axis=0)
    )
    return (
        mixed.reshape(rows, cols, channels),
        grad_fields,
        small[:49].reshape(7, 7, channels),
        small[50],
        small[51],
        grad_wi,
        small[53:].reshape(hidden),
        grad_wo,
        small[52],
        small[49],
    )


def solution(mesh):
    placed = (
        P(("grp", "lat"), "lon", None),
        P(("grp", "lat"), "lon"),
        P(("grp", "lat"), "lon", None),
        P(),
        P(),
        P(),
        P(),
        P(),
        P(),
        P(),
        P(),
    )
    return jax.shard_map(
        per_device,
        mesh=mesh,
        in_specs=placed,
        out_specs=(
            P(("grp", "lat"), "lon", None),
            P(("grp", "lat"), "lon", None),
            P("grp", None, None),
            P("grp"),
            P("grp"),
            P("grp", ("lon", "lat")),
            P("grp"),
            P(("lon", "lat"), "grp"),
            P("grp"),
            P("grp"),
        ),
        check_vma=False,
    )
```

time: 346 us -> 151 us (0.44)
  waiting for transfers between devices: 143 us -> 35.4 us
  Pallas kernels: 0 us -> 61.2 us
  blocking collectives: 60 us -> 0 us
  other arithmetic: 65.3 us -> 9.28 us
  matrix products: 34 us -> 0 us
  between operations: 16.1 us -> 0.99 us
  starting transfers between devices: 15.8 us -> 30.8 us
    reduce_scatter x2 -> x0, waiting for transfers between devices: 133 us -> none  [the longest x1 76.4 us: per_device(): lax.psum_scatter(in_term, ('lon', 'lat'), scatter_dimension=1, tiled=True)]
    pallas_call x0 -> x6, Pallas kernels: none -> 61.2 us  [the longest x1 19.3 us: expand(): pl.pallas_call(expand_kernel, grid=(n_lon,), out_shape=[jax.ShapeDtypeStr...]
    psum x1 -> x0, blocking collectives: 60 us -> none  [per_device(): lax.psum((local_kernel, partial_totals[0], partial_totals[1], partial_tot...]
    reduce_sum x7 -> x0, other arithmetic: 36.7 us -> none  [the longest x4 18 us: kernel_grad(): entries.append(jnp.sum(grad_f * window, axis=(0, 1)))]
    dot_general x6 -> x0, matrix products: 34 us -> none  [the longest x1 8.59 us: pointwise(): d_act = jnp.dot(d_branch, w_out.T, preferred_element_type=jnp.float32)]
    ppermute x8 -> x20, waiting for transfers between devices: 10 us -> 35.4 us  [the longest x12 30.3 us: swap(): return lax.ppermute(values, axis, [(i, i ^ bit) for i in range(count)])]
    convert_element_type x3 -> x1, other arithmetic: 19.6 us -> 0.8 us  [per_device(): masked = fields * land_mask.astype(BF16)[:, :, None]]
    ppermute x8 -> x20, starting transfers between devices: 15.5 us -> 30.8 us  [the longest x12 15.1 us: swap(): return lax.ppermute(values, axis, [(i, i ^ bit) for i in range(count)])]
  transfers between devices with their start and end apart: 11 -> 20, of which waited for: 7 -> 9; matrix products, arithmetic and copies ran while one was open for 11% -> 10% of each run, Pallas kernels for 0% -> 20%
where the time goes in v1:
time: 151 us
  Pallas kernels  61.2 us (41%)
  waiting for transfers between devices  35.4 us (23%)
  starting transfers between devices  30.8 us (20%)
  local copies, waits for them, and re-layouts  12.9 us (9%)
  other arithmetic  9.28 us (6%)
    ppermute x12, waiting for transfers between devices, swap(): return lax.ppermute(values, axis, [(i, i ^ bit) for i in range(count)])  30.3 us
    pallas_call x1, Pallas kernels, expand(): pl.pallas_call(expand_kernel, grid=(n_lon,), out_shape=[jax.ShapeDtypeStr...  19.3 us
    ppermute x12, starting transfers between devices, swap(): return lax.ppermute(values, axis, [(i, i ^ bit) for i in range(count)])  15.1 us
    ppermute x4, starting transfers between devices, end_halo(): return (lax.ppermute(tail, 'lat', ahead), lax.ppermute(head, 'lat', back))  11.4 us
    pallas_call x1, Pallas kernels, project(): pl.pallas_call(project_kernel, grid=(cells // part,), out_shape=[jax.Shap...  11.1 us
    pallas_call x1, Pallas kernels, filter_grad(): pl.pallas_call(filter_grad_kernel, grid=(channels // LANES,), out_shape=j...  10.2 us
    pallas_call x1, Pallas kernels, input_grad(): pl.pallas_call(input_grad_kernel, grid=(channels // LANES,), out_shape=ja...  9.48 us
    pallas_call x1, Pallas kernels, conv_side(): pl.pallas_call(conv_side_kernel, grid=(channels // LANES,), out_shape=jax...  5.62 us
  transfers between devices with their start and end apart: 20, of which 9 were waited for; matrix products, arithmetic and copies ran while one was open for 10% of the time, Pallas kernels for 20%

profile of v1, /device:TPU:0, one launch (start us, length us, event | category | flops | bytes accessed | tf_op | source)
XLA Modules:
  0.0 150.6 jit_solution(12697652213437804583)
XLA Ops:
  3.5 2.0 %collective-permute-start.1 = (bf16[32,3,512]{2,1,0:T(4,128)(2,1)S(1)}, bf16[32,3,512]{2,1,0:T(4,128)(2,1)S(1)}, u32[]{:S(2)}, u32[]{:S(2)}) collective-permute-start(bf16[32,3,512]{2,1,0:T(4,128)(2,1)S(1)} %get-tuple-element.48), channel_id=1, source_target_pairs={{4,0},{8,4},{12,8},{0,12},{5,1},{9,5},{13,9},{1,13},{6,2},{10,6},{... | collective-permute-start | bytes 294920 | tf_op jit(solution)/shard_map/ppermute | solution.py:474
  5.5 3.8 %collective-permute-done.1.r_ref = bf16[32,3,512]{2,1,0:T(4,128)(2,1)S(1)} collective-permute-done((bf16[32,3,512]{2,1,0:T(4,128)(2,1)S(1)}, bf16[32,3,512]{2,1,0:T(4,128)(2,1)S(1)}, u32[]{:S(2)}, u32[]{:S(2)}) %collective-permute-start.1) | collective-permute-done | bytes 98336 | tf_op jit(solution)/shard_map/ppermute | solution.py:474
  9.4 3.5 %collective-permute-start.2 = (bf16[3,38,512]{2,1,0:T(8,128)(2,1)S(1)}, bf16[3,38,512]{2,1,0:T(8,128)(2,1)S(1)}, u32[]{:S(2)}, u32[]{:S(2)}) collective-permute-start(bf16[3,38,512]{2,1,0:T(8,128)(2,1)S(1)} %pad_maximum_fusion.1), channel_id=1, source_target_pairs={{0,1},{1,2},{2,3},{4,5},{5,6},{6,7},{8,9},{9,10},{10,11},{12,13},{... | collective-permute-start | bytes 350216 | tf_op jit(solution)/shard_map/ppermute | solution.py:485
  16.0 5.5 %conv_inner.1.inner_ref = f32[32,16,512]{2,1,0:T(8,128)} custom-call(bf16[32,32,512]{2,1,0:T(8,128)(2,1)} %f_ref.5, f32[32,32,128]{2,1,0:T(8,128)} %broadcast_in_dim.11.m_ref, f32[49,512]{1,0:T(8,128)} %reshape.135.k_ref), custom_call_target="tpu_custom_call" | custom-call | flops 25690112 | bytes 1572864 | tf_op jit(solution)/shard_map/conv_inner/pallas_call | solution.py:79
  21.5 5.6 %conv_side.1.side_ref = f32[32,16,512]{2,1,0:T(8,128)} custom-call(bf16[32,32,512]{2,1,0:T(8,128)(2,1)} %f_ref.5, f32[32,32,128]{2,1,0:T(8,128)} %broadcast_in_dim.11.m_ref, f32[49,512]{1,0:T(8,128)} %reshape.135.k_ref, bf16[32,3,512]{2,1,0:T(4,128)(2,1)} %copy-done.3, bf16[32,3,512]{2,1,0:T(4,128)(2,1)} %copy-done.4), custom_call_target="tpu_custom_call" | custom-call | flops 25690112 | bytes 1572864 | tf_op jit(solution)/shard_map/conv_side/pallas_call | solution.py:94
  28.2 19.3 %expand.1 = (f32[1024,512]{1,0:T(8,128)}, f32[1024,128]{1,0:T(8,128)}, bf16[1024,2048]{1,0:T(8,128)(2,1)}, bf16[1024,2048]{1,0:T(8,128)(2,1)}, bf16[4,4,512,128]...) custom-call(f32[32,16,512]{2,1,0:T(8,128)} %conv_inner.1.inner_ref, ...), custom_call_target="tpu_custom_call" | custom-call | flops 8589934592 | bytes 10485760 | tf_op jit(solution)/shard_map/expand/pallas_call | solution.py:214
  47.5 11.1 %project.1 = (bf16[1024,512]{1,0:T(8,128)(2,1)}, bf16[1024,512]{1,0:T(8,128)(2,1)}, f32[8,512]{1,0:T(8,128)}) custom-call(bf16[1024,2048]{1,0:T(8,128)(2,1)} %get-tuple-element.21.act_ref, bf16[1024,2048]{1,0:T(8,128)(2,1)} %get-tuple-element.22.dpre_ref, bf16[2048,512]{1,0:T(8,128)(2,1)} %wo_ref.3, bf16[512,2048]{1,0:T(8,128)(2,1)} %wi_ref.3, ...), custom_call_target="tpu_custom_call" | custom-call | flops 4294967296 | bytes 8388608 | tf_op jit(solution)/shard_map/project/pallas_call | solution.py:309
  59.6 2.0 %fusion.3 = (bf16[32,3,512]{2,1,0:T(4,128)(2,1)}, bf16[32,3,512]{2,1,0:T(4,128)(2,1)}) fusion(bf16[32,32,512]{2,1,0:T(8,128)(2,1)} %bitcast.51), kind=kLoop, calls=%fused_computation.26 | loop fusion | bytes 393216 | tf_op jit(solution)/shard_map/slice | solution.py:474
  65.3 10.2 %filter_grad.1 = f32[49,512]{1,0:T(8,128)} custom-call(bf16[32,32,512]{2,1,0:T(8,128)(2,1)} %f_ref.5, f32[32,32,128]{2,1,0:T(8,128)} %broadcast_in_dim.11.m_ref, bf16[32,3,512]{2,1,0:T(4,128)(2,1)} %copy-done.3, bf16[32,3,512]{2,1,0:T(4,128)(2,1)} %copy-done.4, bf16[3,38,512]{2,1,0:T(8,128)(2,1)} %copy-done.6, bf16[3,38,512]{2,1,0:T(8,128)(2,1)} %copy-done.7, ...), custom_call_target="tpu_custom_call" | custom-call | flops 51380224 | bytes 3145728 | tf_op jit(solution)/shard_map/filter_grad/pallas_call | solution.py:378
  79.9 1.7 %collective-permute-start.9 = (f32[57,512]{1,0:T(8,128)S(1)}, f32[57,512]{1,0:T(8,128)S(1)}, u32[]{:S(2)}, u32[]{:S(2)}) collective-permute-start(f32[57,512]{1,0:T(8,128)S(1)} %fusion.12), channel_id=1, source_target_pairs={{0,8},{4,12},{8,0},{12,4},{1,9},{5,13},{9,1},{13,5},{2,10},{6,14},... | collective-permute-start | bytes 350216 | tf_op jit(solution)/shard_map/ppermute | solution.py:441
  82.3 5.2 %collective-permute-start.6 = (bf16[3,38,512]{2,1,0:T(8,128)(2,1)}, bf16[3,38,512]{2,1,0:T(8,128)(2,1)}, u32[]{:S(2)}, u32[]{:S(2)}) collective-permute-start(bf16[3,38,512]{2,1,0:T(8,128)(2,1)} %pad_maximum_fusion.3), channel_id=1, source_target_pairs={{0,1},{1,2},{2,3},{4,5},{5,6},{6,7},{8,9},{9,10},{10,11},{12,13},{... | collective-permute-start | bytes 350216 | tf_op jit(solution)/shard_map/ppermute | solution.py:485
  89.2 1.5 collective-permute-start.7
  90.7 2.2 %collective-permute-done.10 = f32[57,512]{1,0:T(8,128)S(1)} collective-permute-done((f32[57,512]{1,0:T(8,128)S(1)}, f32[57,512]{1,0:T(8,128)S(1)}, u32[]{:S(2)}, u32[]{:S(2)}) %collective-permute-start.10) | collective-permute-done | bytes 116768 | tf_op jit(solution)/shard_map/ppermute | solution.py:441
  92.9 2.5 %collective-permute-start.11 = (f32[57,512]{1,0:T(8,128)S(1)}, f32[57,512]{1,0:T(8,128)}, u32[]{:S(2)}, u32[]{:S(2)}) collective-permute-start(f32[57,512]{1,0:T(8,128)S(1)} %add.99), channel_id=1, source_target_pairs={{0,2},{1,3},{2,0},{3,1},{4,6},{5,7},{6,4},{7,5},{8,10},{9,11},{10,... | collective-permute-start | bytes 350216 | tf_op jit(solution)/shard_map/ppermute | solution.py:441
  96.8 9.5 %input_grad.1 = bf16[32,32,512]{2,1,0:T(8,128)(2,1)} custom-call(bf16[32,32,512]{2,1,0:T(8,128)(2,1)} %bitcast.53, bf16[32,3,512]{2,1,0:T(4,128)(2,1)} %copy-done.5, bf16[32,3,512]{2,1,0:T(4,128)(2,1)} %collective-permute-done.5.r_ref, bf16[3,38,512]{2,1,0:T(8,128)(2,1)} %collective-permute-done.6.t_ref, bf16[3,38,512]{2,1,0:T(8,128)(2,1)} %collective-permute-done.7.b_ref, ...), custom_call_target="tpu_custom_call" | custom-call | flops 51380224 | bytes 3145728 | tf_op jit(solution)/shard_map/input_grad/pallas_call | solution.py:414
  108.5 1.7 %convert_add_fusion = f32[2,4,512,128]{3,2,1,0:T(8,128)S(1)} fusion(bf16[2,4,512,128]{3,2,1,0:T(8,128)(2,1)} %collective-permute-done.16, bf16[2,2,4,512,128]{4,3,2,1,0:T(8,128)(2,1)} %bitcast.62, s32[]{:T(128)S(6)} %select_n.77), kind=kLoop, calls=%fused_computation | loop fusion | flops 1572864 | bytes 4194308 | tf_op jit(solution)/shard_map/add | solution.py:456
  110.3 1.9 %collective-permute-start.17 = (bf16[1,4,512,128]{3,2,1,0:T(8,128)(2,1)S(1)}, bf16[1,4,512,128]{3,2,1,0:T(8,128)(2,1)S(1)}, u32[]{:S(2)}, u32[]{:S(2)}) collective-permute-start(bf16[1,4,512,128]{3,2,1,0:T(8,128)(2,1)S(1)} %dynamic-slice_convert_fusion), channel_id=1, source_target_pairs={{0,8},{4,12},{8,0},{12,4},{1,9},{5,13},{9,1},{13,5},{2,10},{6,14},... | collective-permute-start | bytes 1572872 | tf_op jit(solution)/shard_map/ppermute | solution.py:441
  113.4 11.9 %collective-permute-done.17 = bf16[1,4,512,128]{3,2,1,0:T(8,128)(2,1)S(1)} collective-permute-done((bf16[1,4,512,128]{3,2,1,0:T(8,128)(2,1)S(1)}, bf16[1,4,512,128]{3,2,1,0:T(8,128)(2,1)S(1)}, u32[]{:S(2)}, u32[]{:S(2)}) %collective-permute-start.17) | collective-permute-done | bytes 524320 | tf_op jit(solution)/shard_map/ppermute | solution.py:441
  125.4 4.5 %collective-permute-start.18 = (bf16[1,2,512,128]{3,2,1,0:T(8,128)(2,1)S(1)}, bf16[1,2,512,128]{3,2,1,0:T(8,128)(2,1)S(1)}, u32[]{:S(2)}, u32[]{:S(2)}) collective-permute-start(bf16[1,2,512,128]{3,2,1,0:T(8,128)(2,1)S(1)} %fusion.1), channel_id=1, source_target_pairs={{0,1},{1,0},{2,3},{3,2},{4,5},{5,4},{6,7},{7,6},{8,9},{9,8},{10,11... | collective-permute-start | bytes 786440 | tf_op jit(solution)/shard_map/ppermute | solution.py:441
  129.9 3.5 %collective-permute-done.13 = bf16[1,4,512,128]{3,2,1,0:T(8,128)(2,1)S(1)} collective-permute-done((bf16[1,4,512,128]{3,2,1,0:T(8,128)(2,1)S(1)}, bf16[1,4,512,128]{3,2,1,0:T(8,128)(2,1)S(1)}, u32[]{:S(2)}, u32[]{:S(2)}) %collective-permute-start.13) | collective-permute-done | bytes 524320 | tf_op jit(solution)/shard_map/ppermute | solution.py:441
  133.6 2.3 %collective-permute-start.14 = (bf16[1,2,512,128]{3,2,1,0:T(8,128)(2,1)S(1)}, bf16[1,2,512,128]{3,2,1,0:T(8,128)(2,1)S(1)}, u32[]{:S(2)}, u32[]{:S(2)}) collective-permute-start(bf16[1,2,512,128]{3,2,1,0:T(8,128)(2,1)S(1)} %fusion), channel_id=1, source_target_pairs={{0,1},{1,0},{2,3},{3,2},{4,5},{5,4},{6,7},{7,6},{8,9},{9,8},{10,11... | collective-permute-start | bytes 786440 | tf_op jit(solution)/shard_map/ppermute | solution.py:441
  136.7 5.7 %collective-permute-done.14 = bf16[1,2,512,128]{3,2,1,0:T(8,128)(2,1)S(1)} collective-permute-done((bf16[1,2,512,128]{3,2,1,0:T(8,128)(2,1)S(1)}, bf16[1,2,512,128]{3,2,1,0:T(8,128)(2,1)S(1)}, u32[]{:S(2)}, u32[]{:S(2)}) %collective-permute-start.14) | collective-permute-done | bytes 262176 | tf_op jit(solution)/shard_map/ppermute | solution.py:441
  142.6 3.1 %collective-permute-done.19 = bf16[1,1,512,128]{3,2,1,0:T(8,128)(2,1)S(1)} collective-permute-done((bf16[1,1,512,128]{3,2,1,0:T(8,128)(2,1)S(1)}, bf16[1,1,512,128]{3,2,1,0:T(8,128)(2,1)S(1)}, u32[]{:S(2)}, u32[]{:S(2)}) %collective-permute-start.19) | collective-permute-done | bytes 131104 | tf_op jit(solution)/shard_map/ppermute | solution.py:441
  146.5 3.3 %collective-permute-done.15 = bf16[1,1,512,128]{3,2,1,0:T(8,128)(2,1)S(1)} collective-permute-done((bf16[1,1,512,128]{3,2,1,0:T(8,128)(2,1)S(1)}, bf16[1,1,512,128]{3,2,1,0:T(8,128)(2,1)S(1)}, u32[]{:S(2)}, u32[]{:S(2)}) %collective-permute-start.15) | collective-permute-done | bytes 131104 | tf_op jit(solution)/shard_map/ppermute | solution.py:441
  (93 shorter events, 26.0 us)
Async XLA Ops:
  3.0 6.4 %collective-permute-start = (bf16[32,3,512]{2,1,0:T(4,128)(2,1)S(1)}, bf16[32,3,512]{2,1,0:T(4,128)(2,1)S(1)}, u32[]{:S(2)}, u32[]{:S(2)}) collective-permute-start(bf16[32,3,512]{2,1,0:T(4,128)(2,1)S(1)} %get-tuple-element.49), channel_id=1, source_target_pairs={{0,4},{4,8},{8,12},{12,0},{1,5},{5,9},{9,13},{13,1},{2,6},{6,10},{... | collective-permute-start | bytes 294920 | tf_op jit(solution)/shard_map/ppermute | solution.py:473
  3.5 5.8 %collective-permute-start.1 = (bf16[32,3,512]{2,1,0:T(4,128)(2,1)S(1)}, bf16[32,3,512]{2,1,0:T(4,128)(2,1)S(1)}, u32[]{:S(2)}, u32[]{:S(2)}) collective-permute-start(bf16[32,3,512]{2,1,0:T(4,128)(2,1)S(1)} %get-tuple-element.48), channel_id=1, source_target_pairs={{4,0},{8,4},{12,8},{0,12},{5,1},{9,5},{13,9},{1,13},{6,2},{10,6},{... | collective-permute-start | bytes 294920 | tf_op jit(solution)/shard_map/ppermute | solution.py:474
  9.4 17.7 %collective-permute-start.2 = (bf16[3,38,512]{2,1,0:T(8,128)(2,1)S(1)}, bf16[3,38,512]{2,1,0:T(8,128)(2,1)S(1)}, u32[]{:S(2)}, u32[]{:S(2)}) collective-permute-start(bf16[3,38,512]{2,1,0:T(8,128)(2,1)S(1)} %pad_maximum_fusion.1), channel_id=1, source_target_pairs={{0,1},{1,2},{2,3},{4,5},{5,6},{6,7},{8,9},{9,10},{10,11},{12,13},{... | collective-permute-start | bytes 350216 | tf_op jit(solution)/shard_map/ppermute | solution.py:485
  13.0 14.2 %collective-permute-start.3 = (bf16[3,38,512]{2,1,0:T(8,128)(2,1)S(1)}, bf16[3,38,512]{2,1,0:T(8,128)(2,1)S(1)}, u32[]{:S(2)}, u32[]{:S(2)}) collective-permute-start(bf16[3,38,512]{2,1,0:T(8,128)(2,1)S(1)} %pad_maximum_fusion.2), channel_id=1, source_target_pairs={{1,0},{2,1},{3,2},{5,4},{6,5},{7,6},{9,8},{10,9},{11,10},{13,12},{... | collective-permute-start | bytes 350216 | tf_op jit(solution)/shard_map/ppermute | solution.py:485
  47.5 16.3 %copy-start.10 = (f32[1,2048]{1,0:T(1,128)S(1)}, f32[1,2048]{1,0:T(1,128)}, u32[]{:S(2)}) copy-start(f32[1,2048]{1,0:T(1,128)} %get-tuple-element.29) | copy-start | bytes 24580
  58.6 16.8 %copy-start.9 = (f32[1,512]{1,0:T(1,128)S(1)}, f32[1,512]{1,0:T(1,128)}, u32[]{:S(2)}) copy-start(f32[1,512]{1,0:T(1,128)} %get-tuple-element.28) | copy-start | bytes 6148
  59.6 16.9 %copy-start = (bf16[4,4,512,128]{3,2,1,0:T(8,128)(2,1)S(1)}, bf16[4,4,512,128]{3,2,1,0:T(8,128)(2,1)}, u32[]{:S(2)}) copy-start(bf16[4,4,512,128]{3,2,1,0:T(8,128)(2,1)} %get-tuple-element.30) | copy-start | bytes 6291460
  61.6 20.0 %collective-permute-start.4 = (bf16[32,3,512]{2,1,0:T(4,128)(2,1)}, bf16[32,3,512]{2,1,0:T(4,128)(2,1)S(1)}, u32[]{:S(2)}, u32[]{:S(2)}) collective-permute-start(bf16[32,3,512]{2,1,0:T(4,128)(2,1)} %get-tuple-element.45), channel_id=1, source_target_pairs={{0,4},{4,8},{8,12},{12,0},{1,5},{5,9},{9,13},{13,1},{2,6},{6,10},{... | collective-permute-start | bytes 294920 | tf_op jit(solution)/shard_map/ppermute | solution.py:473
  62.5 16.5 %collective-permute-start.5 = (bf16[32,3,512]{2,1,0:T(4,128)(2,1)}, bf16[32,3,512]{2,1,0:T(4,128)(2,1)}, u32[]{:S(2)}, u32[]{:S(2)}) collective-permute-start(bf16[32,3,512]{2,1,0:T(4,128)(2,1)} %get-tuple-element.44), channel_id=1, source_target_pairs={{4,0},{8,4},{12,8},{0,12},{5,1},{9,5},{13,9},{1,13},{6,2},{10,6},{... | collective-permute-start | bytes 294920 | tf_op jit(solution)/shard_map/ppermute | solution.py:474
  76.3 3.5 %collective-permute-start.8 = (f32[57,512]{1,0:T(8,128)S(1)}, f32[57,512]{1,0:T(8,128)S(1)}, u32[]{:S(2)}, u32[]{:S(2)}) collective-permute-start(f32[57,512]{1,0:T(8,128)S(1)} %pad_maximum_fusion), channel_id=1, source_target_pairs={{0,4},{4,0},{8,12},{12,8},{1,5},{5,1},{9,13},{13,9},{2,6},{6,2},{1... | collective-permute-start | bytes 350216 | tf_op jit(solution)/shard_map/ppermute | solution.py:441
  77.5 34.7 %collective-permute-start.12 = (bf16[2,4,512,128]{3,2,1,0:T(8,128)(2,1)}, bf16[2,4,512,128]{3,2,1,0:T(8,128)(2,1)S(1)}, u32[]{:S(2)}, u32[]{:S(2)}) collective-permute-start(bf16[2,4,512,128]{3,2,1,0:T(8,128)(2,1)} %dynamic-slice_bitcast_fusion.1), channel_id=1, source_target_pairs={{0,4},{4,0},{8,12},{12,8},{1,5},{5,1},{9,13},{13,9},{2,6},{6,2},{1... | collective-permute-start | bytes 3145736 | tf_op jit(solution)/shard_map/ppermute | solution.py:441
  79.0 29.5 %collective-permute-start.16 = (bf16[2,4,512,128]{3,2,1,0:T(8,128)(2,1)}, bf16[2,4,512,128]{3,2,1,0:T(8,128)(2,1)}, u32[]{:S(2)}, u32[]{:S(2)}) collective-permute-start(bf16[2,4,512,128]{3,2,1,0:T(8,128)(2,1)} %dynamic-slice_bitcast_fusion), channel_id=1, source_target_pairs={{0,4},{4,0},{8,12},{12,8},{1,5},{5,1},{9,13},{13,9},{2,6},{6,2},{1... | collective-permute-start | bytes 3145736 | tf_op jit(solution)/shard_map/ppermute | solution.py:441
  79.9 7.6 %collective-permute-start.9 = (f32[57,512]{1,0:T(8,128)S(1)}, f32[57,512]{1,0:T(8,128)S(1)}, u32[]{:S(2)}, u32[]{:S(2)}) collective-permute-start(f32[57,512]{1,0:T(8,128)S(1)} %fusion.12), channel_id=1, source_target_pairs={{0,8},{4,12},{8,0},{12,4},{1,9},{5,13},{9,1},{13,5},{2,10},{6,14},... | collective-permute-start | bytes 350216 | tf_op jit(solution)/shard_map/ppermute | solution.py:441
  81.6 15.2 %copy-start.5 = (bf16[32,3,512]{2,1,0:T(4,128)(2,1)}, bf16[32,3,512]{2,1,0:T(4,128)(2,1)S(1)}, u32[]{:S(2)}) copy-start(bf16[32,3,512]{2,1,0:T(4,128)(2,1)S(1)} %collective-permute-done.4.l_ref) | copy-start | bytes 294916
  82.3 13.2 %collective-permute-start.6 = (bf16[3,38,512]{2,1,0:T(8,128)(2,1)}, bf16[3,38,512]{2,1,0:T(8,128)(2,1)}, u32[]{:S(2)}, u32[]{:S(2)}) collective-permute-start(bf16[3,38,512]{2,1,0:T(8,128)(2,1)} %pad_maximum_fusion.3), channel_id=1, source_target_pairs={{0,1},{1,2},{2,3},{4,5},{5,6},{6,7},{8,9},{9,10},{10,11},{12,13},{... | collective-permute-start | bytes 350216 | tf_op jit(solution)/shard_map/ppermute | solution.py:485
  87.5 5.4 %collective-permute-start.10 = (f32[57,512]{1,0:T(8,128)S(1)}, f32[57,512]{1,0:T(8,128)S(1)}, u32[]{:S(2)}, u32[]{:S(2)}) collective-permute-start(f32[57,512]{1,0:T(8,128)S(1)} %add.98), channel_id=1, source_target_pairs={{0,1},{1,0},{2,3},{3,2},{4,5},{5,4},{6,7},{7,6},{8,9},{9,8},{10,11... | collective-permute-start | bytes 350216 | tf_op jit(solution)/shard_map/ppermute | solution.py:441
  89.2 7.5 %collective-permute-start.7 = (bf16[3,38,512]{2,1,0:T(8,128)(2,1)}, bf16[3,38,512]{2,1,0:T(8,128)(2,1)}, u32[]{:S(2)}, u32[]{:S(2)}) collective-permute-start(bf16[3,38,512]{2,1,0:T(8,128)(2,1)} %pad_maximum_fusion.4), channel_id=1, source_target_pairs={{1,0},{2,1},{3,2},{5,4},{6,5},{7,6},{9,8},{10,9},{11,10},{13,12},{... | collective-permute-start | bytes 350216 | tf_op jit(solution)/shard_map/ppermute | solution.py:485
  92.9 13.4 %collective-permute-start.11 = (f32[57,512]{1,0:T(8,128)S(1)}, f32[57,512]{1,0:T(8,128)}, u32[]{:S(2)}, u32[]{:S(2)}) collective-permute-start(f32[57,512]{1,0:T(8,128)S(1)} %add.99), channel_id=1, source_target_pairs={{0,2},{1,3},{2,0},{3,1},{4,6},{5,7},{6,4},{7,5},{8,10},{9,11},{10,... | collective-permute-start | bytes 350216 | tf_op jit(solution)/shard_map/ppermute | solution.py:441
  110.3 14.9 %collective-permute-start.17 = (bf16[1,4,512,128]{3,2,1,0:T(8,128)(2,1)S(1)}, bf16[1,4,512,128]{3,2,1,0:T(8,128)(2,1)S(1)}, u32[]{:S(2)}, u32[]{:S(2)}) collective-permute-start(bf16[1,4,512,128]{3,2,1,0:T(8,128)(2,1)S(1)} %dynamic-slice_convert_fusion), channel_id=1, source_target_pairs={{0,8},{4,12},{8,0},{12,4},{1,9},{5,13},{9,1},{13,5},{2,10},{6,14},... | collective-permute-start | bytes 1572872 | tf_op jit(solution)/shard_map/ppermute | solution.py:441
  112.5 21.0 %collective-permute-start.13 = (bf16[1,4,512,128]{3,2,1,0:T(8,128)(2,1)S(1)}, bf16[1,4,512,128]{3,2,1,0:T(8,128)(2,1)S(1)}, u32[]{:S(2)}, u32[]{:S(2)}) collective-permute-start(bf16[1,4,512,128]{3,2,1,0:T(8,128)(2,1)S(1)} %dynamic-slice_convert_fusion.1), channel_id=1, source_target_pairs={{0,8},{4,12},{8,0},{12,4},{1,9},{5,13},{9,1},{13,5},{2,10},{6,14},... | collective-permute-start | bytes 1572872 | tf_op jit(solution)/shard_map/ppermute | solution.py:441
  125.4 11.1 %collective-permute-start.18 = (bf16[1,2,512,128]{3,2,1,0:T(8,128)(2,1)S(1)}, bf16[1,2,512,128]{3,2,1,0:T(8,128)(2,1)S(1)}, u32[]{:S(2)}, u32[]{:S(2)}) collective-permute-start(bf16[1,2,512,128]{3,2,1,0:T(8,128)(2,1)S(1)} %fusion.1), channel_id=1, source_target_pairs={{0,1},{1,0},{2,3},{3,2},{4,5},{5,4},{6,7},{7,6},{8,9},{9,8},{10,11... | collective-permute-start | bytes 786440 | tf_op jit(solution)/shard_map/ppermute | solution.py:441
  133.6 8.8 %collective-permute-start.14 = (bf16[1,2,512,128]{3,2,1,0:T(8,128)(2,1)S(1)}, bf16[1,2,512,128]{3,2,1,0:T(8,128)(2,1)S(1)}, u32[]{:S(2)}, u32[]{:S(2)}) collective-permute-start(bf16[1,2,512,128]{3,2,1,0:T(8,128)(2,1)S(1)} %fusion), channel_id=1, source_target_pairs={{0,1},{1,0},{2,3},{3,2},{4,5},{5,4},{6,7},{7,6},{8,9},{9,8},{10,11... | collective-permute-start | bytes 786440 | tf_op jit(solution)/shard_map/ppermute | solution.py:441
  136.6 9.0 %collective-permute-start.19 = (bf16[1,1,512,128]{3,2,1,0:T(8,128)(2,1)S(1)}, bf16[1,1,512,128]{3,2,1,0:T(8,128)(2,1)S(1)}, u32[]{:S(2)}, u32[]{:S(2)}) collective-permute-start(bf16[1,1,512,128]{3,2,1,0:T(8,128)(2,1)S(1)} %dynamic-slice_convert_fusion.4), channel_id=1, source_target_pairs={{0,2},{1,3},{2,0},{3,1},{4,6},{5,7},{6,4},{7,5},{8,10},{9,11},{10,... | collective-permute-start | bytes 393224 | tf_op jit(solution)/shard_map/ppermute | solution.py:441
  142.5 7.3 %collective-permute-start.15 = (bf16[1,1,512,128]{3,2,1,0:T(8,128)(2,1)S(1)}, bf16[1,1,512,128]{3,2,1,0:T(8,128)(2,1)S(1)}, u32[]{:S(2)}, u32[]{:S(2)}) collective-permute-start(bf16[1,1,512,128]{3,2,1,0:T(8,128)(2,1)S(1)} %dynamic-slice_convert_fusion.5), channel_id=1, source_target_pairs={{0,2},{1,3},{2,0},{3,1},{4,6},{5,7},{6,4},{7,5},{8,10},{9,11},{10,... | collective-permute-start | bytes 393224 | tf_op jit(solution)/shard_map/ppermute | solution.py:441
  (7 other events, 56.1 us)

commit v2 on v1

v2 whole, which is shorter than its diff:
```python
import functools
import math

import jax
import jax.numpy as jnp
from jax import lax
from jax.experimental import pallas as pl
from jax.experimental.pallas import tpu as pltpu
from jax.sharding import PartitionSpec as P

F32 = jnp.float32
BF16 = jnp.bfloat16
LANES = 128
SUB = 8


def params(mib):
    return pltpu.CompilerParams(vmem_limit_bytes=mib * 1024 * 1024)


def estimate(micros):
    return pl.CostEstimate(
        flops=int(micros * 1.15e9), bytes_accessed=int(micros * 3.6e6), transcendentals=0
    )


def once(shape):
    zeros = (0,) * len(shape)
    return pl.BlockSpec(shape, lambda *_: zeros, pipeline_mode=pl.Buffered(1))


UNUSED = pl.BlockSpec(memory_space=pl.ANY)


def whole_spec(shape):
    zeros = (0,) * len(shape)
    return pl.BlockSpec(shape, lambda *_: zeros)


def shifted(window, row, start, offset):
    if offset % SUB == 0:
        return window[row, pl.ds(start + offset, SUB), :]
    base = start + offset // SUB * SUB
    pair = window[row, pl.ds(base, 2 * SUB), :]
    return pltpu.roll(pair, 2 * SUB - offset % SUB, axis=0)[:SUB]


def tap_rows(k_ref, col_off, flip):
    at = 6 - col_off if flip else col_off
    rows = [k_ref[6 - p if flip else p, at : at + 1, :] for p in range(7)]
    return [jnp.broadcast_to(row, (SUB, LANES)) for row in rows]


def band_conv(window, k_ref, start, rows, pad, flip):
    sums = [None] * rows
    for col_off in range(7):
        weights = tap_rows(k_ref, col_off, flip)
        for src in range(window.shape[0]):
            hits = [(src - pad - row_off + 3, row_off) for row_off in range(7)]
            hits = [(out, row_off) for out, row_off in hits if 0 <= out < rows]
            if not hits:
                continue
            cells = shifted(window, src, start, 5 + col_off)
            for out, row_off in hits:
                term = weights[row_off] * cells
                sums[out] = term if sums[out] is None else sums[out] + term
    return sums


def conv_inner_kernel(f_ref, m_ref, k_ref, o_ref, head_ref, tail_ref, window):
    rows, cols, _ = f_ref.shape
    masked = f_ref[...].astype(F32) * m_ref[...]
    window[:, 8 : 8 + cols, :] = masked
    head_ref[...] = masked[:3].astype(BF16)
    tail_ref[...] = masked[rows - 3 :].astype(BF16)
    for start in range(8, cols - 8, 8):
        sums = band_conv(window, k_ref, start, rows, 0, False)
        for row in range(rows):
            o_ref[row, start - 8 : start, :] = sums[row]


def conv_side_kernel(f_ref, m_ref, k_ref, l_ref, r_ref, o_ref, window):
    rows, cols, _ = f_ref.shape
    window[:, 5:8, :] = l_ref[...].astype(F32)
    window[:, 8 : 8 + cols, :] = f_ref[...].astype(F32) * m_ref[...]
    window[:, 8 + cols : 11 + cols, :] = r_ref[...].astype(F32)
    for at, start in ((0, 0), (8, cols - 8)):
        sums = band_conv(window, k_ref, start, rows, 0, False)
        for row in range(rows):
            o_ref[row, at : at + 8, :] = sums[row]


def by_channels(shape, first=0):
    return pl.BlockSpec(shape[:-1] + (LANES,), lambda c: (0,) * (len(shape) - 1) + (c + first,))


def conv_inner(fields, mask_b, kernel):
    rows, cols, channels = fields.shape
    ends = (3, cols, channels)
    return pl.pallas_call(
        conv_inner_kernel,
        grid=(channels // LANES,),
        out_shape=[
            jax.ShapeDtypeStruct((rows, cols - 16, channels), F32),
            jax.ShapeDtypeStruct(ends, BF16),
            jax.ShapeDtypeStruct(ends, BF16),
        ],
        in_specs=[by_channels(fields.shape), whole_spec(mask_b.shape), by_channels(kernel.shape)],
        out_specs=[by_channels((rows, cols - 16, channels)), by_channels(ends), by_channels(ends)],
        scratch_shapes=[pltpu.VMEM((rows, cols + 16, LANES), F32)],
        compiler_params=params(16),
        cost_estimate=estimate(4),
        name="conv_inner",
    )(fields, mask_b, kernel)


def conv_side(fields, mask_b, kernel, left, right):
    rows, cols, channels = fields.shape
    return pl.pallas_call(
        conv_side_kernel,
        grid=(channels // LANES,),
        out_shape=jax.ShapeDtypeStruct((rows, 16, channels), F32),
        in_specs=[
            by_channels(fields.shape),
            whole_spec(mask_b.shape),
            by_channels(kernel.shape),
            by_channels(left.shape),
            by_channels(right.shape),
        ],
        out_specs=by_channels((rows, 16, channels)),
        scratch_shapes=[pltpu.VMEM((rows, cols + 16, LANES), F32)],
        compiler_params=params(16),
        cost_estimate=estimate(4),
        name="conv_side",
    )(fields, mask_b, kernel, left, right)


def gelu_pair(x):
    root = math.sqrt(2.0 / math.pi)
    square = x * x
    tanh = jnp.tanh(x * (root + (root * 0.044715) * square))
    half = 0.5 * tanh + 0.5
    value = x * half
    slope = half + value * ((1.0 - tanh) * (root + (3.0 * root * 0.044715) * square))
    return value, slope


def hidden_block(normed, normed_t, dbr, dbr_t, wi_ref, bi_ref, wo_ref, act_ref, dpre_ref, gbi_ref, grads_ref):
    cells = normed.shape[0]
    part = 256
    total = None
    for at in range(0, cells, part):
        here = slice(at, at + part)
        pre = jnp.dot(normed[here, :], wi_ref[...], preferred_element_type=F32) + bi_ref[...]
        d_act = lax.dot_general(
            dbr[here, :], wo_ref[...], (((1,), (1,)), ((), ())), preferred_element_type=F32
        )
        value, slope = gelu_pair(pre)
        act_ref[here, :] = value.astype(BF16)
        d_pre = d_act * slope
        dpre_ref[here, :] = d_pre.astype(BF16)
        sums = jnp.sum(d_pre, axis=0, keepdims=True)
        total = sums if total is None else total + sums
    gbi_ref[...] = total
    _, parts, _, width = grads_ref.shape
    for index, (left, right) in enumerate(((dbr_t, act_ref), (normed_t, dpre_ref))):
        grad = jnp.dot(left[...], right[...], preferred_element_type=F32).astype(BF16)
        for lat in range(parts):
            grads_ref[index, lat] = grad[:, lat * width : (lat + 1) * width]


def expand_first_kernel(
    order_ref,
    inner_ref, side_ref, top_ref, bot_ref, k_ref, gain_ref, bias_ref, scale_ref, m_ref, cot_ref,
    wi_ref, bi_ref, wo_ref,
    xhat_ref, inv_ref, gbo_ref, normed, normed_t, dbr, dbr_t, act_ref, dpre_ref, gbi_ref, grads_ref,
    conv, halo,
):
    rows, cols, channels = conv.shape
    cells = rows * cols

    @pl.when(pl.program_id(0) == 0)
    def _():
        conv[:, 0:8, :] = side_ref[:, 0:8, :]
        conv[:, 8 : cols - 8, :] = inner_ref[...]
        conv[:, cols - 8 : cols, :] = side_ref[:, 8:16, :]
        halo[0:3, 5 : 11 + cols, :] = top_ref[...].astype(F32)
        halo[3:6, 5 : 11 + cols, :] = bot_ref[...].astype(F32)
        for block in range(channels // LANES):
            lanes = slice(block * LANES, (block + 1) * LANES)
            for start in range(0, cols, 8):
                outs = list(range(3)) + list(range(rows - 3, rows))
                sums = {out: conv[out, start : start + 8, lanes] for out in outs}
                for col_off in range(7):
                    for src in range(6):
                        lat = src - 3 if src < 3 else rows + src - 3
                        offset = (5 + col_off) % SUB
                        base = start + (5 + col_off) // SUB * SUB
                        pair = halo[src, base : base + 2 * SUB, lanes]
                        cell = pltpu.roll(pair, 2 * SUB - offset, axis=0)[:SUB] if offset else pair[:SUB]
                        for out in outs:
                            row_off = lat - out + 3
                            if 0 <= row_off < 7:
                                tap = k_ref[row_off, col_off : col_off + 1, lanes]
                                sums[out] = sums[out] + tap * cell
                for out in outs:
                    conv[out, start : start + 8, lanes] = sums[out]
        gbo_ref[...] = jnp.zeros_like(gbo_ref)

        chunk = 128
        chunk_rows = chunk // cols

        def standardize(step, _):
            at = pl.multiple_of(step * chunk, chunk)
            here = pl.ds(at, chunk)
            there = pl.ds(step * chunk_rows, chunk_rows)
            x = conv[there].reshape(chunk, channels)
            mean = jnp.mean(x, axis=-1, keepdims=True)
            centered = x - mean
            var = jnp.mean(centered * centered, axis=-1, keepdims=True)
            inv = lax.rsqrt(var + 1e-06)
            xhat = centered * inv
            xhat_ref[here, :] = xhat
            inv_ref[here, :] = jnp.broadcast_to(inv, (chunk, LANES))
            scaled = xhat * gain_ref[...] + bias_ref[...]
            normed[here, :] = scaled.astype(BF16)
            normed_t[:, here] = scaled.T.astype(BF16)
            ocean = jnp.concatenate([m_ref[there].reshape(chunk, LANES)] * (channels // LANES), axis=1)
            grad = ocean * scale_ref[...] * cot_ref[here, :].astype(F32)
            gbo_ref[...] += jnp.sum(grad, axis=0, keepdims=True)
            dbr[here, :] = grad.astype(BF16)
            dbr_t[:, here] = grad.T.astype(BF16)
            return 0

        lax.fori_loop(0, cells // chunk, standardize, 0)

    hidden_block(
        normed, normed_t, dbr, dbr_t, wi_ref, bi_ref, wo_ref, act_ref, dpre_ref, gbi_ref, grads_ref
    )


def expand_second_kernel(
    order_ref, normed, normed_t, dbr, dbr_t, wi_ref, bi_ref, wo_ref, act_in, dpre_in, gbi_in,
    act_ref, dpre_ref, gbi_ref, grads_ref,
):
    hidden_block(
        normed, normed_t, dbr, dbr_t, wi_ref, bi_ref, wo_ref, act_ref, dpre_ref, gbi_ref, grads_ref
    )


def hidden_specs(cells, channels, hidden, n_lon, n_lat, first):
    block = hidden // n_lon
    split = n_lat if (block // n_lat) % LANES == 0 else 1
    weights = [
        pl.BlockSpec((channels, block), lambda h, order: (0, order[h + first])),
        pl.BlockSpec((1, block), lambda h, order: (0, order[h + first])),
        pl.BlockSpec((block, channels), lambda h, order: (order[h + first], 0)),
    ]
    results = [
        pl.BlockSpec((cells, block), lambda h, order: (0, order[h + first])),
        pl.BlockSpec((cells, block), lambda h, order: (0, order[h + first])),
        pl.BlockSpec((1, block), lambda h, order: (0, order[h + first])),
        pl.BlockSpec((2, None, split, channels, block // split), lambda h, order: (0, h, 0, 0, 0)),
    ]
    shapes = [
        jax.ShapeDtypeStruct((cells, hidden), BF16),
        jax.ShapeDtypeStruct((cells, hidden), BF16),
        jax.ShapeDtypeStruct((1, hidden), F32),
        jax.ShapeDtypeStruct((2, n_lon // 2, split, channels, block // split), BF16),
    ]
    return weights, results, shapes


def expand_first(order, inner, side, top, bot, kernel, gain, bias, scale, mask_b, cot, w_in, b_in, w_out, n_lon, n_lat):
    rows, _, channels = inner.shape
    hidden = w_in.shape[1]
    cells, _ = cot.shape
    cols = cells // rows
    weights, results, shapes = hidden_specs(cells, channels, hidden, n_lon, n_lat, 0)
    flat = (cells, channels)
    turned = (channels, cells)
    own = [
        jax.ShapeDtypeStruct(flat, F32),
        jax.ShapeDtypeStruct((cells, LANES), F32),
        jax.ShapeDtypeStruct((1, channels), F32),
        jax.ShapeDtypeStruct(flat, BF16),
        jax.ShapeDtypeStruct(turned, BF16),
        jax.ShapeDtypeStruct(flat, BF16),
        jax.ShapeDtypeStruct(turned, BF16),
    ]
    given = (inner, side, top, bot, kernel, gain, bias, scale, mask_b, cot)
    return pl.pallas_call(
        expand_first_kernel,
        grid_spec=pltpu.PrefetchScalarGridSpec(
            num_scalar_prefetch=1,
            grid=(n_lon // 2,),
            in_specs=[once(x.shape) for x in given] + weights,
            out_specs=[once(x.shape) for x in own] + results,
            scratch_shapes=[
                pltpu.VMEM((rows, cols, channels), F32),
                pltpu.VMEM((6, cols + 16, channels), F32),
            ],
        ),
        out_shape=own + shapes,
        compiler_params=params(32),
        cost_estimate=estimate(12),
        name="expand_first",
    )(order, *given, w_in, b_in, w_out)


def expand_second(order, rows, w_in, b_in, w_out, act, dpre, gbi, n_lon, n_lat):
    cells, channels = rows[0].shape
    hidden = w_in.shape[1]
    weights, results, shapes = hidden_specs(cells, channels, hidden, n_lon, n_lat, n_lon // 2)
    return pl.pallas_call(
        expand_second_kernel,
        grid_spec=pltpu.PrefetchScalarGridSpec(
            num_scalar_prefetch=1,
            grid=(n_lon // 2,),
            in_specs=[once(x.shape) for x in rows] + weights + [UNUSED] * 3,
            out_specs=results,
        ),
        out_shape=shapes,
        input_output_aliases={8: 0, 9: 1, 10: 2},
        compiler_params=params(24),
        cost_estimate=estimate(8),
        name="expand_second",
    )(order, *rows, w_in, b_in, w_out, act, dpre, gbi)


def project_kernel(
    act_ref, dpre_ref, wo_ref, wi_ref, xhat_ref, inv_ref, f_ref, cot_ref, m_ref, scale_ref, gain_ref, bo_ref,
    ahead_wo, ahead_wi,
    mixed_ref, dconv_ref, sums_ref,
):
    cells, channels = xhat_ref.shape

    def wide(ref):
        return jnp.concatenate([ref[...].reshape(cells, LANES)] * (channels // LANES), axis=1)

    @pl.when(pl.program_id(0) == 0)
    def _():
        sums_ref[...] = jnp.zeros_like(sums_ref)

    branch = jnp.dot(act_ref[...], wo_ref[...], preferred_element_type=F32) + bo_ref[...]
    d_normed = lax.dot_general(
        dpre_ref[...], wi_ref[...], (((1,), (1,)), ((), ())), preferred_element_type=F32
    )
    ocean = wide(m_ref) * branch
    mixed_ref[...] = (f_ref[...].astype(F32) + ocean * scale_ref[...]).astype(BF16)
    xhat = xhat_ref[...]
    normed_term = d_normed * xhat
    sums_ref[0:1, :] += jnp.sum(ocean * cot_ref[...].astype(F32), axis=0, keepdims=True)
    sums_ref[1:2, :] += jnp.sum(normed_term, axis=0, keepdims=True)
    sums_ref[2:3, :] += jnp.sum(d_normed, axis=0, keepdims=True)
    e = d_normed * gain_ref[...]
    m1 = jnp.mean(e, axis=-1, keepdims=True)
    m2 = jnp.mean(normed_term * gain_ref[...], axis=-1, keepdims=True)
    dconv_ref[...] = (wide(inv_ref) * (e - m1 - xhat * m2)).astype(BF16)


def project(act, dpre, w_out, w_in, xhat, inv, fields, cot, mask_b, scale, gain, b_out, ahead_wo, ahead_wi):
    cells, hidden = act.shape
    channels = w_out.shape[1]
    part = 256

    def rows_of(width):
        return pl.BlockSpec((part, width), lambda i: (i, 0))

    return pl.pallas_call(
        project_kernel,
        grid=(cells // part,),
        out_shape=[
            jax.ShapeDtypeStruct((cells, channels), BF16),
            jax.ShapeDtypeStruct((cells, channels), BF16),
            jax.ShapeDtypeStruct((SUB, channels), F32),
        ],
        in_specs=[
            rows_of(hidden),
            rows_of(hidden),
            once(w_out.shape),
            once(w_in.shape),
            rows_of(channels),
            rows_of(LANES),
            rows_of(channels),
            rows_of(channels),
            pl.BlockSpec((part // mask_b.shape[1],) + mask_b.shape[1:], lambda i: (i, 0, 0)),
            whole_spec(scale.shape),
            whole_spec(gain.shape),
            whole_spec(b_out.shape),
            UNUSED,
            UNUSED,
        ],
        out_specs=[rows_of(channels), rows_of(channels), whole_spec((SUB, channels))],
        compiler_params=params(24),
        cost_estimate=estimate(9),
        name="project",
    )(act, dpre, w_out, w_in, xhat, inv, fields, cot, mask_b, scale, gain, b_out, ahead_wo, ahead_wi)


def fill_window(window, center, left, right, top, bot):
    rows, cols, _ = center.shape
    window[3 : 3 + rows, 5:8, :] = left[...].astype(F32)
    window[3 : 3 + rows, 8 : 8 + cols, :] = center
    window[3 : 3 + rows, 8 + cols : 11 + cols, :] = right[...].astype(F32)
    window[0:3, 5 : 11 + cols, :] = top[...].astype(F32)
    window[3 + rows : 6 + rows, 5 : 11 + cols, :] = bot[...].astype(F32)


def filter_grad_kernel(
    f_ref, m_ref, l_ref, r_ref, t_ref, b_ref, d_ref, sums_ref, gbo_ref, gbi_ref, ahead_a, ahead_b,
    o_ref, window, grad,
):
    rows, cols, _ = f_ref.shape
    fill_window(window, f_ref[...].astype(F32) * m_ref[...], l_ref, r_ref, t_ref, b_ref)
    grad[...] = d_ref[...].astype(F32)
    for col_off in range(7):

        def band(index, sums):
            start = pl.multiple_of(index * 8, 8)
            sums = list(sums)
            held = {}
            for src in range(rows + 6):
                if src < rows:
                    held[src] = grad[src, pl.ds(start, SUB), :]
                cells = shifted(window, src, start, 5 + col_off)
                for row_off in range(7):
                    out = src - row_off
                    if 0 <= out < rows:
                        sums[row_off] = sums[row_off] + held[out] * cells
            return tuple(sums)

        start = tuple(jnp.zeros((SUB, LANES), F32) for _ in range(7))
        sums = lax.fori_loop(0, cols // 8, band, start)
        for row_off in range(7):
            o_ref[row_off, col_off : col_off + 1, :] = jnp.sum(sums[row_off], axis=0, keepdims=True)
    o_ref[7, 0:3, :] = sums_ref[0:3, :]
    o_ref[7, 3:4, :] = gbo_ref[...]
    o_ref[7, 4:8, :] = gbi_ref[...]
    for row_off in range(7):
        o_ref[row_off, 7:8, :] = jnp.zeros((1, LANES), F32)


def filter_grad(fields, mask_b, left, right, top, bot, d_conv, sums, gbo, gbi, ahead, blocks, first):
    rows, cols, channels = fields.shape

    def part(x):
        return by_channels(x.shape, first)

    return pl.pallas_call(
        filter_grad_kernel,
        grid=(blocks,),
        out_shape=jax.ShapeDtypeStruct((8, 8, blocks * LANES), F32),
        in_specs=[
            part(fields),
            whole_spec(mask_b.shape),
            part(left),
            part(right),
            part(top),
            part(bot),
            part(d_conv),
            part(sums),
            part(gbo),
            part(gbi),
            UNUSED,
            UNUSED,
        ],
        out_specs=by_channels((8, 8, blocks * LANES)),
        scratch_shapes=[
            pltpu.VMEM((rows + 6, cols + 16, LANES), F32),
            pltpu.VMEM((rows, cols, LANES), F32),
        ],
        compiler_params=params(16),
        cost_estimate=estimate(4),
        name="filter_grad",
    )(fields, mask_b, left, right, top, bot, d_conv, sums, gbo, gbi, *ahead)


def input_grad_kernel(d_ref, l_ref, r_ref, t_ref, b_ref, k_ref, m_ref, cot_ref, a_ref, b2_ref, o_ref, window, grad):
    rows, cols, _ = d_ref.shape
    fill_window(window, d_ref[...].astype(F32), l_ref, r_ref, t_ref, b_ref)
    for start in range(0, cols, 8):
        sums = band_conv(window, k_ref, start, rows, 3, True)
        for row in range(rows):
            grad[row, start : start + 8, :] = sums[row]
    o_ref[...] = (cot_ref[...].astype(F32) + m_ref[...] * grad[...]).astype(BF16)


def input_grad_more_kernel(d_ref, l_ref, r_ref, t_ref, b_ref, k_ref, m_ref, cot_ref, a_ref, b2_ref, old_ref, o_ref, window, grad):
    input_grad_kernel(d_ref, l_ref, r_ref, t_ref, b_ref, k_ref, m_ref, cot_ref, a_ref, b2_ref, o_ref, window, grad)


def input_grad(d_conv, left, right, top, bot, kernel, mask_b, cot, ahead, blocks, first, old=None):
    rows, cols, channels = d_conv.shape

    def part(x):
        return by_channels(x.shape, first)

    more = [] if old is None else [old]
    return pl.pallas_call(
        input_grad_kernel if old is None else input_grad_more_kernel,
        grid=(blocks,),
        out_shape=jax.ShapeDtypeStruct((rows, cols, channels), BF16),
        in_specs=[
            part(d_conv),
            part(left),
            part(right),
            part(top),
            part(bot),
            part(kernel),
            whole_spec(mask_b.shape),
            part(cot),
        ]
        + [UNUSED] * (2 + len(more)),
        out_specs=part(d_conv),
        scratch_shapes=[
            pltpu.VMEM((rows + 6, cols + 16, LANES), F32),
            pltpu.VMEM((rows, cols, LANES), F32),
        ],
        input_output_aliases={} if old is None else {10: 0},
        compiler_params=params(16),
        cost_estimate=estimate(4),
        name="input_grad",
    )(d_conv, left, right, top, bot, kernel, mask_b, cot, *ahead, *more)


def swap(values, axis, bit):
    count = lax.axis_size(axis)
    return lax.ppermute(values, axis, [(i, i ^ bit) for i in range(count)])


def bits_of(axis):
    return [1 << k for k in range(int(math.log2(lax.axis_size(axis))))]


def halves(values, axis, dim, bit):
    mine = (lax.axis_index(axis) // bit) % 2
    shape = values.shape
    paired = values.reshape(shape[:dim] + (shape[dim] // 2, 2) + shape[dim + 1 :])
    kept = lax.dynamic_index_in_dim(paired, mine, dim + 1, keepdims=False)
    sent = lax.dynamic_index_in_dim(paired, 1 - mine, dim + 1, keepdims=False)
    return kept, sent.astype(BF16)


def total_sum(values):
    for axis in ("lon", "lat"):
        for bit in bits_of(axis):
            values = values + swap(values, axis, bit)
    return values


def side_halo(cells):
    count = lax.axis_size("lon")
    ahead = [(i, (i + 1) % count) for i in range(count)]
    back = [((i + 1) % count, i) for i in range(count)]
    cols = cells.shape[1]
    return (
        lax.ppermute(cells[:, cols - 3 :], "lon", ahead),
        lax.ppermute(cells[:, :3], "lon", back),
    )


def end_halo(head, tail, left, right):
    count = lax.axis_size("lat")
    ahead = [(i, i + 1) for i in range(count - 1)]
    back = [(i + 1, i) for i in range(count - 1)]
    rows = left.shape[0]
    tail = jnp.concatenate([left[rows - 3 :], tail, right[rows - 3 :]], axis=1)
    head = jnp.concatenate([left[:3], head, right[:3]], axis=1)
    return lax.ppermute(tail, "lat", ahead), lax.ppermute(head, "lat", back)


def per_device(
    fields,
    land_mask,
    cotangent,
    kernel,
    layer_norm_gain,
    layer_norm_bias,
    w_in,
    b_in,
    w_out,
    b_out,
    layer_scale,
):
    rows, cols, channels = fields.shape
    cells = rows * cols
    hidden = w_in.shape[1]
    n_lon, n_lat = lax.axis_size("lon"), lax.axis_size("lat")
    gain, bias = layer_norm_gain.reshape(1, -1), layer_norm_bias.reshape(1, -1)
    scale = layer_scale.reshape(1, -1)
    mask_b = jnp.broadcast_to(land_mask.astype(F32)[:, :, None], (rows, cols, LANES))
    cot_rows = cotangent.reshape(cells, channels)
    ocean = land_mask.astype(BF16)[:, :, None]
    edges = jnp.concatenate([fields[:, :3] * ocean[:, :3], fields[:, cols - 3 :] * ocean[:, cols - 3 :]], axis=1)

    left, right = side_halo(edges)
    inner, head, tail = conv_inner(fields, mask_b, kernel)
    top, bot = end_halo(head, tail, left, right)
    side = conv_side(fields, mask_b, kernel, left, right)

    core = lax.axis_index("lon") % 2
    pairs = 2 * jnp.arange(n_lon // 2, dtype=jnp.int32)
    order = jnp.concatenate([pairs + 1 - core, pairs + core])
    xhat, inv, g_bo, *row_forms, act, d_pre, g_bi, sent = expand_first(
        order, inner, side, top, bot, kernel, gain, bias, scale, mask_b, cot_rows,
        w_in, b_in.reshape(1, -1), w_out, n_lon, n_lat,
    )
    got = swap(sent, "lon", 1)
    act, d_pre, g_bi, kept = expand_second(
        order, row_forms, w_in, b_in.reshape(1, -1), w_out, act, d_pre, g_bi, n_lon, n_lat
    )

    def width_split(grads):
        if grads.shape[1] != n_lat:
            grads = grads.reshape(n_lon // 2, channels, n_lat, -1).transpose(0, 2, 1, 3)
        return grads

    owned = [width_split(kept[i]).astype(F32) + width_split(got[i]).astype(F32) for i in range(2)]
    steps = [("lon", 0, bit) for bit in bits_of("lon")[1:]] + [("lat", 1, bit) for bit in bits_of("lat")]
    cut = [halves(x, *steps[0][:2], steps[0][2]) for x in owned]

    mixed, d_conv, sums = project(
        act, d_pre, w_out, w_in, xhat, inv, fields.reshape(cells, channels), cot_rows, mask_b,
        scale, gain, b_out.reshape(1, -1), cut[0][1], cut[1][1],
    )
    d_conv = d_conv.reshape(rows, cols, channels)
    d_left, d_right = side_halo(d_conv)
    half = channels // LANES // 2
    g_bi = g_bi.reshape(-1, channels)
    low = filter_grad(
        fields, mask_b, left, right, top, bot, d_conv, sums, g_bo, g_bi, (sums, sums), half, 0
    )
    d_top, d_bot = end_halo(d_conv[:3], d_conv[rows - 3 :], d_left, d_right)
    high = filter_grad(
        fields, mask_b, left, right, top, bot, d_conv, sums, g_bo, g_bi, (d_left, low), half, half
    )

    def advance(index, step):
        axis, dim, bit = steps[step]
        kept, sent = cut[index]
        owned[index] = kept + swap(sent, axis, bit).astype(F32)
        if step + 1 < len(steps):
            axis, dim, bit = steps[step + 1]
            cut[index] = halves(owned[index], axis, dim, bit)

    for step in range(len(steps) - 2):
        advance(0, step)
    small = jnp.concatenate([low, high], axis=2)
    small = total_sum(small)
    grad_fields = input_grad(
        d_conv, d_left, d_right, d_top, d_bot, kernel, mask_b, cotangent, (cut[0][1], high), half, 0
    )
    for step in range(len(steps) - 2):
        advance(1, step)
    advance(0, len(steps) - 2)
    grad_fields = input_grad(
        d_conv, d_left, d_right, d_top, d_bot, kernel, mask_b, cotangent, (cut[0][1], cut[1][1]), half, half,
        grad_fields,
    )
    advance(1, len(steps) - 2)
    advance(0, len(steps) - 1)
    advance(1, len(steps) - 1)
    return (
        mixed.reshape(rows, cols, channels),
        grad_fields,
        small[:7, :7],
        small[7, 1],
        small[7, 2],
        owned[1][0, 0],
        small[7, 4:].reshape(hidden),
        owned[0][0, 0].T,
        small[7, 3],
        small[7, 0],
    )


def solution(mesh):
    placed = (
        P(("grp", "lat"), "lon", None),
        P(("grp", "lat"), "lon"),
        P(("grp", "lat"), "lon", None),
        P(),
        P(),
        P(),
        P(),
        P(),
        P(),
        P(),
        P(),
    )
    return jax.shard_map(
        per_device,
        mesh=mesh,
        in_specs=placed,
        out_specs=(
            P(("grp", "lat"), "lon", None),
            P(("grp", "lat"), "lon", None),
            P("grp", None, None),
            P("grp"),
            P("grp"),
            P("grp", ("lon", "lat")),
            P("grp"),
            P(("lon", "lat"), "grp"),
            P("grp"),
            P("grp"),
        ),
        check_vma=False,
    )
```

time: 151 us -> 147 us (0.974)
  local copies, waits for them, and re-layouts: 12.9 us -> 35.6 us
  waiting for transfers between devices: 35.4 us -> 18 us
  Pallas kernels: 61.2 us -> 55.2 us
  other arithmetic: 9.28 us -> 6.25 us
    unnamed x25 -> x75, local copies, waits for them, and re-layouts: 1.49 us -> 33.1 us
    ppermute x12 -> x11, waiting for transfers between devices: 30.3 us -> 9.96 us  [swap(): return lax.ppermute(values, axis, [(i, i ^ bit) for i in range(count)])]
    ppermute x2, waiting for transfers between devices: 0.01 us -> 7.17 us  [side_halo(): lax.ppermute(cells[:, cols - 3:], 'lon', ahead)]
    pallas_call x1, Pallas kernels: 11.1 us -> 6.58 us  [project(): pl.pallas_call(project_kernel, grid=(cells // part,), out_shape=[jax.Shap...]
    ppermute x2, waiting for transfers between devices: 3.8 us -> 0.01 us  [side_halo(): lax.ppermute(cells[:, :3], 'lon', back)]
    concatenate x5 -> x6, other arithmetic: 2.39 us -> 0.27 us  [the longest x2 0.09 us: end_halo(): tail = jnp.concatenate([left[rows - 3:], tail, right[rows - 3:]], axis=1)]
    squeeze x2 -> x0, local copies, waits for them, and re-layouts: 2.08 us -> none  [scatter_sum(): sent = lax.dynamic_index_in_dim(paired, 1 - mine, dim + 1, keepdims=False)]
    slice x2 -> x1, local copies, waits for them, and re-layouts: 2.08 us -> 0.11 us  [side_halo(): cells[:, :3]]
  transfers between devices with their start and end apart: 20 -> 19, of which waited for: 9 -> 7; matrix products, arithmetic and copies ran while one was open for 10% -> 3% of each run, Pallas kernels for 20% -> 30%
where the time goes in v2:
time: 147 us; the launch traced here: 146 us
  Pallas kernels  55.2 us (38%)
  local copies, waits for them, and re-layouts  35.6 us (24%)
  starting transfers between devices  30 us (20%)
  waiting for transfers between devices  18 us (12%)
  other arithmetic  6.25 us (4%)
    unnamed x75, local copies, waits for them, and re-layouts  33.1 us
    ppermute x11, starting transfers between devices, swap(): return lax.ppermute(values, axis, [(i, i ^ bit) for i in range(count)])  13.9 us
    pallas_call x1, Pallas kernels, expand_first(): pl.pallas_call(expand_first_kernel, grid_spec=pltpu.PrefetchScalarGridSpe...  11.6 us
    ppermute x4, starting transfers between devices, end_halo(): return (lax.ppermute(tail, 'lat', ahead), lax.ppermute(head, 'lat', back))  11.6 us
    pallas_call x2, Pallas kernels, input_grad(): pl.pallas_call(input_grad_kernel if old is None else input_grad_more_kern...  10.8 us
    ppermute x11, waiting for transfers between devices, swap(): return lax.ppermute(values, axis, [(i, i ^ bit) for i in range(count)])  9.96 us
    pallas_call x2, Pallas kernels, filter_grad(): pl.pallas_call(filter_grad_kernel, grid=(blocks,), out_shape=jax.ShapeDty...  9.92 us
    ppermute x2, waiting for transfers between devices, side_halo(): lax.ppermute(cells[:, cols - 3:], 'lon', ahead)  7.17 us
  transfers between devices with their start and end apart: 19, of which 7 were waited for; matrix products, arithmetic and copies ran while one was open for 3% of the time, Pallas kernels for 30%

profile of v2, /device:TPU:0, one launch (start us, length us, event | category | flops | bytes accessed | tf_op | source)
XLA Modules:
  0.0 146.3 jit_solution(18237950364910807320)
XLA Ops:
  3.2 2.0 %collective-permute-start.1 = (bf16[32,3,512]{2,1,0:T(4,128)(2,1)S(1)}, bf16[32,3,512]{2,1,0:T(4,128)(2,1)S(1)}, u32[]{:S(2)}, u32[]{:S(2)}) collective-permute-start(bf16[32,3,512]{2,1,0:T(4,128)(2,1)S(1)} %get-tuple-element.78), channel_id=1, source_target_pairs={{4,0},{8,4},{12,8},{0,12},{5,1},{9,5},{13,9},{1,13},{6,2},{10,6},{... | collective-permute-start | bytes 294920 | tf_op jit(solution)/shard_map/ppermute | solution.py:559
  7.6 4.6 %conv_inner.1 = (f32[32,16,512]{2,1,0:T(8,128)S(1)}, bf16[3,32,512]{2,1,0:T(8,128)(2,1)S(1)}, bf16[3,32,512]{2,1,0:T(8,128)(2,1)S(1)}) custom-call(bf16[32,32,512]{2,1,0:T(8,128)(2,1)S(1)} %copy-done, f32[32,32,128]{2,1,0:T(8,128)S(1)} %broadcast_in_dim.4.m_ref, f32[7,7,512]{2,1,0:T(8,128)S(1)} %copy-done.10), custom_call_target="tpu_custom_call" | custom-call | flops 4600000000 | bytes 14400000 | tf_op jit(solution)/shard_map/conv_inner/pallas_call | solution.py:100
  12.4 4.2 %collective-permute-start.2 = (bf16[3,38,512]{2,1,0:T(8,128)(2,1)S(1)}, bf16[3,38,512]{2,1,0:T(8,128)(2,1)S(1)}, u32[]{:S(2)}, u32[]{:S(2)}) collective-permute-start(bf16[3,38,512]{2,1,0:T(8,128)(2,1)S(1)} %pad_maximum_fusion.1), channel_id=1, source_target_pairs={{0,1},{1,2},{2,3},{4,5},{5,6},{6,7},{8,9},{9,10},{10,11},{12,13},{... | collective-permute-start | bytes 350216 | tf_op jit(solution)/shard_map/ppermute | solution.py:570
  18.3 4.6 %conv_side.1.side_ref = f32[32,16,512]{2,1,0:T(8,128)S(1)} custom-call(bf16[32,32,512]{2,1,0:T(8,128)(2,1)S(1)} %copy-done, f32[32,32,128]{2,1,0:T(8,128)S(1)} %broadcast_in_dim.4.m_ref, f32[7,7,512]{2,1,0:T(8,128)S(1)} %copy-done.10, bf16[32,3,512]{2,1,0:T(4,128)(2,1)S(1)} %collective-permute-done.l_ref, bf16[32,3,512]{2,1,0:T(4,128)(2,1)S(1)} %collective-permute-done.1.r_ref), custom_call_target="tpu_custom_call" | custom-call | flops 4600000000 | bytes 14400000 | tf_op jit(solution)/shard_map/conv_side/pallas_call | solution.py:119
  23.9 11.6 %expand_first.1 = (f32[1024,512]{1,0:T(8,128)S(1)}, f32[1024,128]{1,0:T(8,128)S(1)}, f32[1,512]{1,0:T(1,128)S(1)}, bf16[1024,512]{1,0:T(8,128)(2,1)S(1)}, bf16[5...) custom-call(s32[4]{0:T(128)S(1)} %pad_add_fusion.order_ref, ...), custom_call_target="tpu_custom_call" | custom-call | flops 13799999488 | bytes 43200000 | tf_op jit(solution)/shard_map/expand_first/pallas_call | solution.py:292
  35.5 2.0 %copy-done.17 = bf16[1024,2048]{1,0:T(8,128)(2,1)} copy-done((bf16[1024,2048]{1,0:T(8,128)(2,1)}, bf16[1024,2048]{1,0:T(8,128)(2,1)S(1)}, u32[]{:S(2)}) %copy-start.17) | copy-done | bytes 4194328
  46.7 2.2 %copy-done.18 = bf16[1024,2048]{1,0:T(8,128)(2,1)S(1)} copy-done((bf16[1024,2048]{1,0:T(8,128)(2,1)S(1)}, bf16[1024,2048]{1,0:T(8,128)(2,1)}, u32[]{:S(2)}) %copy-start.18) | copy-done | bytes 4194328
  48.9 2.2 %copy-done.21 = bf16[1024,2048]{1,0:T(8,128)(2,1)S(1)} copy-done((bf16[1024,2048]{1,0:T(8,128)(2,1)S(1)}, bf16[1024,2048]{1,0:T(8,128)(2,1)}, u32[]{:S(2)}) %copy-start.21) | copy-done | bytes 4194328
  56.0 7.1 %expand_second.1 = (bf16[1024,2048]{1,0:T(8,128)(2,1)S(1)}, bf16[1024,2048]{1,0:T(8,128)(2,1)S(1)}, f32[1,2048]{1,0:T(1,128)S(1)}, bf16[2,2,4,512,128]{4,3,2,1,0:T(8,128)(2,1)S(1)}) custom-call(s32[4]{0:T(128)S(1)} %pad_add_fusion.order_ref, bf16[1024,512]{1,0:T(8,128)(2,1)S(1)} %copy-done.27, ...), custom_call_target="tpu_custom_call", output_to_operand_aliasing={{0}: (8, {}), {1}: (9, {}), {2}: (10, {})} | custom-call | flops 9200000000 | bytes 28800000 | tf_op jit(solution)/shard_map/expand_second/pallas_call | solution.py:315
  65.1 2.0 %copy-done.22 = bf16[1024,2048]{1,0:T(8,128)(2,1)} copy-done((bf16[1024,2048]{1,0:T(8,128)(2,1)}, bf16[1024,2048]{1,0:T(8,128)(2,1)S(1)}, u32[]{:S(2)}) %copy-start.22) | copy-done | bytes 4194328
  68.3 2.2 %convert_add_fusion = (f32[1,2,4,512,128]{4,3,2,1,0:T(8,128)S(1)}, f32[1,2,4,512,128]{4,3,2,1,0:T(8,128)S(1)}) fusion(bf16[2,2,4,512,128]{4,3,2,1,0:T(8,128)(2,1)} %collective-permute-done.4, bf16[2,2,4,512,128]{4,3,2,1,0:T(8,128)(2,1)S(1)} %get-tuple-element.45), kind=kLoop, calls=%fused_computation | loop fusion | flops 3145728 | bytes 8388608 | tf_op jit(solution)/shard_map/add | solution.py:619
  73.1 2.2 %copy-done.23 = bf16[1024,2048]{1,0:T(8,128)(2,1)S(1)} copy-done((bf16[1024,2048]{1,0:T(8,128)(2,1)S(1)}, bf16[1024,2048]{1,0:T(8,128)(2,1)}, u32[]{:S(2)}) %copy-start.23) | copy-done | bytes 4194328
  78.0 6.6 %project.1 = (bf16[1024,512]{1,0:T(8,128)(2,1)}, bf16[1024,512]{1,0:T(8,128)(2,1)S(1)}, f32[8,512]{1,0:T(8,128)S(1)}) custom-call(bf16[1024,2048]{1,0:T(8,128)(2,1)S(1)} %copy-done.20, bf16[1024,2048]{1,0:T(8,128)(2,1)S(1)} %copy-done.23, bf16[2048,512]{1,0:T(8,128)(2,1)S(1)} %copy-done.7, bf16[512,2048]{1,0:T(8,128)(2,1)S(1)} %copy-done.4, ...), custom_call_target="tpu_custom_call" | custom-call | flops 10350000128 | bytes 32400000 | tf_op jit(solution)/shard_map/project/pallas_call | solution.py:370
  86.6 5.0 %filter_grad.2.ahead_b = f32[8,8,256]{2,1,0:T(8,128)S(1)} custom-call(bf16[32,32,512]{2,1,0:T(8,128)(2,1)S(1)} %copy-done.1, f32[32,32,128]{2,1,0:T(8,128)S(1)} %broadcast_in_dim.4.m_ref, bf16[32,3,512]{2,1,0:T(4,128)(2,1)S(1)} %collective-permute-done.l_ref, bf16[32,3,512]{2,1,0:T(4,128)(2,1)S(1)} %collective-permute-done.1.r_ref, ...), custom_call_target="tpu_custom_call" | custom-call | flops 4600000000 | bytes 14400000 | tf_op jit(solution)/shard_map/filter_grad/pallas_call | solution.py:450
  91.6 7.2 %collective-permute-done.5.ahead_a.l_ref = bf16[32,3,512]{2,1,0:T(4,128)(2,1)S(1)} collective-permute-done((bf16[32,3,512]{2,1,0:T(4,128)(2,1)S(1)}, bf16[32,3,512]{2,1,0:T(4,128)(2,1)S(1)}, u32[]{:S(2)}, u32[]{:S(2)}) %collective-permute-start.5) | collective-permute-done | bytes 98336 | tf_op jit(solution)/shard_map/ppermute | solution.py:558
  98.7 5.0 %filter_grad.3.b2_ref = f32[8,8,256]{2,1,0:T(8,128)S(1)} custom-call(bf16[32,32,512]{2,1,0:T(8,128)(2,1)S(1)} %copy-done.1, f32[32,32,128]{2,1,0:T(8,128)S(1)} %broadcast_in_dim.4.m_ref, bf16[32,3,512]{2,1,0:T(4,128)(2,1)S(1)} %collective-permute-done.l_ref, bf16[32,3,512]{2,1,0:T(4,128)(2,1)S(1)} %collective-permute-done.1.r_ref, ...), custom_call_target="tpu_custom_call" | custom-call | flops 4600000000 | bytes 14400000 | tf_op jit(solution)/shard_map/filter_grad/pallas_call | solution.py:450
  106.8 4.0 %collective-permute-done.13 = f32[8,8,512]{2,1,0:T(8,128)S(1)} collective-permute-done((f32[8,8,512]{2,1,0:T(8,128)S(1)}, f32[8,8,512]{2,1,0:T(8,128)S(1)}, u32[]{:S(2)}, u32[]{:S(2)}) %collective-permute-start.13) | collective-permute-done | bytes 131104 | tf_op jit(solution)/shard_map/ppermute | solution.py:529
  114.0 4.6 %collective-permute-start.7 = (bf16[3,38,512]{2,1,0:T(8,128)(2,1)S(1)}, bf16[3,38,512]{2,1,0:T(8,128)(2,1)S(1)}, u32[]{:S(2)}, u32[]{:S(2)}) collective-permute-start(bf16[3,38,512]{2,1,0:T(8,128)(2,1)S(1)} %pad_maximum_fusion.3), channel_id=1, source_target_pairs={{0,1},{1,2},{2,3},{4,5},{5,6},{6,7},{8,9},{9,10},{10,11},{12,13},{... | collective-permute-start | bytes 350216 | tf_op jit(solution)/shard_map/ppermute | solution.py:570
  118.6 2.7 %collective-permute-start.15 = (f32[8,8,512]{2,1,0:T(8,128)S(1)}, f32[8,8,512]{2,1,0:T(8,128)S(1)}, u32[]{:S(2)}, u32[]{:S(2)}) collective-permute-start(f32[8,8,512]{2,1,0:T(8,128)S(1)} %add.112), channel_id=1, source_target_pairs={{0,2},{1,3},{2,0},{3,1},{4,6},{5,7},{6,4},{7,5},{8,10},{9,11},{10,... | collective-permute-start | bytes 393224 | tf_op jit(solution)/shard_map/ppermute | solution.py:529
  121.7 2.1 %collective-permute-start.16 = (bf16[1,2,512,128]{3,2,1,0:T(8,128)(2,1)S(1)}, bf16[1,2,512,128]{3,2,1,0:T(8,128)(2,1)S(1)}, u32[]{:S(2)}, u32[]{:S(2)}) collective-permute-start(bf16[1,2,512,128]{3,2,1,0:T(8,128)(2,1)S(1)} %fusion.3.b2_ref), channel_id=1, source_target_pairs={{0,1},{1,0},{2,3},{3,2},{4,5},{5,4},{6,7},{7,6},{8,9},{9,8},{10,11... | collective-permute-start | bytes 786440 | tf_op jit(solution)/shard_map/ppermute | solution.py:529
  123.8 5.4 %input_grad.2.old_ref = bf16[32,32,512]{2,1,0:T(8,128)(2,1)} custom-call(bf16[32,32,512]{2,1,0:T(8,128)(2,1)S(1)} %bitcast.59, bf16[32,3,512]{2,1,0:T(4,128)(2,1)S(1)} %collective-permute-done.5.ahead_a.l_ref, bf16[32,3,512]{2,1,0:T(4,128)(2,1)S(1)} %collective-permute-done.6.r_ref, bf16[3,38,512]{2,1,0:T(8,128)(2,1)S(1)} %collective-permute-done.7.t_ref, ...), custom_call_target="tpu_custom_call" | custom-call | flops 4600000000 | bytes 14400000 | tf_op jit(solution)/shard_map/input_grad/pallas_call | solution.py:500
  131.3 2.8 %collective-permute-start.18 = (bf16[1,1,512,128]{3,2,1,0:T(8,128)(2,1)S(1)}, bf16[1,1,512,128]{3,2,1,0:T(8,128)(2,1)S(1)}, u32[]{:S(2)}, u32[]{:S(2)}) collective-permute-start(bf16[1,1,512,128]{3,2,1,0:T(8,128)(2,1)S(1)} %dynamic-slice_convert_fusion.3.a_ref), channel_id=1, source_target_pairs={{0,2},{1,3},{2,0},{3,1},{4,6},{5,7},{6,4},{7,5},{8,10},{9,11},{10,... | collective-permute-start | bytes 393224 | tf_op jit(solution)/shard_map/ppermute | solution.py:529
  134.1 4.1 %collective-permute-done.16 = bf16[1,2,512,128]{3,2,1,0:T(8,128)(2,1)S(1)} collective-permute-done((bf16[1,2,512,128]{3,2,1,0:T(8,128)(2,1)S(1)}, bf16[1,2,512,128]{3,2,1,0:T(8,128)(2,1)S(1)}, u32[]{:S(2)}, u32[]{:S(2)}) %collective-permute-start.16) | collective-permute-done | bytes 262176 | tf_op jit(solution)/shard_map/ppermute | solution.py:529
  138.9 5.4 %input_grad.3 = bf16[32,32,512]{2,1,0:T(8,128)(2,1)} custom-call(bf16[32,32,512]{2,1,0:T(8,128)(2,1)S(1)} %bitcast.60, bf16[32,3,512]{2,1,0:T(4,128)(2,1)S(1)} %collective-permute-done.5.ahead_a.l_ref, bf16[32,3,512]{2,1,0:T(4,128)(2,1)S(1)} %collective-permute-done.6.r_ref, ...), custom_call_target="tpu_custom_call", output_to_operand_aliasing={{}: (10, {})} | custom-call | flops 4600000000 | bytes 14400000 | tf_op jit(solution)/shard_map/input_grad/pallas_call | solution.py:500
  (137 shorter events, 43.6 us)
Async XLA Ops:
  2.7 9.6 %collective-permute-start = (bf16[32,3,512]{2,1,0:T(4,128)(2,1)S(1)}, bf16[32,3,512]{2,1,0:T(4,128)(2,1)S(1)}, u32[]{:S(2)}, u32[]{:S(2)}) collective-permute-start(bf16[32,3,512]{2,1,0:T(4,128)(2,1)S(1)} %get-tuple-element.79), channel_id=1, source_target_pairs={{0,4},{4,8},{8,12},{12,0},{1,5},{5,9},{9,13},{13,1},{2,6},{6,10},{... | collective-permute-start | bytes 294920 | tf_op jit(solution)/shard_map/ppermute | solution.py:558
  3.2 9.1 %collective-permute-start.1 = (bf16[32,3,512]{2,1,0:T(4,128)(2,1)S(1)}, bf16[32,3,512]{2,1,0:T(4,128)(2,1)S(1)}, u32[]{:S(2)}, u32[]{:S(2)}) collective-permute-start(bf16[32,3,512]{2,1,0:T(4,128)(2,1)S(1)} %get-tuple-element.78), channel_id=1, source_target_pairs={{4,0},{8,4},{12,8},{0,12},{5,1},{9,5},{13,9},{1,13},{6,2},{10,6},{... | collective-permute-start | bytes 294920 | tf_op jit(solution)/shard_map/ppermute | solution.py:559
  12.4 10.5 %collective-permute-start.2 = (bf16[3,38,512]{2,1,0:T(8,128)(2,1)S(1)}, bf16[3,38,512]{2,1,0:T(8,128)(2,1)S(1)}, u32[]{:S(2)}, u32[]{:S(2)}) collective-permute-start(bf16[3,38,512]{2,1,0:T(8,128)(2,1)S(1)} %pad_maximum_fusion.1), channel_id=1, source_target_pairs={{0,1},{1,2},{2,3},{4,5},{5,6},{6,7},{8,9},{9,10},{10,11},{12,13},{... | collective-permute-start | bytes 350216 | tf_op jit(solution)/shard_map/ppermute | solution.py:570
  16.7 7.1 %copy-start.2 = (bf16[512,2048]{1,0:T(8,128)(2,1)S(1)}, bf16[512,2048]{1,0:T(8,128)(2,1)}, u32[]{:S(2)}) copy-start(bf16[512,2048]{1,0:T(8,128)(2,1)} %wi_ref.5) | copy-start | bytes 6291460
  16.7 7.1 %copy-start.5 = (bf16[2048,512]{1,0:T(8,128)(2,1)S(1)}, bf16[2048,512]{1,0:T(8,128)(2,1)}, u32[]{:S(2)}) copy-start(bf16[2048,512]{1,0:T(8,128)(2,1)} %wo_ref.5) | copy-start | bytes 6291460
  16.7 7.1 %copy-start.8 = (bf16[32,32,512]{2,1,0:T(8,128)(2,1)S(1)}, bf16[32,32,512]{2,1,0:T(8,128)(2,1)}, u32[]{:S(2)}) copy-start(bf16[32,32,512]{2,1,0:T(8,128)(2,1)} %cot_ref.3) | copy-start | bytes 3145732
  16.7 7.1 %copy-start.11 = (f32[7,7,512]{2,1,0:T(8,128)S(1)}, f32[7,7,512]{2,1,0:T(8,128)}, u32[]{:S(2)}) copy-start(f32[7,7,512]{2,1,0:T(8,128)} %k_ref.9) | copy-start | bytes 301060
  16.7 7.1 %copy-start.12 = (f32[2048]{0:T(1024)S(1)}, f32[2048]{0:T(1024)}, u32[]{:S(2)}) copy-start(f32[2048]{0:T(1024)} %param.18) | copy-start | bytes 24580
  16.8 7.0 %collective-permute-start.3 = (bf16[3,38,512]{2,1,0:T(8,128)(2,1)S(1)}, bf16[3,38,512]{2,1,0:T(8,128)(2,1)S(1)}, u32[]{:S(2)}, u32[]{:S(2)}) collective-permute-start(bf16[3,38,512]{2,1,0:T(8,128)(2,1)S(1)} %pad_maximum_fusion.2), channel_id=1, source_target_pairs={{1,0},{2,1},{3,2},{5,4},{6,5},{7,6},{9,8},{10,9},{11,10},{13,12},{... | collective-permute-start | bytes 350216 | tf_op jit(solution)/shard_map/ppermute | solution.py:570
  43.5 24.8 %collective-permute-start.4 = (bf16[2,2,4,512,128]{4,3,2,1,0:T(8,128)(2,1)}, bf16[2,2,4,512,128]{4,3,2,1,0:T(8,128)(2,1)}, u32[]{:S(2)}, u32[]{:S(2)}) collective-permute-start(bf16[2,2,4,512,128]{4,3,2,1,0:T(8,128)(2,1)} %get-tuple-element.46), channel_id=1, source_target_pairs={{0,4},{4,0},{8,12},{12,8},{1,5},{5,1},{9,13},{13,9},{2,6},{6,2},{1... | collective-permute-start | bytes 6291464 | tf_op jit(solution)/shard_map/ppermute | solution.py:529
  70.6 50.7 %collective-permute-start.9 = (bf16[1,4,512,128]{3,2,1,0:T(8,128)(2,1)S(1)}, bf16[1,4,512,128]{3,2,1,0:T(8,128)(2,1)S(1)}, u32[]{:S(2)}, u32[]{:S(2)}) collective-permute-start(bf16[1,4,512,128]{3,2,1,0:T(8,128)(2,1)S(1)} %fusion.ahead_wo), channel_id=1, source_target_pairs={{0,8},{4,12},{8,0},{12,4},{1,9},{5,13},{9,1},{13,5},{2,10},{6,14},... | collective-permute-start | bytes 1572872 | tf_op jit(solution)/shard_map/ppermute | solution.py:529
  72.3 49.2 %collective-permute-start.11 = (bf16[1,4,512,128]{3,2,1,0:T(8,128)(2,1)S(1)}, bf16[1,4,512,128]{3,2,1,0:T(8,128)(2,1)S(1)}, u32[]{:S(2)}, u32[]{:S(2)}) collective-permute-start(bf16[1,4,512,128]{3,2,1,0:T(8,128)(2,1)S(1)} %fusion.1.ahead_wi), channel_id=1, source_target_pairs={{0,8},{4,12},{8,0},{12,4},{1,9},{5,13},{9,1},{13,5},{2,10},{6,14},... | collective-permute-start | bytes 1572872 | tf_op jit(solution)/shard_map/ppermute | solution.py:529
  84.7 14.1 %collective-permute-start.5 = (bf16[32,3,512]{2,1,0:T(4,128)(2,1)S(1)}, bf16[32,3,512]{2,1,0:T(4,128)(2,1)S(1)}, u32[]{:S(2)}, u32[]{:S(2)}) collective-permute-start(bf16[32,3,512]{2,1,0:T(4,128)(2,1)S(1)} %get-tuple-element.77), channel_id=1, source_target_pairs={{0,4},{4,8},{8,12},{12,0},{1,5},{5,9},{9,13},{13,1},{2,6},{6,10},{... | collective-permute-start | bytes 294920 | tf_op jit(solution)/shard_map/ppermute | solution.py:558
  85.2 21.5 %collective-permute-start.6 = (bf16[32,3,512]{2,1,0:T(4,128)(2,1)S(1)}, bf16[32,3,512]{2,1,0:T(4,128)(2,1)S(1)}, u32[]{:S(2)}, u32[]{:S(2)}) collective-permute-start(bf16[32,3,512]{2,1,0:T(4,128)(2,1)S(1)} %get-tuple-element.76), channel_id=1, source_target_pairs={{4,0},{8,4},{12,8},{0,12},{5,1},{9,5},{13,9},{1,13},{6,2},{10,6},{... | collective-permute-start | bytes 294920 | tf_op jit(solution)/shard_map/ppermute | solution.py:559
  103.7 1.4 collective-permute-start.12
  105.2 5.6 %collective-permute-start.13 = (f32[8,8,512]{2,1,0:T(8,128)S(1)}, f32[8,8,512]{2,1,0:T(8,128)S(1)}, u32[]{:S(2)}, u32[]{:S(2)}) collective-permute-start(f32[8,8,512]{2,1,0:T(8,128)S(1)} %fusion.5), channel_id=1, source_target_pairs={{0,8},{4,12},{8,0},{12,4},{1,9},{5,13},{9,1},{13,5},{2,10},{6,14},... | collective-permute-start | bytes 393224 | tf_op jit(solution)/shard_map/ppermute | solution.py:529
  110.8 7.8 %collective-permute-start.14 = (f32[8,8,512]{2,1,0:T(8,128)S(1)}, f32[8,8,512]{2,1,0:T(8,128)S(1)}, u32[]{:S(2)}, u32[]{:S(2)}) collective-permute-start(f32[8,8,512]{2,1,0:T(8,128)S(1)} %add.111), channel_id=1, source_target_pairs={{0,1},{1,0},{2,3},{3,2},{4,5},{5,4},{6,7},{7,6},{8,9},{9,8},{10,11... | collective-permute-start | bytes 393224 | tf_op jit(solution)/shard_map/ppermute | solution.py:529
  112.7 11.1 %collective-permute-start.8 = (bf16[3,38,512]{2,1,0:T(8,128)(2,1)S(1)}, bf16[3,38,512]{2,1,0:T(8,128)(2,1)S(1)}, u32[]{:S(2)}, u32[]{:S(2)}) collective-permute-start(bf16[3,38,512]{2,1,0:T(8,128)(2,1)S(1)} %pad_maximum_fusion.4), channel_id=1, source_target_pairs={{1,0},{2,1},{3,2},{5,4},{6,5},{7,6},{9,8},{10,9},{11,10},{13,12},{... | collective-permute-start | bytes 350216 | tf_op jit(solution)/shard_map/ppermute | solution.py:570
  114.0 9.7 %collective-permute-start.7 = (bf16[3,38,512]{2,1,0:T(8,128)(2,1)S(1)}, bf16[3,38,512]{2,1,0:T(8,128)(2,1)S(1)}, u32[]{:S(2)}, u32[]{:S(2)}) collective-permute-start(bf16[3,38,512]{2,1,0:T(8,128)(2,1)S(1)} %pad_maximum_fusion.3), channel_id=1, source_target_pairs={{0,1},{1,2},{2,3},{4,5},{5,6},{6,7},{8,9},{9,10},{10,11},{12,13},{... | collective-permute-start | bytes 350216 | tf_op jit(solution)/shard_map/ppermute | solution.py:570
  118.6 10.5 %collective-permute-start.15 = (f32[8,8,512]{2,1,0:T(8,128)S(1)}, f32[8,8,512]{2,1,0:T(8,128)S(1)}, u32[]{:S(2)}, u32[]{:S(2)}) collective-permute-start(f32[8,8,512]{2,1,0:T(8,128)S(1)} %add.112), channel_id=1, source_target_pairs={{0,2},{1,3},{2,0},{3,1},{4,6},{5,7},{6,4},{7,5},{8,10},{9,11},{10,... | collective-permute-start | bytes 393224 | tf_op jit(solution)/shard_map/ppermute | solution.py:529
  121.5 9.8 %collective-permute-start.10 = (bf16[1,2,512,128]{3,2,1,0:T(8,128)(2,1)S(1)}, bf16[1,2,512,128]{3,2,1,0:T(8,128)(2,1)S(1)}, u32[]{:S(2)}, u32[]{:S(2)}) collective-permute-start(bf16[1,2,512,128]{3,2,1,0:T(8,128)(2,1)S(1)} %fusion.2.a_ref), channel_id=1, source_target_pairs={{0,1},{1,0},{2,3},{3,2},{4,5},{5,4},{6,7},{7,6},{8,9},{9,8},{10,11... | collective-permute-start | bytes 786440 | tf_op jit(solution)/shard_map/ppermute | solution.py:529
  121.7 16.5 %collective-permute-start.16 = (bf16[1,2,512,128]{3,2,1,0:T(8,128)(2,1)S(1)}, bf16[1,2,512,128]{3,2,1,0:T(8,128)(2,1)S(1)}, u32[]{:S(2)}, u32[]{:S(2)}) collective-permute-start(bf16[1,2,512,128]{3,2,1,0:T(8,128)(2,1)S(1)} %fusion.3.b2_ref), channel_id=1, source_target_pairs={{0,1},{1,0},{2,3},{3,2},{4,5},{5,4},{6,7},{7,6},{8,9},{9,8},{10,11... | collective-permute-start | bytes 786440 | tf_op jit(solution)/shard_map/ppermute | solution.py:529
  131.3 13.0 %collective-permute-start.18 = (bf16[1,1,512,128]{3,2,1,0:T(8,128)(2,1)S(1)}, bf16[1,1,512,128]{3,2,1,0:T(8,128)(2,1)S(1)}, u32[]{:S(2)}, u32[]{:S(2)}) collective-permute-start(bf16[1,1,512,128]{3,2,1,0:T(8,128)(2,1)S(1)} %dynamic-slice_convert_fusion.3.a_ref), channel_id=1, source_target_pairs={{0,2},{1,3},{2,0},{3,1},{4,6},{5,7},{6,4},{7,5},{8,10},{9,11},{10,... | collective-permute-start | bytes 393224 | tf_op jit(solution)/shard_map/ppermute | solution.py:529
  138.2 7.3 %collective-permute-start.17 = (bf16[1,1,512,128]{3,2,1,0:T(8,128)(2,1)S(1)}, bf16[1,1,512,128]{3,2,1,0:T(8,128)(2,1)S(1)}, u32[]{:S(2)}, u32[]{:S(2)}) collective-permute-start(bf16[1,1,512,128]{3,2,1,0:T(8,128)(2,1)S(1)} %dynamic-slice_convert_fusion.2), channel_id=1, source_target_pairs={{0,2},{1,3},{2,0},{3,1},{4,6},{5,7},{6,4},{7,5},{8,10},{9,11},{10,... | collective-permute-start | bytes 393224 | tf_op jit(solution)/shard_map/ppermute | solution.py:529
  (31 other events, 74.0 us)

commit v3 on v2

--- a/solution.py
+++ b/solution.py
@@ -108,7 +108,7 @@
         in_specs=[by_channels(fields.shape), whole_spec(mask_b.shape), by_channels(kernel.shape)],
         out_specs=[by_channels((rows, cols - 16, channels)), by_channels(ends), by_channels(ends)],
         scratch_shapes=[pltpu.VMEM((rows, cols + 16, LANES), F32)],
-        compiler_params=params(16),
+        compiler_params=params(56),
         cost_estimate=estimate(4),
         name="conv_inner",
     )(fields, mask_b, kernel)
@@ -129,7 +129,7 @@
         ],
         out_specs=by_channels((rows, 16, channels)),
         scratch_shapes=[pltpu.VMEM((rows, cols + 16, LANES), F32)],
-        compiler_params=params(16),
+        compiler_params=params(56),
         cost_estimate=estimate(4),
         name="conv_side",
     )(fields, mask_b, kernel, left, right)
@@ -145,7 +145,9 @@
     return value, slope
 
 
-def hidden_block(normed, normed_t, dbr, dbr_t, wi_ref, bi_ref, wo_ref, act_ref, dpre_ref, gbi_ref, grads_ref):
+def hidden_block(
+    normed, normed_t, dbr, dbr_t, wi_ref, bi_ref, wo_ref, act_ref, dpre_ref, gbi_ref, sent_ref, kept_ref
+):
     cells = normed.shape[0]
     part = 256
     total = None
@@ -162,18 +164,24 @@
         sums = jnp.sum(d_pre, axis=0, keepdims=True)
         total = sums if total is None else total + sums
     gbi_ref[...] = total
-    _, parts, _, width = grads_ref.shape
+    _, parts, _, width = sent_ref.shape
+    first = pl.program_id(0) < pl.num_programs(0) // 2
     for index, (left, right) in enumerate(((dbr_t, act_ref), (normed_t, dpre_ref))):
         grad = jnp.dot(left[...], right[...], preferred_element_type=F32).astype(BF16)
-        for lat in range(parts):
-            grads_ref[index, lat] = grad[:, lat * width : (lat + 1) * width]
+
+        def store(ref):
+            for lat in range(parts):
+                ref[index, lat] = grad[:, lat * width : (lat + 1) * width]
+
+        pl.when(first)(functools.partial(store, sent_ref))
+        pl.when(jnp.logical_not(first))(functools.partial(store, kept_ref))
 
 
 def expand_first_kernel(
     order_ref,
     inner_ref, side_ref, top_ref, bot_ref, k_ref, gain_ref, bias_ref, scale_ref, m_ref, cot_ref,
     wi_ref, bi_ref, wo_ref,
-    xhat_ref, inv_ref, gbo_ref, normed, normed_t, dbr, dbr_t, act_ref, dpre_ref, gbi_ref, grads_ref,
+    xhat_ref, inv_ref, gbo_ref, normed, normed_t, dbr, dbr_t, act_ref, dpre_ref, gbi_ref, sent_ref, kept_ref,
     conv, halo,
 ):
     rows, cols, channels = conv.shape
@@ -235,22 +243,24 @@
         lax.fori_loop(0, cells // chunk, standardize, 0)
 
     hidden_block(
-        normed, normed_t, dbr, dbr_t, wi_ref, bi_ref, wo_ref, act_ref, dpre_ref, gbi_ref, grads_ref
+        normed, normed_t, dbr, dbr_t, wi_ref, bi_ref, wo_ref, act_ref, dpre_ref, gbi_ref, sent_ref, kept_ref
     )
 
 
 def expand_second_kernel(
     order_ref, normed, normed_t, dbr, dbr_t, wi_ref, bi_ref, wo_ref, act_in, dpre_in, gbi_in,
-    act_ref, dpre_ref, gbi_ref, grads_ref,
+    act_ref, dpre_ref, gbi_ref, sent_ref, kept_ref,
 ):
     hidden_block(
-        normed, normed_t, dbr, dbr_t, wi_ref, bi_ref, wo_ref, act_ref, dpre_ref, gbi_ref, grads_ref
+        normed, normed_t, dbr, dbr_t, wi_ref, bi_ref, wo_ref, act_ref, dpre_ref, gbi_ref, sent_ref, kept_ref
     )
 
 
 def hidden_specs(cells, channels, hidden, n_lon, n_lat, first):
     block = hidden // n_lon
     split = n_lat if (block // n_lat) % LANES == 0 else 1
+    turn = n_lon // 4
+    grads = (2, None, split, channels, block // split)
     weights = [
         pl.BlockSpec((channels, block), lambda h, order: (0, order[h + first])),
         pl.BlockSpec((1, block), lambda h, order: (0, order[h + first])),
@@ -260,13 +270,15 @@
         pl.BlockSpec((cells, block), lambda h, order: (0, order[h + first])),
         pl.BlockSpec((cells, block), lambda h, order: (0, order[h + first])),
         pl.BlockSpec((1, block), lambda h, order: (0, order[h + first])),
-        pl.BlockSpec((2, None, split, channels, block // split), lambda h, order: (0, h, 0, 0, 0)),
+        pl.BlockSpec(grads, lambda h, order: (0, jnp.minimum(h, turn - 1), 0, 0, 0)),
+        pl.BlockSpec(grads, lambda h, order: (0, jnp.maximum(h - turn, 0), 0, 0, 0)),
     ]
     shapes = [
         jax.ShapeDtypeStruct((cells, hidden), BF16),
         jax.ShapeDtypeStruct((cells, hidden), BF16),
         jax.ShapeDtypeStruct((1, hidden), F32),
-        jax.ShapeDtypeStruct((2, n_lon // 2, split, channels, block // split), BF16),
+        jax.ShapeDtypeStruct((2, turn, split, channels, block // split), BF16),
+        jax.ShapeDtypeStruct((2, turn, split, channels, block // split), BF16),
     ]
     return weights, results, shapes
 
@@ -302,7 +314,7 @@
             ],
         ),
         out_shape=own + shapes,
-        compiler_params=params(32),
+        compiler_params=params(56),
         cost_estimate=estimate(12),
         name="expand_first",
     )(order, *given, w_in, b_in, w_out)
@@ -322,80 +334,119 @@
         ),
         out_shape=shapes,
         input_output_aliases={8: 0, 9: 1, 10: 2},
-        compiler_params=params(24),
+        compiler_params=params(56),
         cost_estimate=estimate(8),
         name="expand_second",
     )(order, *rows, w_in, b_in, w_out, act, dpre, gbi)
 
 
-def project_kernel(
-    act_ref, dpre_ref, wo_ref, wi_ref, xhat_ref, inv_ref, f_ref, cot_ref, m_ref, scale_ref, gain_ref, bo_ref,
-    ahead_wo, ahead_wi,
-    mixed_ref, dconv_ref, sums_ref,
-):
-    cells, channels = xhat_ref.shape
-
-    def wide(ref):
-        return jnp.concatenate([ref[...].reshape(cells, LANES)] * (channels // LANES), axis=1)
+def norm_back_kernel(dpre_ref, wi_ref, xhat_ref, inv_ref, gain_ref, ahead_ref, dconv_ref, sums_ref):
+    channels = xhat_ref.shape[1]
 
     @pl.when(pl.program_id(0) == 0)
     def _():
         sums_ref[...] = jnp.zeros_like(sums_ref)
 
-    branch = jnp.dot(act_ref[...], wo_ref[...], preferred_element_type=F32) + bo_ref[...]
     d_normed = lax.dot_general(
         dpre_ref[...], wi_ref[...], (((1,), (1,)), ((), ())), preferred_element_type=F32
     )
-    ocean = wide(m_ref) * branch
-    mixed_ref[...] = (f_ref[...].astype(F32) + ocean * scale_ref[...]).astype(BF16)
     xhat = xhat_ref[...]
     normed_term = d_normed * xhat
-    sums_ref[0:1, :] += jnp.sum(ocean * cot_ref[...].astype(F32), axis=0, keepdims=True)
-    sums_ref[1:2, :] += jnp.sum(normed_term, axis=0, keepdims=True)
-    sums_ref[2:3, :] += jnp.sum(d_normed, axis=0, keepdims=True)
+    sums_ref[0:1, :] += jnp.sum(normed_term, axis=0, keepdims=True)
+    sums_ref[1:2, :] += jnp.sum(d_normed, axis=0, keepdims=True)
     e = d_normed * gain_ref[...]
     m1 = jnp.mean(e, axis=-1, keepdims=True)
     m2 = jnp.mean(normed_term * gain_ref[...], axis=-1, keepdims=True)
-    dconv_ref[...] = (wide(inv_ref) * (e - m1 - xhat * m2)).astype(BF16)
-
-
-def project(act, dpre, w_out, w_in, xhat, inv, fields, cot, mask_b, scale, gain, b_out, ahead_wo, ahead_wi):
+    inv = jnp.concatenate([inv_ref[...]] * (channels // LANES), axis=1)
+    dconv_ref[...] = (inv * (e - m1 - xhat * m2)).astype(BF16)
+
+
+def norm_back(dpre, w_in, xhat, inv, gain, ahead):
+    cells, hidden = dpre.shape
+    channels = w_in.shape[0]
+    part = 256
+
+    def rows_of(width):
+        return pl.BlockSpec((part, width), lambda i: (i, 0))
+
+    return pl.pallas_call(
+        norm_back_kernel,
+        grid=(cells // part,),
+        out_shape=[
+            jax.ShapeDtypeStruct((cells, channels), BF16),
+            jax.ShapeDtypeStruct((SUB, channels), F32),
+        ],
+        in_specs=[
+            rows_of(hidden),
+            once(w_in.shape),
+            rows_of(channels),
+            rows_of(LANES),
+            whole_spec(gain.shape),
+            UNUSED,
+        ],
+        out_specs=[rows_of(channels), whole_spec((SUB, channels))],
+        compiler_params=params(56),
+        cost_estimate=estimate(4),
+        name="norm_back",
+    )(dpre, w_in, xhat, inv, gain, ahead)
+
+
+def project_kernel(
+    act_ref, wo_ref, f_ref, cot_ref, m_ref, scale_ref, bo_ref, kept_ref, got_ref,
+    mixed_ref, sums_ref, sent_ref,
+):
+    cells, channels = f_ref.shape
+
+    @pl.when(pl.program_id(0) == 0)
+    def _():
+        sums_ref[...] = jnp.zeros_like(sums_ref)
+
+    branch = jnp.dot(act_ref[...], wo_ref[...], preferred_element_type=F32) + bo_ref[...]
+    ocean = jnp.concatenate([m_ref[...].reshape(cells, LANES)] * (channels // LANES), axis=1) * branch
+    mixed_ref[...] = (f_ref[...].astype(F32) + ocean * scale_ref[...]).astype(BF16)
+    sums_ref[0:1, :] += jnp.sum(ocean * cot_ref[...].astype(F32), axis=0, keepdims=True)
+    sent_ref[...] = (kept_ref[...].astype(F32) + got_ref[...].astype(F32)).astype(BF16)
+
+
+def project(act, w_out, fields, cot, mask_b, scale, b_out, kept, got):
     cells, hidden = act.shape
     channels = w_out.shape[1]
     part = 256
+    steps = cells // part
 
     def rows_of(width):
         return pl.BlockSpec((part, width), lambda i: (i, 0))
 
+    grads = kept.shape[1:3] + (channels // steps, kept.shape[4])
+    both = pl.BlockSpec((None,) + grads, lambda i: (1, 0, 0, i, 0))
     return pl.pallas_call(
         project_kernel,
-        grid=(cells // part,),
+        grid=(steps,),
         out_shape=[
             jax.ShapeDtypeStruct((cells, channels), BF16),
-            jax.ShapeDtypeStruct((cells, channels), BF16),
             jax.ShapeDtypeStruct((SUB, channels), F32),
+            jax.ShapeDtypeStruct(kept.shape[1:], BF16),
         ],
         in_specs=[
             rows_of(hidden),
-            rows_of(hidden),
             once(w_out.shape),
-            once(w_in.shape),
-            rows_of(channels),
-            rows_of(LANES),
             rows_of(channels),
             rows_of(channels),
             pl.BlockSpec((part // mask_b.shape[1],) + mask_b.shape[1:], lambda i: (i, 0, 0)),
             whole_spec(scale.shape),
-            whole_spec(gain.shape),
             whole_spec(b_out.shape),
-            UNUSED,
-            UNUSED,
-        ],
-        out_specs=[rows_of(channels), rows_of(channels), whole_spec((SUB, channels))],
-        compiler_params=params(24),
-        cost_estimate=estimate(9),
+            both,
+            both,
+        ],
+        out_specs=[
+            rows_of(channels),
+            whole_spec((SUB, channels)),
+            pl.BlockSpec(grads, lambda i: (0, 0, i, 0)),
+        ],
+        compiler_params=params(56),
+        cost_estimate=estimate(4),
         name="project",
-    )(act, dpre, w_out, w_in, xhat, inv, fields, cot, mask_b, scale, gain, b_out, ahead_wo, ahead_wi)
+    )(act, w_out, fields, cot, mask_b, scale, b_out, kept, got)
 
 
 def fill_window(window, center, left, right, top, bot):
@@ -408,7 +459,7 @@
 
 
 def filter_grad_kernel(
-    f_ref, m_ref, l_ref, r_ref, t_ref, b_ref, d_ref, sums_ref, gbo_ref, gbi_ref, ahead_a, ahead_b,
+    f_ref, m_ref, l_ref, r_ref, t_ref, b_ref, d_ref, gsc_ref, sums_ref, gbo_ref, gbi_ref,
     o_ref, window, grad,
 ):
     rows, cols, _ = f_ref.shape
@@ -434,23 +485,24 @@
         sums = lax.fori_loop(0, cols // 8, band, start)
         for row_off in range(7):
             o_ref[row_off, col_off : col_off + 1, :] = jnp.sum(sums[row_off], axis=0, keepdims=True)
-    o_ref[7, 0:3, :] = sums_ref[0:3, :]
+    o_ref[7, 0:1, :] = gsc_ref[0:1, :]
+    o_ref[7, 1:3, :] = sums_ref[0:2, :]
     o_ref[7, 3:4, :] = gbo_ref[...]
     o_ref[7, 4:8, :] = gbi_ref[...]
     for row_off in range(7):
         o_ref[row_off, 7:8, :] = jnp.zeros((1, LANES), F32)
 
 
-def filter_grad(fields, mask_b, left, right, top, bot, d_conv, sums, gbo, gbi, ahead, blocks, first):
+def filter_grad(fields, mask_b, left, right, top, bot, d_conv, gsc, sums, gbo, gbi):
     rows, cols, channels = fields.shape
 
     def part(x):
-        return by_channels(x.shape, first)
+        return by_channels(x.shape)
 
     return pl.pallas_call(
         filter_grad_kernel,
-        grid=(blocks,),
-        out_shape=jax.ShapeDtypeStruct((8, 8, blocks * LANES), F32),
+        grid=(channels // LANES,),
+        out_shape=jax.ShapeDtypeStruct((8, 8, channels), F32),
         in_specs=[
             part(fields),
             whole_spec(mask_b.shape),
@@ -459,24 +511,23 @@
             part(top),
             part(bot),
             part(d_conv),
+            part(gsc),
             part(sums),
             part(gbo),
             part(gbi),
-            UNUSED,
-            UNUSED,
-        ],
-        out_specs=by_channels((8, 8, blocks * LANES)),
+        ],
+        out_specs=by_channels((8, 8, channels)),
         scratch_shapes=[
             pltpu.VMEM((rows + 6, cols + 16, LANES), F32),
             pltpu.VMEM((rows, cols, LANES), F32),
         ],
-        compiler_params=params(16),
+        compiler_params=params(56),
         cost_estimate=estimate(4),
         name="filter_grad",
-    )(fields, mask_b, left, right, top, bot, d_conv, sums, gbo, gbi, *ahead)
-
-
-def input_grad_kernel(d_ref, l_ref, r_ref, t_ref, b_ref, k_ref, m_ref, cot_ref, a_ref, b2_ref, o_ref, window, grad):
+    )(fields, mask_b, left, right, top, bot, d_conv, gsc, sums, gbo, gbi)
+
+
+def input_grad_kernel(d_ref, l_ref, r_ref, t_ref, b_ref, k_ref, m_ref, cot_ref, o_ref, window, grad):
     rows, cols, _ = d_ref.shape
     fill_window(window, d_ref[...].astype(F32), l_ref, r_ref, t_ref, b_ref)
     for start in range(0, cols, 8):
@@ -486,11 +537,11 @@
     o_ref[...] = (cot_ref[...].astype(F32) + m_ref[...] * grad[...]).astype(BF16)
 
 
-def input_grad_more_kernel(d_ref, l_ref, r_ref, t_ref, b_ref, k_ref, m_ref, cot_ref, a_ref, b2_ref, old_ref, o_ref, window, grad):
-    input_grad_kernel(d_ref, l_ref, r_ref, t_ref, b_ref, k_ref, m_ref, cot_ref, a_ref, b2_ref, o_ref, window, grad)
-
-
-def input_grad(d_conv, left, right, top, bot, kernel, mask_b, cot, ahead, blocks, first, old=None):
+def input_grad_more_kernel(d_ref, l_ref, r_ref, t_ref, b_ref, k_ref, m_ref, cot_ref, old_ref, o_ref, window, grad):
+    input_grad_kernel(d_ref, l_ref, r_ref, t_ref, b_ref, k_ref, m_ref, cot_ref, o_ref, window, grad)
+
+
+def input_grad(d_conv, left, right, top, bot, kernel, mask_b, cot, blocks, first, old=None):
     rows, cols, channels = d_conv.shape
 
     def part(x):
@@ -511,17 +562,17 @@
             whole_spec(mask_b.shape),
             part(cot),
         ]
-        + [UNUSED] * (2 + len(more)),
+        + [UNUSED] * len(more),
         out_specs=part(d_conv),
         scratch_shapes=[
             pltpu.VMEM((rows + 6, cols + 16, LANES), F32),
             pltpu.VMEM((rows, cols, LANES), F32),
         ],
-        input_output_aliases={} if old is None else {10: 0},
-        compiler_params=params(16),
+        input_output_aliases={} if old is None else {8: 0},
+        compiler_params=params(56),
         cost_estimate=estimate(4),
         name="input_grad",
-    )(d_conv, left, right, top, bot, kernel, mask_b, cot, *ahead, *more)
+    )(d_conv, left, right, top, bot, kernel, mask_b, cot, *more)
 
 
 def swap(values, axis, bit):
@@ -531,6 +582,10 @@
 
 def bits_of(axis):
     return [1 << k for k in range(int(math.log2(lax.axis_size(axis))))]
+
+
+def after(value, *others):
+    return lax.optimization_barrier((value,) + others)[0]
 
 
 def halves(values, axis, dim, bit):
@@ -542,31 +597,25 @@
     return kept, sent.astype(BF16)
 
 
-def total_sum(values):
-    for axis in ("lon", "lat"):
-        for bit in bits_of(axis):
-            values = values + swap(values, axis, bit)
-    return values
-
-
-def side_halo(cells):
+def side_halo(last, first):
     count = lax.axis_size("lon")
     ahead = [(i, (i + 1) % count) for i in range(count)]
     back = [((i + 1) % count, i) for i in range(count)]
-    cols = cells.shape[1]
+    return lax.ppermute(last, "lon", ahead), lax.ppermute(first, "lon", back)
+
+
+def end_rows(head, tail, left, right):
+    rows = left.shape[0]
     return (
-        lax.ppermute(cells[:, cols - 3 :], "lon", ahead),
-        lax.ppermute(cells[:, :3], "lon", back),
-    )
-
-
-def end_halo(head, tail, left, right):
+        jnp.concatenate([left[rows - 3 :], tail, right[rows - 3 :]], axis=1),
+        jnp.concatenate([left[:3], head, right[:3]], axis=1),
+    )
+
+
+def end_halo(tail, head):
     count = lax.axis_size("lat")
     ahead = [(i, i + 1) for i in range(count - 1)]
     back = [(i + 1, i) for i in range(count - 1)]
-    rows = left.shape[0]
-    tail = jnp.concatenate([left[rows - 3 :], tail, right[rows - 3 :]], axis=1)
-    head = jnp.concatenate([left[:3], head, right[:3]], axis=1)
     return lax.ppermute(tail, "lat", ahead), lax.ppermute(head, "lat", back)
 
 
@@ -592,75 +641,89 @@
     mask_b = jnp.broadcast_to(land_mask.astype(F32)[:, :, None], (rows, cols, LANES))
     cot_rows = cotangent.reshape(cells, channels)
     ocean = land_mask.astype(BF16)[:, :, None]
-    edges = jnp.concatenate([fields[:, :3] * ocean[:, :3], fields[:, cols - 3 :] * ocean[:, cols - 3 :]], axis=1)
-
-    left, right = side_halo(edges)
+    left, right = side_halo(fields[:, cols - 3 :] * ocean[:, cols - 3 :], fields[:, :3] * ocean[:, :3])
     inner, head, tail = conv_inner(fields, mask_b, kernel)
-    top, bot = end_halo(head, tail, left, right)
+    top, bot = end_halo(*end_rows(head, tail, left, right))
     side = conv_side(fields, mask_b, kernel, left, right)
 
-    core = lax.axis_index("lon") % 2
-    pairs = 2 * jnp.arange(n_lon // 2, dtype=jnp.int32)
-    order = jnp.concatenate([pairs + 1 - core, pairs + core])
-    xhat, inv, g_bo, *row_forms, act, d_pre, g_bi, sent = expand_first(
+    lon = lax.axis_index("lon")
+    core, side_y = lon % 2, (lon // 2) % 2
+    quads = 4 * jnp.arange(n_lon // 4, dtype=jnp.int32)
+    order = jnp.concatenate(
+        [quads + 2 * y + c for y in (1 - side_y, side_y) for c in (1 - core, core)]
+    )
+    xhat, inv, g_bo, *row_forms, act, d_pre, g_bi, sent_far, kept_far = expand_first(
         order, inner, side, top, bot, kernel, gain, bias, scale, mask_b, cot_rows,
         w_in, b_in.reshape(1, -1), w_out, n_lon, n_lat,
     )
-    got = swap(sent, "lon", 1)
-    act, d_pre, g_bi, kept = expand_second(
+    got_far = swap(sent_far, "lon", 1)
+    act, d_pre, g_bi, sent_near, kept_near = expand_second(
         order, row_forms, w_in, b_in.reshape(1, -1), w_out, act, d_pre, g_bi, n_lon, n_lat
     )
-
-    def width_split(grads):
-        if grads.shape[1] != n_lat:
-            grads = grads.reshape(n_lon // 2, channels, n_lat, -1).transpose(0, 2, 1, 3)
-        return grads
-
-    owned = [width_split(kept[i]).astype(F32) + width_split(got[i]).astype(F32) for i in range(2)]
-    steps = [("lon", 0, bit) for bit in bits_of("lon")[1:]] + [("lat", 1, bit) for bit in bits_of("lat")]
-    cut = [halves(x, *steps[0][:2], steps[0][2]) for x in owned]
-
-    mixed, d_conv, sums = project(
-        act, d_pre, w_out, w_in, xhat, inv, fields.reshape(cells, channels), cot_rows, mask_b,
-        scale, gain, b_out.reshape(1, -1), cut[0][1], cut[1][1],
-    )
+    got_near = swap(sent_near, "lon", 1)
+
+    far_wo = (kept_far[0].astype(F32) + got_far[0].astype(F32)).astype(BF16)
+    got_wo = swap(far_wo, "lon", 2)
+    d_conv, sums = norm_back(d_pre, w_in, xhat, inv, gain, far_wo)
     d_conv = d_conv.reshape(rows, cols, channels)
-    d_left, d_right = side_halo(d_conv)
-    half = channels // LANES // 2
-    g_bi = g_bi.reshape(-1, channels)
-    low = filter_grad(
-        fields, mask_b, left, right, top, bot, d_conv, sums, g_bo, g_bi, (sums, sums), half, 0
-    )
-    d_top, d_bot = end_halo(d_conv[:3], d_conv[rows - 3 :], d_left, d_right)
-    high = filter_grad(
-        fields, mask_b, left, right, top, bot, d_conv, sums, g_bo, g_bi, (d_left, low), half, half
-    )
-
-    def advance(index, step):
+    d_last, d_first = d_conv[:, cols - 3 :], d_conv[:, :3]
+    d_left, d_right = side_halo(d_last, d_first)
+    mixed, g_scale, far_wi = project(
+        after(act, d_last, d_first), w_out, fields.reshape(cells, channels), cot_rows, mask_b, scale,
+        b_out.reshape(1, -1), kept_far, got_far,
+    )
+    got_wi = swap(far_wi, "lon", 2)
+    d_tail, d_head = end_rows(
+        d_conv[:3], d_conv[rows - 3 :], after(d_left, mixed), after(d_right, mixed)
+    )
+    d_top, d_bot = end_halo(d_tail, d_head)
+
+    steps = [("lon", 0, bit) for bit in bits_of("lon")[2:]] + [("lat", 1, bit) for bit in bits_of("lat")]
+    owned, cut = [None, None], [None, None]
+
+    def begin(index, got, last):
+        both = after(kept_near[index], last).astype(F32) + after(got_near[index], last).astype(F32)
+        x = both + after(got, last).astype(F32)
+        if x.shape[1] != n_lat:
+            x = x.reshape(n_lon // 4, channels, n_lat, -1).transpose(0, 2, 1, 3)
+        cut[index] = halves(x, *steps[0])
+
+    def advance(index, step, last):
         axis, dim, bit = steps[step]
         kept, sent = cut[index]
-        owned[index] = kept + swap(sent, axis, bit).astype(F32)
+        owned[index] = after(kept, last) + after(swap(sent, axis, bit), last).astype(F32)
         if step + 1 < len(steps):
-            axis, dim, bit = steps[step + 1]
-            cut[index] = halves(owned[index], axis, dim, bit)
-
+            cut[index] = halves(owned[index], *steps[step + 1])
+
+    hops = [(axis, bit) for axis in ("lon", "lat") for bit in bits_of(axis)]
+
+    def spread(hop, last):
+        return after(small, last) + after(swap(small, *hops[hop]), last)
+
+    begin(0, got_wo, mixed)
+    small = filter_grad(
+        after(fields, d_tail, d_head, far_wi, cut[0][1]), mask_b, left, right, top, bot, d_conv,
+        g_scale, sums, g_bo, g_bi.reshape(-1, channels),
+    )
+    for step in range(len(steps) - 1):
+        advance(0, step, small)
+    begin(1, got_wi, small)
     for step in range(len(steps) - 2):
-        advance(0, step)
-    small = jnp.concatenate([low, high], axis=2)
-    small = total_sum(small)
+        advance(1, step, small)
+    half = channels // LANES // 2
+    back = (d_left, d_right, d_top, d_bot, kernel, mask_b, cotangent)
+    grad_fields = input_grad(after(d_conv, small, cut[0][1], cut[1][1]), *back, half, 0)
+    small = spread(0, grad_fields)
+    advance(1, len(steps) - 2, grad_fields)
+    advance(0, len(steps) - 1, grad_fields)
+    grad_fields = input_grad(after(d_conv, small, cut[1][1]), *back, half // 2, half, grad_fields)
+    small = spread(1, grad_fields)
     grad_fields = input_grad(
-        d_conv, d_left, d_right, d_top, d_bot, kernel, mask_b, cotangent, (cut[0][1], high), half, 0
-    )
-    for step in range(len(steps) - 2):
-        advance(1, step)
-    advance(0, len(steps) - 2)
-    grad_fields = input_grad(
-        d_conv, d_left, d_right, d_top, d_bot, kernel, mask_b, cotangent, (cut[0][1], cut[1][1]), half, half,
-        grad_fields,
-    )
-    advance(1, len(steps) - 2)
-    advance(0, len(steps) - 1)
-    advance(1, len(steps) - 1)
+        after(d_conv, small), *back, half // 2, half + half // 2, grad_fields
+    )
+    for hop in range(2, len(hops)):
+        small = spread(hop, grad_fields)
+    advance(1, len(steps) - 1, grad_fields)
     return (
         mixed.reshape(rows, cols, channels),
         grad_fields,

time: 147 us -> 144 us (0.980)
  Pallas kernels: 55.2 us -> 82.8 us
  local copies, waits for them, and re-layouts: 35.6 us -> 9.53 us
  waiting for transfers between devices: 18 us -> 9.26 us
  other arithmetic: 6.25 us -> 11.7 us
    unnamed x75 -> x19, local copies, waits for them, and re-layouts: 33.1 us -> 2.17 us
    pallas_call x3, Pallas kernels: 16.5 us -> 26.5 us  [the longest x1 11.6 us: filter_grad(): pl.pallas_call(filter_grad_kernel, grid=(channels // LANES,), out_shape=j...]
    ppermute x4, waiting for transfers between devices: 7.17 us -> 0.01 us  [side_halo(): return (lax.ppermute(last, 'lon', ahead), lax.ppermute(first, 'lon', back))]
    pallas_call x1, Pallas kernels: 11.6 us -> 17.3 us  [expand_first(): pl.pallas_call(expand_first_kernel, grid_spec=pltpu.PrefetchScalarGridSpe...]
    pallas_call x1, Pallas kernels: 7.11 us -> 11.7 us  [expand_second(): pl.pallas_call(expand_second_kernel, grid_spec=pltpu.PrefetchScalarGridSp...]
    pallas_call x2 -> x3, Pallas kernels: 10.8 us -> 14.9 us  [input_grad(): pl.pallas_call(input_grad_kernel if old is None else input_grad_more_kern...]
    concatenate x6 -> x5, other arithmetic: 0.27 us -> 3.95 us  [the longest x2 1.71 us: end_rows(): jnp.concatenate([left[rows - 3:], tail, right[rows - 3:]], axis=1)]
    slice x6 -> x5, local copies, waits for them, and re-layouts: 0.16 us -> 2.13 us  [the longest x1 1.14 us: per_device(): d_last, d_first = (d_conv[:, cols - 3:], d_conv[:, :3])]
  transfers between devices with their start and end apart: 19 -> 20, of which waited for: 7 -> 2; matrix products, arithmetic and copies ran while one was open for 3% -> 11% of each run, Pallas kernels for 30% -> 46%
where the time goes in v3:
time: 144 us; the launch traced here: 143 us
  Pallas kernels  82.8 us (58%)
  starting transfers between devices  29 us (20%)
  other arithmetic  11.7 us (8%)
  local copies, waits for them, and re-layouts  9.53 us (7%)
  waiting for transfers between devices  9.26 us (6%)
    pallas_call x1, Pallas kernels, expand_first(): pl.pallas_call(expand_first_kernel, grid_spec=pltpu.PrefetchScalarGridSpe...  17.3 us
    pallas_call x3, Pallas kernels, input_grad(): pl.pallas_call(input_grad_kernel if old is None else input_grad_more_kern...  14.9 us
    ppermute x12, starting transfers between devices, swap(): return lax.ppermute(values, axis, [(i, i ^ bit) for i in range(count)])  12.7 us
    ppermute x4, starting transfers between devices, end_halo(): return (lax.ppermute(tail, 'lat', ahead), lax.ppermute(head, 'lat', back))  12 us
    pallas_call x1, Pallas kernels, expand_second(): pl.pallas_call(expand_second_kernel, grid_spec=pltpu.PrefetchScalarGridSp...  11.7 us
    pallas_call x1, Pallas kernels, filter_grad(): pl.pallas_call(filter_grad_kernel, grid=(channels // LANES,), out_shape=j...  11.6 us
    ppermute x12, waiting for transfers between devices, swap(): return lax.ppermute(values, axis, [(i, i ^ bit) for i in range(count)])  9.24 us
    pallas_call x1, Pallas kernels, norm_back(): pl.pallas_call(norm_back_kernel, grid=(cells // part,), out_shape=[jax.Sh...  7.67 us
  transfers between devices with their start and end apart: 20, of which 2 were waited for; matrix products, arithmetic and copies ran while one was open for 11% of the time, Pallas kernels for 46%

profile of v3, /device:TPU:0, one launch (start us, length us, event | category | flops | bytes accessed | tf_op | source)
XLA Modules:
  0.0 143.4 jit_solution(7541226298365389418)
XLA Ops:
  3.2 2.0 %collective-permute-start.1 = (bf16[32,3,512]{2,1,0:T(4,128)(2,1)S(1)}, bf16[32,3,512]{2,1,0:T(4,128)(2,1)S(1)}, u32[]{:S(2)}, u32[]{:S(2)}) collective-permute-start(bf16[32,3,512]{2,1,0:T(4,128)(2,1)S(1)} %get-tuple-element.126), channel_id=1, source_target_pairs={{4,0},{8,4},{12,8},{0,12},{5,1},{9,5},{13,9},{1,13},{6,2},{10,6},{... | collective-permute-start | bytes 294920 | tf_op jit(solution)/shard_map/ppermute | solution.py:604
  6.2 6.3 %conv_inner.1 = (f32[32,16,512]{2,1,0:T(8,128)}, bf16[3,32,512]{2,1,0:T(8,128)(2,1)}, bf16[3,32,512]{2,1,0:T(8,128)(2,1)}) custom-call(bf16[32,32,512]{2,1,0:T(8,128)(2,1)} %f_ref.4, f32[32,32,128]{2,1,0:T(8,128)} %broadcast_in_dim.4.m_ref, f32[7,7,512]{2,1,0:T(8,128)} %k_ref.11), custom_call_target="tpu_custom_call" | custom-call | flops 4600000000 | bytes 14400000 | tf_op jit(solution)/shard_map/conv_inner/pallas_call | solution.py:100
  14.2 4.2 %collective-permute-start.2 = (bf16[3,38,512]{2,1,0:T(8,128)(2,1)S(1)}, bf16[3,38,512]{2,1,0:T(8,128)(2,1)S(1)}, u32[]{:S(2)}, u32[]{:S(2)}) collective-permute-start(bf16[3,38,512]{2,1,0:T(8,128)(2,1)S(1)} %pad_maximum_fusion), channel_id=1, source_target_pairs={{0,1},{1,2},{2,3},{4,5},{5,6},{6,7},{8,9},{9,10},{10,11},{12,13},{... | collective-permute-start | bytes 350216 | tf_op jit(solution)/shard_map/ppermute | solution.py:619
  19.3 1.3 collective-permute-start.3
  20.6 6.1 %conv_side.1.side_ref = f32[32,16,512]{2,1,0:T(8,128)} custom-call(bf16[32,32,512]{2,1,0:T(8,128)(2,1)} %f_ref.4, f32[32,32,128]{2,1,0:T(8,128)} %broadcast_in_dim.4.m_ref, f32[7,7,512]{2,1,0:T(8,128)} %k_ref.11, bf16[32,3,512]{2,1,0:T(4,128)(2,1)} %copy-done.2, bf16[32,3,512]{2,1,0:T(4,128)(2,1)} %copy-done.3), custom_call_target="tpu_custom_call" | custom-call | flops 4600000000 | bytes 14400000 | tf_op jit(solution)/shard_map/conv_side/pallas_call | solution.py:119
  27.5 17.3 %expand_first.1 = (f32[1024,512]{1,0:T(8,128)}, f32[1024,128]{1,0:T(8,128)}, f32[1,512]{1,0:T(1,128)}, bf16[1024,512]{1,0:T(8,128)(2,1)}, bf16[512,1024]{1,0:T(8...) custom-call(s32[4]{0:T(128)} %pad_add_fusion.order_ref, ...), custom_call_target="tpu_custom_call" | custom-call | flops 13799999488 | bytes 43200000 | tf_op jit(solution)/shard_map/expand_first/pallas_call | solution.py:304
  44.9 11.7 %expand_second.1 = (bf16[1024,2048]{1,0:T(8,128)(2,1)}, bf16[1024,2048]{1,0:T(8,128)(2,1)}, f32[1,2048]{1,0:T(1,128)}, bf16[2,1,4,512,128]{4,3,2,1,0:T(8,128)(2,1)}, bf16[2,1,4,512,128]{4,3,2,1,0:T(8,128)(2,1)}) custom-call(s32[4]{0:T(128)} %pad_add_fusion.order_ref, ...), custom_call_target="tpu_custom_call", output_to_operand_aliasing={{0}: (8, {}), {1}: (9, {}), {2}: (10, {})} | custom-call | flops 9200000000 | bytes 28800000 | tf_op jit(solution)/shard_map/expand_second/pallas_call | solution.py:327
  58.8 1.4 reduce.3
  60.8 1.3 fusion.ahead_ref
  62.1 1.6 %collective-permute-start.8 = (bf16[1,4,512,128]{3,2,1,0:T(8,128)(2,1)S(1)}, bf16[1,4,512,128]{3,2,1,0:T(8,128)(2,1)S(1)}, u32[]{:S(2)}, u32[]{:S(2)}) collective-permute-start(bf16[1,4,512,128]{3,2,1,0:T(8,128)(2,1)S(1)} %fusion.ahead_ref), channel_id=1, source_target_pairs={{0,8},{4,12},{8,0},{12,4},{1,9},{5,13},{9,1},{13,5},{2,10},{6,14},... | collective-permute-start | bytes 1572872 | tf_op jit(solution)/shard_map/ppermute | solution.py:580
  63.7 7.7 %norm_back.1 = (bf16[1024,512]{1,0:T(8,128)(2,1)}, f32[8,512]{1,0:T(8,128)}) custom-call(bf16[1024,2048]{1,0:T(8,128)(2,1)} %get-tuple-element.75.dpre_ref, bf16[512,2048]{1,0:T(8,128)(2,1)} %wi_ref.5, f32[1024,512]{1,0:T(8,128)} %get-tuple-element.76.xhat_ref, f32[1024,128]{1,0:T(8,128)} %get-tuple-element.77.inv_ref, f32[1,512]{1,0:T(1,128)} %bitcast.82, ...), custom_call_target="tpu_custom_call" | custom-call | flops 4600000000 | bytes 14400000 | tf_op jit(solution)/shard_map/norm_back/pallas_call | solution.py:372
  72.6 1.7 %collective-permute-start.6 = (bf16[32,3,512]{2,1,0:T(4,128)(2,1)S(1)}, bf16[32,3,512]{2,1,0:T(4,128)(2,1)S(1)}, u32[]{:S(2)}, u32[]{:S(2)}) collective-permute-start(bf16[32,3,512]{2,1,0:T(4,128)(2,1)S(1)} %get-tuple-element.124), channel_id=1, source_target_pairs={{4,0},{8,4},{12,8},{0,12},{5,1},{9,5},{13,9},{1,13},{6,2},{10,6},{... | collective-permute-start | bytes 294920 | tf_op jit(solution)/shard_map/ppermute | solution.py:604
  74.4 7.3 %project.1 = (bf16[1024,512]{1,0:T(8,128)(2,1)}, f32[8,512]{1,0:T(8,128)}, bf16[1,4,512,128]{3,2,1,0:T(8,128)(2,1)}) custom-call(bf16[1024,2048]{1,0:T(8,128)(2,1)} %get-tuple-element.81.act_ref, bf16[2048,512]{1,0:T(8,128)(2,1)} %wo_ref.5, bf16[1024,512]{1,0:T(8,128)(2,1)} %bitcast.70, bf16[1024,512]{1,0:T(8,128)(2,1)} %bitcast.77, ...), custom_call_target="tpu_custom_call" | custom-call | flops 4600000000 | bytes 14400000 | tf_op jit(solution)/shard_map/project/pallas_call | solution.py:422
  84.2 5.2 %collective-permute-start.11 = (bf16[3,38,512]{2,1,0:T(8,128)(2,1)}, bf16[3,38,512]{2,1,0:T(8,128)(2,1)}, u32[]{:S(2)}, u32[]{:S(2)}) collective-permute-start(bf16[3,38,512]{2,1,0:T(8,128)(2,1)} %pad_maximum_fusion.2), channel_id=1, source_target_pairs={{0,1},{1,2},{2,3},{4,5},{5,6},{6,7},{8,9},{9,10},{10,11},{12,13},{... | collective-permute-start | bytes 350216 | tf_op jit(solution)/shard_map/ppermute | solution.py:619
  92.5 2.6 %collective-permute-start.9 = (bf16[1,2,512,128]{2,3,1,0:T(8,128)(2,1)}, bf16[1,2,512,128]{2,3,1,0:T(8,128)(2,1)S(1)}, u32[]{:S(2)}, u32[]{:S(2)}) collective-permute-start(bf16[1,2,512,128]{2,3,1,0:T(8,128)(2,1)} %bitcast.57), channel_id=1, source_target_pairs={{0,1},{1,0},{2,3},{3,2},{4,5},{5,4},{6,7},{7,6},{8,9},{9,8},{10,11... | collective-permute-start | bytes 786440 | tf_op jit(solution)/shard_map/ppermute | solution.py:580
  95.1 11.6 %filter_grad.1 = f32[8,8,512]{2,1,0:T(8,128)} custom-call(bf16[32,32,512]{2,1,0:T(8,128)(2,1)} %f_ref.4, f32[32,32,128]{2,1,0:T(8,128)} %broadcast_in_dim.4.m_ref, bf16[32,3,512]{2,1,0:T(4,128)(2,1)} %copy-done.2, bf16[32,3,512]{2,1,0:T(4,128)(2,1)} %copy-done.3, bf16[3,38,512]{2,1,0:T(8,128)(2,1)} %copy-done.6, bf16[3,38,512]{2,1,0:T(8,128)(2,1)} %copy-done.7, ...), custom_call_target="tpu_custom_call" | custom-call | flops 4600000000 | bytes 14400000 | tf_op jit(solution)/shard_map/filter_grad/pallas_call | solution.py:502
  108.5 2.6 %collective-permute-start.19 = (bf16[1,1,512,128]{2,3,1,0:T(8,128)(2,1)S(1)}, bf16[1,1,512,128]{2,3,1,0:T(8,128)(2,1)S(1)}, u32[]{:S(2)}, u32[]{:S(2)}) collective-permute-start(bf16[1,1,512,128]{2,3,1,0:T(8,128)(2,1)S(1)} %dynamic-slice_convert_fusion.1), channel_id=1, source_target_pairs={{0,2},{1,3},{2,0},{3,1},{4,6},{5,7},{6,4},{7,5},{8,10},{9,11},{10,... | collective-permute-start | bytes 393224 | tf_op jit(solution)/shard_map/ppermute | solution.py:580
  111.2 6.5 %input_grad.3.old_ref = bf16[32,32,512]{2,1,0:T(8,128)(2,1)} custom-call(bf16[32,32,512]{2,1,0:T(8,128)(2,1)} %bitcast.67, bf16[32,3,512]{2,1,0:T(4,128)(2,1)} %copy-done.4, bf16[32,3,512]{2,1,0:T(4,128)(2,1)} %copy-done.5, bf16[3,38,512]{2,1,0:T(8,128)(2,1)} %collective-permute-done.11.t_ref, bf16[3,38,512]{2,1,0:T(8,128)(2,1)} %collective-permute-done.12.b_ref, ...), custom_call_target="tpu_custom_call" | custom-call | flops 4600000000 | bytes 14400000 | tf_op jit(solution)/shard_map/input_grad/pallas_call | solution.py:551
  117.7 2.1 %collective-permute-done.14 = bf16[1,2,512,128]{3,2,1,0:T(8,128)(2,1)S(1)} collective-permute-done((bf16[1,2,512,128]{3,2,1,0:T(8,128)(2,1)S(1)}, bf16[1,2,512,128]{3,2,1,0:T(8,128)(2,1)S(1)}, u32[]{:S(2)}, u32[]{:S(2)}) %collective-permute-start.14) | collective-permute-done | bytes 262176 | tf_op jit(solution)/shard_map/ppermute | solution.py:580
  120.0 1.4 collective-permute-start.15
  121.8 4.2 %input_grad.4.old_ref = bf16[32,32,512]{2,1,0:T(8,128)(2,1)} custom-call(bf16[32,32,512]{2,1,0:T(8,128)(2,1)} %bitcast.68, bf16[32,3,512]{2,1,0:T(4,128)(2,1)} %copy-done.4, bf16[32,3,512]{2,1,0:T(4,128)(2,1)} %copy-done.5, bf16[3,38,512]{2,1,0:T(8,128)(2,1)} %collective-permute-done.11.t_ref, ...), custom_call_target="tpu_custom_call", output_to_operand_aliasing={{}: (8, {})} | custom-call | flops 4600000000 | bytes 14400000 | tf_op jit(solution)/shard_map/input_grad/pallas_call | solution.py:551
  126.0 2.5 %collective-permute-start.16 = (f32[8,8,512]{2,1,0:T(8,128)S(1)}, f32[8,8,512]{2,1,0:T(8,128)S(1)}, u32[]{:S(2)}, u32[]{:S(2)}) collective-permute-start(f32[8,8,512]{2,1,0:T(8,128)S(1)} %add.141), channel_id=1, source_target_pairs={{0,1},{1,0},{2,3},{3,2},{4,5},{5,4},{6,7},{7,6},{8,9},{9,8},{10,11... | collective-permute-start | bytes 393224 | tf_op jit(solution)/shard_map/ppermute | solution.py:580
  128.5 4.2 %input_grad.5 = bf16[32,32,512]{2,1,0:T(8,128)(2,1)} custom-call(bf16[32,32,512]{2,1,0:T(8,128)(2,1)} %bitcast.69, bf16[32,3,512]{2,1,0:T(4,128)(2,1)} %copy-done.4, bf16[32,3,512]{2,1,0:T(4,128)(2,1)} %copy-done.5, bf16[3,38,512]{2,1,0:T(8,128)(2,1)} %collective-permute-done.11.t_ref, ...), custom_call_target="tpu_custom_call", output_to_operand_aliasing={{}: (8, {})} | custom-call | flops 4600000000 | bytes 14400000 | tf_op jit(solution)/shard_map/input_grad/pallas_call | solution.py:551
  134.4 7.1 %collective-permute-done.17 = f32[8,8,512]{2,1,0:T(8,128)S(1)} collective-permute-done((f32[8,8,512]{2,1,0:T(8,128)S(1)}, f32[8,8,512]{2,1,0:T(8,128)S(1)}, u32[]{:S(2)}, u32[]{:S(2)}) %collective-permute-start.17) | collective-permute-done | bytes 131104 | tf_op jit(solution)/shard_map/ppermute | solution.py:580
  (86 shorter events, 22.4 us)
Async XLA Ops:
  2.7 10.4 %collective-permute-start = (bf16[32,3,512]{2,1,0:T(4,128)(2,1)S(1)}, bf16[32,3,512]{2,1,0:T(4,128)(2,1)S(1)}, u32[]{:S(2)}, u32[]{:S(2)}) collective-permute-start(bf16[32,3,512]{2,1,0:T(4,128)(2,1)S(1)} %get-tuple-element.127), channel_id=1, source_target_pairs={{0,4},{4,8},{8,12},{12,0},{1,5},{5,9},{9,13},{13,1},{2,6},{6,10},{... | collective-permute-start | bytes 294920 | tf_op jit(solution)/shard_map/ppermute | solution.py:604
  3.2 9.9 %collective-permute-start.1 = (bf16[32,3,512]{2,1,0:T(4,128)(2,1)S(1)}, bf16[32,3,512]{2,1,0:T(4,128)(2,1)S(1)}, u32[]{:S(2)}, u32[]{:S(2)}) collective-permute-start(bf16[32,3,512]{2,1,0:T(4,128)(2,1)S(1)} %get-tuple-element.126), channel_id=1, source_target_pairs={{4,0},{8,4},{12,8},{0,12},{5,1},{9,5},{13,9},{1,13},{6,2},{10,6},{... | collective-permute-start | bytes 294920 | tf_op jit(solution)/shard_map/ppermute | solution.py:604
  13.1 7.5 %copy-start.3 = (bf16[32,3,512]{2,1,0:T(4,128)(2,1)}, bf16[32,3,512]{2,1,0:T(4,128)(2,1)S(1)}, u32[]{:S(2)}) copy-start(bf16[32,3,512]{2,1,0:T(4,128)(2,1)S(1)} %collective-permute-done.1.r_ref) | copy-start | bytes 294916
  14.2 12.6 %collective-permute-start.2 = (bf16[3,38,512]{2,1,0:T(8,128)(2,1)S(1)}, bf16[3,38,512]{2,1,0:T(8,128)(2,1)S(1)}, u32[]{:S(2)}, u32[]{:S(2)}) collective-permute-start(bf16[3,38,512]{2,1,0:T(8,128)(2,1)S(1)} %pad_maximum_fusion), channel_id=1, source_target_pairs={{0,1},{1,2},{2,3},{4,5},{5,6},{6,7},{8,9},{9,10},{10,11},{12,13},{... | collective-permute-start | bytes 350216 | tf_op jit(solution)/shard_map/ppermute | solution.py:619
  19.3 7.5 %collective-permute-start.3 = (bf16[3,38,512]{2,1,0:T(8,128)(2,1)S(1)}, bf16[3,38,512]{2,1,0:T(8,128)(2,1)S(1)}, u32[]{:S(2)}, u32[]{:S(2)}) collective-permute-start(bf16[3,38,512]{2,1,0:T(8,128)(2,1)S(1)} %pad_maximum_fusion.1), channel_id=1, source_target_pairs={{1,0},{2,1},{3,2},{5,4},{6,5},{7,6},{9,8},{10,9},{11,10},{13,12},{... | collective-permute-start | bytes 350216 | tf_op jit(solution)/shard_map/ppermute | solution.py:619
  44.8 16.0 %collective-permute-start.4 = (bf16[2,1,4,512,128]{4,3,2,1,0:T(8,128)(2,1)}, bf16[2,1,4,512,128]{4,3,2,1,0:T(8,128)(2,1)}, u32[]{:S(2)}, u32[]{:S(2)}) collective-permute-start(bf16[2,1,4,512,128]{4,3,2,1,0:T(8,128)(2,1)} %get-tuple-element.79), channel_id=1, source_target_pairs={{0,4},{4,0},{8,12},{12,8},{1,5},{5,1},{9,13},{13,9},{2,6},{6,2},{1... | collective-permute-start | bytes 3145736 | tf_op jit(solution)/shard_map/ppermute | solution.py:580
  56.5 17.8 %collective-permute-start.7 = (bf16[2,1,4,512,128]{4,3,2,1,0:T(8,128)(2,1)}, bf16[2,1,4,512,128]{4,3,2,1,0:T(8,128)(2,1)S(1)}, u32[]{:S(2)}, u32[]{:S(2)}) collective-permute-start(bf16[2,1,4,512,128]{4,3,2,1,0:T(8,128)(2,1)} %get-tuple-element.88), channel_id=1, source_target_pairs={{0,4},{4,0},{8,12},{12,8},{1,5},{5,1},{9,13},{13,9},{2,6},{6,2},{1... | collective-permute-start | bytes 3145736 | tf_op jit(solution)/shard_map/ppermute | solution.py:580
  62.1 29.2 %collective-permute-start.8 = (bf16[1,4,512,128]{3,2,1,0:T(8,128)(2,1)S(1)}, bf16[1,4,512,128]{3,2,1,0:T(8,128)(2,1)S(1)}, u32[]{:S(2)}, u32[]{:S(2)}) collective-permute-start(bf16[1,4,512,128]{3,2,1,0:T(8,128)(2,1)S(1)} %fusion.ahead_ref), channel_id=1, source_target_pairs={{0,8},{4,12},{8,0},{12,4},{1,9},{5,13},{9,1},{13,5},{2,10},{6,14},... | collective-permute-start | bytes 1572872 | tf_op jit(solution)/shard_map/ppermute | solution.py:580
  72.5 10.9 %collective-permute-start.5 = (bf16[32,3,512]{2,1,0:T(4,128)(2,1)S(1)}, bf16[32,3,512]{2,1,0:T(4,128)(2,1)S(1)}, u32[]{:S(2)}, u32[]{:S(2)}) collective-permute-start(bf16[32,3,512]{2,1,0:T(4,128)(2,1)S(1)} %get-tuple-element.125), channel_id=1, source_target_pairs={{0,4},{4,8},{8,12},{12,0},{1,5},{5,9},{9,13},{13,1},{2,6},{6,10},{... | collective-permute-start | bytes 294920 | tf_op jit(solution)/shard_map/ppermute | solution.py:604
  72.6 10.8 %collective-permute-start.6 = (bf16[32,3,512]{2,1,0:T(4,128)(2,1)S(1)}, bf16[32,3,512]{2,1,0:T(4,128)(2,1)S(1)}, u32[]{:S(2)}, u32[]{:S(2)}) collective-permute-start(bf16[32,3,512]{2,1,0:T(4,128)(2,1)S(1)} %get-tuple-element.124), channel_id=1, source_target_pairs={{4,0},{8,4},{12,8},{0,12},{5,1},{9,5},{13,9},{1,13},{6,2},{10,6},{... | collective-permute-start | bytes 294920 | tf_op jit(solution)/shard_map/ppermute | solution.py:604
  82.6 24.1 %collective-permute-start.10 = (bf16[1,4,512,128]{3,2,1,0:T(8,128)(2,1)}, bf16[1,4,512,128]{3,2,1,0:T(8,128)(2,1)}, u32[]{:S(2)}, u32[]{:S(2)}) collective-permute-start(bf16[1,4,512,128]{3,2,1,0:T(8,128)(2,1)} %get-tuple-element.85), channel_id=1, source_target_pairs={{0,8},{4,12},{8,0},{12,4},{1,9},{5,13},{9,1},{13,5},{2,10},{6,14},... | collective-permute-start | bytes 1572872 | tf_op jit(solution)/shard_map/ppermute | solution.py:580
  83.4 8.1 %copy-start.4 = (bf16[32,3,512]{2,1,0:T(4,128)(2,1)}, bf16[32,3,512]{2,1,0:T(4,128)(2,1)S(1)}, u32[]{:S(2)}) copy-start(bf16[32,3,512]{2,1,0:T(4,128)(2,1)S(1)} %collective-permute-done.5.l_ref) | copy-start | bytes 294916
  83.4 8.2 %copy-start.5 = (bf16[32,3,512]{2,1,0:T(4,128)(2,1)}, bf16[32,3,512]{2,1,0:T(4,128)(2,1)S(1)}, u32[]{:S(2)}) copy-start(bf16[32,3,512]{2,1,0:T(4,128)(2,1)S(1)} %collective-permute-done.6.r_ref) | copy-start | bytes 294916
  84.2 27.0 %collective-permute-start.11 = (bf16[3,38,512]{2,1,0:T(8,128)(2,1)}, bf16[3,38,512]{2,1,0:T(8,128)(2,1)}, u32[]{:S(2)}, u32[]{:S(2)}) collective-permute-start(bf16[3,38,512]{2,1,0:T(8,128)(2,1)} %pad_maximum_fusion.2), channel_id=1, source_target_pairs={{0,1},{1,2},{2,3},{4,5},{5,6},{6,7},{8,9},{9,10},{10,11},{12,13},{... | collective-permute-start | bytes 350216 | tf_op jit(solution)/shard_map/ppermute | solution.py:619
  90.1 21.1 %collective-permute-start.12 = (bf16[3,38,512]{2,1,0:T(8,128)(2,1)}, bf16[3,38,512]{2,1,0:T(8,128)(2,1)}, u32[]{:S(2)}, u32[]{:S(2)}) collective-permute-start(bf16[3,38,512]{2,1,0:T(8,128)(2,1)} %pad_maximum_fusion.3), channel_id=1, source_target_pairs={{1,0},{2,1},{3,2},{5,4},{6,5},{7,6},{9,8},{10,9},{11,10},{13,12},{... | collective-permute-start | bytes 350216 | tf_op jit(solution)/shard_map/ppermute | solution.py:619
  92.5 15.9 %collective-permute-start.9 = (bf16[1,2,512,128]{2,3,1,0:T(8,128)(2,1)}, bf16[1,2,512,128]{2,3,1,0:T(8,128)(2,1)S(1)}, u32[]{:S(2)}, u32[]{:S(2)}) collective-permute-start(bf16[1,2,512,128]{2,3,1,0:T(8,128)(2,1)} %bitcast.57), channel_id=1, source_target_pairs={{0,1},{1,0},{2,3},{3,2},{4,5},{5,4},{6,7},{7,6},{8,9},{9,8},{10,11... | collective-permute-start | bytes 786440 | tf_op jit(solution)/shard_map/ppermute | solution.py:580
  106.7 11.0 %collective-permute-start.13 = (f32[8,8,512]{2,1,0:T(8,128)}, f32[8,8,512]{2,1,0:T(8,128)S(1)}, u32[]{:S(2)}, u32[]{:S(2)}) collective-permute-start(f32[8,8,512]{2,1,0:T(8,128)} %filter_grad.1), channel_id=1, source_target_pairs={{0,4},{4,0},{8,12},{12,8},{1,5},{5,1},{9,13},{13,9},{2,6},{6,2},{1... | collective-permute-start | bytes 393224 | tf_op jit(solution)/shard_map/ppermute | solution.py:580
  108.3 11.6 %collective-permute-start.14 = (bf16[1,2,512,128]{3,2,1,0:T(8,128)(2,1)S(1)}, bf16[1,2,512,128]{3,2,1,0:T(8,128)(2,1)S(1)}, u32[]{:S(2)}, u32[]{:S(2)}) collective-permute-start(bf16[1,2,512,128]{3,2,1,0:T(8,128)(2,1)S(1)} %fusion.1), channel_id=1, source_target_pairs={{0,1},{1,0},{2,3},{3,2},{4,5},{5,4},{6,7},{7,6},{8,9},{9,8},{10,11... | collective-permute-start | bytes 786440 | tf_op jit(solution)/shard_map/ppermute | solution.py:580
  108.5 11.4 %copy-start.1 = (f32[8,8,512]{2,1,0:T(8,128)S(1)}, f32[8,8,512]{2,1,0:T(8,128)}, u32[]{:S(2)}) copy-start(f32[8,8,512]{2,1,0:T(8,128)} %filter_grad.1) | copy-start | bytes 393220
  108.5 13.2 %collective-permute-start.19 = (bf16[1,1,512,128]{2,3,1,0:T(8,128)(2,1)S(1)}, bf16[1,1,512,128]{2,3,1,0:T(8,128)(2,1)S(1)}, u32[]{:S(2)}, u32[]{:S(2)}) collective-permute-start(bf16[1,1,512,128]{2,3,1,0:T(8,128)(2,1)S(1)} %dynamic-slice_convert_fusion.1), channel_id=1, source_target_pairs={{0,2},{1,3},{2,0},{3,1},{4,6},{5,7},{6,4},{7,5},{8,10},{9,11},{10,... | collective-permute-start | bytes 393224 | tf_op jit(solution)/shard_map/ppermute | solution.py:580
  120.0 6.0 %collective-permute-start.15 = (f32[8,8,512]{2,1,0:T(8,128)S(1)}, f32[8,8,512]{2,1,0:T(8,128)S(1)}, u32[]{:S(2)}, u32[]{:S(2)}) collective-permute-start(f32[8,8,512]{2,1,0:T(8,128)S(1)} %add.139), channel_id=1, source_target_pairs={{0,8},{4,12},{8,0},{12,4},{1,9},{5,13},{9,1},{13,5},{2,10},{6,14},... | collective-permute-start | bytes 393224 | tf_op jit(solution)/shard_map/ppermute | solution.py:580
  121.3 11.4 %collective-permute-start.18 = (bf16[1,1,512,128]{3,2,1,0:T(8,128)(2,1)S(1)}, bf16[1,1,512,128]{3,2,1,0:T(8,128)(2,1)S(1)}, u32[]{:S(2)}, u32[]{:S(2)}) collective-permute-start(bf16[1,1,512,128]{3,2,1,0:T(8,128)(2,1)S(1)} %dynamic-slice_convert_fusion), channel_id=1, source_target_pairs={{0,2},{1,3},{2,0},{3,1},{4,6},{5,7},{6,4},{7,5},{8,10},{9,11},{10,... | collective-permute-start | bytes 393224 | tf_op jit(solution)/shard_map/ppermute | solution.py:580
  126.0 7.5 %collective-permute-start.16 = (f32[8,8,512]{2,1,0:T(8,128)S(1)}, f32[8,8,512]{2,1,0:T(8,128)S(1)}, u32[]{:S(2)}, u32[]{:S(2)}) collective-permute-start(f32[8,8,512]{2,1,0:T(8,128)S(1)} %add.141), channel_id=1, source_target_pairs={{0,1},{1,0},{2,3},{3,2},{4,5},{5,4},{6,7},{7,6},{8,9},{9,8},{10,11... | collective-permute-start | bytes 393224 | tf_op jit(solution)/shard_map/ppermute | solution.py:580
  133.5 8.0 %collective-permute-start.17 = (f32[8,8,512]{2,1,0:T(8,128)S(1)}, f32[8,8,512]{2,1,0:T(8,128)S(1)}, u32[]{:S(2)}, u32[]{:S(2)}) collective-permute-start(f32[8,8,512]{2,1,0:T(8,128)S(1)} %add.142), channel_id=1, source_target_pairs={{0,2},{1,3},{2,0},{3,1},{4,6},{5,7},{6,4},{7,5},{8,10},{9,11},{10,... | collective-permute-start | bytes 393224 | tf_op jit(solution)/shard_map/ppermute | solution.py:580
  (4 other events, 10.4 us)

commit v4 on v3

--- a/solution.py
+++ b/solution.py
@@ -145,49 +145,20 @@
     return value, slope
 
 
-def hidden_block(
-    normed, normed_t, dbr, dbr_t, wi_ref, bi_ref, wo_ref, act_ref, dpre_ref, gbi_ref, sent_ref, kept_ref
-):
-    cells = normed.shape[0]
-    part = 256
-    total = None
-    for at in range(0, cells, part):
-        here = slice(at, at + part)
-        pre = jnp.dot(normed[here, :], wi_ref[...], preferred_element_type=F32) + bi_ref[...]
-        d_act = lax.dot_general(
-            dbr[here, :], wo_ref[...], (((1,), (1,)), ((), ())), preferred_element_type=F32
-        )
-        value, slope = gelu_pair(pre)
-        act_ref[here, :] = value.astype(BF16)
-        d_pre = d_act * slope
-        dpre_ref[here, :] = d_pre.astype(BF16)
-        sums = jnp.sum(d_pre, axis=0, keepdims=True)
-        total = sums if total is None else total + sums
-    gbi_ref[...] = total
-    _, parts, _, width = sent_ref.shape
-    first = pl.program_id(0) < pl.num_programs(0) // 2
-    for index, (left, right) in enumerate(((dbr_t, act_ref), (normed_t, dpre_ref))):
-        grad = jnp.dot(left[...], right[...], preferred_element_type=F32).astype(BF16)
-
-        def store(ref):
-            for lat in range(parts):
-                ref[index, lat] = grad[:, lat * width : (lat + 1) * width]
-
-        pl.when(first)(functools.partial(store, sent_ref))
-        pl.when(jnp.logical_not(first))(functools.partial(store, kept_ref))
-
-
-def expand_first_kernel(
+def expand_kernel(
     order_ref,
     inner_ref, side_ref, top_ref, bot_ref, k_ref, gain_ref, bias_ref, scale_ref, m_ref, cot_ref,
     wi_ref, bi_ref, wo_ref,
-    xhat_ref, inv_ref, gbo_ref, normed, normed_t, dbr, dbr_t, act_ref, dpre_ref, gbi_ref, sent_ref, kept_ref,
-    conv, halo,
+    gbo_ref, dconv_ref, sums_ref, act_ref, gbi_ref, sent_ref, kept_wo_ref, kept_wi_ref,
+    conv, halo, inv_s, normed, normed_t, dbr, dbr_t, dpre, d_normed,
 ):
     rows, cols, channels = conv.shape
     cells = rows * cols
-
-    @pl.when(pl.program_id(0) == 0)
+    chunk = 128
+    chunk_rows = chunk // cols
+    step_now = pl.program_id(0)
+
+    @pl.when(step_now == 0)
     def _():
         conv[:, 0:8, :] = side_ref[:, 0:8, :]
         conv[:, 8 : cols - 8, :] = inner_ref[...]
@@ -215,9 +186,6 @@
                     conv[out, start : start + 8, lanes] = sums[out]
         gbo_ref[...] = jnp.zeros_like(gbo_ref)
 
-        chunk = 128
-        chunk_rows = chunk // cols
-
         def standardize(step, _):
             at = pl.multiple_of(step * chunk, chunk)
             here = pl.ds(at, chunk)
@@ -228,8 +196,8 @@
             var = jnp.mean(centered * centered, axis=-1, keepdims=True)
             inv = lax.rsqrt(var + 1e-06)
             xhat = centered * inv
-            xhat_ref[here, :] = xhat
-            inv_ref[here, :] = jnp.broadcast_to(inv, (chunk, LANES))
+            conv[there] = xhat.reshape(chunk_rows, cols, channels)
+            inv_s[here, :] = jnp.broadcast_to(inv, (chunk, LANES))
             scaled = xhat * gain_ref[...] + bias_ref[...]
             normed[here, :] = scaled.astype(BF16)
             normed_t[:, here] = scaled.T.astype(BF16)
@@ -238,194 +206,168 @@
             gbo_ref[...] += jnp.sum(grad, axis=0, keepdims=True)
             dbr[here, :] = grad.astype(BF16)
             dbr_t[:, here] = grad.T.astype(BF16)
+            d_normed[here, :] = jnp.zeros((chunk, channels), F32)
             return 0
 
         lax.fori_loop(0, cells // chunk, standardize, 0)
 
-    hidden_block(
-        normed, normed_t, dbr, dbr_t, wi_ref, bi_ref, wo_ref, act_ref, dpre_ref, gbi_ref, sent_ref, kept_ref
-    )
-
-
-def expand_second_kernel(
-    order_ref, normed, normed_t, dbr, dbr_t, wi_ref, bi_ref, wo_ref, act_in, dpre_in, gbi_in,
-    act_ref, dpre_ref, gbi_ref, sent_ref, kept_ref,
-):
-    hidden_block(
-        normed, normed_t, dbr, dbr_t, wi_ref, bi_ref, wo_ref, act_ref, dpre_ref, gbi_ref, sent_ref, kept_ref
-    )
-
-
-def hidden_specs(cells, channels, hidden, n_lon, n_lat, first):
-    block = hidden // n_lon
-    split = n_lat if (block // n_lat) % LANES == 0 else 1
-    turn = n_lon // 4
-    grads = (2, None, split, channels, block // split)
-    weights = [
-        pl.BlockSpec((channels, block), lambda h, order: (0, order[h + first])),
-        pl.BlockSpec((1, block), lambda h, order: (0, order[h + first])),
-        pl.BlockSpec((block, channels), lambda h, order: (order[h + first], 0)),
-    ]
-    results = [
-        pl.BlockSpec((cells, block), lambda h, order: (0, order[h + first])),
-        pl.BlockSpec((cells, block), lambda h, order: (0, order[h + first])),
-        pl.BlockSpec((1, block), lambda h, order: (0, order[h + first])),
-        pl.BlockSpec(grads, lambda h, order: (0, jnp.minimum(h, turn - 1), 0, 0, 0)),
-        pl.BlockSpec(grads, lambda h, order: (0, jnp.maximum(h - turn, 0), 0, 0, 0)),
-    ]
-    shapes = [
-        jax.ShapeDtypeStruct((cells, hidden), BF16),
-        jax.ShapeDtypeStruct((cells, hidden), BF16),
-        jax.ShapeDtypeStruct((1, hidden), F32),
-        jax.ShapeDtypeStruct((2, turn, split, channels, block // split), BF16),
-        jax.ShapeDtypeStruct((2, turn, split, channels, block // split), BF16),
-    ]
-    return weights, results, shapes
-
-
-def expand_first(order, inner, side, top, bot, kernel, gain, bias, scale, mask_b, cot, w_in, b_in, w_out, n_lon, n_lat):
+    part = 256
+    starts = list(range(0, cells, part))
+
+    def products(at):
+        here = slice(at, at + part)
+        pre = jnp.dot(normed[here, :], wi_ref[...], preferred_element_type=F32)
+        d_act = lax.dot_general(
+            dbr[here, :], wo_ref[...], (((1,), (1,)), ((), ())), preferred_element_type=F32
+        )
+        return pre, d_act
+
+    total = None
+    ahead = products(0)
+    for at in starts:
+        here = slice(at, at + part)
+        pre, d_act = ahead
+        if at + part < cells:
+            ahead = products(at + part)
+        value, slope = gelu_pair(pre + bi_ref[...])
+        act_ref[here, :] = value.astype(BF16)
+        d_pre = d_act * slope
+        dpre[here, :] = d_pre.astype(BF16)
+        sums = jnp.sum(d_pre, axis=0, keepdims=True)
+        total = sums if total is None else total + sums
+        d_normed[here, :] += lax.dot_general(
+            dpre[here, :], wi_ref[...], (((1,), (1,)), ((), ())), preferred_element_type=F32
+        )
+    gbi_ref[...] = total
+    _, parts, _, width = sent_ref.shape
+    first = step_now < pl.num_programs(0) // 2
+    for index, (left, right, kept_ref) in enumerate(
+        ((dbr_t, act_ref, kept_wo_ref), (normed_t, dpre, kept_wi_ref))
+    ):
+        grad = jnp.dot(left[...], right[...], preferred_element_type=F32).astype(BF16)
+
+        def store(ref):
+            for lat in range(parts):
+                ref[lat] = grad[:, lat * width : (lat + 1) * width]
+
+        pl.when(first)(functools.partial(store, sent_ref.at[index]))
+        pl.when(jnp.logical_not(first))(functools.partial(store, kept_ref))
+
+    @pl.when(step_now == pl.num_programs(0) - 1)
+    def _():
+        sums_ref[...] = jnp.zeros_like(sums_ref)
+
+        def norm_back(step, _):
+            here = pl.ds(pl.multiple_of(step * chunk, chunk), chunk)
+            there = pl.ds(step * chunk_rows, chunk_rows)
+            grad = d_normed[here, :]
+            xhat = conv[there].reshape(chunk, channels)
+            term = grad * xhat
+            sums_ref[0:1, :] += jnp.sum(term, axis=0, keepdims=True)
+            sums_ref[1:2, :] += jnp.sum(grad, axis=0, keepdims=True)
+            e = grad * gain_ref[...]
+            m1 = jnp.mean(e, axis=-1, keepdims=True)
+            m2 = jnp.mean(term * gain_ref[...], axis=-1, keepdims=True)
+            inv = jnp.concatenate([inv_s[here, :]] * (channels // LANES), axis=1)
+            dconv_ref[here, :] = (inv * (e - m1 - xhat * m2)).astype(BF16)
+            return 0
+
+        lax.fori_loop(0, cells // chunk, norm_back, 0)
+
+
+def expand(order, inner, side, top, bot, kernel, gain, bias, scale, mask_b, cot, w_in, b_in, w_out, n_lon, n_lat):
     rows, _, channels = inner.shape
     hidden = w_in.shape[1]
     cells, _ = cot.shape
     cols = cells // rows
-    weights, results, shapes = hidden_specs(cells, channels, hidden, n_lon, n_lat, 0)
-    flat = (cells, channels)
-    turned = (channels, cells)
-    own = [
-        jax.ShapeDtypeStruct(flat, F32),
-        jax.ShapeDtypeStruct((cells, LANES), F32),
-        jax.ShapeDtypeStruct((1, channels), F32),
-        jax.ShapeDtypeStruct(flat, BF16),
-        jax.ShapeDtypeStruct(turned, BF16),
-        jax.ShapeDtypeStruct(flat, BF16),
-        jax.ShapeDtypeStruct(turned, BF16),
-    ]
+    block = hidden // n_lon
+    split = n_lat if (block // n_lat) % LANES == 0 else 1
+    turn = n_lon // 2
+    grads = (split, channels, block // split)
     given = (inner, side, top, bot, kernel, gain, bias, scale, mask_b, cot)
+
+    def sent_at(h, order):
+        return (0, jnp.minimum(h, turn - 1), 0, 0, 0)
+
+    def kept_at(h, order):
+        return (jnp.maximum(h - turn, 0), 0, 0, 0)
+
     return pl.pallas_call(
-        expand_first_kernel,
+        expand_kernel,
         grid_spec=pltpu.PrefetchScalarGridSpec(
             num_scalar_prefetch=1,
-            grid=(n_lon // 2,),
-            in_specs=[once(x.shape) for x in given] + weights,
-            out_specs=[once(x.shape) for x in own] + results,
+            grid=(n_lon,),
+            in_specs=[once(x.shape) for x in given]
+            + [
+                pl.BlockSpec((channels, block), lambda h, order: (0, order[h])),
+                pl.BlockSpec((1, block), lambda h, order: (0, order[h])),
+                pl.BlockSpec((block, channels), lambda h, order: (order[h], 0)),
+            ],
+            out_specs=[
+                once((1, channels)),
+                once((cells, channels)),
+                once((SUB, channels)),
+                pl.BlockSpec((cells, block), lambda h, order: (0, order[h])),
+                pl.BlockSpec((1, block), lambda h, order: (0, order[h])),
+                pl.BlockSpec((2, None) + grads, sent_at),
+                pl.BlockSpec((None,) + grads, kept_at),
+                pl.BlockSpec((None,) + grads, kept_at),
+            ],
             scratch_shapes=[
                 pltpu.VMEM((rows, cols, channels), F32),
                 pltpu.VMEM((6, cols + 16, channels), F32),
+                pltpu.VMEM((cells, LANES), F32),
+                pltpu.VMEM((cells, channels), BF16),
+                pltpu.VMEM((channels, cells), BF16),
+                pltpu.VMEM((cells, channels), BF16),
+                pltpu.VMEM((channels, cells), BF16),
+                pltpu.VMEM((cells, block), BF16),
+                pltpu.VMEM((cells, channels), F32),
             ],
         ),
-        out_shape=own + shapes,
+        out_shape=[
+            jax.ShapeDtypeStruct((1, channels), F32),
+            jax.ShapeDtypeStruct((cells, channels), BF16),
+            jax.ShapeDtypeStruct((SUB, channels), F32),
+            jax.ShapeDtypeStruct((cells, hidden), BF16),
+            jax.ShapeDtypeStruct((1, hidden), F32),
+            jax.ShapeDtypeStruct((2, turn) + grads, BF16),
+            jax.ShapeDtypeStruct((turn,) + grads, BF16),
+            jax.ShapeDtypeStruct((turn,) + grads, BF16),
+        ],
         compiler_params=params(56),
-        cost_estimate=estimate(12),
-        name="expand_first",
+        cost_estimate=estimate(20),
+        name="expand",
     )(order, *given, w_in, b_in, w_out)
 
 
-def expand_second(order, rows, w_in, b_in, w_out, act, dpre, gbi, n_lon, n_lat):
-    cells, channels = rows[0].shape
-    hidden = w_in.shape[1]
-    weights, results, shapes = hidden_specs(cells, channels, hidden, n_lon, n_lat, n_lon // 2)
-    return pl.pallas_call(
-        expand_second_kernel,
-        grid_spec=pltpu.PrefetchScalarGridSpec(
-            num_scalar_prefetch=1,
-            grid=(n_lon // 2,),
-            in_specs=[once(x.shape) for x in rows] + weights + [UNUSED] * 3,
-            out_specs=results,
-        ),
-        out_shape=shapes,
-        input_output_aliases={8: 0, 9: 1, 10: 2},
-        compiler_params=params(56),
-        cost_estimate=estimate(8),
-        name="expand_second",
-    )(order, *rows, w_in, b_in, w_out, act, dpre, gbi)
-
-
-def norm_back_kernel(dpre_ref, wi_ref, xhat_ref, inv_ref, gain_ref, ahead_ref, dconv_ref, sums_ref):
-    channels = xhat_ref.shape[1]
+def project_kernel(act_ref, wo_ref, f_ref, cot_ref, m_ref, scale_ref, bo_ref, mixed_ref, sums_ref):
+    cells, channels = f_ref.shape
 
     @pl.when(pl.program_id(0) == 0)
     def _():
         sums_ref[...] = jnp.zeros_like(sums_ref)
 
-    d_normed = lax.dot_general(
-        dpre_ref[...], wi_ref[...], (((1,), (1,)), ((), ())), preferred_element_type=F32
-    )
-    xhat = xhat_ref[...]
-    normed_term = d_normed * xhat
-    sums_ref[0:1, :] += jnp.sum(normed_term, axis=0, keepdims=True)
-    sums_ref[1:2, :] += jnp.sum(d_normed, axis=0, keepdims=True)
-    e = d_normed * gain_ref[...]
-    m1 = jnp.mean(e, axis=-1, keepdims=True)
-    m2 = jnp.mean(normed_term * gain_ref[...], axis=-1, keepdims=True)
-    inv = jnp.concatenate([inv_ref[...]] * (channels // LANES), axis=1)
-    dconv_ref[...] = (inv * (e - m1 - xhat * m2)).astype(BF16)
-
-
-def norm_back(dpre, w_in, xhat, inv, gain, ahead):
-    cells, hidden = dpre.shape
-    channels = w_in.shape[0]
+    branch = jnp.dot(act_ref[...], wo_ref[...], preferred_element_type=F32) + bo_ref[...]
+    ocean = jnp.concatenate([m_ref[...].reshape(cells, LANES)] * (channels // LANES), axis=1) * branch
+    mixed_ref[...] = (f_ref[...].astype(F32) + ocean * scale_ref[...]).astype(BF16)
+    sums_ref[0:1, :] += jnp.sum(ocean * cot_ref[...].astype(F32), axis=0, keepdims=True)
+
+
+def project(act, w_out, fields, cot, mask_b, scale, b_out):
+    cells, hidden = act.shape
+    channels = w_out.shape[1]
     part = 256
 
     def rows_of(width):
         return pl.BlockSpec((part, width), lambda i: (i, 0))
 
     return pl.pallas_call(
-        norm_back_kernel,
+        project_kernel,
         grid=(cells // part,),
         out_shape=[
             jax.ShapeDtypeStruct((cells, channels), BF16),
             jax.ShapeDtypeStruct((SUB, channels), F32),
-        ],
-        in_specs=[
-            rows_of(hidden),
-            once(w_in.shape),
-            rows_of(channels),
-            rows_of(LANES),
-            whole_spec(gain.shape),
-            UNUSED,
-        ],
-        out_specs=[rows_of(channels), whole_spec((SUB, channels))],
-        compiler_params=params(56),
-        cost_estimate=estimate(4),
-        name="norm_back",
-    )(dpre, w_in, xhat, inv, gain, ahead)
-
-
-def project_kernel(
-    act_ref, wo_ref, f_ref, cot_ref, m_ref, scale_ref, bo_ref, kept_ref, got_ref,
-    mixed_ref, sums_ref, sent_ref,
-):
-    cells, channels = f_ref.shape
-
-    @pl.when(pl.program_id(0) == 0)
-    def _():
-        sums_ref[...] = jnp.zeros_like(sums_ref)
-
-    branch = jnp.dot(act_ref[...], wo_ref[...], preferred_element_type=F32) + bo_ref[...]
-    ocean = jnp.concatenate([m_ref[...].reshape(cells, LANES)] * (channels // LANES), axis=1) * branch
-    mixed_ref[...] = (f_ref[...].astype(F32) + ocean * scale_ref[...]).astype(BF16)
-    sums_ref[0:1, :] += jnp.sum(ocean * cot_ref[...].astype(F32), axis=0, keepdims=True)
-    sent_ref[...] = (kept_ref[...].astype(F32) + got_ref[...].astype(F32)).astype(BF16)
-
-
-def project(act, w_out, fields, cot, mask_b, scale, b_out, kept, got):
-    cells, hidden = act.shape
-    channels = w_out.shape[1]
-    part = 256
-    steps = cells // part
-
-    def rows_of(width):
-        return pl.BlockSpec((part, width), lambda i: (i, 0))
-
-    grads = kept.shape[1:3] + (channels // steps, kept.shape[4])
-    both = pl.BlockSpec((None,) + grads, lambda i: (1, 0, 0, i, 0))
-    return pl.pallas_call(
-        project_kernel,
-        grid=(steps,),
-        out_shape=[
-            jax.ShapeDtypeStruct((cells, channels), BF16),
-            jax.ShapeDtypeStruct((SUB, channels), F32),
-            jax.ShapeDtypeStruct(kept.shape[1:], BF16),
         ],
         in_specs=[
             rows_of(hidden),
@@ -435,18 +377,12 @@
             pl.BlockSpec((part // mask_b.shape[1],) + mask_b.shape[1:], lambda i: (i, 0, 0)),
             whole_spec(scale.shape),
             whole_spec(b_out.shape),
-            both,
-            both,
         ],
-        out_specs=[
-            rows_of(channels),
-            whole_spec((SUB, channels)),
-            pl.BlockSpec(grads, lambda i: (0, 0, i, 0)),
-        ],
+        out_specs=[rows_of(channels), whole_spec((SUB, channels))],
         compiler_params=params(56),
         cost_estimate=estimate(4),
         name="project",
-    )(act, w_out, fields, cot, mask_b, scale, b_out, kept, got)
+    )(act, w_out, fields, cot, mask_b, scale, b_out)
 
 
 def fill_window(window, center, left, right, top, bot):
@@ -459,7 +395,7 @@
 
 
 def filter_grad_kernel(
-    f_ref, m_ref, l_ref, r_ref, t_ref, b_ref, d_ref, gsc_ref, sums_ref, gbo_ref, gbi_ref,
+    f_ref, m_ref, l_ref, r_ref, t_ref, b_ref, d_ref, gsc_ref, sums_ref, gbo_ref, gbi_0, gbi_1, gbi_2, gbi_3,
     o_ref, window, grad,
 ):
     rows, cols, _ = f_ref.shape
@@ -488,7 +424,8 @@
     o_ref[7, 0:1, :] = gsc_ref[0:1, :]
     o_ref[7, 1:3, :] = sums_ref[0:2, :]
     o_ref[7, 3:4, :] = gbo_ref[...]
-    o_ref[7, 4:8, :] = gbi_ref[...]
+    for at, gbi_ref in enumerate((gbi_0, gbi_1, gbi_2, gbi_3)):
+        o_ref[7, 4 + at : 5 + at, :] = gbi_ref[...]
     for row_off in range(7):
         o_ref[row_off, 7:8, :] = jnp.zeros((1, LANES), F32)
 
@@ -514,8 +451,8 @@
             part(gsc),
             part(sums),
             part(gbo),
-            part(gbi),
-        ],
+        ]
+        + [by_channels(gbi.shape, at * (channels // LANES)) for at in range(4)],
         out_specs=by_channels((8, 8, channels)),
         scratch_shapes=[
             pltpu.VMEM((rows + 6, cols + 16, LANES), F32),
@@ -524,7 +461,7 @@
         compiler_params=params(56),
         cost_estimate=estimate(4),
         name="filter_grad",
-    )(fields, mask_b, left, right, top, bot, d_conv, gsc, sums, gbo, gbi)
+    )(fields, mask_b, left, right, top, bot, d_conv, gsc, sums, gbo, gbi, gbi, gbi, gbi)
 
 
 def input_grad_kernel(d_ref, l_ref, r_ref, t_ref, b_ref, k_ref, m_ref, cot_ref, o_ref, window, grad):
@@ -650,40 +587,36 @@
     core, side_y = lon % 2, (lon // 2) % 2
     quads = 4 * jnp.arange(n_lon // 4, dtype=jnp.int32)
     order = jnp.concatenate(
-        [quads + 2 * y + c for y in (1 - side_y, side_y) for c in (1 - core, core)]
-    )
-    xhat, inv, g_bo, *row_forms, act, d_pre, g_bi, sent_far, kept_far = expand_first(
+        [quads + 2 * y + c for c in (1 - core, core) for y in (1 - side_y, side_y)]
+    )
+    g_bo, d_conv, sums, act, g_bi, sent, kept_wo, kept_wi = expand(
         order, inner, side, top, bot, kernel, gain, bias, scale, mask_b, cot_rows,
         w_in, b_in.reshape(1, -1), w_out, n_lon, n_lat,
     )
-    got_far = swap(sent_far, "lon", 1)
-    act, d_pre, g_bi, sent_near, kept_near = expand_second(
-        order, row_forms, w_in, b_in.reshape(1, -1), w_out, act, d_pre, g_bi, n_lon, n_lat
-    )
-    got_near = swap(sent_near, "lon", 1)
-
-    far_wo = (kept_far[0].astype(F32) + got_far[0].astype(F32)).astype(BF16)
-    got_wo = swap(far_wo, "lon", 2)
-    d_conv, sums = norm_back(d_pre, w_in, xhat, inv, gain, far_wo)
+    got = swap(sent, "lon", 1)
     d_conv = d_conv.reshape(rows, cols, channels)
     d_last, d_first = d_conv[:, cols - 3 :], d_conv[:, :3]
     d_left, d_right = side_halo(d_last, d_first)
-    mixed, g_scale, far_wi = project(
+    mixed, g_scale = project(
         after(act, d_last, d_first), w_out, fields.reshape(cells, channels), cot_rows, mask_b, scale,
-        b_out.reshape(1, -1), kept_far, got_far,
-    )
-    got_wi = swap(far_wi, "lon", 2)
+        b_out.reshape(1, -1),
+    )
     d_tail, d_head = end_rows(
         d_conv[:3], d_conv[rows - 3 :], after(d_left, mixed), after(d_right, mixed)
     )
     d_top, d_bot = end_halo(d_tail, d_head)
+    got = after(got, mixed)
+    far = n_lon // 4
+    kept = (kept_wo, kept_wi)
+    far_sums = [(kept[i][:far].astype(F32) + got[i, :far].astype(F32)).astype(BF16) for i in range(2)]
+    got_far = [swap(x, "lon", 2) for x in far_sums]
 
     steps = [("lon", 0, bit) for bit in bits_of("lon")[2:]] + [("lat", 1, bit) for bit in bits_of("lat")]
     owned, cut = [None, None], [None, None]
 
-    def begin(index, got, last):
-        both = after(kept_near[index], last).astype(F32) + after(got_near[index], last).astype(F32)
-        x = both + after(got, last).astype(F32)
+    def begin(index, last):
+        both = after(kept[index], last)[far:].astype(F32) + after(got, last)[index, far:].astype(F32)
+        x = both + after(got_far[index], last).astype(F32)
         if x.shape[1] != n_lat:
             x = x.reshape(n_lon // 4, channels, n_lat, -1).transpose(0, 2, 1, 3)
         cut[index] = halves(x, *steps[0])
@@ -700,26 +633,29 @@
     def spread(hop, last):
         return after(small, last) + after(swap(small, *hops[hop]), last)
 
-    begin(0, got_wo, mixed)
     small = filter_grad(
-        after(fields, d_tail, d_head, far_wi, cut[0][1]), mask_b, left, right, top, bot, d_conv,
-        g_scale, sums, g_bo, g_bi.reshape(-1, channels),
-    )
-    for step in range(len(steps) - 1):
+        after(fields, d_tail, d_head, *far_sums), mask_b, left, right, top, bot, d_conv,
+        g_scale, sums, g_bo, g_bi,
+    )
+    begin(0, small)
+    for step in range(len(steps) - 2):
         advance(0, step, small)
-    begin(1, got_wi, small)
-    for step in range(len(steps) - 2):
-        advance(1, step, small)
     half = channels // LANES // 2
     back = (d_left, d_right, d_top, d_bot, kernel, mask_b, cotangent)
-    grad_fields = input_grad(after(d_conv, small, cut[0][1], cut[1][1]), *back, half, 0)
+    grad_fields = input_grad(after(d_conv, small, cut[0][1]), *back, half, 0)
     small = spread(0, grad_fields)
+    advance(0, len(steps) - 2, grad_fields)
+    begin(1, grad_fields)
+    for step in range(len(steps) - 2):
+        advance(1, step, grad_fields)
+    grad_fields = input_grad(
+        after(d_conv, small, cut[0][1], cut[1][1]), *back, half // 2, half, grad_fields
+    )
+    small = spread(1, grad_fields)
+    advance(0, len(steps) - 1, grad_fields)
     advance(1, len(steps) - 2, grad_fields)
-    advance(0, len(steps) - 1, grad_fields)
-    grad_fields = input_grad(after(d_conv, small, cut[1][1]), *back, half // 2, half, grad_fields)
-    small = spread(1, grad_fields)
     grad_fields = input_grad(
-        after(d_conv, small), *back, half // 2, half + half // 2, grad_fields
+        after(d_conv, small, cut[1][1]), *back, half // 2, half + half // 2, grad_fields
     )
     for hop in range(2, len(hops)):
         small = spread(hop, grad_fields)

time: 144 us -> 134 us (0.931)
  Pallas kernels: 82.8 us -> 74.3 us
  waiting for transfers between devices: 9.26 us -> 14 us
  local copies, waits for them, and re-layouts: 9.53 us -> 6.38 us
  other arithmetic: 11.7 us -> 9.25 us
    pallas_call x4 -> x2, Pallas kernels: 43.9 us -> 35.5 us  [the longest x1 28.4 us: expand(): pl.pallas_call(expand_kernel, grid_spec=pltpu.PrefetchScalarGridSpec(num_...]
    ppermute x12 -> x11, waiting for transfers between devices: 9.24 us -> 14 us  [swap(): return lax.ppermute(values, axis, [(i, i ^ bit) for i in range(count)])]
    ppermute x12 -> x11, starting transfers between devices: 12.7 us -> 11.6 us  [swap(): return lax.ppermute(values, axis, [(i, i ^ bit) for i in range(count)])]
  transfers between devices with their start and end apart: 20 -> 19, of which waited for: 2 -> 4; matrix products, arithmetic and copies ran while one was open for 11% -> 7% of each run, Pallas kernels for 46% -> 34%
where the time goes in v4:
time: 134 us; the launch traced here: 133 us
  Pallas kernels  74.3 us (55%)
  starting transfers between devices  28.3 us (21%)
  waiting for transfers between devices  14 us (10%)
  other arithmetic  9.25 us (7%)
  local copies, waits for them, and re-layouts  6.38 us (5%)
    pallas_call x1, Pallas kernels, expand(): pl.pallas_call(expand_kernel, grid_spec=pltpu.PrefetchScalarGridSpec(num_...  28.4 us
    pallas_call x3, Pallas kernels, input_grad(): pl.pallas_call(input_grad_kernel if old is None else input_grad_more_kern...  14.9 us
    ppermute x11, waiting for transfers between devices, swap(): return lax.ppermute(values, axis, [(i, i ^ bit) for i in range(count)])  14 us
    ppermute x4, starting transfers between devices, end_halo(): return (lax.ppermute(tail, 'lat', ahead), lax.ppermute(head, 'lat', back))  12.6 us
    ppermute x11, starting transfers between devices, swap(): return lax.ppermute(values, axis, [(i, i ^ bit) for i in range(count)])  11.6 us
    pallas_call x1, Pallas kernels, filter_grad(): pl.pallas_call(filter_grad_kernel, grid=(channels // LANES,), out_shape=j...  11.6 us
    pallas_call x1, Pallas kernels, project(): pl.pallas_call(project_kernel, grid=(cells // part,), out_shape=[jax.Shap...  7.12 us
    pallas_call x1, Pallas kernels, conv_inner(): pl.pallas_call(conv_inner_kernel, grid=(channels // LANES,), out_shape=[j...  6.26 us
  transfers between devices with their start and end apart: 19, of which 4 were waited for; matrix products, arithmetic and copies ran while one was open for 7% of the time, Pallas kernels for 34%

profile of v4, /device:TPU:0, one launch (start us, length us, event | category | flops | bytes accessed | tf_op | source)
XLA Modules:
  0.0 133.4 jit_solution(14064789721406616896)
XLA Ops:
  3.2 2.0 %collective-permute-start.1 = (bf16[32,3,512]{2,1,0:T(4,128)(2,1)S(1)}, bf16[32,3,512]{2,1,0:T(4,128)(2,1)S(1)}, u32[]{:S(2)}, u32[]{:S(2)}) collective-permute-start(bf16[32,3,512]{2,1,0:T(4,128)(2,1)S(1)} %get-tuple-element.102), channel_id=1, source_target_pairs={{4,0},{8,4},{12,8},{0,12},{5,1},{9,5},{13,9},{1,13},{6,2},{10,6},{... | collective-permute-start | bytes 294920 | tf_op jit(solution)/shard_map/ppermute | solution.py:541
  6.3 6.3 %conv_inner.1 = (f32[32,16,512]{2,1,0:T(8,128)}, bf16[3,32,512]{2,1,0:T(8,128)(2,1)}, bf16[3,32,512]{2,1,0:T(8,128)(2,1)}) custom-call(bf16[32,32,512]{2,1,0:T(8,128)(2,1)} %f_ref.4, f32[32,32,128]{2,1,0:T(8,128)} %broadcast_in_dim.4.m_ref, f32[7,7,512]{2,1,0:T(8,128)} %k_ref.11), custom_call_target="tpu_custom_call" | custom-call | flops 4600000000 | bytes 14400000 | tf_op jit(solution)/shard_map/conv_inner/pallas_call | solution.py:100
  14.2 4.2 %collective-permute-start.2 = (bf16[3,38,512]{2,1,0:T(8,128)(2,1)S(1)}, bf16[3,38,512]{2,1,0:T(8,128)(2,1)S(1)}, u32[]{:S(2)}, u32[]{:S(2)}) collective-permute-start(bf16[3,38,512]{2,1,0:T(8,128)(2,1)S(1)} %pad_maximum_fusion), channel_id=1, source_target_pairs={{0,1},{1,2},{2,3},{4,5},{5,6},{6,7},{8,9},{9,10},{10,11},{12,13},{... | collective-permute-start | bytes 350216 | tf_op jit(solution)/shard_map/ppermute | solution.py:556
  19.4 1.3 collective-permute-start.3
  20.7 6.1 %conv_side.1.side_ref = f32[32,16,512]{2,1,0:T(8,128)} custom-call(bf16[32,32,512]{2,1,0:T(8,128)(2,1)} %f_ref.4, f32[32,32,128]{2,1,0:T(8,128)} %broadcast_in_dim.4.m_ref, f32[7,7,512]{2,1,0:T(8,128)} %k_ref.11, bf16[32,3,512]{2,1,0:T(4,128)(2,1)} %copy-done.5, bf16[32,3,512]{2,1,0:T(4,128)(2,1)} %copy-done.6), custom_call_target="tpu_custom_call" | custom-call | flops 4600000000 | bytes 14400000 | tf_op jit(solution)/shard_map/conv_side/pallas_call | solution.py:119
  27.6 28.4 %expand.1 = (f32[1,512]{1,0:T(1,128)}, bf16[1024,512]{1,0:T(8,128)(2,1)}, f32[8,512]{1,0:T(8,128)}, bf16[1024,2048]{1,0:T(8,128)(2,1)}, f32[1,2048]{1,0:T(1,128)...) custom-call(s32[4]{0:T(128)} %pad_add_fusion.order_ref, ...), custom_call_target="tpu_custom_call" | custom-call | flops 23000000512 | bytes 72000000 | tf_op jit(solution)/shard_map/expand/pallas_call | solution.py:295
  57.2 1.6 %collective-permute-start.5 = (bf16[32,3,512]{2,1,0:T(4,128)(2,1)S(1)}, bf16[32,3,512]{2,1,0:T(4,128)(2,1)S(1)}, u32[]{:S(2)}, u32[]{:S(2)}) collective-permute-start(bf16[32,3,512]{2,1,0:T(4,128)(2,1)S(1)} %get-tuple-element.100), channel_id=1, source_target_pairs={{4,0},{8,4},{12,8},{0,12},{5,1},{9,5},{13,9},{1,13},{6,2},{10,6},{... | collective-permute-start | bytes 294920 | tf_op jit(solution)/shard_map/ppermute | solution.py:541
  58.8 7.1 %project.1 = (bf16[1024,512]{1,0:T(8,128)(2,1)}, f32[8,512]{1,0:T(8,128)}) custom-call(bf16[1024,2048]{1,0:T(8,128)(2,1)} %get-tuple-element.58.act_ref, bf16[2048,512]{1,0:T(8,128)(2,1)} %wo_ref.3, bf16[1024,512]{1,0:T(8,128)(2,1)} %bitcast.73, bf16[1024,512]{1,0:T(8,128)(2,1)} %bitcast.80, f32[32,32,128]{2,1,0:T(8,128)} %broadcast_in_dim.4.m_ref, ...), custom_call_target="tpu_custom_call" | custom-call | flops 4600000000 | bytes 14400000 | tf_op jit(solution)/shard_map/project/pallas_call | solution.py:365
  67.0 1.3 collective-permute-start.9
  68.4 1.4 %fusion.2 = (bf16[1,4,512,128]{3,2,1,0:T(8,128)(2,1)}, bf16[1,4,512,128]{3,2,1,0:T(8,128)(2,1)S(1)}) fusion(bf16[2,2,4,512,128]{4,3,2,1,0:T(8,128)(2,1)S(1)} %collective-permute-done.6, bf16[2,4,512,128]{3,2,1,0:T(8,128)(2,1)S(1)} %copy-done.1, bf16[2,4,512,128]{3,2,1,0:T(8,128)(2,1)S(1)} %copy-done.3), kind=kLoop, calls=%fused_computation.5 | loop fusion | flops 2097152 | bytes 3145728 | tf_op jit(solution)/shard_map/convert_element_type | solution.py:611
  70.3 5.8 %collective-permute-start.8 = (bf16[3,38,512]{2,1,0:T(8,128)(2,1)S(1)}, bf16[3,38,512]{2,1,0:T(8,128)(2,1)}, u32[]{:S(2)}, u32[]{:S(2)}) collective-permute-start(bf16[3,38,512]{2,1,0:T(8,128)(2,1)S(1)} %pad_maximum_fusion.2), channel_id=1, source_target_pairs={{0,1},{1,2},{2,3},{4,5},{5,6},{6,7},{8,9},{9,10},{10,11},{12,13},{... | collective-permute-start | bytes 350216 | tf_op jit(solution)/shard_map/ppermute | solution.py:556
  76.1 11.6 %filter_grad.1 = f32[8,8,512]{2,1,0:T(8,128)} custom-call(bf16[32,32,512]{2,1,0:T(8,128)(2,1)} %f_ref.4, f32[32,32,128]{2,1,0:T(8,128)} %broadcast_in_dim.4.m_ref, bf16[32,3,512]{2,1,0:T(4,128)(2,1)} %copy-done.5, bf16[32,3,512]{2,1,0:T(4,128)(2,1)} %copy-done.6, bf16[3,38,512]{2,1,0:T(8,128)(2,1)} %copy-done.9, bf16[3,38,512]{2,1,0:T(8,128)(2,1)} %copy-done.10, ...), custom_call_target="tpu_custom_call" | custom-call | flops 4600000000 | bytes 14400000 | tf_op jit(solution)/shard_map/filter_grad/pallas_call | solution.py:439
  87.7 1.6 %collective-permute-start.12 = (bf16[1,4,512,128]{3,2,1,0:T(8,128)(2,1)}, bf16[1,4,512,128]{3,2,1,0:T(8,128)(2,1)}, u32[]{:S(2)}, u32[]{:S(2)}) collective-permute-start(bf16[1,4,512,128]{3,2,1,0:T(8,128)(2,1)} %get-tuple-element.96), channel_id=1, source_target_pairs={{0,8},{4,12},{8,0},{12,4},{1,9},{5,13},{9,1},{13,5},{2,10},{6,14},... | collective-permute-start | bytes 1572872 | tf_op jit(solution)/shard_map/ppermute | solution.py:517
  89.7 1.6 %collective-permute-start.11 = (bf16[1,2,512,128]{2,3,1,0:T(8,128)(2,1)S(1)}, bf16[1,2,512,128]{2,3,1,0:T(8,128)(2,1)S(1)}, u32[]{:S(2)}, u32[]{:S(2)}) collective-permute-start(bf16[1,2,512,128]{2,3,1,0:T(8,128)(2,1)S(1)} %bitcast.67), channel_id=1, source_target_pairs={{0,1},{1,0},{2,3},{3,2},{4,5},{5,4},{6,7},{7,6},{8,9},{9,8},{10,11... | collective-permute-start | bytes 786440 | tf_op jit(solution)/shard_map/ppermute | solution.py:517
  91.3 6.5 %input_grad.3.old_ref = bf16[32,32,512]{2,1,0:T(8,128)(2,1)} custom-call(bf16[32,32,512]{2,1,0:T(8,128)(2,1)} %bitcast.70, bf16[32,3,512]{2,1,0:T(4,128)(2,1)} %copy-done.8, bf16[32,3,512]{2,1,0:T(4,128)(2,1)} %copy-done.7, bf16[3,38,512]{2,1,0:T(8,128)(2,1)} %collective-permute-done.8.t_ref, bf16[3,38,512]{2,1,0:T(8,128)(2,1)} %collective-permute-done.9.b_ref, ...), custom_call_target="tpu_custom_call" | custom-call | flops 4600000000 | bytes 14400000 | tf_op jit(solution)/shard_map/input_grad/pallas_call | solution.py:488
  97.9 4.9 %collective-permute-done.12 = bf16[1,4,512,128]{3,2,1,0:T(8,128)(2,1)} collective-permute-done((bf16[1,4,512,128]{3,2,1,0:T(8,128)(2,1)}, bf16[1,4,512,128]{3,2,1,0:T(8,128)(2,1)}, u32[]{:S(2)}, u32[]{:S(2)}) %collective-permute-start.12) | collective-permute-done | bytes 524320 | tf_op jit(solution)/shard_map/ppermute | solution.py:517
  102.8 1.4 %fusion = f32[1,4,512,128]{3,2,1,0:T(8,128)S(1)} fusion(bf16[1,4,512,128]{3,2,1,0:T(8,128)(2,1)} %collective-permute-done.12, bf16[2,2,4,512,128]{4,3,2,1,0:T(8,128)(2,1)} %copy-done, bf16[2,4,512,128]{3,2,1,0:T(8,128)(2,1)S(1)} %copy-done.2), kind=kLoop, calls=%fused_computation.1 | loop fusion | flops 1310720 | bytes 2621440 | tf_op jit(solution)/shard_map/add | solution.py:619
  104.5 1.6 %collective-permute-start.14 = (bf16[1,2,512,128]{3,2,1,0:T(8,128)(2,1)S(1)}, bf16[1,2,512,128]{3,2,1,0:T(8,128)(2,1)S(1)}, u32[]{:S(2)}, u32[]{:S(2)}) collective-permute-start(bf16[1,2,512,128]{3,2,1,0:T(8,128)(2,1)S(1)} %fusion.4), channel_id=1, source_target_pairs={{0,1},{1,0},{2,3},{3,2},{4,5},{5,4},{6,7},{7,6},{8,9},{9,8},{10,11... | collective-permute-start | bytes 786440 | tf_op jit(solution)/shard_map/ppermute | solution.py:517
  106.8 1.7 %collective-permute-start.18 = (bf16[1,1,512,128]{2,3,1,0:T(8,128)(2,1)S(1)}, bf16[1,1,512,128]{2,3,1,0:T(8,128)(2,1)S(1)}, u32[]{:S(2)}, u32[]{:S(2)}) collective-permute-start(bf16[1,1,512,128]{2,3,1,0:T(8,128)(2,1)S(1)} %dynamic-slice_convert_fusion.1), channel_id=1, source_target_pairs={{0,2},{1,3},{2,0},{3,1},{4,6},{5,7},{6,4},{7,5},{8,10},{9,11},{10,... | collective-permute-start | bytes 393224 | tf_op jit(solution)/shard_map/ppermute | solution.py:517
  108.5 4.2 %input_grad.4.old_ref = bf16[32,32,512]{2,1,0:T(8,128)(2,1)} custom-call(bf16[32,32,512]{2,1,0:T(8,128)(2,1)} %bitcast.71, bf16[32,3,512]{2,1,0:T(4,128)(2,1)} %copy-done.8, bf16[32,3,512]{2,1,0:T(4,128)(2,1)} %copy-done.7, bf16[3,38,512]{2,1,0:T(8,128)(2,1)} %collective-permute-done.8.t_ref, ...), custom_call_target="tpu_custom_call", output_to_operand_aliasing={{}: (8, {})} | custom-call | flops 4600000000 | bytes 14400000 | tf_op jit(solution)/shard_map/input_grad/pallas_call | solution.py:488
  112.7 3.0 %collective-permute-done.14 = bf16[1,2,512,128]{3,2,1,0:T(8,128)(2,1)S(1)} collective-permute-done((bf16[1,2,512,128]{3,2,1,0:T(8,128)(2,1)S(1)}, bf16[1,2,512,128]{3,2,1,0:T(8,128)(2,1)S(1)}, u32[]{:S(2)}, u32[]{:S(2)}) %collective-permute-start.14) | collective-permute-done | bytes 262176 | tf_op jit(solution)/shard_map/ppermute | solution.py:517
  117.0 2.1 %collective-permute-start.15 = (f32[8,8,512]{2,1,0:T(8,128)S(1)}, f32[8,8,512]{2,1,0:T(8,128)S(1)}, u32[]{:S(2)}, u32[]{:S(2)}) collective-permute-start(f32[8,8,512]{2,1,0:T(8,128)S(1)} %add.135), channel_id=1, source_target_pairs={{0,1},{1,0},{2,3},{3,2},{4,5},{5,4},{6,7},{7,6},{8,9},{9,8},{10,11... | collective-permute-start | bytes 393224 | tf_op jit(solution)/shard_map/ppermute | solution.py:517
  119.2 4.2 %input_grad.5 = bf16[32,32,512]{2,1,0:T(8,128)(2,1)} custom-call(bf16[32,32,512]{2,1,0:T(8,128)(2,1)} %bitcast.72, bf16[32,3,512]{2,1,0:T(4,128)(2,1)} %copy-done.8, bf16[32,3,512]{2,1,0:T(4,128)(2,1)} %copy-done.7, bf16[3,38,512]{2,1,0:T(8,128)(2,1)} %collective-permute-done.8.t_ref, ...), custom_call_target="tpu_custom_call", output_to_operand_aliasing={{}: (8, {})} | custom-call | flops 4600000000 | bytes 14400000 | tf_op jit(solution)/shard_map/input_grad/pallas_call | solution.py:488
  126.6 5.0 %collective-permute-done.16 = f32[8,8,512]{2,1,0:T(8,128)S(1)} collective-permute-done((f32[8,8,512]{2,1,0:T(8,128)S(1)}, f32[8,8,512]{2,1,0:T(8,128)S(1)}, u32[]{:S(2)}, u32[]{:S(2)}) %collective-permute-start.16) | collective-permute-done | bytes 131104 | tf_op jit(solution)/shard_map/ppermute | solution.py:517
  (83 shorter events, 17.5 us)
Async XLA Ops:
  2.7 10.4 %collective-permute-start = (bf16[32,3,512]{2,1,0:T(4,128)(2,1)S(1)}, bf16[32,3,512]{2,1,0:T(4,128)(2,1)S(1)}, u32[]{:S(2)}, u32[]{:S(2)}) collective-permute-start(bf16[32,3,512]{2,1,0:T(4,128)(2,1)S(1)} %get-tuple-element.103), channel_id=1, source_target_pairs={{0,4},{4,8},{8,12},{12,0},{1,5},{5,9},{9,13},{13,1},{2,6},{6,10},{... | collective-permute-start | bytes 294920 | tf_op jit(solution)/shard_map/ppermute | solution.py:541
  3.2 10.0 %collective-permute-start.1 = (bf16[32,3,512]{2,1,0:T(4,128)(2,1)S(1)}, bf16[32,3,512]{2,1,0:T(4,128)(2,1)S(1)}, u32[]{:S(2)}, u32[]{:S(2)}) collective-permute-start(bf16[32,3,512]{2,1,0:T(4,128)(2,1)S(1)} %get-tuple-element.102), channel_id=1, source_target_pairs={{4,0},{8,4},{12,8},{0,12},{5,1},{9,5},{13,9},{1,13},{6,2},{10,6},{... | collective-permute-start | bytes 294920 | tf_op jit(solution)/shard_map/ppermute | solution.py:541
  14.2 12.6 %collective-permute-start.2 = (bf16[3,38,512]{2,1,0:T(8,128)(2,1)S(1)}, bf16[3,38,512]{2,1,0:T(8,128)(2,1)S(1)}, u32[]{:S(2)}, u32[]{:S(2)}) collective-permute-start(bf16[3,38,512]{2,1,0:T(8,128)(2,1)S(1)} %pad_maximum_fusion), channel_id=1, source_target_pairs={{0,1},{1,2},{2,3},{4,5},{5,6},{6,7},{8,9},{9,10},{10,11},{12,13},{... | collective-permute-start | bytes 350216 | tf_op jit(solution)/shard_map/ppermute | solution.py:556
  19.4 7.5 %collective-permute-start.3 = (bf16[3,38,512]{2,1,0:T(8,128)(2,1)S(1)}, bf16[3,38,512]{2,1,0:T(8,128)(2,1)S(1)}, u32[]{:S(2)}, u32[]{:S(2)}) collective-permute-start(bf16[3,38,512]{2,1,0:T(8,128)(2,1)S(1)} %pad_maximum_fusion.1), channel_id=1, source_target_pairs={{1,0},{2,1},{3,2},{5,4},{6,5},{7,6},{9,8},{10,9},{11,10},{13,12},{... | collective-permute-start | bytes 350216 | tf_op jit(solution)/shard_map/ppermute | solution.py:556
  55.9 12.4 %collective-permute-start.6 = (bf16[2,2,4,512,128]{4,3,2,1,0:T(8,128)(2,1)}, bf16[2,2,4,512,128]{4,3,2,1,0:T(8,128)(2,1)S(1)}, u32[]{:S(2)}, u32[]{:S(2)}) collective-permute-start(bf16[2,2,4,512,128]{4,3,2,1,0:T(8,128)(2,1)} %get-tuple-element.63), channel_id=1, source_target_pairs={{0,4},{4,0},{8,12},{12,8},{1,5},{5,1},{9,13},{13,9},{2,6},{6,2},{1... | collective-permute-start | bytes 6291464 | tf_op jit(solution)/shard_map/ppermute | solution.py:517
  57.2 9.7 %collective-permute-start.5 = (bf16[32,3,512]{2,1,0:T(4,128)(2,1)S(1)}, bf16[32,3,512]{2,1,0:T(4,128)(2,1)S(1)}, u32[]{:S(2)}, u32[]{:S(2)}) collective-permute-start(bf16[32,3,512]{2,1,0:T(4,128)(2,1)S(1)} %get-tuple-element.100), channel_id=1, source_target_pairs={{4,0},{8,4},{12,8},{0,12},{5,1},{9,5},{13,9},{1,13},{6,2},{10,6},{... | collective-permute-start | bytes 294920 | tf_op jit(solution)/shard_map/ppermute | solution.py:541
  58.8 8.1 %collective-permute-start.4 = (bf16[32,3,512]{2,1,0:T(4,128)(2,1)S(1)}, bf16[32,3,512]{2,1,0:T(4,128)(2,1)S(1)}, u32[]{:S(2)}, u32[]{:S(2)}) collective-permute-start(bf16[32,3,512]{2,1,0:T(4,128)(2,1)S(1)} %get-tuple-element.101), channel_id=1, source_target_pairs={{0,4},{4,8},{8,12},{12,0},{1,5},{5,9},{9,13},{13,1},{2,6},{6,10},{... | collective-permute-start | bytes 294920 | tf_op jit(solution)/shard_map/ppermute | solution.py:541
  58.8 9.5 %copy-start.1 = (bf16[2,4,512,128]{3,2,1,0:T(8,128)(2,1)S(1)}, bf16[2,4,512,128]{3,2,1,0:T(8,128)(2,1)}, u32[]{:S(2)}) copy-start(bf16[2,4,512,128]{3,2,1,0:T(8,128)(2,1)} %get-tuple-element.79) | copy-start | bytes 3145732
  58.8 9.5 %copy-start.3 = (bf16[2,4,512,128]{3,2,1,0:T(8,128)(2,1)S(1)}, bf16[2,4,512,128]{3,2,1,0:T(8,128)(2,1)}, u32[]{:S(2)}) copy-start(bf16[2,4,512,128]{3,2,1,0:T(8,128)(2,1)} %get-tuple-element.71) | copy-start | bytes 3145732
  66.9 20.8 %copy-start.8 = (bf16[32,3,512]{2,1,0:T(4,128)(2,1)}, bf16[32,3,512]{2,1,0:T(4,128)(2,1)S(1)}, u32[]{:S(2)}) copy-start(bf16[32,3,512]{2,1,0:T(4,128)(2,1)S(1)} %collective-permute-done.4.l_ref) | copy-start | bytes 294916
  67.0 24.3 %collective-permute-start.9 = (bf16[3,38,512]{2,1,0:T(8,128)(2,1)S(1)}, bf16[3,38,512]{2,1,0:T(8,128)(2,1)}, u32[]{:S(2)}, u32[]{:S(2)}) collective-permute-start(bf16[3,38,512]{2,1,0:T(8,128)(2,1)S(1)} %pad_maximum_fusion.3), channel_id=1, source_target_pairs={{1,0},{2,1},{3,2},{5,4},{6,5},{7,6},{9,8},{10,9},{11,10},{13,12},{... | collective-permute-start | bytes 350216 | tf_op jit(solution)/shard_map/ppermute | solution.py:556
  68.3 21.0 %copy-start = (bf16[2,2,4,512,128]{4,3,2,1,0:T(8,128)(2,1)}, bf16[2,2,4,512,128]{4,3,2,1,0:T(8,128)(2,1)S(1)}, u32[]{:S(2)}) copy-start(bf16[2,2,4,512,128]{4,3,2,1,0:T(8,128)(2,1)S(1)} %collective-permute-done.6) | copy-start | bytes 6291460
  69.7 19.6 %collective-permute-start.7 = (bf16[1,4,512,128]{3,2,1,0:T(8,128)(2,1)S(1)}, bf16[1,4,512,128]{3,2,1,0:T(8,128)(2,1)S(1)}, u32[]{:S(2)}, u32[]{:S(2)}) collective-permute-start(bf16[1,4,512,128]{3,2,1,0:T(8,128)(2,1)S(1)} %get-tuple-element.97), channel_id=1, source_target_pairs={{0,8},{4,12},{8,0},{12,4},{1,9},{5,13},{9,1},{13,5},{2,10},{6,14},... | collective-permute-start | bytes 1572872 | tf_op jit(solution)/shard_map/ppermute | solution.py:517
  70.3 21.0 %collective-permute-start.8 = (bf16[3,38,512]{2,1,0:T(8,128)(2,1)S(1)}, bf16[3,38,512]{2,1,0:T(8,128)(2,1)}, u32[]{:S(2)}, u32[]{:S(2)}) collective-permute-start(bf16[3,38,512]{2,1,0:T(8,128)(2,1)S(1)} %pad_maximum_fusion.2), channel_id=1, source_target_pairs={{0,1},{1,2},{2,3},{4,5},{5,6},{6,7},{8,9},{9,10},{10,11},{12,13},{... | collective-permute-start | bytes 350216 | tf_op jit(solution)/shard_map/ppermute | solution.py:556
  87.7 15.1 %collective-permute-start.12 = (bf16[1,4,512,128]{3,2,1,0:T(8,128)(2,1)}, bf16[1,4,512,128]{3,2,1,0:T(8,128)(2,1)}, u32[]{:S(2)}, u32[]{:S(2)}) collective-permute-start(bf16[1,4,512,128]{3,2,1,0:T(8,128)(2,1)} %get-tuple-element.96), channel_id=1, source_target_pairs={{0,8},{4,12},{8,0},{12,4},{1,9},{5,13},{9,1},{13,5},{2,10},{6,14},... | collective-permute-start | bytes 1572872 | tf_op jit(solution)/shard_map/ppermute | solution.py:517
  89.3 15.1 %collective-permute-start.10 = (f32[8,8,512]{2,1,0:T(8,128)}, f32[8,8,512]{2,1,0:T(8,128)S(1)}, u32[]{:S(2)}, u32[]{:S(2)}) collective-permute-start(f32[8,8,512]{2,1,0:T(8,128)} %filter_grad.1), channel_id=1, source_target_pairs={{0,4},{4,0},{8,12},{12,8},{1,5},{5,1},{9,13},{13,9},{2,6},{6,2},{1... | collective-permute-start | bytes 393224 | tf_op jit(solution)/shard_map/ppermute | solution.py:517
  89.7 13.1 %copy-start.2 = (bf16[2,4,512,128]{3,2,1,0:T(8,128)(2,1)S(1)}, bf16[2,4,512,128]{3,2,1,0:T(8,128)(2,1)}, u32[]{:S(2)}) copy-start(bf16[2,4,512,128]{3,2,1,0:T(8,128)(2,1)} %get-tuple-element.79) | copy-start | bytes 3145732
  89.7 17.0 %collective-permute-start.11 = (bf16[1,2,512,128]{2,3,1,0:T(8,128)(2,1)S(1)}, bf16[1,2,512,128]{2,3,1,0:T(8,128)(2,1)S(1)}, u32[]{:S(2)}, u32[]{:S(2)}) collective-permute-start(bf16[1,2,512,128]{2,3,1,0:T(8,128)(2,1)S(1)} %bitcast.67), channel_id=1, source_target_pairs={{0,1},{1,0},{2,3},{3,2},{4,5},{5,4},{6,7},{7,6},{8,9},{9,8},{10,11... | collective-permute-start | bytes 786440 | tf_op jit(solution)/shard_map/ppermute | solution.py:517
  104.5 11.2 %collective-permute-start.14 = (bf16[1,2,512,128]{3,2,1,0:T(8,128)(2,1)S(1)}, bf16[1,2,512,128]{3,2,1,0:T(8,128)(2,1)S(1)}, u32[]{:S(2)}, u32[]{:S(2)}) collective-permute-start(bf16[1,2,512,128]{3,2,1,0:T(8,128)(2,1)S(1)} %fusion.4), channel_id=1, source_target_pairs={{0,1},{1,0},{2,3},{3,2},{4,5},{5,4},{6,7},{7,6},{8,9},{9,8},{10,11... | collective-permute-start | bytes 786440 | tf_op jit(solution)/shard_map/ppermute | solution.py:517
  106.1 9.7 %collective-permute-start.13 = (f32[8,8,512]{2,1,0:T(8,128)S(1)}, f32[8,8,512]{2,1,0:T(8,128)S(1)}, u32[]{:S(2)}, u32[]{:S(2)}) collective-permute-start(f32[8,8,512]{2,1,0:T(8,128)S(1)} %add.128), channel_id=1, source_target_pairs={{0,8},{4,12},{8,0},{12,4},{1,9},{5,13},{9,1},{13,5},{2,10},{6,14},... | collective-permute-start | bytes 393224 | tf_op jit(solution)/shard_map/ppermute | solution.py:517
  106.8 12.4 %collective-permute-start.18 = (bf16[1,1,512,128]{2,3,1,0:T(8,128)(2,1)S(1)}, bf16[1,1,512,128]{2,3,1,0:T(8,128)(2,1)S(1)}, u32[]{:S(2)}, u32[]{:S(2)}) collective-permute-start(bf16[1,1,512,128]{2,3,1,0:T(8,128)(2,1)S(1)} %dynamic-slice_convert_fusion.1), channel_id=1, source_target_pairs={{0,2},{1,3},{2,0},{3,1},{4,6},{5,7},{6,4},{7,5},{8,10},{9,11},{10,... | collective-permute-start | bytes 393224 | tf_op jit(solution)/shard_map/ppermute | solution.py:517
  115.8 9.3 %collective-permute-start.17 = (bf16[1,1,512,128]{3,2,1,0:T(8,128)(2,1)S(1)}, bf16[1,1,512,128]{3,2,1,0:T(8,128)(2,1)S(1)}, u32[]{:S(2)}, u32[]{:S(2)}) collective-permute-start(bf16[1,1,512,128]{3,2,1,0:T(8,128)(2,1)S(1)} %dynamic-slice_convert_fusion), channel_id=1, source_target_pairs={{0,2},{1,3},{2,0},{3,1},{4,6},{5,7},{6,4},{7,5},{8,10},{9,11},{10,... | collective-permute-start | bytes 393224 | tf_op jit(solution)/shard_map/ppermute | solution.py:517
  117.0 7.5 %collective-permute-start.15 = (f32[8,8,512]{2,1,0:T(8,128)S(1)}, f32[8,8,512]{2,1,0:T(8,128)S(1)}, u32[]{:S(2)}, u32[]{:S(2)}) collective-permute-start(f32[8,8,512]{2,1,0:T(8,128)S(1)} %add.135), channel_id=1, source_target_pairs={{0,1},{1,0},{2,3},{3,2},{4,5},{5,4},{6,7},{7,6},{8,9},{9,8},{10,11... | collective-permute-start | bytes 393224 | tf_op jit(solution)/shard_map/ppermute | solution.py:517
  124.5 7.0 %collective-permute-start.16 = (f32[8,8,512]{2,1,0:T(8,128)S(1)}, f32[8,8,512]{2,1,0:T(8,128)S(1)}, u32[]{:S(2)}, u32[]{:S(2)}) collective-permute-start(f32[8,8,512]{2,1,0:T(8,128)S(1)} %add.137), channel_id=1, source_target_pairs={{0,2},{1,3},{2,0},{3,1},{4,6},{5,7},{6,4},{7,5},{8,10},{9,11},{10,... | collective-permute-start | bytes 393224 | tf_op jit(solution)/shard_map/ppermute | solution.py:517
  (6 other events, 26.0 us)

commit v5 on v4

v5 whole, which is shorter than its diff:
```python
import functools
import math

import jax
import jax.numpy as jnp
from jax import lax
from jax.experimental import pallas as pl
from jax.experimental.pallas import tpu as pltpu
from jax.sharding import PartitionSpec as P

F32 = jnp.float32
BF16 = jnp.bfloat16
LANES = 128
SUB = 8


def params(mib):
    return pltpu.CompilerParams(vmem_limit_bytes=mib * 1024 * 1024)


def estimate(micros):
    return pl.CostEstimate(
        flops=int(micros * 1.15e9), bytes_accessed=int(micros * 3.6e6), transcendentals=0
    )


def once(shape):
    zeros = (0,) * len(shape)
    return pl.BlockSpec(shape, lambda *_: zeros, pipeline_mode=pl.Buffered(1))


UNUSED = pl.BlockSpec(memory_space=pl.ANY)


def whole_spec(shape):
    zeros = (0,) * len(shape)
    return pl.BlockSpec(shape, lambda *_: zeros)


def shifted(window, row, start, offset):
    if offset % SUB == 0:
        return window[row, pl.ds(start + offset, SUB), :]
    base = start + offset // SUB * SUB
    pair = window[row, pl.ds(base, 2 * SUB), :]
    return pltpu.roll(pair, 2 * SUB - offset % SUB, axis=0)[:SUB]


def tap_rows(k_ref, col_off, flip):
    at = 6 - col_off if flip else col_off
    rows = [k_ref[6 - p if flip else p, at : at + 1, :] for p in range(7)]
    return [jnp.broadcast_to(row, (SUB, LANES)) for row in rows]


def band_conv(window, k_ref, start, rows, pad, flip):
    sums = [None] * rows
    for col_off in range(7):
        weights = tap_rows(k_ref, col_off, flip)
        for src in range(window.shape[0]):
            hits = [(src - pad - row_off + 3, row_off) for row_off in range(7)]
            hits = [(out, row_off) for out, row_off in hits if 0 <= out < rows]
            if not hits:
                continue
            cells = shifted(window, src, start, 5 + col_off)
            for out, row_off in hits:
                term = weights[row_off] * cells
                sums[out] = term if sums[out] is None else sums[out] + term
    return sums


def mask_column(m_ref, row, start, count):
    line = m_ref[pl.ds(row, 1), :].astype(F32)
    spot = lax.broadcasted_iota(jnp.int32, (count, line.shape[1]), 1)
    want = lax.broadcasted_iota(jnp.int32, (count, line.shape[1]), 0) + start
    return jnp.sum(jnp.where(spot == want, line, 0.0), axis=1, keepdims=True)


def spread_mask(m_ref, wide):
    @pl.when(pl.program_id(0) == 0)
    def _():
        rows, cols, _ = wide.shape

        def one(row, _):
            column = mask_column(m_ref, row, 0, cols)
            wide[pl.ds(row, 1)] = jnp.broadcast_to(column, (cols, LANES))[None]
            return 0

        lax.fori_loop(0, rows, one, 0)


def conv_inner_kernel(f_ref, m_ref, k_ref, o_ref, head_ref, tail_ref, window, wide):
    rows, cols, _ = f_ref.shape
    spread_mask(m_ref, wide)
    masked = f_ref[...].astype(F32) * wide[...]
    window[:, 8 : 8 + cols, :] = masked
    head_ref[...] = masked[:3].astype(BF16)
    tail_ref[...] = masked[rows - 3 :].astype(BF16)
    for start in range(8, cols - 8, 8):
        sums = band_conv(window, k_ref, start, rows, 0, False)
        for row in range(rows):
            o_ref[row, start - 8 : start, :] = sums[row]


def conv_side_kernel(f_ref, m_ref, k_ref, l_ref, r_ref, o_ref, window, wide):
    rows, cols, _ = f_ref.shape
    spread_mask(m_ref, wide)
    window[:, 5:8, :] = l_ref[...].astype(F32)
    window[:, 8 : 8 + cols, :] = f_ref[...].astype(F32) * wide[...]
    window[:, 8 + cols : 11 + cols, :] = r_ref[...].astype(F32)
    for at, start in ((0, 0), (8, cols - 8)):
        sums = band_conv(window, k_ref, start, rows, 0, False)
        for row in range(rows):
            o_ref[row, at : at + 8, :] = sums[row]


def by_channels(shape, first=0):
    return pl.BlockSpec(shape[:-1] + (LANES,), lambda c: (0,) * (len(shape) - 1) + (c + first,))


def conv_inner(fields, mask, kernel):
    rows, cols, channels = fields.shape
    ends = (3, cols, channels)
    return pl.pallas_call(
        conv_inner_kernel,
        grid=(channels // LANES,),
        out_shape=[
            jax.ShapeDtypeStruct((rows, cols - 16, channels), F32),
            jax.ShapeDtypeStruct(ends, BF16),
            jax.ShapeDtypeStruct(ends, BF16),
        ],
        in_specs=[by_channels(fields.shape), whole_spec(mask.shape), by_channels(kernel.shape)],
        out_specs=[by_channels((rows, cols - 16, channels)), by_channels(ends), by_channels(ends)],
        scratch_shapes=[
            pltpu.VMEM((rows, cols + 16, LANES), F32),
            pltpu.VMEM((rows, cols, LANES), F32),
        ],
        compiler_params=params(56),
        cost_estimate=estimate(4),
        name="conv_inner",
    )(fields, mask, kernel)


def conv_side(fields, mask, kernel, left, right):
    rows, cols, channels = fields.shape
    return pl.pallas_call(
        conv_side_kernel,
        grid=(channels // LANES,),
        out_shape=jax.ShapeDtypeStruct((rows, 16, channels), F32),
        in_specs=[
            by_channels(fields.shape),
            whole_spec(mask.shape),
            by_channels(kernel.shape),
            by_channels(left.shape),
            by_channels(right.shape),
        ],
        out_specs=by_channels((rows, 16, channels)),
        scratch_shapes=[
            pltpu.VMEM((rows, cols + 16, LANES), F32),
            pltpu.VMEM((rows, cols, LANES), F32),
        ],
        compiler_params=params(56),
        cost_estimate=estimate(4),
        name="conv_side",
    )(fields, mask, kernel, left, right)


def gelu_twice(x):
    root = math.sqrt(2.0 / math.pi)
    inner = root + (root * 0.044715) * (x * x)
    tanh = jnp.tanh(x * inner)
    both = 1.0 + tanh
    value = x * both
    slope = both + value * ((1.0 - tanh) * (3.0 * inner - 2.0 * root))
    return value, slope


def expand_kernel(
    order_ref,
    inner_ref, side_ref, top_ref, bot_ref, k_ref, gain_ref, bias_ref, scale_ref, bo_ref, m_ref, cot_ref, f_ref,
    wi_ref, bi_ref, wo_ref,
    dconv_ref, mixed_ref, sums_ref, gbi_ref, sent_ref, kept_ref,
    conv, halo, inv_s, normed, normed_t, dbr, dbr_t, act, dpre, d_normed, branch, pre_s, dact_s,
):
    rows, cols, channels = conv.shape
    cells = rows * cols
    strip = 16
    chunk = 128
    step_now = pl.program_id(0)
    wide = channels // LANES

    def strips(body):
        def one(row, _):
            for at in range(0, cols, strip):
                body(row, at, pl.ds(pl.multiple_of(row * cols + at, strip), strip))
            return 0

        lax.fori_loop(0, rows, one, 0)

    @pl.when(step_now == 0)
    def _():
        conv[:, 0:8, :] = side_ref[:, 0:8, :]
        conv[:, 8 : cols - 8, :] = inner_ref[...]
        conv[:, cols - 8 : cols, :] = side_ref[:, 8:16, :]
        halo[0:3, 5 : 11 + cols, :] = top_ref[...].astype(F32)
        halo[3:6, 5 : 11 + cols, :] = bot_ref[...].astype(F32)
        for block in range(wide):
            lanes = slice(block * LANES, (block + 1) * LANES)
            for start in range(0, cols, 8):
                outs = list(range(3)) + list(range(rows - 3, rows))
                sums = {out: conv[out, start : start + 8, lanes] for out in outs}
                for col_off in range(7):
                    for src in range(6):
                        lat = src - 3 if src < 3 else rows + src - 3
                        offset = (5 + col_off) % SUB
                        base = start + (5 + col_off) // SUB * SUB
                        pair = halo[src, base : base + 2 * SUB, lanes]
                        cell = pltpu.roll(pair, 2 * SUB - offset, axis=0)[:SUB] if offset else pair[:SUB]
                        for out in outs:
                            row_off = lat - out + 3
                            if 0 <= row_off < 7:
                                tap = k_ref[row_off, col_off : col_off + 1, lanes]
                                sums[out] = sums[out] + tap * cell
                for out in outs:
                    conv[out, start : start + 8, lanes] = sums[out]
        sums_ref[...] = jnp.zeros_like(sums_ref)

        def standardize(row, at, here):
            x = conv[row, at : at + strip, :]
            mean = jnp.mean(x, axis=-1, keepdims=True)
            centered = x - mean
            var = jnp.mean(centered * centered, axis=-1, keepdims=True)
            inv = lax.rsqrt(var + 1e-06)
            xhat = centered * inv
            conv[row, at : at + strip, :] = xhat
            inv_s[here, :] = jnp.broadcast_to(inv, (strip, LANES))
            normed[here, :] = (xhat * gain_ref[...] + bias_ref[...]).astype(BF16)
            grad = mask_column(m_ref, row, at, strip) * (scale_ref[...] * cot_ref[here, :].astype(F32))
            sums_ref[0] += grad[:SUB] + grad[SUB:]
            dbr[here, :] = (0.5 * grad).astype(BF16)

        strips(standardize)
        for at in range(0, cells, chunk):
            here = slice(at, at + chunk)
            normed_t[:, here] = normed[here, :].T
            dbr_t[:, here] = dbr[here, :].T

    part = 256
    count = cells // part
    block = act.shape[1]
    cut = min(block, 256)

    def products(index):
        here = slice(index * part, (index + 1) * part)
        pre_s[index % 2] = jnp.dot(normed[here, :], wi_ref[...], preferred_element_type=F32)
        dact_s[index % 2] = lax.dot_general(
            dbr[here, :], wo_ref[...], (((1,), (1,)), ((), ())), preferred_element_type=F32
        )

    first_block = step_now == 0

    def project(index):
        here = slice(index * part, (index + 1) * part)
        branch[here, :] = jnp.where(first_block, 0.0, branch[here, :]) + jnp.dot(
            act[here, :], wo_ref[...], preferred_element_type=F32
        )
        d_normed[here, :] = jnp.where(first_block, 0.0, d_normed[here, :]) + lax.dot_general(
            dpre[here, :], wi_ref[...], (((1,), (1,)), ((), ())), preferred_element_type=F32
        )

    totals = [jnp.zeros((SUB, cut), F32) for _ in range(0, block, cut)]
    products(0)
    for index in range(count):
        if index + 1 < count:
            products(index + 1)
        for at in range(0, part, strip):
            here = slice(index * part + at, index * part + at + strip)
            for which, left in enumerate(range(0, block, cut)):
                lanes = slice(left, left + cut)
                x = pre_s[index % 2, at : at + strip, lanes] + bi_ref[:, lanes]
                value, slope = gelu_twice(x)
                act[here, lanes] = value.astype(BF16)
                d_pre = dact_s[index % 2, at : at + strip, lanes] * slope
                dpre[here, lanes] = d_pre.astype(BF16)
                totals[which] = totals[which] + (d_pre[:SUB] + d_pre[SUB:])
        if index > 0:
            project(index - 1)
    project(count - 1)
    for which, left in enumerate(range(0, block, cut)):
        gbi_ref[:, left : left + cut] = jnp.sum(totals[which], axis=0, keepdims=True)
    _, parts, _, width = sent_ref.shape
    is_sent = step_now < pl.num_programs(0) // 2
    for index, (rows_t, source) in enumerate(((dbr_t, act), (normed_t, dpre))):
        for left in range(0, block, cut):
            grad = jnp.dot(
                rows_t[...], source[:, left : left + cut], preferred_element_type=F32
            ).astype(BF16)

            def store(ref):
                for at in range(0, cut, min(width, cut)):
                    lat, into = divmod(left + at, width)
                    size = min(width, cut)
                    ref[index, lat, :, into : into + size] = grad[:, at : at + size]

            pl.when(is_sent)(functools.partial(store, sent_ref))
            pl.when(jnp.logical_not(is_sent))(functools.partial(store, kept_ref))

    @pl.when(step_now == pl.num_programs(0) - 1)
    def _():
        def norm_back(row, at, here):
            cot = cot_ref[here, :].astype(F32)
            ocean = mask_column(m_ref, row, at, strip) * (0.5 * branch[here, :] + bo_ref[...])
            mixed_ref[here, :] = (f_ref[here, :].astype(F32) + ocean * scale_ref[...]).astype(BF16)
            term = ocean * cot
            sums_ref[1] += term[:SUB] + term[SUB:]
            grad = d_normed[here, :]
            xhat = conv[row, at : at + strip, :]
            term = grad * xhat
            sums_ref[2] += term[:SUB] + term[SUB:]
            sums_ref[3] += grad[:SUB] + grad[SUB:]
            e = grad * gain_ref[...]
            m1 = jnp.mean(e, axis=-1, keepdims=True)
            m2 = jnp.mean(term * gain_ref[...], axis=-1, keepdims=True)
            inv = jnp.concatenate([inv_s[here, :]] * wide, axis=1)
            dconv_ref[here, :] = (inv * (e - m1 - xhat * m2)).astype(BF16)

        strips(norm_back)


def expand(
    order, inner, side, top, bot, kernel, gain, bias, scale, b_out, mask, cot, fields, w_in, b_in, w_out, n_lon, n_lat
):
    rows, _, channels = inner.shape
    hidden = w_in.shape[1]
    cells, _ = cot.shape
    cols = cells // rows
    block = hidden // n_lon
    split = n_lat if (block // n_lat) % LANES == 0 else 1
    turn = n_lon // 2
    grads = (split, channels, block // split)
    given = (inner, side, top, bot, kernel, gain, bias, scale, b_out, mask, cot, fields)

    def sent_at(h, order):
        return (0, jnp.minimum(h, turn - 1), 0, 0, 0)

    def kept_at(h, order):
        return (0, jnp.maximum(h - turn, 0), 0, 0, 0)

    return pl.pallas_call(
        expand_kernel,
        grid_spec=pltpu.PrefetchScalarGridSpec(
            num_scalar_prefetch=1,
            grid=(n_lon,),
            in_specs=[once(x.shape) for x in given]
            + [
                pl.BlockSpec((channels, block), lambda h, order: (0, order[h])),
                pl.BlockSpec((1, block), lambda h, order: (0, order[h])),
                pl.BlockSpec((block, channels), lambda h, order: (order[h], 0)),
            ],
            out_specs=[
                once((cells, channels)),
                once((cells, channels)),
                once((4, SUB, channels)),
                pl.BlockSpec((1, block), lambda h, order: (0, order[h])),
                pl.BlockSpec((2, None) + grads, sent_at),
                pl.BlockSpec((2, None) + grads, kept_at),
            ],
            scratch_shapes=[
                pltpu.VMEM((rows, cols, channels), F32),
                pltpu.VMEM((6, cols + 16, channels), F32),
                pltpu.VMEM((cells, LANES), F32),
                pltpu.VMEM((cells, channels), BF16),
                pltpu.VMEM((channels, cells), BF16),
                pltpu.VMEM((cells, channels), BF16),
                pltpu.VMEM((channels, cells), BF16),
                pltpu.VMEM((cells, block), BF16),
                pltpu.VMEM((cells, block), BF16),
                pltpu.VMEM((cells, channels), F32),
                pltpu.VMEM((cells, channels), F32),
                pltpu.VMEM((2, 256, block), F32),
                pltpu.VMEM((2, 256, block), F32),
            ],
        ),
        out_shape=[
            jax.ShapeDtypeStruct((cells, channels), BF16),
            jax.ShapeDtypeStruct((cells, channels), BF16),
            jax.ShapeDtypeStruct((4, SUB, channels), F32),
            jax.ShapeDtypeStruct((1, hidden), F32),
            jax.ShapeDtypeStruct((2, turn) + grads, BF16),
            jax.ShapeDtypeStruct((2, turn) + grads, BF16),
        ],
        compiler_params=params(56),
        cost_estimate=estimate(20),
        name="expand",
    )(order, *given, w_in, b_in, w_out)


def fill_window(window, center, left, right, top, bot):
    rows, cols, _ = center.shape
    window[3 : 3 + rows, 5:8, :] = left[...].astype(F32)
    window[3 : 3 + rows, 8 : 8 + cols, :] = center
    window[3 : 3 + rows, 8 + cols : 11 + cols, :] = right[...].astype(F32)
    window[0:3, 5 : 11 + cols, :] = top[...].astype(F32)
    window[3 + rows : 6 + rows, 5 : 11 + cols, :] = bot[...].astype(F32)


def filter_grad_kernel(
    f_ref, m_ref, l_ref, r_ref, t_ref, b_ref, d_ref, sums_ref, gbi_0, gbi_1, gbi_2, gbi_3,
    o_ref, window, grad, wide,
):
    rows, cols, _ = f_ref.shape
    spread_mask(m_ref, wide)
    fill_window(window, f_ref[...].astype(F32) * wide[...], l_ref, r_ref, t_ref, b_ref)
    grad[...] = d_ref[...].astype(F32)
    for col_off in range(7):

        def band(index, sums):
            start = pl.multiple_of(index * 8, 8)
            sums = list(sums)
            held = {}
            for src in range(rows + 6):
                if src < rows:
                    held[src] = grad[src, pl.ds(start, SUB), :]
                cells = shifted(window, src, start, 5 + col_off)
                for row_off in range(7):
                    out = src - row_off
                    if 0 <= out < rows:
                        sums[row_off] = sums[row_off] + held[out] * cells
            return tuple(sums)

        start = tuple(jnp.zeros((SUB, LANES), F32) for _ in range(7))
        sums = lax.fori_loop(0, cols // 8, band, start)
        for row_off in range(7):
            o_ref[row_off, col_off : col_off + 1, :] = jnp.sum(sums[row_off], axis=0, keepdims=True)
    for at, source in enumerate((1, 2, 3, 0)):
        o_ref[7, at : at + 1, :] = jnp.sum(sums_ref[source], axis=0, keepdims=True)
    for at, gbi_ref in enumerate((gbi_0, gbi_1, gbi_2, gbi_3)):
        o_ref[7, 4 + at : 5 + at, :] = gbi_ref[...]
    for row_off in range(7):
        o_ref[row_off, 7:8, :] = jnp.zeros((1, LANES), F32)


def filter_grad(fields, mask, left, right, top, bot, d_conv, sums, gbi):
    rows, cols, channels = fields.shape

    def part(x):
        return by_channels(x.shape)

    return pl.pallas_call(
        filter_grad_kernel,
        grid=(channels // LANES,),
        out_shape=jax.ShapeDtypeStruct((8, 8, channels), F32),
        in_specs=[
            part(fields),
            whole_spec(mask.shape),
            part(left),
            part(right),
            part(top),
            part(bot),
            part(d_conv),
            part(sums),
        ]
        + [by_channels(gbi.shape, at * (channels // LANES)) for at in range(4)],
        out_specs=by_channels((8, 8, channels)),
        scratch_shapes=[
            pltpu.VMEM((rows + 6, cols + 16, LANES), F32),
            pltpu.VMEM((rows, cols, LANES), F32),
            pltpu.VMEM((rows, cols, LANES), F32),
        ],
        compiler_params=params(56),
        cost_estimate=estimate(4),
        name="filter_grad",
    )(fields, mask, left, right, top, bot, d_conv, sums, gbi, gbi, gbi, gbi)


def input_grad_kernel(d_ref, l_ref, r_ref, t_ref, b_ref, k_ref, m_ref, cot_ref, o_ref, window, grad, wide):
    rows, cols, _ = d_ref.shape
    spread_mask(m_ref, wide)
    fill_window(window, d_ref[...].astype(F32), l_ref, r_ref, t_ref, b_ref)
    for start in range(0, cols, 8):
        sums = band_conv(window, k_ref, start, rows, 3, True)
        for row in range(rows):
            grad[row, start : start + 8, :] = sums[row]
    o_ref[...] = (cot_ref[...].astype(F32) + wide[...] * grad[...]).astype(BF16)


def input_grad_more_kernel(d_ref, l_ref, r_ref, t_ref, b_ref, k_ref, m_ref, cot_ref, old_ref, o_ref, window, grad, wide):
    input_grad_kernel(d_ref, l_ref, r_ref, t_ref, b_ref, k_ref, m_ref, cot_ref, o_ref, window, grad, wide)


def input_grad(d_conv, left, right, top, bot, kernel, mask, cot, blocks, first, old=None):
    rows, cols, channels = d_conv.shape

    def part(x):
        return by_channels(x.shape, first)

    more = [] if old is None else [old]
    return pl.pallas_call(
        input_grad_kernel if old is None else input_grad_more_kernel,
        grid=(blocks,),
        out_shape=jax.ShapeDtypeStruct((rows, cols, channels), BF16),
        in_specs=[
            part(d_conv),
            part(left),
            part(right),
            part(top),
            part(bot),
            part(kernel),
            whole_spec(mask.shape),
            part(cot),
        ]
        + [UNUSED] * len(more),
        out_specs=part(d_conv),
        scratch_shapes=[
            pltpu.VMEM((rows + 6, cols + 16, LANES), F32),
            pltpu.VMEM((rows, cols, LANES), F32),
            pltpu.VMEM((rows, cols, LANES), F32),
        ],
        input_output_aliases={} if old is None else {8: 0},
        compiler_params=params(56),
        cost_estimate=estimate(4),
        name="input_grad",
    )(d_conv, left, right, top, bot, kernel, mask, cot, *more)


def swap(values, axis, bit):
    count = lax.axis_size(axis)
    return lax.ppermute(values, axis, [(i, i ^ bit) for i in range(count)])


def bits_of(axis):
    return [1 << k for k in range(int(math.log2(lax.axis_size(axis))))]


def after(value, *others):
    return lax.optimization_barrier((value,) + others)[0]


def halves(values, axis, dim, bit):
    mine = (lax.axis_index(axis) // bit) % 2 == 1
    shape = values.shape
    paired = values.reshape(shape[:dim] + (shape[dim] // 2, 2) + shape[dim + 1 :])
    low = lax.index_in_dim(paired, 0, dim + 1, keepdims=False)
    high = lax.index_in_dim(paired, 1, dim + 1, keepdims=False)
    return jnp.where(mine, high, low), jnp.where(mine, low, high).astype(BF16)


def side_halo(last, first):
    count = lax.axis_size("lon")
    ahead = [(i, (i + 1) % count) for i in range(count)]
    back = [((i + 1) % count, i) for i in range(count)]
    return lax.ppermute(last, "lon", ahead), lax.ppermute(first, "lon", back)


def end_rows(head, tail, left, right):
    rows = left.shape[0]
    return (
        jnp.concatenate([left[rows - 3 :], tail, right[rows - 3 :]], axis=1),
        jnp.concatenate([left[:3], head, right[:3]], axis=1),
    )


def end_halo(tail, head):
    count = lax.axis_size("lat")
    ahead = [(i, i + 1) for i in range(count - 1)]
    back = [(i + 1, i) for i in range(count - 1)]
    return lax.ppermute(tail, "lat", ahead), lax.ppermute(head, "lat", back)


def per_device(
    fields,
    land_mask,
    cotangent,
    kernel,
    layer_norm_gain,
    layer_norm_bias,
    w_in,
    b_in,
    w_out,
    b_out,
    layer_scale,
):
    rows, cols, channels = fields.shape
    cells = rows * cols
    hidden = w_in.shape[1]
    n_lon, n_lat = lax.axis_size("lon"), lax.axis_size("lat")
    gain, bias = layer_norm_gain.reshape(1, -1), layer_norm_bias.reshape(1, -1)
    scale = layer_scale.reshape(1, -1)
    cot_rows = cotangent.reshape(cells, channels)
    ocean = land_mask.astype(BF16)[:, :, None]
    left, right = side_halo(fields[:, cols - 3 :] * ocean[:, cols - 3 :], fields[:, :3] * ocean[:, :3])
    inner, head, tail = conv_inner(fields, land_mask, kernel)
    top, bot = end_halo(*end_rows(head, tail, left, right))
    side = conv_side(fields, land_mask, kernel, left, right)

    lon = lax.axis_index("lon")
    core, side_y = lon % 2, (lon // 2) % 2
    quads = 4 * jnp.arange(n_lon // 4, dtype=jnp.int32)
    order = jnp.concatenate(
        [quads + 2 * y + c for c in (1 - core, core) for y in (1 - side_y, side_y)]
    )
    d_conv, mixed, sums, g_bi, sent, kept = expand(
        order, inner, side, top, bot, kernel, gain, bias, scale, b_out.reshape(1, -1), land_mask, cot_rows,
        fields.reshape(cells, channels), w_in, b_in.reshape(1, -1), w_out, n_lon, n_lat,
    )
    got = swap(sent, "lon", 1)
    d_conv = d_conv.reshape(rows, cols, channels)
    d_left, d_right = side_halo(d_conv[:, cols - 3 :], d_conv[:, :3])
    d_tail, d_head = end_rows(d_conv[:3], d_conv[rows - 3 :], d_left, d_right)
    d_top, d_bot = end_halo(d_tail, d_head)

    far = n_lon // 4
    border = channels * 5 // 8
    pieces = (slice(0, border), slice(border, channels))
    far_sums = [
        (kept[:, :far, :, piece].astype(F32) + got[:, :far, :, piece].astype(F32)).astype(BF16)
        for piece in pieces
    ]
    got_far = [swap(x, "lon", 2) for x in far_sums]
    steps = [("lon", 1, bit) for bit in bits_of("lon")[2:]] + [("lat", 2, bit) for bit in bits_of("lat")]
    owned, cut = [None, None], [None, None]

    def begin(index, last):
        here = pieces[index]
        x = after(kept, last)[:, far:, :, here].astype(F32) + after(got, last)[:, far:, :, here].astype(F32)
        x = x + after(got_far[index], last).astype(F32)
        if x.shape[2] != n_lat:
            x = x.reshape(2, far, x.shape[3], n_lat, -1).transpose(0, 1, 3, 2, 4)
        cut[index] = halves(x, *steps[0])

    def advance(index, step, last):
        axis, dim, bit = steps[step]
        mine, sent = cut[index]
        owned[index] = after(mine, last) + after(swap(sent, axis, bit), last).astype(F32)
        if step + 1 < len(steps):
            cut[index] = halves(owned[index], *steps[step + 1])

    hops = [(axis, bit) for axis in ("lon", "lat") for bit in bits_of(axis)]

    def spread(hop, last):
        return after(small, last) + after(swap(small, *hops[hop]), last)

    small = filter_grad(
        after(fields, d_tail, d_head, far_sums[0]), land_mask, left, right, top, bot, d_conv, sums, g_bi
    )
    begin(0, small)
    for step in range(len(steps) - 2):
        advance(0, step, small)
    half = channels // LANES // 2
    back = (d_left, d_right, d_top, d_bot, kernel, land_mask, cotangent)
    grad_fields = input_grad(after(d_conv, small, cut[0][1], far_sums[1]), *back, half, 0)
    small = spread(0, grad_fields)
    advance(0, len(steps) - 2, grad_fields)
    begin(1, grad_fields)
    for step in range(len(steps) - 2):
        advance(1, step, grad_fields)
    grad_fields = input_grad(
        after(d_conv, small, cut[0][1], cut[1][1]), *back, half // 2, half, grad_fields
    )
    small = spread(1, grad_fields)
    advance(0, len(steps) - 1, grad_fields)
    advance(1, len(steps) - 2, grad_fields)
    grad_fields = input_grad(
        after(d_conv, small, cut[1][1]), *back, half // 2, half + half // 2, grad_fields
    )
    for hop in range(2, len(hops)):
        small = spread(hop, grad_fields)
    advance(1, len(steps) - 1, grad_fields)
    grad_w = jnp.concatenate([x[:, 0, 0] for x in owned], axis=1)
    return (
        mixed.reshape(rows, cols, channels),
        grad_fields,
        small[:7, :7],
        small[7, 1],
        small[7, 2],
        grad_w[1],
        small[7, 4:].reshape(hidden),
        grad_w[0].T,
        small[7, 3],
        small[7, 0],
    )


def solution(mesh):
    placed = (
        P(("grp", "lat"), "lon", None),
        P(("grp", "lat"), "lon"),
        P(("grp", "lat"), "lon", None),
        P(),
        P(),
        P(),
        P(),
        P(),
        P(),
        P(),
        P(),
    )
    return jax.shard_map(
        per_device,
        mesh=mesh,
        in_specs=placed,
        out_specs=(
            P(("grp", "lat"), "lon", None),
            P(("grp", "lat"), "lon", None),
            P("grp", None, None),
            P("grp"),
            P("grp"),
            P("grp", ("lon", "lat")),
            P("grp"),
            P(("lon", "lat"), "grp"),
            P("grp"),
            P("grp"),
        ),
        check_vma=False,
    )
```

time: 134 us -> 147 us (1.097)
  Pallas kernels: 74.3 us -> 92.6 us
  waiting for transfers between devices: 14 us -> 7.85 us
  other arithmetic: 9.25 us -> 7.57 us
    pallas_call x1, Pallas kernels: 28.4 us -> 39 us  [expand(): pl.pallas_call(expand_kernel, grid_spec=pltpu.PrefetchScalarGridSpec(num_...]
    ppermute x11, waiting for transfers between devices: 14 us -> 3.47 us  [swap(): return lax.ppermute(values, axis, [(i, i ^ bit) for i in range(count)])]
    pallas_call x3, Pallas kernels: 14.9 us -> 22.2 us  [input_grad(): pl.pallas_call(input_grad_kernel if old is None else input_grad_more_kern...]
    pallas_call x1 -> x0, Pallas kernels: 7.12 us -> none  [project(): pl.pallas_call(project_kernel, grid=(cells // part,), out_shape=[jax.Shap...]
    ppermute x4, waiting for transfers between devices: 0.01 us -> 4.37 us  [side_halo(): return (lax.ppermute(last, 'lon', ahead), lax.ppermute(first, 'lon', back))]
    unnamed x25 -> x23, local copies, waits for them, and re-layouts: 1.47 us -> 4.11 us
    pallas_call x1, Pallas kernels: 11.6 us -> 14.2 us  [filter_grad(): pl.pallas_call(filter_grad_kernel, grid=(channels // LANES,), out_shape=j...]
    pallas_call x1, Pallas kernels: 6.14 us -> 8.58 us  [conv_side(): pl.pallas_call(conv_side_kernel, grid=(channels // LANES,), out_shape=jax...]
  transfers between devices with their start and end apart: 19 -> 19, of which waited for: 4 -> 3; matrix products, arithmetic and copies ran while one was open for 7% -> 5% of each run, Pallas kernels for 34% -> 37%
where the time goes in v5:
time: 147 us; the launch traced here: 146 us
  Pallas kernels  92.6 us (63%)
  starting transfers between devices  29.6 us (20%)
  waiting for transfers between devices  7.85 us (5%)
  local copies, waits for them, and re-layouts  7.71 us (5%)
  other arithmetic  7.57 us (5%)
    pallas_call x1, Pallas kernels, expand(): pl.pallas_call(expand_kernel, grid_spec=pltpu.PrefetchScalarGridSpec(num_...  39 us
    pallas_call x3, Pallas kernels, input_grad(): pl.pallas_call(input_grad_kernel if old is None else input_grad_more_kern...  22.2 us
    pallas_call x1, Pallas kernels, filter_grad(): pl.pallas_call(filter_grad_kernel, grid=(channels // LANES,), out_shape=j...  14.2 us
    ppermute x11, starting transfers between devices, swap(): return lax.ppermute(values, axis, [(i, i ^ bit) for i in range(count)])  13.8 us
    ppermute x4, starting transfers between devices, end_halo(): return (lax.ppermute(tail, 'lat', ahead), lax.ppermute(head, 'lat', back))  11.5 us
    pallas_call x1, Pallas kernels, conv_inner(): pl.pallas_call(conv_inner_kernel, grid=(channels // LANES,), out_shape=[j...  8.63 us
    pallas_call x1, Pallas kernels, conv_side(): pl.pallas_call(conv_side_kernel, grid=(channels // LANES,), out_shape=jax...  8.58 us
    ppermute x4, waiting for transfers between devices, side_halo(): return (lax.ppermute(last, 'lon', ahead), lax.ppermute(first, 'lon', back))  4.37 us
  transfers between devices with their start and end apart: 19, of which 3 were waited for; matrix products, arithmetic and copies ran while one was open for 5% of the time, Pallas kernels for 37%

profile of v5, /device:TPU:0, one launch (start us, length us, event | category | flops | bytes accessed | tf_op | source)
XLA Modules:
  0.0 146.3 jit_solution(3219860581882602665)
XLA Ops:
  1.4 1.2 slice_multiply_fusion
  3.2 2.0 %collective-permute-start.1 = (bf16[32,3,512]{2,1,0:T(4,128)(2,1)S(1)}, bf16[32,3,512]{2,1,0:T(4,128)(2,1)S(1)}, u32[]{:S(2)}, u32[]{:S(2)}) collective-permute-start(bf16[32,3,512]{2,1,0:T(4,128)(2,1)S(1)} %get-tuple-element.96), channel_id=1, source_target_pairs={{4,0},{8,4},{12,8},{0,12},{5,1},{9,5},{13,9},{1,13},{6,2},{10,6},{... | collective-permute-start | bytes 294920 | tf_op jit(solution)/shard_map/ppermute | solution.py:550
  5.2 8.6 %conv_inner.1 = (f32[32,16,512]{2,1,0:T(8,128)}, bf16[3,32,512]{2,1,0:T(8,128)(2,1)}, bf16[3,32,512]{2,1,0:T(8,128)(2,1)}) custom-call(bf16[32,32,512]{2,1,0:T(8,128)(2,1)} %f_ref.4, s32[32,32]{1,0:T(8,128)} %m_ref.13, f32[7,7,512]{2,1,0:T(8,128)} %k_ref.11), custom_call_target="tpu_custom_call" | custom-call | flops 4600000000 | bytes 14400000 | tf_op jit(solution)/shard_map/conv_inner/pallas_call | solution.py:122
  15.5 4.2 %collective-permute-start.2 = (bf16[3,38,512]{2,1,0:T(8,128)(2,1)S(1)}, bf16[3,38,512]{2,1,0:T(8,128)(2,1)S(1)}, u32[]{:S(2)}, u32[]{:S(2)}) collective-permute-start(bf16[3,38,512]{2,1,0:T(8,128)(2,1)S(1)} %pad_maximum_fusion.1), channel_id=1, source_target_pairs={{0,1},{1,2},{2,3},{4,5},{5,6},{6,7},{8,9},{9,10},{10,11},{12,13},{... | collective-permute-start | bytes 350216 | tf_op jit(solution)/shard_map/ppermute | solution.py:565
  20.6 1.3 collective-permute-start.3
  22.0 8.6 %conv_side.1.side_ref = f32[32,16,512]{2,1,0:T(8,128)} custom-call(bf16[32,32,512]{2,1,0:T(8,128)(2,1)} %f_ref.4, s32[32,32]{1,0:T(8,128)} %m_ref.13, f32[7,7,512]{2,1,0:T(8,128)} %k_ref.11, bf16[32,3,512]{2,1,0:T(4,128)(2,1)} %copy-done.2, bf16[32,3,512]{2,1,0:T(4,128)(2,1)} %copy-done.3), custom_call_target="tpu_custom_call" | custom-call | flops 4600000000 | bytes 14400000 | tf_op jit(solution)/shard_map/conv_side/pallas_call | solution.py:144
  31.2 39.0 %expand.1 = (bf16[1024,512]{1,0:T(8,128)(2,1)}, bf16[1024,512]{1,0:T(8,128)(2,1)}, f32[4,8,512]{2,1,0:T(8,128)}, f32[1,2048]{1,0:T(1,128)}, bf16[2,2,4,512,128]{...) custom-call(s32[4]{0:T(128)} %pad_add_fusion.order_ref, f32[32,16,512]{2,1,0:T(8,128)} %get-tuple-element.45.inner_ref, ...), custom_call_target="tpu_custom_call" | custom-call | flops 23000000512 | bytes 72000000 | tf_op jit(solution)/shard_map/expand/pallas_call | solution.py:347
  70.4 1.1 fusion.9
  71.5 1.6 %collective-permute-start.5 = (bf16[32,3,512]{2,1,0:T(4,128)(2,1)S(1)}, bf16[32,3,512]{2,1,0:T(4,128)(2,1)S(1)}, u32[]{:S(2)}, u32[]{:S(2)}) collective-permute-start(bf16[32,3,512]{2,1,0:T(4,128)(2,1)S(1)} %get-tuple-element.95), channel_id=1, source_target_pairs={{4,0},{8,4},{12,8},{0,12},{5,1},{9,5},{13,9},{1,13},{6,2},{10,6},{... | collective-permute-start | bytes 294920 | tf_op jit(solution)/shard_map/ppermute | solution.py:550
  74.2 1.9 %collective-permute-done.5.r_ref = bf16[32,3,512]{2,1,0:T(4,128)(2,1)S(1)} collective-permute-done((bf16[32,3,512]{2,1,0:T(4,128)(2,1)S(1)}, bf16[32,3,512]{2,1,0:T(4,128)(2,1)S(1)}, u32[]{:S(2)}, u32[]{:S(2)}) %collective-permute-start.5) | collective-permute-done | bytes 98336 | tf_op jit(solution)/shard_map/ppermute | solution.py:550
  76.1 2.4 %collective-permute-done.4.l_ref = bf16[32,3,512]{2,1,0:T(4,128)(2,1)S(1)} collective-permute-done((bf16[32,3,512]{2,1,0:T(4,128)(2,1)S(1)}, bf16[32,3,512]{2,1,0:T(4,128)(2,1)S(1)}, u32[]{:S(2)}, u32[]{:S(2)}) %collective-permute-start.4) | collective-permute-done | bytes 98336 | tf_op jit(solution)/shard_map/ppermute | solution.py:550
  78.6 4.5 %collective-permute-start.8 = (bf16[3,38,512]{2,1,0:T(8,128)(2,1)S(1)}, bf16[3,38,512]{2,1,0:T(8,128)(2,1)S(1)}, u32[]{:S(2)}, u32[]{:S(2)}) collective-permute-start(bf16[3,38,512]{2,1,0:T(8,128)(2,1)S(1)} %pad_maximum_fusion.3), channel_id=1, source_target_pairs={{0,1},{1,2},{2,3},{4,5},{5,6},{6,7},{8,9},{9,10},{10,11},{12,13},{... | collective-permute-start | bytes 350216 | tf_op jit(solution)/shard_map/ppermute | solution.py:565
  83.2 1.5 %collective-permute-start.9 = (bf16[3,38,512]{2,1,0:T(8,128)(2,1)S(1)}, bf16[3,38,512]{2,1,0:T(8,128)(2,1)S(1)}, u32[]{:S(2)}, u32[]{:S(2)}) collective-permute-start(bf16[3,38,512]{2,1,0:T(8,128)(2,1)S(1)} %pad_maximum_fusion.4), channel_id=1, source_target_pairs={{1,0},{2,1},{3,2},{5,4},{6,5},{7,6},{9,8},{10,9},{11,10},{13,12},{... | collective-permute-start | bytes 350216 | tf_op jit(solution)/shard_map/ppermute | solution.py:565
  84.7 1.3 add_convert_fusion
  87.0 14.2 %filter_grad.1 = f32[8,8,512]{2,1,0:T(8,128)} custom-call(bf16[32,32,512]{2,1,0:T(8,128)(2,1)} %f_ref.4, s32[32,32]{1,0:T(8,128)} %m_ref.13, bf16[32,3,512]{2,1,0:T(4,128)(2,1)} %copy-done.2, bf16[32,3,512]{2,1,0:T(4,128)(2,1)} %copy-done.3, bf16[3,38,512]{2,1,0:T(8,128)(2,1)} %copy-done.6, bf16[3,38,512]{2,1,0:T(8,128)(2,1)} %copy-done.7, ...), custom_call_target="tpu_custom_call" | custom-call | flops 4600000000 | bytes 14400000 | tf_op jit(solution)/shard_map/filter_grad/pallas_call | solution.py:447
  101.4 1.1 collective-permute-start.12
  103.0 2.7 %collective-permute-start.11 = (bf16[2,1,2,320,128]{4,3,0,2,1:T(8,128)(2,1)S(1)}, bf16[2,1,2,320,128]{4,3,0,2,1:T(8,128)(2,1)S(1)}, u32[]{:S(2)}, u32[]{:S(2)}) collective-permute-start(bf16[2,1,2,320,128]{4,3,0,2,1:T(8,128)(2,1)S(1)} %fusion), channel_id=1, source_target_pairs={{0,1},{1,0},{2,3},{3,2},{4,5},{5,4},{6,7},{7,6},{8,9},{9,8},{10,11... | collective-permute-start | bytes 983048 | tf_op jit(solution)/shard_map/ppermute | solution.py:526
  107.0 8.9 %input_grad.3.old_ref = bf16[32,32,512]{2,1,0:T(8,128)(2,1)} custom-call(bf16[32,32,512]{2,1,0:T(8,128)(2,1)} %bitcast.66, bf16[32,3,512]{2,1,0:T(4,128)(2,1)} %copy-done.5, bf16[32,3,512]{2,1,0:T(4,128)(2,1)} %copy-done.4, bf16[3,38,512]{2,1,0:T(8,128)(2,1)} %copy-done.8, bf16[3,38,512]{2,1,0:T(8,128)(2,1)} %copy-done.9, f32[7,7,512]{2,1,0:T(8,128)} %k_ref.11, ...), custom_call_target="tpu_custom_call" | custom-call | flops 4600000000 | bytes 14400000 | tf_op jit(solution)/shard_map/input_grad/pallas_call | solution.py:496
  118.2 3.1 %collective-permute-start.17 = (bf16[2,1,1,320,128]{4,3,0,2,1:T(8,128)(2,1)S(1)}, bf16[2,1,1,320,128]{4,3,0,2,1:T(8,128)(2,1)S(1)}, u32[]{:S(2)}, u32[]{:S(2)}) collective-permute-start(bf16[2,1,1,320,128]{4,3,0,2,1:T(8,128)(2,1)S(1)} %fusion.5), channel_id=1, source_target_pairs={{0,2},{1,3},{2,0},{3,1},{4,6},{5,7},{6,4},{7,5},{8,10},{9,11},{10,... | collective-permute-start | bytes 491528 | tf_op jit(solution)/shard_map/ppermute | solution.py:526
  121.2 6.6 %input_grad.4.old_ref = bf16[32,32,512]{2,1,0:T(8,128)(2,1)} custom-call(bf16[32,32,512]{2,1,0:T(8,128)(2,1)} %bitcast.67, bf16[32,3,512]{2,1,0:T(4,128)(2,1)} %copy-done.5, bf16[32,3,512]{2,1,0:T(4,128)(2,1)} %copy-done.4, bf16[3,38,512]{2,1,0:T(8,128)(2,1)} %copy-done.8, bf16[3,38,512]{2,1,0:T(8,128)(2,1)} %copy-done.9, ...), custom_call_target="tpu_custom_call", output_to_operand_aliasing={{}: (8, {})} | custom-call | flops 4600000000 | bytes 14400000 | tf_op jit(solution)/shard_map/input_grad/pallas_call | solution.py:496
  128.1 1.6 %collective-permute-start.15 = (f32[8,8,512]{2,1,0:T(8,128)S(1)}, f32[8,8,512]{2,1,0:T(8,128)S(1)}, u32[]{:S(2)}, u32[]{:S(2)}) collective-permute-start(f32[8,8,512]{2,1,0:T(8,128)S(1)} %add.112), channel_id=1, source_target_pairs={{0,1},{1,0},{2,3},{3,2},{4,5},{5,4},{6,7},{7,6},{8,9},{9,8},{10,11... | collective-permute-start | bytes 393224 | tf_op jit(solution)/shard_map/ppermute | solution.py:526
  130.1 6.6 %input_grad.5 = bf16[32,32,512]{2,1,0:T(8,128)(2,1)} custom-call(bf16[32,32,512]{2,1,0:T(8,128)(2,1)} %bitcast.68, bf16[32,3,512]{2,1,0:T(4,128)(2,1)} %copy-done.5, bf16[32,3,512]{2,1,0:T(4,128)(2,1)} %copy-done.4, bf16[3,38,512]{2,1,0:T(8,128)(2,1)} %copy-done.8, bf16[3,38,512]{2,1,0:T(8,128)(2,1)} %copy-done.9, ...), custom_call_target="tpu_custom_call", output_to_operand_aliasing={{}: (8, {})} | custom-call | flops 4600000000 | bytes 14400000 | tf_op jit(solution)/shard_map/input_grad/pallas_call | solution.py:496
  136.7 2.6 %collective-permute-start.16 = (f32[8,8,512]{2,1,0:T(8,128)S(1)}, f32[8,8,512]{2,1,0:T(8,128)S(1)}, u32[]{:S(2)}, u32[]{:S(2)}) collective-permute-start(f32[8,8,512]{2,1,0:T(8,128)S(1)} %add.114), channel_id=1, source_target_pairs={{0,2},{1,3},{2,0},{3,1},{4,6},{5,7},{6,4},{7,5},{8,10},{9,11},{10,... | collective-permute-start | bytes 393224 | tf_op jit(solution)/shard_map/ppermute | solution.py:526
  141.0 3.4 %collective-permute-done.16 = f32[8,8,512]{2,1,0:T(8,128)S(1)} collective-permute-done((f32[8,8,512]{2,1,0:T(8,128)S(1)}, f32[8,8,512]{2,1,0:T(8,128)S(1)}, u32[]{:S(2)}, u32[]{:S(2)}) %collective-permute-start.16) | collective-permute-done | bytes 131104 | tf_op jit(solution)/shard_map/ppermute | solution.py:526
  (83 shorter events, 14.9 us)
Async XLA Ops:
  2.7 11.8 %collective-permute-start = (bf16[32,3,512]{2,1,0:T(4,128)(2,1)S(1)}, bf16[32,3,512]{2,1,0:T(4,128)(2,1)S(1)}, u32[]{:S(2)}, u32[]{:S(2)}) collective-permute-start(bf16[32,3,512]{2,1,0:T(4,128)(2,1)S(1)} %get-tuple-element.97), channel_id=1, source_target_pairs={{0,4},{4,8},{8,12},{12,0},{1,5},{5,9},{9,13},{13,1},{2,6},{6,10},{... | collective-permute-start | bytes 294920 | tf_op jit(solution)/shard_map/ppermute | solution.py:550
  3.2 11.3 %collective-permute-start.1 = (bf16[32,3,512]{2,1,0:T(4,128)(2,1)S(1)}, bf16[32,3,512]{2,1,0:T(4,128)(2,1)S(1)}, u32[]{:S(2)}, u32[]{:S(2)}) collective-permute-start(bf16[32,3,512]{2,1,0:T(4,128)(2,1)S(1)} %get-tuple-element.96), channel_id=1, source_target_pairs={{4,0},{8,4},{12,8},{0,12},{5,1},{9,5},{13,9},{1,13},{6,2},{10,6},{... | collective-permute-start | bytes 294920 | tf_op jit(solution)/shard_map/ppermute | solution.py:550
  14.4 7.5 %copy-start.3 = (bf16[32,3,512]{2,1,0:T(4,128)(2,1)}, bf16[32,3,512]{2,1,0:T(4,128)(2,1)S(1)}, u32[]{:S(2)}) copy-start(bf16[32,3,512]{2,1,0:T(4,128)(2,1)S(1)} %collective-permute-done.1.r_ref) | copy-start | bytes 294916
  14.5 7.5 %copy-start.2 = (bf16[32,3,512]{2,1,0:T(4,128)(2,1)}, bf16[32,3,512]{2,1,0:T(4,128)(2,1)S(1)}, u32[]{:S(2)}) copy-start(bf16[32,3,512]{2,1,0:T(4,128)(2,1)S(1)} %collective-permute-done.l_ref) | copy-start | bytes 294916
  15.5 15.1 %collective-permute-start.2 = (bf16[3,38,512]{2,1,0:T(8,128)(2,1)S(1)}, bf16[3,38,512]{2,1,0:T(8,128)(2,1)S(1)}, u32[]{:S(2)}, u32[]{:S(2)}) collective-permute-start(bf16[3,38,512]{2,1,0:T(8,128)(2,1)S(1)} %pad_maximum_fusion.1), channel_id=1, source_target_pairs={{0,1},{1,2},{2,3},{4,5},{5,6},{6,7},{8,9},{9,10},{10,11},{12,13},{... | collective-permute-start | bytes 350216 | tf_op jit(solution)/shard_map/ppermute | solution.py:565
  20.6 9.9 %collective-permute-start.3 = (bf16[3,38,512]{2,1,0:T(8,128)(2,1)S(1)}, bf16[3,38,512]{2,1,0:T(8,128)(2,1)S(1)}, u32[]{:S(2)}, u32[]{:S(2)}) collective-permute-start(bf16[3,38,512]{2,1,0:T(8,128)(2,1)S(1)} %pad_maximum_fusion.2), channel_id=1, source_target_pairs={{1,0},{2,1},{3,2},{5,4},{6,5},{7,6},{9,8},{10,9},{11,10},{13,12},{... | collective-permute-start | bytes 350216 | tf_op jit(solution)/shard_map/ppermute | solution.py:565
  70.3 14.5 %collective-permute-start.6 = (bf16[2,2,4,512,128]{4,3,2,1,0:T(8,128)(2,1)}, bf16[2,2,4,512,128]{4,3,2,1,0:T(8,128)(2,1)S(1)}, u32[]{:S(2)}, u32[]{:S(2)}) collective-permute-start(bf16[2,2,4,512,128]{4,3,2,1,0:T(8,128)(2,1)} %get-tuple-element.51), channel_id=1, source_target_pairs={{0,4},{4,0},{8,12},{12,8},{1,5},{5,1},{9,13},{13,9},{2,6},{6,2},{1... | collective-permute-start | bytes 6291464 | tf_op jit(solution)/shard_map/ppermute | solution.py:526
  71.5 4.6 %collective-permute-start.5 = (bf16[32,3,512]{2,1,0:T(4,128)(2,1)S(1)}, bf16[32,3,512]{2,1,0:T(4,128)(2,1)S(1)}, u32[]{:S(2)}, u32[]{:S(2)}) collective-permute-start(bf16[32,3,512]{2,1,0:T(4,128)(2,1)S(1)} %get-tuple-element.95), channel_id=1, source_target_pairs={{4,0},{8,4},{12,8},{0,12},{5,1},{9,5},{13,9},{1,13},{6,2},{10,6},{... | collective-permute-start | bytes 294920 | tf_op jit(solution)/shard_map/ppermute | solution.py:550
  74.1 4.4 %collective-permute-start.4 = (bf16[32,3,512]{2,1,0:T(4,128)(2,1)S(1)}, bf16[32,3,512]{2,1,0:T(4,128)(2,1)S(1)}, u32[]{:S(2)}, u32[]{:S(2)}) collective-permute-start(bf16[32,3,512]{2,1,0:T(4,128)(2,1)S(1)} %get-tuple-element.94), channel_id=1, source_target_pairs={{0,4},{4,8},{8,12},{12,0},{1,5},{5,9},{9,13},{13,1},{2,6},{6,10},{... | collective-permute-start | bytes 294920 | tf_op jit(solution)/shard_map/ppermute | solution.py:550
  76.1 25.1 %copy-start.4 = (bf16[32,3,512]{2,1,0:T(4,128)(2,1)}, bf16[32,3,512]{2,1,0:T(4,128)(2,1)S(1)}, u32[]{:S(2)}) copy-start(bf16[32,3,512]{2,1,0:T(4,128)(2,1)S(1)} %collective-permute-done.5.r_ref) | copy-start | bytes 294916
  78.5 22.7 %copy-start.5 = (bf16[32,3,512]{2,1,0:T(4,128)(2,1)}, bf16[32,3,512]{2,1,0:T(4,128)(2,1)S(1)}, u32[]{:S(2)}) copy-start(bf16[32,3,512]{2,1,0:T(4,128)(2,1)S(1)} %collective-permute-done.4.l_ref) | copy-start | bytes 294916
  78.6 27.1 %collective-permute-start.8 = (bf16[3,38,512]{2,1,0:T(8,128)(2,1)S(1)}, bf16[3,38,512]{2,1,0:T(8,128)(2,1)S(1)}, u32[]{:S(2)}, u32[]{:S(2)}) collective-permute-start(bf16[3,38,512]{2,1,0:T(8,128)(2,1)S(1)} %pad_maximum_fusion.3), channel_id=1, source_target_pairs={{0,1},{1,2},{2,3},{4,5},{5,6},{6,7},{8,9},{9,10},{10,11},{12,13},{... | collective-permute-start | bytes 350216 | tf_op jit(solution)/shard_map/ppermute | solution.py:565
  83.2 22.5 %collective-permute-start.9 = (bf16[3,38,512]{2,1,0:T(8,128)(2,1)S(1)}, bf16[3,38,512]{2,1,0:T(8,128)(2,1)S(1)}, u32[]{:S(2)}, u32[]{:S(2)}) collective-permute-start(bf16[3,38,512]{2,1,0:T(8,128)(2,1)S(1)} %pad_maximum_fusion.4), channel_id=1, source_target_pairs={{1,0},{2,1},{3,2},{5,4},{6,5},{7,6},{9,8},{10,9},{11,10},{13,12},{... | collective-permute-start | bytes 350216 | tf_op jit(solution)/shard_map/ppermute | solution.py:565
  86.0 16.6 %collective-permute-start.7 = (bf16[2,1,4,320,128]{4,3,2,1,0:T(8,128)(2,1)S(1)}, bf16[2,1,4,320,128]{4,3,2,1,0:T(8,128)(2,1)S(1)}, u32[]{:S(2)}, u32[]{:S(2)}) collective-permute-start(bf16[2,1,4,320,128]{4,3,2,1,0:T(8,128)(2,1)S(1)} %add_convert_fusion), channel_id=1, source_target_pairs={{0,8},{4,12},{8,0},{12,4},{1,9},{5,13},{9,1},{13,5},{2,10},{6,14},... | collective-permute-start | bytes 1966088 | tf_op jit(solution)/shard_map/ppermute | solution.py:526
  87.0 14.3 %copy-start = (bf16[2,2,4,512,128]{4,3,2,1,0:T(8,128)(2,1)S(1)}, bf16[2,2,4,512,128]{4,3,2,1,0:T(8,128)(2,1)}, u32[]{:S(2)}) copy-start(bf16[2,2,4,512,128]{4,3,2,1,0:T(8,128)(2,1)} %get-tuple-element.63) | copy-start | bytes 6291460
  101.2 14.7 %collective-permute-start.10 = (f32[8,8,512]{2,1,0:T(8,128)}, f32[8,8,512]{2,1,0:T(8,128)S(1)}, u32[]{:S(2)}, u32[]{:S(2)}) collective-permute-start(f32[8,8,512]{2,1,0:T(8,128)} %filter_grad.1), channel_id=1, source_target_pairs={{0,4},{4,0},{8,12},{12,8},{1,5},{5,1},{9,13},{13,9},{2,6},{6,2},{1... | collective-permute-start | bytes 393224 | tf_op jit(solution)/shard_map/ppermute | solution.py:526
  101.4 14.5 %collective-permute-start.12 = (bf16[2,1,4,192,128]{4,3,2,1,0:T(8,128)(2,1)S(1)}, bf16[2,1,4,192,128]{4,3,2,1,0:T(8,128)(2,1)S(1)}, u32[]{:S(2)}, u32[]{:S(2)}) collective-permute-start(bf16[2,1,4,192,128]{4,3,2,1,0:T(8,128)(2,1)S(1)} %add_convert_fusion.1), channel_id=1, source_target_pairs={{0,8},{4,12},{8,0},{12,4},{1,9},{5,13},{9,1},{13,5},{2,10},{6,14},... | collective-permute-start | bytes 1179656 | tf_op jit(solution)/shard_map/ppermute | solution.py:526
  103.0 15.1 %collective-permute-start.11 = (bf16[2,1,2,320,128]{4,3,0,2,1:T(8,128)(2,1)S(1)}, bf16[2,1,2,320,128]{4,3,0,2,1:T(8,128)(2,1)S(1)}, u32[]{:S(2)}, u32[]{:S(2)}) collective-permute-start(bf16[2,1,2,320,128]{4,3,0,2,1:T(8,128)(2,1)S(1)} %fusion), channel_id=1, source_target_pairs={{0,1},{1,0},{2,3},{3,2},{4,5},{5,4},{6,7},{7,6},{8,9},{9,8},{10,11... | collective-permute-start | bytes 983048 | tf_op jit(solution)/shard_map/ppermute | solution.py:526
  116.8 11.0 %collective-permute-start.13 = (f32[8,8,512]{2,1,0:T(8,128)S(1)}, f32[8,8,512]{2,1,0:T(8,128)S(1)}, u32[]{:S(2)}, u32[]{:S(2)}) collective-permute-start(f32[8,8,512]{2,1,0:T(8,128)S(1)} %add.107), channel_id=1, source_target_pairs={{0,8},{4,12},{8,0},{12,4},{1,9},{5,13},{9,1},{13,5},{2,10},{6,14},... | collective-permute-start | bytes 393224 | tf_op jit(solution)/shard_map/ppermute | solution.py:526
  117.9 10.0 %collective-permute-start.14 = (bf16[2,1,2,192,128]{4,3,0,2,1:T(8,128)(2,1)S(1)}, bf16[2,1,2,192,128]{4,3,0,2,1:T(8,128)(2,1)S(1)}, u32[]{:S(2)}, u32[]{:S(2)}) collective-permute-start(bf16[2,1,2,192,128]{4,3,0,2,1:T(8,128)(2,1)S(1)} %fusion.4), channel_id=1, source_target_pairs={{0,1},{1,0},{2,3},{3,2},{4,5},{5,4},{6,7},{7,6},{8,9},{9,8},{10,11... | collective-permute-start | bytes 589832 | tf_op jit(solution)/shard_map/ppermute | solution.py:526
  118.2 11.9 %collective-permute-start.17 = (bf16[2,1,1,320,128]{4,3,0,2,1:T(8,128)(2,1)S(1)}, bf16[2,1,1,320,128]{4,3,0,2,1:T(8,128)(2,1)S(1)}, u32[]{:S(2)}, u32[]{:S(2)}) collective-permute-start(bf16[2,1,1,320,128]{4,3,0,2,1:T(8,128)(2,1)S(1)} %fusion.5), channel_id=1, source_target_pairs={{0,2},{1,3},{2,0},{3,1},{4,6},{5,7},{6,4},{7,5},{8,10},{9,11},{10,... | collective-permute-start | bytes 491528 | tf_op jit(solution)/shard_map/ppermute | solution.py:526
  128.1 8.6 %collective-permute-start.15 = (f32[8,8,512]{2,1,0:T(8,128)S(1)}, f32[8,8,512]{2,1,0:T(8,128)S(1)}, u32[]{:S(2)}, u32[]{:S(2)}) collective-permute-start(f32[8,8,512]{2,1,0:T(8,128)S(1)} %add.112), channel_id=1, source_target_pairs={{0,1},{1,0},{2,3},{3,2},{4,5},{5,4},{6,7},{7,6},{8,9},{9,8},{10,11... | collective-permute-start | bytes 393224 | tf_op jit(solution)/shard_map/ppermute | solution.py:526
  129.7 9.7 %collective-permute-start.18 = (bf16[2,1,1,192,128]{4,3,0,2,1:T(8,128)(2,1)S(1)}, bf16[2,1,1,192,128]{4,3,0,2,1:T(8,128)(2,1)S(1)}, u32[]{:S(2)}, u32[]{:S(2)}) collective-permute-start(bf16[2,1,1,192,128]{4,3,0,2,1:T(8,128)(2,1)S(1)} %fusion.6), channel_id=1, source_target_pairs={{0,2},{1,3},{2,0},{3,1},{4,6},{5,7},{6,4},{7,5},{8,10},{9,11},{10,... | collective-permute-start | bytes 294920 | tf_op jit(solution)/shard_map/ppermute | solution.py:526
  136.7 7.7 %collective-permute-start.16 = (f32[8,8,512]{2,1,0:T(8,128)S(1)}, f32[8,8,512]{2,1,0:T(8,128)S(1)}, u32[]{:S(2)}, u32[]{:S(2)}) collective-permute-start(f32[8,8,512]{2,1,0:T(8,128)S(1)} %add.114), channel_id=1, source_target_pairs={{0,2},{1,3},{2,0},{3,1},{4,6},{5,7},{6,4},{7,5},{8,10},{9,11},{10,... | collective-permute-start | bytes 393224 | tf_op jit(solution)/shard_map/ppermute | solution.py:526
  (5 other events, 3.5 us)

commit v6 on v5

--- a/solution.py
+++ b/solution.py
@@ -51,65 +51,43 @@
     return [jnp.broadcast_to(row, (SUB, LANES)) for row in rows]
 
 
-def band_conv(window, k_ref, start, rows, pad, flip):
-    sums = [None] * rows
-    for col_off in range(7):
-        weights = tap_rows(k_ref, col_off, flip)
-        for src in range(window.shape[0]):
-            hits = [(src - pad - row_off + 3, row_off) for row_off in range(7)]
-            hits = [(out, row_off) for out, row_off in hits if 0 <= out < rows]
-            if not hits:
-                continue
-            cells = shifted(window, src, start, 5 + col_off)
-            for out, row_off in hits:
-                term = weights[row_off] * cells
-                sums[out] = term if sums[out] is None else sums[out] + term
-    return sums
-
-
-def mask_column(m_ref, row, start, count):
-    line = m_ref[pl.ds(row, 1), :].astype(F32)
-    spot = lax.broadcasted_iota(jnp.int32, (count, line.shape[1]), 1)
-    want = lax.broadcasted_iota(jnp.int32, (count, line.shape[1]), 0) + start
-    return jnp.sum(jnp.where(spot == want, line, 0.0), axis=1, keepdims=True)
-
-
-def spread_mask(m_ref, wide):
-    @pl.when(pl.program_id(0) == 0)
-    def _():
-        rows, cols, _ = wide.shape
-
-        def one(row, _):
-            column = mask_column(m_ref, row, 0, cols)
-            wide[pl.ds(row, 1)] = jnp.broadcast_to(column, (cols, LANES))[None]
-            return 0
-
-        lax.fori_loop(0, rows, one, 0)
-
-
-def conv_inner_kernel(f_ref, m_ref, k_ref, o_ref, head_ref, tail_ref, window, wide):
+def band_conv(window, k_ref, o_ref, start, into, pad, flip):
+    rows = o_ref.shape[0]
+    bound = window.shape[0]
+    part = 16
+    for top in range(0, rows, part):
+        sums = {}
+        for col_off in range(7):
+            weights = tap_rows(k_ref, col_off, flip)
+            sources = range(max(0, top + pad - 3), min(bound, top + pad + part + 3))
+            cells = {src: shifted(window, src, start, 5 + col_off) for src in sources}
+            for row_off in range(7):
+                for out in range(top, top + part):
+                    src = out + pad + row_off - 3
+                    if src in cells:
+                        term = weights[row_off] * cells[src]
+                        sums[out] = sums[out] + term if out in sums else term
+        for out in range(top, top + part):
+            o_ref[out, into : into + SUB, :] = sums[out]
+
+
+def conv_inner_kernel(f_ref, m_ref, k_ref, o_ref, head_ref, tail_ref, window):
     rows, cols, _ = f_ref.shape
-    spread_mask(m_ref, wide)
-    masked = f_ref[...].astype(F32) * wide[...]
+    masked = f_ref[...].astype(F32) * m_ref[...]
     window[:, 8 : 8 + cols, :] = masked
     head_ref[...] = masked[:3].astype(BF16)
     tail_ref[...] = masked[rows - 3 :].astype(BF16)
     for start in range(8, cols - 8, 8):
-        sums = band_conv(window, k_ref, start, rows, 0, False)
-        for row in range(rows):
-            o_ref[row, start - 8 : start, :] = sums[row]
-
-
-def conv_side_kernel(f_ref, m_ref, k_ref, l_ref, r_ref, o_ref, window, wide):
+        band_conv(window, k_ref, o_ref, start, start - 8, 0, False)
+
+
+def conv_side_kernel(f_ref, m_ref, k_ref, l_ref, r_ref, o_ref, window):
     rows, cols, _ = f_ref.shape
-    spread_mask(m_ref, wide)
     window[:, 5:8, :] = l_ref[...].astype(F32)
-    window[:, 8 : 8 + cols, :] = f_ref[...].astype(F32) * wide[...]
+    window[:, 8 : 8 + cols, :] = f_ref[...].astype(F32) * m_ref[...]
     window[:, 8 + cols : 11 + cols, :] = r_ref[...].astype(F32)
     for at, start in ((0, 0), (8, cols - 8)):
-        sums = band_conv(window, k_ref, start, rows, 0, False)
-        for row in range(rows):
-            o_ref[row, at : at + 8, :] = sums[row]
+        band_conv(window, k_ref, o_ref, start, at, 0, False)
 
 
 def by_channels(shape, first=0):
@@ -129,10 +107,7 @@
         ],
         in_specs=[by_channels(fields.shape), whole_spec(mask.shape), by_channels(kernel.shape)],
         out_specs=[by_channels((rows, cols - 16, channels)), by_channels(ends), by_channels(ends)],
-        scratch_shapes=[
-            pltpu.VMEM((rows, cols + 16, LANES), F32),
-            pltpu.VMEM((rows, cols, LANES), F32),
-        ],
+        scratch_shapes=[pltpu.VMEM((rows, cols + 16, LANES), F32)],
         compiler_params=params(56),
         cost_estimate=estimate(4),
         name="conv_inner",
@@ -153,10 +128,7 @@
             by_channels(right.shape),
         ],
         out_specs=by_channels((rows, 16, channels)),
-        scratch_shapes=[
-            pltpu.VMEM((rows, cols + 16, LANES), F32),
-            pltpu.VMEM((rows, cols, LANES), F32),
-        ],
+        scratch_shapes=[pltpu.VMEM((rows, cols + 16, LANES), F32)],
         compiler_params=params(56),
         cost_estimate=estimate(4),
         name="conv_side",
@@ -188,12 +160,14 @@
     wide = channels // LANES
 
     def strips(body):
-        def one(row, _):
-            for at in range(0, cols, strip):
-                body(row, at, pl.ds(pl.multiple_of(row * cols + at, strip), strip))
+        def some(index, _):
+            for more in range(4):
+                row = index * 4 + more
+                for at in range(0, cols, strip):
+                    body(row, at, pl.ds(pl.multiple_of(row * cols + at, strip), strip))
             return 0
 
-        lax.fori_loop(0, rows, one, 0)
+        lax.fori_loop(0, rows // 4, some, 0)
 
     @pl.when(step_now == 0)
     def _():
@@ -233,7 +207,8 @@
             conv[row, at : at + strip, :] = xhat
             inv_s[here, :] = jnp.broadcast_to(inv, (strip, LANES))
             normed[here, :] = (xhat * gain_ref[...] + bias_ref[...]).astype(BF16)
-            grad = mask_column(m_ref, row, at, strip) * (scale_ref[...] * cot_ref[here, :].astype(F32))
+            ocean = jnp.concatenate([m_ref[row, at : at + strip, :]] * wide, axis=1)
+            grad = ocean * (scale_ref[...] * cot_ref[here, :].astype(F32))
             sums_ref[0] += grad[:SUB] + grad[SUB:]
             dbr[here, :] = (0.5 * grad).astype(BF16)
 
@@ -307,7 +282,8 @@
     def _():
         def norm_back(row, at, here):
             cot = cot_ref[here, :].astype(F32)
-            ocean = mask_column(m_ref, row, at, strip) * (0.5 * branch[here, :] + bo_ref[...])
+            ocean = jnp.concatenate([m_ref[row, at : at + strip, :]] * wide, axis=1)
+            ocean = ocean * (0.5 * branch[here, :] + bo_ref[...])
             mixed_ref[here, :] = (f_ref[here, :].astype(F32) + ocean * scale_ref[...]).astype(BF16)
             term = ocean * cot
             sums_ref[1] += term[:SUB] + term[SUB:]
@@ -404,11 +380,10 @@
 
 def filter_grad_kernel(
     f_ref, m_ref, l_ref, r_ref, t_ref, b_ref, d_ref, sums_ref, gbi_0, gbi_1, gbi_2, gbi_3,
-    o_ref, window, grad, wide,
+    o_ref, window, grad,
 ):
     rows, cols, _ = f_ref.shape
-    spread_mask(m_ref, wide)
-    fill_window(window, f_ref[...].astype(F32) * wide[...], l_ref, r_ref, t_ref, b_ref)
+    fill_window(window, f_ref[...].astype(F32) * m_ref[...], l_ref, r_ref, t_ref, b_ref)
     grad[...] = d_ref[...].astype(F32)
     for col_off in range(7):
 
@@ -423,13 +398,15 @@
                 for row_off in range(7):
                     out = src - row_off
                     if 0 <= out < rows:
-                        sums[row_off] = sums[row_off] + held[out] * cells
+                        at = row_off + 7 * (src % 3)
+                        sums[at] = sums[at] + held[out] * cells
             return tuple(sums)
 
-        start = tuple(jnp.zeros((SUB, LANES), F32) for _ in range(7))
+        start = tuple(jnp.zeros((SUB, LANES), F32) for _ in range(21))
         sums = lax.fori_loop(0, cols // 8, band, start)
         for row_off in range(7):
-            o_ref[row_off, col_off : col_off + 1, :] = jnp.sum(sums[row_off], axis=0, keepdims=True)
+            total = sums[row_off] + sums[row_off + 7] + sums[row_off + 14]
+            o_ref[row_off, col_off : col_off + 1, :] = jnp.sum(total, axis=0, keepdims=True)
     for at, source in enumerate((1, 2, 3, 0)):
         o_ref[7, at : at + 1, :] = jnp.sum(sums_ref[source], axis=0, keepdims=True)
     for at, gbi_ref in enumerate((gbi_0, gbi_1, gbi_2, gbi_3)):
@@ -463,7 +440,6 @@
         scratch_shapes=[
             pltpu.VMEM((rows + 6, cols + 16, LANES), F32),
             pltpu.VMEM((rows, cols, LANES), F32),
-            pltpu.VMEM((rows, cols, LANES), F32),
         ],
         compiler_params=params(56),
         cost_estimate=estimate(4),
@@ -471,19 +447,16 @@
     )(fields, mask, left, right, top, bot, d_conv, sums, gbi, gbi, gbi, gbi)
 
 
-def input_grad_kernel(d_ref, l_ref, r_ref, t_ref, b_ref, k_ref, m_ref, cot_ref, o_ref, window, grad, wide):
+def input_grad_kernel(d_ref, l_ref, r_ref, t_ref, b_ref, k_ref, m_ref, cot_ref, o_ref, window, grad):
     rows, cols, _ = d_ref.shape
-    spread_mask(m_ref, wide)
     fill_window(window, d_ref[...].astype(F32), l_ref, r_ref, t_ref, b_ref)
     for start in range(0, cols, 8):
-        sums = band_conv(window, k_ref, start, rows, 3, True)
-        for row in range(rows):
-            grad[row, start : start + 8, :] = sums[row]
-    o_ref[...] = (cot_ref[...].astype(F32) + wide[...] * grad[...]).astype(BF16)
-
-
-def input_grad_more_kernel(d_ref, l_ref, r_ref, t_ref, b_ref, k_ref, m_ref, cot_ref, old_ref, o_ref, window, grad, wide):
-    input_grad_kernel(d_ref, l_ref, r_ref, t_ref, b_ref, k_ref, m_ref, cot_ref, o_ref, window, grad, wide)
+        band_conv(window, k_ref, grad, start, start, 3, True)
+    o_ref[...] = (cot_ref[...].astype(F32) + m_ref[...] * grad[...]).astype(BF16)
+
+
+def input_grad_more_kernel(d_ref, l_ref, r_ref, t_ref, b_ref, k_ref, m_ref, cot_ref, old_ref, o_ref, window, grad):
+    input_grad_kernel(d_ref, l_ref, r_ref, t_ref, b_ref, k_ref, m_ref, cot_ref, o_ref, window, grad)
 
 
 def input_grad(d_conv, left, right, top, bot, kernel, mask, cot, blocks, first, old=None):
@@ -512,7 +485,6 @@
         scratch_shapes=[
             pltpu.VMEM((rows + 6, cols + 16, LANES), F32),
             pltpu.VMEM((rows, cols, LANES), F32),
-            pltpu.VMEM((rows, cols, LANES), F32),
         ],
         input_output_aliases={} if old is None else {8: 0},
         compiler_params=params(56),
@@ -585,11 +557,12 @@
     gain, bias = layer_norm_gain.reshape(1, -1), layer_norm_bias.reshape(1, -1)
     scale = layer_scale.reshape(1, -1)
     cot_rows = cotangent.reshape(cells, channels)
+    mask = jnp.broadcast_to(land_mask.astype(F32)[:, :, None], (rows, cols, LANES))
     ocean = land_mask.astype(BF16)[:, :, None]
     left, right = side_halo(fields[:, cols - 3 :] * ocean[:, cols - 3 :], fields[:, :3] * ocean[:, :3])
-    inner, head, tail = conv_inner(fields, land_mask, kernel)
+    inner, head, tail = conv_inner(fields, mask, kernel)
     top, bot = end_halo(*end_rows(head, tail, left, right))
-    side = conv_side(fields, land_mask, kernel, left, right)
+    side = conv_side(fields, mask, kernel, left, right)
 
     lon = lax.axis_index("lon")
     core, side_y = lon % 2, (lon // 2) % 2
@@ -598,7 +571,7 @@
         [quads + 2 * y + c for c in (1 - core, core) for y in (1 - side_y, side_y)]
     )
     d_conv, mixed, sums, g_bi, sent, kept = expand(
-        order, inner, side, top, bot, kernel, gain, bias, scale, b_out.reshape(1, -1), land_mask, cot_rows,
+        order, inner, side, top, bot, kernel, gain, bias, scale, b_out.reshape(1, -1), mask, cot_rows,
         fields.reshape(cells, channels), w_in, b_in.reshape(1, -1), w_out, n_lon, n_lat,
     )
     got = swap(sent, "lon", 1)
@@ -639,29 +612,29 @@
         return after(small, last) + after(swap(small, *hops[hop]), last)
 
     small = filter_grad(
-        after(fields, d_tail, d_head, far_sums[0]), land_mask, left, right, top, bot, d_conv, sums, g_bi
+        after(fields, d_tail, d_head, far_sums[0]), mask, left, right, top, bot, d_conv, sums, g_bi
     )
     begin(0, small)
     for step in range(len(steps) - 2):
         advance(0, step, small)
-    half = channels // LANES // 2
-    back = (d_left, d_right, d_top, d_bot, kernel, land_mask, cotangent)
-    grad_fields = input_grad(after(d_conv, small, cut[0][1], far_sums[1]), *back, half, 0)
+    quarter = channels // LANES // 4
+    back = (d_left, d_right, d_top, d_bot, kernel, mask, cotangent)
+    grad_fields = input_grad(after(d_conv, small, cut[0][1], far_sums[1]), *back, quarter, 0)
     small = spread(0, grad_fields)
+    grad_fields = input_grad(after(d_conv, small), *back, quarter, quarter, grad_fields)
+    small = spread(1, grad_fields)
     advance(0, len(steps) - 2, grad_fields)
     begin(1, grad_fields)
     for step in range(len(steps) - 2):
         advance(1, step, grad_fields)
     grad_fields = input_grad(
-        after(d_conv, small, cut[0][1], cut[1][1]), *back, half // 2, half, grad_fields
-    )
-    small = spread(1, grad_fields)
+        after(d_conv, small, cut[0][1], cut[1][1]), *back, quarter, 2 * quarter, grad_fields
+    )
+    small = spread(2, grad_fields)
     advance(0, len(steps) - 1, grad_fields)
     advance(1, len(steps) - 2, grad_fields)
-    grad_fields = input_grad(
-        after(d_conv, small, cut[1][1]), *back, half // 2, half + half // 2, grad_fields
-    )
-    for hop in range(2, len(hops)):
+    grad_fields = input_grad(after(d_conv, small, cut[1][1]), *back, quarter, 3 * quarter, grad_fields)
+    for hop in range(3, len(hops)):
         small = spread(hop, grad_fields)
     advance(1, len(steps) - 1, grad_fields)
     grad_w = jnp.concatenate([x[:, 0, 0] for x in owned], axis=1)

time: 147 us -> 132 us (0.90)
  Pallas kernels: 92.6 us -> 75 us
  waiting for transfers between devices: 7.85 us -> 10.7 us
    pallas_call x1, Pallas kernels: 39 us -> 33.2 us  [expand(): pl.pallas_call(expand_kernel, grid_spec=pltpu.PrefetchScalarGridSpec(num_...]
    pallas_call x3 -> x4, Pallas kernels: 22.2 us -> 17.2 us  [input_grad(): pl.pallas_call(input_grad_kernel if old is None else input_grad_more_kern...]
    ppermute x11, waiting for transfers between devices: 3.47 us -> 6.31 us  [swap(): return lax.ppermute(values, axis, [(i, i ^ bit) for i in range(count)])]
    pallas_call x1, Pallas kernels: 8.63 us -> 6.27 us  [conv_inner(): pl.pallas_call(conv_inner_kernel, grid=(channels // LANES,), out_shape=[j...]
    pallas_call x1, Pallas kernels: 8.58 us -> 6.27 us  [conv_side(): pl.pallas_call(conv_side_kernel, grid=(channels // LANES,), out_shape=jax...]
    pallas_call x1, Pallas kernels: 14.2 us -> 12.1 us  [filter_grad(): pl.pallas_call(filter_grad_kernel, grid=(channels // LANES,), out_shape=j...]
    unnamed x23 -> x19, local copies, waits for them, and re-layouts: 4.11 us -> 2.13 us
  transfers between devices with their start and end apart: 19 -> 19, of which waited for: 3 -> 6; matrix products, arithmetic and copies ran while one was open for 5% -> 6% of each run, Pallas kernels for 37% -> 32%
where the time goes in v6:
time: 132 us; the launch traced here: 131 us
  Pallas kernels  75 us (57%)
  starting transfers between devices  30.4 us (23%)
  waiting for transfers between devices  10.7 us (8%)
  other arithmetic  7.66 us (6%)
  local copies, waits for them, and re-layouts  6.73 us (5%)
    pallas_call x1, Pallas kernels, expand(): pl.pallas_call(expand_kernel, grid_spec=pltpu.PrefetchScalarGridSpec(num_...  33.2 us
    pallas_call x4, Pallas kernels, input_grad(): pl.pallas_call(input_grad_kernel if old is None else input_grad_more_kern...  17.2 us
    ppermute x11, starting transfers between devices, swap(): return lax.ppermute(values, axis, [(i, i ^ bit) for i in range(count)])  14.1 us
    pallas_call x1, Pallas kernels, filter_grad(): pl.pallas_call(filter_grad_kernel, grid=(channels // LANES,), out_shape=j...  12.1 us
    ppermute x4, starting transfers between devices, end_halo(): return (lax.ppermute(tail, 'lat', ahead), lax.ppermute(head, 'lat', back))  12 us
    ppermute x11, waiting for transfers between devices, swap(): return lax.ppermute(values, axis, [(i, i ^ bit) for i in range(count)])  6.31 us
    pallas_call x1, Pallas kernels, conv_inner(): pl.pallas_call(conv_inner_kernel, grid=(channels // LANES,), out_shape=[j...  6.27 us
    pallas_call x1, Pallas kernels, conv_side(): pl.pallas_call(conv_side_kernel, grid=(channels // LANES,), out_shape=jax...  6.27 us
  transfers between devices with their start and end apart: 19, of which 6 were waited for; matrix products, arithmetic and copies ran while one was open for 6% of the time, Pallas kernels for 32%

profile of v6, /device:TPU:0, one launch (start us, length us, event | category | flops | bytes accessed | tf_op | source)
XLA Modules:
  0.0 131.5 jit_solution(14896537806520963465)
XLA Ops:
  3.2 2.0 %collective-permute-start.1 = (bf16[32,3,512]{2,1,0:T(4,128)(2,1)S(1)}, bf16[32,3,512]{2,1,0:T(4,128)(2,1)S(1)}, u32[]{:S(2)}, u32[]{:S(2)}) collective-permute-start(bf16[32,3,512]{2,1,0:T(4,128)(2,1)S(1)} %get-tuple-element.98), channel_id=1, source_target_pairs={{4,0},{8,4},{12,8},{0,12},{5,1},{9,5},{13,9},{1,13},{6,2},{10,6},{... | collective-permute-start | bytes 294920 | tf_op jit(solution)/shard_map/ppermute | solution.py:522
  6.3 6.3 %conv_inner.1 = (f32[32,16,512]{2,1,0:T(8,128)}, bf16[3,32,512]{2,1,0:T(8,128)(2,1)}, bf16[3,32,512]{2,1,0:T(8,128)(2,1)}) custom-call(bf16[32,32,512]{2,1,0:T(8,128)(2,1)} %f_ref.4, f32[32,32,128]{2,1,0:T(8,128)} %broadcast_in_dim.4.m_ref, f32[7,7,512]{2,1,0:T(8,128)} %k_ref.13), custom_call_target="tpu_custom_call" | custom-call | flops 4600000000 | bytes 14400000 | tf_op jit(solution)/shard_map/conv_inner/pallas_call | solution.py:100
  14.2 4.2 %collective-permute-start.2 = (bf16[3,38,512]{2,1,0:T(8,128)(2,1)S(1)}, bf16[3,38,512]{2,1,0:T(8,128)(2,1)S(1)}, u32[]{:S(2)}, u32[]{:S(2)}) collective-permute-start(bf16[3,38,512]{2,1,0:T(8,128)(2,1)S(1)} %pad_maximum_fusion.1), channel_id=1, source_target_pairs={{0,1},{1,2},{2,3},{4,5},{5,6},{6,7},{8,9},{9,10},{10,11},{12,13},{... | collective-permute-start | bytes 350216 | tf_op jit(solution)/shard_map/ppermute | solution.py:537
  19.4 1.3 collective-permute-start.3
  20.7 6.3 %conv_side.1.side_ref = f32[32,16,512]{2,1,0:T(8,128)} custom-call(bf16[32,32,512]{2,1,0:T(8,128)(2,1)} %f_ref.4, f32[32,32,128]{2,1,0:T(8,128)} %broadcast_in_dim.4.m_ref, f32[7,7,512]{2,1,0:T(8,128)} %k_ref.13, bf16[32,3,512]{2,1,0:T(4,128)(2,1)} %copy-done.2, bf16[32,3,512]{2,1,0:T(4,128)(2,1)} %copy-done.3), custom_call_target="tpu_custom_call" | custom-call | flops 4600000000 | bytes 14400000 | tf_op jit(solution)/shard_map/conv_side/pallas_call | solution.py:119
  27.7 33.2 %expand.1 = (bf16[1024,512]{1,0:T(8,128)(2,1)}, bf16[1024,512]{1,0:T(8,128)(2,1)}, f32[4,8,512]{2,1,0:T(8,128)}, f32[1,2048]{1,0:T(1,128)}, bf16[2,2,4,512,128]{...) custom-call(s32[4]{0:T(128)} %pad_add_fusion.order_ref, f32[32,16,512]{2,1,0:T(8,128)} %get-tuple-element.46.inner_ref, ...), custom_call_target="tpu_custom_call" | custom-call | flops 23000000512 | bytes 72000000 | tf_op jit(solution)/shard_map/expand/pallas_call | solution.py:323
  62.1 1.6 %collective-permute-start.5 = (bf16[32,3,512]{2,1,0:T(4,128)(2,1)S(1)}, bf16[32,3,512]{2,1,0:T(4,128)(2,1)S(1)}, u32[]{:S(2)}, u32[]{:S(2)}) collective-permute-start(bf16[32,3,512]{2,1,0:T(4,128)(2,1)S(1)} %get-tuple-element.97), channel_id=1, source_target_pairs={{4,0},{8,4},{12,8},{0,12},{5,1},{9,5},{13,9},{1,13},{6,2},{10,6},{... | collective-permute-start | bytes 294920 | tf_op jit(solution)/shard_map/ppermute | solution.py:522
  64.7 1.9 %collective-permute-done.5.r_ref = bf16[32,3,512]{2,1,0:T(4,128)(2,1)S(1)} collective-permute-done((bf16[32,3,512]{2,1,0:T(4,128)(2,1)S(1)}, bf16[32,3,512]{2,1,0:T(4,128)(2,1)S(1)}, u32[]{:S(2)}, u32[]{:S(2)}) %collective-permute-start.5) | collective-permute-done | bytes 98336 | tf_op jit(solution)/shard_map/ppermute | solution.py:522
  66.7 2.4 %collective-permute-done.4.l_ref = bf16[32,3,512]{2,1,0:T(4,128)(2,1)S(1)} collective-permute-done((bf16[32,3,512]{2,1,0:T(4,128)(2,1)S(1)}, bf16[32,3,512]{2,1,0:T(4,128)(2,1)S(1)}, u32[]{:S(2)}, u32[]{:S(2)}) %collective-permute-start.4) | collective-permute-done | bytes 98336 | tf_op jit(solution)/shard_map/ppermute | solution.py:522
  69.2 5.2 %collective-permute-start.8 = (bf16[3,38,512]{2,1,0:T(8,128)(2,1)S(1)}, bf16[3,38,512]{2,1,0:T(8,128)(2,1)}, u32[]{:S(2)}, u32[]{:S(2)}) collective-permute-start(bf16[3,38,512]{2,1,0:T(8,128)(2,1)S(1)} %pad_maximum_fusion.3), channel_id=1, source_target_pairs={{0,1},{1,2},{2,3},{4,5},{5,6},{6,7},{8,9},{9,10},{10,11},{12,13},{... | collective-permute-start | bytes 350216 | tf_op jit(solution)/shard_map/ppermute | solution.py:537
  74.4 1.3 collective-permute-start.9
  75.8 1.3 add_convert_fusion
  78.1 12.1 %filter_grad.1 = f32[8,8,512]{2,1,0:T(8,128)} custom-call(bf16[32,32,512]{2,1,0:T(8,128)(2,1)} %f_ref.4, f32[32,32,128]{2,1,0:T(8,128)} %broadcast_in_dim.4.m_ref, bf16[32,3,512]{2,1,0:T(4,128)(2,1)} %copy-done.2, bf16[32,3,512]{2,1,0:T(4,128)(2,1)} %copy-done.3, bf16[3,38,512]{2,1,0:T(8,128)(2,1)} %copy-done.6, bf16[3,38,512]{2,1,0:T(8,128)(2,1)} %copy-done.7, ...), custom_call_target="tpu_custom_call" | custom-call | flops 4600000000 | bytes 14400000 | tf_op jit(solution)/shard_map/filter_grad/pallas_call | solution.py:424
  92.4 2.4 %collective-permute-start.12 = (bf16[2,1,2,320,128]{4,3,0,2,1:T(8,128)(2,1)S(1)}, bf16[2,1,2,320,128]{4,3,0,2,1:T(8,128)(2,1)S(1)}, u32[]{:S(2)}, u32[]{:S(2)}) collective-permute-start(bf16[2,1,2,320,128]{4,3,0,2,1:T(8,128)(2,1)S(1)} %fusion), channel_id=1, source_target_pairs={{0,1},{1,0},{2,3},{3,2},{4,5},{5,4},{6,7},{7,6},{8,9},{9,8},{10,11... | collective-permute-start | bytes 983048 | tf_op jit(solution)/shard_map/ppermute | solution.py:498
  94.9 4.3 %input_grad.4.old_ref = bf16[32,32,512]{2,1,0:T(8,128)(2,1)} custom-call(bf16[32,32,512]{2,1,0:T(8,128)(2,1)} %bitcast.66, bf16[32,3,512]{2,1,0:T(4,128)(2,1)} %copy-done.5, bf16[32,3,512]{2,1,0:T(4,128)(2,1)} %copy-done.4, bf16[3,38,512]{2,1,0:T(8,128)(2,1)} %collective-permute-done.8.t_ref, bf16[3,38,512]{2,1,0:T(8,128)(2,1)} %collective-permute-done.9.b_ref, ...), custom_call_target="tpu_custom_call" | custom-call | flops 4600000000 | bytes 14400000 | tf_op jit(solution)/shard_map/input_grad/pallas_call | solution.py:469
  99.2 1.7 %collective-permute-start.11 = (f32[8,8,512]{2,1,0:T(8,128)S(1)}, f32[8,8,512]{2,1,0:T(8,128)S(1)}, u32[]{:S(2)}, u32[]{:S(2)}) collective-permute-start(f32[8,8,512]{2,1,0:T(8,128)S(1)} %add.107), channel_id=1, source_target_pairs={{0,8},{4,12},{8,0},{12,4},{1,9},{5,13},{9,1},{13,5},{2,10},{6,14},... | collective-permute-start | bytes 393224 | tf_op jit(solution)/shard_map/ppermute | solution.py:498
  100.9 4.3 %input_grad.5.old_ref = bf16[32,32,512]{2,1,0:T(8,128)(2,1)} custom-call(bf16[32,32,512]{2,1,0:T(8,128)(2,1)} %bitcast.67, bf16[32,3,512]{2,1,0:T(4,128)(2,1)} %copy-done.5, bf16[32,3,512]{2,1,0:T(4,128)(2,1)} %copy-done.4, bf16[3,38,512]{2,1,0:T(8,128)(2,1)} %collective-permute-done.8.t_ref, ...), custom_call_target="tpu_custom_call", output_to_operand_aliasing={{}: (8, {})} | custom-call | flops 4600000000 | bytes 14400000 | tf_op jit(solution)/shard_map/input_grad/pallas_call | solution.py:469
  105.7 2.1 %collective-permute-start.14 = (f32[8,8,512]{2,1,0:T(8,128)S(1)}, f32[8,8,512]{2,1,0:T(8,128)S(1)}, u32[]{:S(2)}, u32[]{:S(2)}) collective-permute-start(f32[8,8,512]{2,1,0:T(8,128)S(1)} %add.108), channel_id=1, source_target_pairs={{0,1},{1,0},{2,3},{3,2},{4,5},{5,4},{6,7},{7,6},{8,9},{9,8},{10,11... | collective-permute-start | bytes 393224 | tf_op jit(solution)/shard_map/ppermute | solution.py:498
  107.9 2.6 %collective-permute-start.17 = (bf16[2,1,1,320,128]{4,3,0,2,1:T(8,128)(2,1)S(1)}, bf16[2,1,1,320,128]{4,3,0,2,1:T(8,128)(2,1)S(1)}, u32[]{:S(2)}, u32[]{:S(2)}) collective-permute-start(bf16[2,1,1,320,128]{4,3,0,2,1:T(8,128)(2,1)S(1)} %fusion.5), channel_id=1, source_target_pairs={{0,2},{1,3},{2,0},{3,1},{4,6},{5,7},{6,4},{7,5},{8,10},{9,11},{10,... | collective-permute-start | bytes 491528 | tf_op jit(solution)/shard_map/ppermute | solution.py:498
  110.5 4.3 %input_grad.6.old_ref = bf16[32,32,512]{2,1,0:T(8,128)(2,1)} custom-call(bf16[32,32,512]{2,1,0:T(8,128)(2,1)} %bitcast.68, bf16[32,3,512]{2,1,0:T(4,128)(2,1)} %copy-done.5, bf16[32,3,512]{2,1,0:T(4,128)(2,1)} %copy-done.4, bf16[3,38,512]{2,1,0:T(8,128)(2,1)} %collective-permute-done.8.t_ref, ...), custom_call_target="tpu_custom_call", output_to_operand_aliasing={{}: (8, {})} | custom-call | flops 4600000000 | bytes 14400000 | tf_op jit(solution)/shard_map/input_grad/pallas_call | solution.py:469
  114.8 2.6 %collective-permute-done.14 = f32[8,8,512]{2,1,0:T(8,128)S(1)} collective-permute-done((f32[8,8,512]{2,1,0:T(8,128)S(1)}, f32[8,8,512]{2,1,0:T(8,128)S(1)}, u32[]{:S(2)}, u32[]{:S(2)}) %collective-permute-start.14) | collective-permute-done | bytes 131104 | tf_op jit(solution)/shard_map/ppermute | solution.py:498
  118.5 2.1 %collective-permute-start.18 = (bf16[2,1,1,192,128]{4,3,0,2,1:T(8,128)(2,1)S(1)}, bf16[2,1,1,192,128]{4,3,0,2,1:T(8,128)(2,1)S(1)}, u32[]{:S(2)}, u32[]{:S(2)}) collective-permute-start(bf16[2,1,1,192,128]{4,3,0,2,1:T(8,128)(2,1)S(1)} %fusion.6), channel_id=1, source_target_pairs={{0,2},{1,3},{2,0},{3,1},{4,6},{5,7},{6,4},{7,5},{8,10},{9,11},{10,... | collective-permute-start | bytes 294920 | tf_op jit(solution)/shard_map/ppermute | solution.py:498
  120.6 4.3 %input_grad.7 = bf16[32,32,512]{2,1,0:T(8,128)(2,1)} custom-call(bf16[32,32,512]{2,1,0:T(8,128)(2,1)} %bitcast.69, bf16[32,3,512]{2,1,0:T(4,128)(2,1)} %copy-done.5, bf16[32,3,512]{2,1,0:T(4,128)(2,1)} %copy-done.4, bf16[3,38,512]{2,1,0:T(8,128)(2,1)} %collective-permute-done.8.t_ref, ...), custom_call_target="tpu_custom_call", output_to_operand_aliasing={{}: (8, {})} | custom-call | flops 4600000000 | bytes 14400000 | tf_op jit(solution)/shard_map/input_grad/pallas_call | solution.py:469
  124.9 2.4 %collective-permute-done.16 = f32[8,8,512]{2,1,0:T(8,128)S(1)} collective-permute-done((f32[8,8,512]{2,1,0:T(8,128)S(1)}, f32[8,8,512]{2,1,0:T(8,128)S(1)}, u32[]{:S(2)}, u32[]{:S(2)}) %collective-permute-start.16) | collective-permute-done | bytes 131104 | tf_op jit(solution)/shard_map/ppermute | solution.py:498
  (81 shorter events, 18.2 us)
Async XLA Ops:
  2.7 10.4 %collective-permute-start = (bf16[32,3,512]{2,1,0:T(4,128)(2,1)S(1)}, bf16[32,3,512]{2,1,0:T(4,128)(2,1)S(1)}, u32[]{:S(2)}, u32[]{:S(2)}) collective-permute-start(bf16[32,3,512]{2,1,0:T(4,128)(2,1)S(1)} %get-tuple-element.99), channel_id=1, source_target_pairs={{0,4},{4,8},{8,12},{12,0},{1,5},{5,9},{9,13},{13,1},{2,6},{6,10},{... | collective-permute-start | bytes 294920 | tf_op jit(solution)/shard_map/ppermute | solution.py:522
  3.2 9.9 %collective-permute-start.1 = (bf16[32,3,512]{2,1,0:T(4,128)(2,1)S(1)}, bf16[32,3,512]{2,1,0:T(4,128)(2,1)S(1)}, u32[]{:S(2)}, u32[]{:S(2)}) collective-permute-start(bf16[32,3,512]{2,1,0:T(4,128)(2,1)S(1)} %get-tuple-element.98), channel_id=1, source_target_pairs={{4,0},{8,4},{12,8},{0,12},{5,1},{9,5},{13,9},{1,13},{6,2},{10,6},{... | collective-permute-start | bytes 294920 | tf_op jit(solution)/shard_map/ppermute | solution.py:522
  13.2 7.5 %copy-start.3 = (bf16[32,3,512]{2,1,0:T(4,128)(2,1)}, bf16[32,3,512]{2,1,0:T(4,128)(2,1)S(1)}, u32[]{:S(2)}) copy-start(bf16[32,3,512]{2,1,0:T(4,128)(2,1)S(1)} %collective-permute-done.1.r_ref) | copy-start | bytes 294916
  13.2 7.5 %copy-start.2 = (bf16[32,3,512]{2,1,0:T(4,128)(2,1)}, bf16[32,3,512]{2,1,0:T(4,128)(2,1)S(1)}, u32[]{:S(2)}) copy-start(bf16[32,3,512]{2,1,0:T(4,128)(2,1)S(1)} %collective-permute-done.l_ref) | copy-start | bytes 294916
  14.2 12.8 %collective-permute-start.2 = (bf16[3,38,512]{2,1,0:T(8,128)(2,1)S(1)}, bf16[3,38,512]{2,1,0:T(8,128)(2,1)S(1)}, u32[]{:S(2)}, u32[]{:S(2)}) collective-permute-start(bf16[3,38,512]{2,1,0:T(8,128)(2,1)S(1)} %pad_maximum_fusion.1), channel_id=1, source_target_pairs={{0,1},{1,2},{2,3},{4,5},{5,6},{6,7},{8,9},{9,10},{10,11},{12,13},{... | collective-permute-start | bytes 350216 | tf_op jit(solution)/shard_map/ppermute | solution.py:537
  19.4 7.6 %collective-permute-start.3 = (bf16[3,38,512]{2,1,0:T(8,128)(2,1)S(1)}, bf16[3,38,512]{2,1,0:T(8,128)(2,1)S(1)}, u32[]{:S(2)}, u32[]{:S(2)}) collective-permute-start(bf16[3,38,512]{2,1,0:T(8,128)(2,1)S(1)} %pad_maximum_fusion.2), channel_id=1, source_target_pairs={{1,0},{2,1},{3,2},{5,4},{6,5},{7,6},{9,8},{10,9},{11,10},{13,12},{... | collective-permute-start | bytes 350216 | tf_op jit(solution)/shard_map/ppermute | solution.py:537
  60.8 14.9 %collective-permute-start.6 = (bf16[2,2,4,512,128]{4,3,2,1,0:T(8,128)(2,1)}, bf16[2,2,4,512,128]{4,3,2,1,0:T(8,128)(2,1)S(1)}, u32[]{:S(2)}, u32[]{:S(2)}) collective-permute-start(bf16[2,2,4,512,128]{4,3,2,1,0:T(8,128)(2,1)} %get-tuple-element.52), channel_id=1, source_target_pairs={{0,4},{4,0},{8,12},{12,8},{1,5},{5,1},{9,13},{13,9},{2,6},{6,2},{1... | collective-permute-start | bytes 6291464 | tf_op jit(solution)/shard_map/ppermute | solution.py:498
  62.1 4.6 %collective-permute-start.5 = (bf16[32,3,512]{2,1,0:T(4,128)(2,1)S(1)}, bf16[32,3,512]{2,1,0:T(4,128)(2,1)S(1)}, u32[]{:S(2)}, u32[]{:S(2)}) collective-permute-start(bf16[32,3,512]{2,1,0:T(4,128)(2,1)S(1)} %get-tuple-element.97), channel_id=1, source_target_pairs={{4,0},{8,4},{12,8},{0,12},{5,1},{9,5},{13,9},{1,13},{6,2},{10,6},{... | collective-permute-start | bytes 294920 | tf_op jit(solution)/shard_map/ppermute | solution.py:522
  64.7 4.4 %collective-permute-start.4 = (bf16[32,3,512]{2,1,0:T(4,128)(2,1)S(1)}, bf16[32,3,512]{2,1,0:T(4,128)(2,1)S(1)}, u32[]{:S(2)}, u32[]{:S(2)}) collective-permute-start(bf16[32,3,512]{2,1,0:T(4,128)(2,1)S(1)} %get-tuple-element.96), channel_id=1, source_target_pairs={{0,4},{4,8},{8,12},{12,0},{1,5},{5,9},{9,13},{13,1},{2,6},{6,10},{... | collective-permute-start | bytes 294920 | tf_op jit(solution)/shard_map/ppermute | solution.py:522
  66.7 23.5 %copy-start.4 = (bf16[32,3,512]{2,1,0:T(4,128)(2,1)}, bf16[32,3,512]{2,1,0:T(4,128)(2,1)S(1)}, u32[]{:S(2)}) copy-start(bf16[32,3,512]{2,1,0:T(4,128)(2,1)S(1)} %collective-permute-done.5.r_ref) | copy-start | bytes 294916
  69.1 21.0 %copy-start.5 = (bf16[32,3,512]{2,1,0:T(4,128)(2,1)}, bf16[32,3,512]{2,1,0:T(4,128)(2,1)S(1)}, u32[]{:S(2)}) copy-start(bf16[32,3,512]{2,1,0:T(4,128)(2,1)S(1)} %collective-permute-done.4.l_ref) | copy-start | bytes 294916
  69.2 25.7 %collective-permute-start.8 = (bf16[3,38,512]{2,1,0:T(8,128)(2,1)S(1)}, bf16[3,38,512]{2,1,0:T(8,128)(2,1)}, u32[]{:S(2)}, u32[]{:S(2)}) collective-permute-start(bf16[3,38,512]{2,1,0:T(8,128)(2,1)S(1)} %pad_maximum_fusion.3), channel_id=1, source_target_pairs={{0,1},{1,2},{2,3},{4,5},{5,6},{6,7},{8,9},{9,10},{10,11},{12,13},{... | collective-permute-start | bytes 350216 | tf_op jit(solution)/shard_map/ppermute | solution.py:537
  74.4 20.4 %collective-permute-start.9 = (bf16[3,38,512]{2,1,0:T(8,128)(2,1)S(1)}, bf16[3,38,512]{2,1,0:T(8,128)(2,1)}, u32[]{:S(2)}, u32[]{:S(2)}) collective-permute-start(bf16[3,38,512]{2,1,0:T(8,128)(2,1)S(1)} %pad_maximum_fusion.4), channel_id=1, source_target_pairs={{1,0},{2,1},{3,2},{5,4},{6,5},{7,6},{9,8},{10,9},{11,10},{13,12},{... | collective-permute-start | bytes 350216 | tf_op jit(solution)/shard_map/ppermute | solution.py:537
  77.0 15.0 %collective-permute-start.7 = (bf16[2,1,4,320,128]{4,3,2,1,0:T(8,128)(2,1)S(1)}, bf16[2,1,4,320,128]{4,3,2,1,0:T(8,128)(2,1)S(1)}, u32[]{:S(2)}, u32[]{:S(2)}) collective-permute-start(bf16[2,1,4,320,128]{4,3,2,1,0:T(8,128)(2,1)S(1)} %add_convert_fusion), channel_id=1, source_target_pairs={{0,8},{4,12},{8,0},{12,4},{1,9},{5,13},{9,1},{13,5},{2,10},{6,14},... | collective-permute-start | bytes 1966088 | tf_op jit(solution)/shard_map/ppermute | solution.py:498
  78.1 12.2 %copy-start = (bf16[2,2,4,512,128]{4,3,2,1,0:T(8,128)(2,1)S(1)}, bf16[2,2,4,512,128]{4,3,2,1,0:T(8,128)(2,1)}, u32[]{:S(2)}) copy-start(bf16[2,2,4,512,128]{4,3,2,1,0:T(8,128)(2,1)} %get-tuple-element.67) | copy-start | bytes 6291460
  90.1 9.1 %collective-permute-start.10 = (f32[8,8,512]{2,1,0:T(8,128)}, f32[8,8,512]{2,1,0:T(8,128)S(1)}, u32[]{:S(2)}, u32[]{:S(2)}) collective-permute-start(f32[8,8,512]{2,1,0:T(8,128)} %filter_grad.1), channel_id=1, source_target_pairs={{0,4},{4,0},{8,12},{12,8},{1,5},{5,1},{9,13},{13,9},{2,6},{6,2},{1... | collective-permute-start | bytes 393224 | tf_op jit(solution)/shard_map/ppermute | solution.py:498
  90.3 14.9 %collective-permute-start.13 = (bf16[2,1,4,192,128]{4,3,2,1,0:T(8,128)(2,1)S(1)}, bf16[2,1,4,192,128]{4,3,2,1,0:T(8,128)(2,1)S(1)}, u32[]{:S(2)}, u32[]{:S(2)}) collective-permute-start(bf16[2,1,4,192,128]{4,3,2,1,0:T(8,128)(2,1)S(1)} %add_convert_fusion.1), channel_id=1, source_target_pairs={{0,8},{4,12},{8,0},{12,4},{1,9},{5,13},{9,1},{13,5},{2,10},{6,14},... | collective-permute-start | bytes 1179656 | tf_op jit(solution)/shard_map/ppermute | solution.py:498
  92.4 15.3 %collective-permute-start.12 = (bf16[2,1,2,320,128]{4,3,0,2,1:T(8,128)(2,1)S(1)}, bf16[2,1,2,320,128]{4,3,0,2,1:T(8,128)(2,1)S(1)}, u32[]{:S(2)}, u32[]{:S(2)}) collective-permute-start(bf16[2,1,2,320,128]{4,3,0,2,1:T(8,128)(2,1)S(1)} %fusion), channel_id=1, source_target_pairs={{0,1},{1,0},{2,3},{3,2},{4,5},{5,4},{6,7},{7,6},{8,9},{9,8},{10,11... | collective-permute-start | bytes 983048 | tf_op jit(solution)/shard_map/ppermute | solution.py:498
  99.2 6.5 %collective-permute-start.11 = (f32[8,8,512]{2,1,0:T(8,128)S(1)}, f32[8,8,512]{2,1,0:T(8,128)S(1)}, u32[]{:S(2)}, u32[]{:S(2)}) collective-permute-start(f32[8,8,512]{2,1,0:T(8,128)S(1)} %add.107), channel_id=1, source_target_pairs={{0,8},{4,12},{8,0},{12,4},{1,9},{5,13},{9,1},{13,5},{2,10},{6,14},... | collective-permute-start | bytes 393224 | tf_op jit(solution)/shard_map/ppermute | solution.py:498
  105.5 11.9 %collective-permute-start.15 = (bf16[2,1,2,192,128]{4,3,0,2,1:T(8,128)(2,1)S(1)}, bf16[2,1,2,192,128]{4,3,0,2,1:T(8,128)(2,1)S(1)}, u32[]{:S(2)}, u32[]{:S(2)}) collective-permute-start(bf16[2,1,2,192,128]{4,3,0,2,1:T(8,128)(2,1)S(1)} %fusion.4), channel_id=1, source_target_pairs={{0,1},{1,0},{2,3},{3,2},{4,5},{5,4},{6,7},{7,6},{8,9},{9,8},{10,11... | collective-permute-start | bytes 589832 | tf_op jit(solution)/shard_map/ppermute | solution.py:498
  105.7 11.7 %collective-permute-start.14 = (f32[8,8,512]{2,1,0:T(8,128)S(1)}, f32[8,8,512]{2,1,0:T(8,128)S(1)}, u32[]{:S(2)}, u32[]{:S(2)}) collective-permute-start(f32[8,8,512]{2,1,0:T(8,128)S(1)} %add.108), channel_id=1, source_target_pairs={{0,1},{1,0},{2,3},{3,2},{4,5},{5,4},{6,7},{7,6},{8,9},{9,8},{10,11... | collective-permute-start | bytes 393224 | tf_op jit(solution)/shard_map/ppermute | solution.py:498
  107.9 12.7 %collective-permute-start.17 = (bf16[2,1,1,320,128]{4,3,0,2,1:T(8,128)(2,1)S(1)}, bf16[2,1,1,320,128]{4,3,0,2,1:T(8,128)(2,1)S(1)}, u32[]{:S(2)}, u32[]{:S(2)}) collective-permute-start(bf16[2,1,1,320,128]{4,3,0,2,1:T(8,128)(2,1)S(1)} %fusion.5), channel_id=1, source_target_pairs={{0,2},{1,3},{2,0},{3,1},{4,6},{5,7},{6,4},{7,5},{8,10},{9,11},{10,... | collective-permute-start | bytes 491528 | tf_op jit(solution)/shard_map/ppermute | solution.py:498
  117.6 9.8 %collective-permute-start.16 = (f32[8,8,512]{2,1,0:T(8,128)S(1)}, f32[8,8,512]{2,1,0:T(8,128)S(1)}, u32[]{:S(2)}, u32[]{:S(2)}) collective-permute-start(f32[8,8,512]{2,1,0:T(8,128)S(1)} %add.113), channel_id=1, source_target_pairs={{0,2},{1,3},{2,0},{3,1},{4,6},{5,7},{6,4},{7,5},{8,10},{9,11},{10,... | collective-permute-start | bytes 393224 | tf_op jit(solution)/shard_map/ppermute | solution.py:498
  118.5 10.8 %collective-permute-start.18 = (bf16[2,1,1,192,128]{4,3,0,2,1:T(8,128)(2,1)S(1)}, bf16[2,1,1,192,128]{4,3,0,2,1:T(8,128)(2,1)S(1)}, u32[]{:S(2)}, u32[]{:S(2)}) collective-permute-start(bf16[2,1,1,192,128]{4,3,0,2,1:T(8,128)(2,1)S(1)} %fusion.6), channel_id=1, source_target_pairs={{0,2},{1,3},{2,0},{3,1},{4,6},{5,7},{6,4},{7,5},{8,10},{9,11},{10,... | collective-permute-start | bytes 294920 | tf_op jit(solution)/shard_map/ppermute | solution.py:498
  (3 other events, 8.1 us)

commit v7 on v6

--- a/solution.py
+++ b/solution.py
@@ -38,60 +38,69 @@
 
 
 def shifted(window, row, start, offset):
-    if offset % SUB == 0:
-        return window[row, pl.ds(start + offset, SUB), :]
-    base = start + offset // SUB * SUB
-    pair = window[row, pl.ds(base, 2 * SUB), :]
-    return pltpu.roll(pair, 2 * SUB - offset % SUB, axis=0)[:SUB]
-
-
-def tap_rows(k_ref, col_off, flip):
-    at = 6 - col_off if flip else col_off
-    rows = [k_ref[6 - p if flip else p, at : at + 1, :] for p in range(7)]
-    return [jnp.broadcast_to(row, (SUB, LANES)) for row in rows]
-
-
-def band_conv(window, k_ref, o_ref, start, into, pad, flip):
-    rows = o_ref.shape[0]
-    bound = window.shape[0]
-    part = 16
-    for top in range(0, rows, part):
-        sums = {}
-        for col_off in range(7):
-            weights = tap_rows(k_ref, col_off, flip)
-            sources = range(max(0, top + pad - 3), min(bound, top + pad + part + 3))
-            cells = {src: shifted(window, src, start, 5 + col_off) for src in sources}
-            for row_off in range(7):
-                for out in range(top, top + part):
-                    src = out + pad + row_off - 3
-                    if src in cells:
-                        term = weights[row_off] * cells[src]
-                        sums[out] = sums[out] + term if out in sums else term
-        for out in range(top, top + part):
-            o_ref[out, into : into + SUB, :] = sums[out]
+    return window[row, pl.ds(start + offset, SUB), :]
+
+
+def lane_block(index):
+    return pl.ds(pl.multiple_of(index * LANES, LANES), LANES)
+
+
+def each_lane_block(channels, body):
+    def one(index, _):
+        body(lane_block(index))
+        return 0
+
+    lax.fori_loop(0, channels // LANES, one, 0)
+
+
+def band_conv(window, k_ref, lanes, starts, rows, pad, flip):
+    sums = {}
+    for col_off in range(7):
+        at = 6 - col_off if flip else col_off
+        weights = [k_ref[6 - p if flip else p, at : at + 1, lanes] for p in range(7)]
+        for start in starts:
+            for src in range(window.shape[0]):
+                hits = [(src - pad - row_off + 3, row_off) for row_off in range(7)]
+                hits = [(out, row_off) for out, row_off in hits if 0 <= out < rows]
+                if not hits:
+                    continue
+                cells = shifted(window, src, start, 5 + col_off)
+                for out, row_off in hits:
+                    term = weights[row_off] * cells
+                    key = (out, start)
+                    sums[key] = sums[key] + term if key in sums else term
+    return sums
 
 
 def conv_inner_kernel(f_ref, m_ref, k_ref, o_ref, head_ref, tail_ref, window):
-    rows, cols, _ = f_ref.shape
-    masked = f_ref[...].astype(F32) * m_ref[...]
-    window[:, 8 : 8 + cols, :] = masked
-    head_ref[...] = masked[:3].astype(BF16)
-    tail_ref[...] = masked[rows - 3 :].astype(BF16)
-    for start in range(8, cols - 8, 8):
-        band_conv(window, k_ref, o_ref, start, start - 8, 0, False)
+    rows, cols, channels = f_ref.shape
+
+    def block(lanes):
+        masked = f_ref[:, :, lanes].astype(F32) * m_ref[...]
+        window[:, 8 : 8 + cols, :] = masked
+        head_ref[:, :, lanes] = masked[:3].astype(BF16)
+        tail_ref[:, :, lanes] = masked[rows - 3 :].astype(BF16)
+        for start in range(8, cols - 8, 8):
+            sums = band_conv(window, k_ref, lanes, (start,), rows, 0, False)
+            for row in range(rows):
+                o_ref[row, start - 8 : start, lanes] = sums[row, start]
+
+    each_lane_block(channels, block)
 
 
 def conv_side_kernel(f_ref, m_ref, k_ref, l_ref, r_ref, o_ref, window):
-    rows, cols, _ = f_ref.shape
-    window[:, 5:8, :] = l_ref[...].astype(F32)
-    window[:, 8 : 8 + cols, :] = f_ref[...].astype(F32) * m_ref[...]
-    window[:, 8 + cols : 11 + cols, :] = r_ref[...].astype(F32)
-    for at, start in ((0, 0), (8, cols - 8)):
-        band_conv(window, k_ref, o_ref, start, at, 0, False)
-
-
-def by_channels(shape, first=0):
-    return pl.BlockSpec(shape[:-1] + (LANES,), lambda c: (0,) * (len(shape) - 1) + (c + first,))
+    rows, cols, channels = f_ref.shape
+
+    def block(lanes):
+        window[:, 5:8, :] = l_ref[:, :, lanes].astype(F32)
+        window[:, 8 : 8 + cols, :] = f_ref[:, :, lanes].astype(F32) * m_ref[...]
+        window[:, 8 + cols : 11 + cols, :] = r_ref[:, :, lanes].astype(F32)
+        for at, start in ((0, 0), (8, cols - 8)):
+            sums = band_conv(window, k_ref, lanes, (start,), rows, 0, False)
+            for row in range(rows):
+                o_ref[row, at : at + 8, lanes] = sums[row, start]
+
+    each_lane_block(channels, block)
 
 
 def conv_inner(fields, mask, kernel):
@@ -99,14 +108,11 @@
     ends = (3, cols, channels)
     return pl.pallas_call(
         conv_inner_kernel,
-        grid=(channels // LANES,),
         out_shape=[
             jax.ShapeDtypeStruct((rows, cols - 16, channels), F32),
             jax.ShapeDtypeStruct(ends, BF16),
             jax.ShapeDtypeStruct(ends, BF16),
         ],
-        in_specs=[by_channels(fields.shape), whole_spec(mask.shape), by_channels(kernel.shape)],
-        out_specs=[by_channels((rows, cols - 16, channels)), by_channels(ends), by_channels(ends)],
         scratch_shapes=[pltpu.VMEM((rows, cols + 16, LANES), F32)],
         compiler_params=params(56),
         cost_estimate=estimate(4),
@@ -118,16 +124,7 @@
     rows, cols, channels = fields.shape
     return pl.pallas_call(
         conv_side_kernel,
-        grid=(channels // LANES,),
         out_shape=jax.ShapeDtypeStruct((rows, 16, channels), F32),
-        in_specs=[
-            by_channels(fields.shape),
-            whole_spec(mask.shape),
-            by_channels(kernel.shape),
-            by_channels(left.shape),
-            by_channels(right.shape),
-        ],
-        out_specs=by_channels((rows, 16, channels)),
         scratch_shapes=[pltpu.VMEM((rows, cols + 16, LANES), F32)],
         compiler_params=params(56),
         cost_estimate=estimate(4),
@@ -196,6 +193,8 @@
                 for out in outs:
                     conv[out, start : start + 8, lanes] = sums[out]
         sums_ref[...] = jnp.zeros_like(sums_ref)
+        branch[...] = jnp.zeros_like(branch)
+        d_normed[...] = jnp.zeros_like(d_normed)
 
         def standardize(row, at, here):
             x = conv[row, at : at + strip, :]
@@ -230,14 +229,10 @@
             dbr[here, :], wo_ref[...], (((1,), (1,)), ((), ())), preferred_element_type=F32
         )
 
-    first_block = step_now == 0
-
     def project(index):
         here = slice(index * part, (index + 1) * part)
-        branch[here, :] = jnp.where(first_block, 0.0, branch[here, :]) + jnp.dot(
-            act[here, :], wo_ref[...], preferred_element_type=F32
-        )
-        d_normed[here, :] = jnp.where(first_block, 0.0, d_normed[here, :]) + lax.dot_general(
+        branch[here, :] += jnp.dot(act[here, :], wo_ref[...], preferred_element_type=F32)
+        d_normed[here, :] += lax.dot_general(
             dpre[here, :], wi_ref[...], (((1,), (1,)), ((), ())), preferred_element_type=F32
         )
 
@@ -369,74 +364,57 @@
     )(order, *given, w_in, b_in, w_out)
 
 
-def fill_window(window, center, left, right, top, bot):
-    rows, cols, _ = center.shape
-    window[3 : 3 + rows, 5:8, :] = left[...].astype(F32)
-    window[3 : 3 + rows, 8 : 8 + cols, :] = center
-    window[3 : 3 + rows, 8 + cols : 11 + cols, :] = right[...].astype(F32)
-    window[0:3, 5 : 11 + cols, :] = top[...].astype(F32)
-    window[3 + rows : 6 + rows, 5 : 11 + cols, :] = bot[...].astype(F32)
-
-
 def filter_grad_kernel(
-    f_ref, m_ref, l_ref, r_ref, t_ref, b_ref, d_ref, sums_ref, gbi_0, gbi_1, gbi_2, gbi_3,
-    o_ref, window, grad,
+    f_ref, m_ref, l_ref, r_ref, t_ref, b_ref, d_ref, sums_ref, gbi_ref, o_ref, window, grad
 ):
-    rows, cols, _ = f_ref.shape
-    fill_window(window, f_ref[...].astype(F32) * m_ref[...], l_ref, r_ref, t_ref, b_ref)
-    grad[...] = d_ref[...].astype(F32)
-    for col_off in range(7):
-
-        def band(index, sums):
-            start = pl.multiple_of(index * 8, 8)
-            sums = list(sums)
-            held = {}
-            for src in range(rows + 6):
-                if src < rows:
-                    held[src] = grad[src, pl.ds(start, SUB), :]
-                cells = shifted(window, src, start, 5 + col_off)
-                for row_off in range(7):
-                    out = src - row_off
-                    if 0 <= out < rows:
-                        at = row_off + 7 * (src % 3)
-                        sums[at] = sums[at] + held[out] * cells
-            return tuple(sums)
-
-        start = tuple(jnp.zeros((SUB, LANES), F32) for _ in range(21))
-        sums = lax.fori_loop(0, cols // 8, band, start)
+    rows, cols, channels = f_ref.shape
+    blocks = channels // LANES
+
+    def block(index, _):
+        lanes = lane_block(index)
+        window[0:3, 5 : 11 + cols, :] = t_ref[:, :, lanes].astype(F32)
+        window[3 : 3 + rows, 5:8, :] = l_ref[:, :, lanes].astype(F32)
+        window[3 : 3 + rows, 8 : 8 + cols, :] = f_ref[:, :, lanes].astype(F32) * m_ref[...]
+        window[3 : 3 + rows, 8 + cols : 11 + cols, :] = r_ref[:, :, lanes].astype(F32)
+        window[3 + rows : 6 + rows, 5 : 11 + cols, :] = b_ref[:, :, lanes].astype(F32)
+        grad[...] = d_ref[:, :, lanes].astype(F32)
+        for col_off in range(7):
+
+            def band(step, sums):
+                start = pl.multiple_of(step * SUB, SUB)
+                sums = list(sums)
+                held = {}
+                for src in range(rows + 6):
+                    if src < rows:
+                        held[src] = grad[src, pl.ds(start, SUB), :]
+                    cells = shifted(window, src, start, 5 + col_off)
+                    for row_off in range(7):
+                        out = src - row_off
+                        if 0 <= out < rows:
+                            sums[row_off] = sums[row_off] + held[out] * cells
+                return tuple(sums)
+
+            sums = tuple(jnp.zeros((SUB, LANES), F32) for _ in range(7))
+            sums = lax.fori_loop(0, cols // SUB, band, sums)
+            for row_off in range(7):
+                at = row_off * 8 + col_off
+                o_ref[index, at : at + 1, :] = jnp.sum(sums[row_off], axis=0, keepdims=True)
         for row_off in range(7):
-            total = sums[row_off] + sums[row_off + 7] + sums[row_off + 14]
-            o_ref[row_off, col_off : col_off + 1, :] = jnp.sum(total, axis=0, keepdims=True)
-    for at, source in enumerate((1, 2, 3, 0)):
-        o_ref[7, at : at + 1, :] = jnp.sum(sums_ref[source], axis=0, keepdims=True)
-    for at, gbi_ref in enumerate((gbi_0, gbi_1, gbi_2, gbi_3)):
-        o_ref[7, 4 + at : 5 + at, :] = gbi_ref[...]
-    for row_off in range(7):
-        o_ref[row_off, 7:8, :] = jnp.zeros((1, LANES), F32)
+            o_ref[index, row_off * 8 + 7 : row_off * 8 + 8, :] = jnp.zeros((1, LANES), F32)
+        for at, source in enumerate((1, 2, 3, 0)):
+            o_ref[index, 56 + at : 57 + at, :] = jnp.sum(sums_ref[source, :, lanes], axis=0, keepdims=True)
+        for at in range(4):
+            o_ref[index, 60 + at : 61 + at, :] = gbi_ref[:, lane_block(at * blocks + index)]
+        return 0
+
+    lax.fori_loop(0, blocks, block, 0)
 
 
 def filter_grad(fields, mask, left, right, top, bot, d_conv, sums, gbi):
     rows, cols, channels = fields.shape
-
-    def part(x):
-        return by_channels(x.shape)
-
     return pl.pallas_call(
         filter_grad_kernel,
-        grid=(channels // LANES,),
-        out_shape=jax.ShapeDtypeStruct((8, 8, channels), F32),
-        in_specs=[
-            part(fields),
-            whole_spec(mask.shape),
-            part(left),
-            part(right),
-            part(top),
-            part(bot),
-            part(d_conv),
-            part(sums),
-        ]
-        + [by_channels(gbi.shape, at * (channels // LANES)) for at in range(4)],
-        out_specs=by_channels((8, 8, channels)),
+        out_shape=jax.ShapeDtypeStruct((channels // LANES, 64, LANES), F32),
         scratch_shapes=[
             pltpu.VMEM((rows + 6, cols + 16, LANES), F32),
             pltpu.VMEM((rows, cols, LANES), F32),
@@ -444,53 +422,59 @@
         compiler_params=params(56),
         cost_estimate=estimate(4),
         name="filter_grad",
-    )(fields, mask, left, right, top, bot, d_conv, sums, gbi, gbi, gbi, gbi)
-
-
-def input_grad_kernel(d_ref, l_ref, r_ref, t_ref, b_ref, k_ref, m_ref, cot_ref, o_ref, window, grad):
-    rows, cols, _ = d_ref.shape
-    fill_window(window, d_ref[...].astype(F32), l_ref, r_ref, t_ref, b_ref)
-    for start in range(0, cols, 8):
-        band_conv(window, k_ref, grad, start, start, 3, True)
-    o_ref[...] = (cot_ref[...].astype(F32) + m_ref[...] * grad[...]).astype(BF16)
-
-
-def input_grad_more_kernel(d_ref, l_ref, r_ref, t_ref, b_ref, k_ref, m_ref, cot_ref, old_ref, o_ref, window, grad):
-    input_grad_kernel(d_ref, l_ref, r_ref, t_ref, b_ref, k_ref, m_ref, cot_ref, o_ref, window, grad)
-
-
-def input_grad(d_conv, left, right, top, bot, kernel, mask, cot, blocks, first, old=None):
+    )(fields, mask, left, right, top, bot, d_conv, sums, gbi)
+
+
+def input_grad_kernel(first, d_ref, l_ref, r_ref, t_ref, b_ref, k_ref, m_ref, cot_ref, *rest):
+    o_ref, window, grad = rest[-3:]
+    rows, cols, channels = d_ref.shape
+    tall = o_ref.shape[0]
+    low, high = max(0, first - 3), min(rows, first + tall + 3)
+    inside = slice(low - first + 3, high - first + 3)
+
+    def block(lanes):
+        if first < 3:
+            window[0 : 3 - first, 5 : 11 + cols, :] = t_ref[first:3, :, lanes].astype(F32)
+        if first + tall > rows - 3:
+            below = first + tall + 3 - rows
+            window[tall + 6 - below : tall + 6, 5 : 11 + cols, :] = b_ref[:below, :, lanes].astype(F32)
+        window[inside, 5:8, :] = l_ref[low:high, :, lanes].astype(F32)
+        window[inside, 8 : 8 + cols, :] = d_ref[low:high, :, lanes].astype(F32)
+        window[inside, 8 + cols : 11 + cols, :] = r_ref[low:high, :, lanes].astype(F32)
+        for sums in [band_conv(window, k_ref, lanes, range(0, cols, SUB), tall, 3, True)]:
+            for (row, start), value in sums.items():
+                grad[row, start : start + SUB, :] = value
+        o_ref[:, :, lanes] = (cot_ref[:, :, lanes].astype(F32) + m_ref[...] * grad[...]).astype(BF16)
+
+    each_lane_block(channels, block)
+
+
+def input_grad(d_conv, left, right, top, bot, kernel, mask, cot, part, parts, old=None):
     rows, cols, channels = d_conv.shape
-
-    def part(x):
-        return by_channels(x.shape, first)
-
+    tall = rows // parts
+
+    def rows_of(width):
+        return pl.BlockSpec((tall, cols, width), lambda i: (part, 0, 0))
+
+    whole = (d_conv, left, right, top, bot, kernel)
     more = [] if old is None else [old]
     return pl.pallas_call(
-        input_grad_kernel if old is None else input_grad_more_kernel,
-        grid=(blocks,),
+        functools.partial(input_grad_kernel, part * tall),
+        grid=(1,),
         out_shape=jax.ShapeDtypeStruct((rows, cols, channels), BF16),
-        in_specs=[
-            part(d_conv),
-            part(left),
-            part(right),
-            part(top),
-            part(bot),
-            part(kernel),
-            whole_spec(mask.shape),
-            part(cot),
-        ]
+        in_specs=[once(x.shape) for x in whole]
+        + [rows_of(LANES), rows_of(channels)]
         + [UNUSED] * len(more),
-        out_specs=part(d_conv),
+        out_specs=rows_of(channels),
         scratch_shapes=[
-            pltpu.VMEM((rows + 6, cols + 16, LANES), F32),
-            pltpu.VMEM((rows, cols, LANES), F32),
+            pltpu.VMEM((tall + 6, cols + 16, LANES), F32),
+            pltpu.VMEM((tall, cols, LANES), F32),
         ],
-        input_output_aliases={} if old is None else {8: 0},
+        input_output_aliases={8: 0} if more else {},
         compiler_params=params(56),
         cost_estimate=estimate(4),
         name="input_grad",
-    )(d_conv, left, right, top, bot, kernel, mask, cot, *more)
+    )(*whole, mask, cot, *more)
 
 
 def swap(values, axis, bit):
@@ -577,19 +561,20 @@
     got = swap(sent, "lon", 1)
     d_conv = d_conv.reshape(rows, cols, channels)
     d_left, d_right = side_halo(d_conv[:, cols - 3 :], d_conv[:, :3])
-    d_tail, d_head = end_rows(d_conv[:3], d_conv[rows - 3 :], d_left, d_right)
-    d_top, d_bot = end_halo(d_tail, d_head)
 
     far = n_lon // 4
-    border = channels * 5 // 8
+    border = channels * 3 // 4
     pieces = (slice(0, border), slice(border, channels))
     far_sums = [
         (kept[:, :far, :, piece].astype(F32) + got[:, :far, :, piece].astype(F32)).astype(BF16)
         for piece in pieces
     ]
-    got_far = [swap(x, "lon", 2) for x in far_sums]
+    d_tail, d_head = end_rows(
+        d_conv[:3], d_conv[rows - 3 :], after(d_left, far_sums[0]), after(d_right, far_sums[0])
+    )
+    d_top, d_bot = end_halo(d_tail, d_head)
     steps = [("lon", 1, bit) for bit in bits_of("lon")[2:]] + [("lat", 2, bit) for bit in bits_of("lat")]
-    owned, cut = [None, None], [None, None]
+    got_far, owned, cut = [swap(far_sums[0], "lon", 2), None], [None, None], [None, None]
 
     def begin(index, last):
         here = pieces[index]
@@ -599,17 +584,26 @@
             x = x.reshape(2, far, x.shape[3], n_lat, -1).transpose(0, 1, 3, 2, 4)
         cut[index] = halves(x, *steps[0])
 
-    def advance(index, step, last):
+    def advance(index, step, last, came=None):
         axis, dim, bit = steps[step]
         mine, sent = cut[index]
-        owned[index] = after(mine, last) + after(swap(sent, axis, bit), last).astype(F32)
+        if came is None:
+            came = after(swap(sent, axis, bit), last)
+        owned[index] = after(mine, last) + came.astype(F32)
         if step + 1 < len(steps):
             cut[index] = halves(owned[index], *steps[step + 1])
 
-    hops = [(axis, bit) for axis in ("lon", "lat") for bit in bits_of(axis)]
-
-    def spread(hop, last):
-        return after(small, last) + after(swap(small, *hops[hop]), last)
+    def pack(sent, small):
+        high = lax.reduce_precision(small, 8, 7)
+        low = lax.reduce_precision(small - high, 8, 7)
+        flat = [x.astype(BF16).reshape(-1, LANES) for x in (sent, high, low)]
+        return jnp.concatenate(flat), high + low
+
+    def ride(load, small, shape, axis, bit, last):
+        came = after(swap(load, axis, bit), last)
+        size, more = math.prod(shape) // LANES, small.size // LANES
+        both = came[size : size + more].astype(F32) + came[size + more :].astype(F32)
+        return came[:size].reshape(shape), after(small, last) + both.reshape(small.shape)
 
     small = filter_grad(
         after(fields, d_tail, d_head, far_sums[0]), mask, left, right, top, bot, d_conv, sums, g_bi
@@ -617,27 +611,25 @@
     begin(0, small)
     for step in range(len(steps) - 2):
         advance(0, step, small)
-    quarter = channels // LANES // 4
     back = (d_left, d_right, d_top, d_bot, kernel, mask, cotangent)
-    grad_fields = input_grad(after(d_conv, small, cut[0][1], far_sums[1]), *back, quarter, 0)
-    small = spread(0, grad_fields)
-    grad_fields = input_grad(after(d_conv, small), *back, quarter, quarter, grad_fields)
-    small = spread(1, grad_fields)
+    grad_fields = input_grad(after(d_conv, small, cut[0][1]), *back, 0, 4)
+    small = after(small, grad_fields) + after(swap(small, "lon", 1), grad_fields)
     advance(0, len(steps) - 2, grad_fields)
+    load, small = pack(far_sums[1], small)
+    grad_fields = input_grad(after(d_conv, load, cut[0][1]), *back, 1, 4, grad_fields)
+    got_far[1], small = ride(load, small, far_sums[1].shape, "lon", 2, grad_fields)
     begin(1, grad_fields)
-    for step in range(len(steps) - 2):
-        advance(1, step, grad_fields)
-    grad_fields = input_grad(
-        after(d_conv, small, cut[0][1], cut[1][1]), *back, quarter, 2 * quarter, grad_fields
-    )
-    small = spread(2, grad_fields)
     advance(0, len(steps) - 1, grad_fields)
-    advance(1, len(steps) - 2, grad_fields)
-    grad_fields = input_grad(after(d_conv, small, cut[1][1]), *back, quarter, 3 * quarter, grad_fields)
-    for hop in range(3, len(hops)):
-        small = spread(hop, grad_fields)
-    advance(1, len(steps) - 1, grad_fields)
+    for step, (axis, _, bit) in enumerate(steps):
+        shape = cut[1][1].shape
+        load, small = pack(cut[1][1], small)
+        if step >= len(steps) - 2:
+            part = step + 4 - len(steps)
+            grad_fields = input_grad(after(d_conv, load), *back, part, 4, grad_fields)
+        came, small = ride(load, small, shape, axis, bit, grad_fields)
+        advance(1, step, grad_fields, came)
     grad_w = jnp.concatenate([x[:, 0, 0] for x in owned], axis=1)
+    small = small.transpose(1, 0, 2).reshape(8, 8, channels)
     return (
         mixed.reshape(rows, cols, channels),
         grad_fields,

time: 132 us -> 131 us (level)
  starting transfers between devices: 30.4 us -> 27.8 us
  Pallas kernels: 75 us -> 72.5 us
  waiting for transfers between devices: 10.7 us -> 12.9 us
  local copies, waits for them, and re-layouts: 6.73 us -> 8.18 us
    ppermute x11 -> x8, waiting for transfers between devices: 6.31 us -> 12.9 us  [swap(): return lax.ppermute(values, axis, [(i, i ^ bit) for i in range(count)])]
    ppermute x4, waiting for transfers between devices: 4.37 us -> 0.01 us  [side_halo(): return (lax.ppermute(last, 'lon', ahead), lax.ppermute(first, 'lon', back))]
    pallas_call x7, Pallas kernels: 41.8 us -> 39 us  [the longest x4 16.5 us: input_grad(): pl.pallas_call(functools.partial(input_grad_kernel, part * tall), grid=(1...]
    ppermute x11 -> x8, starting transfers between devices: 14.1 us -> 12 us  [swap(): return lax.ppermute(values, axis, [(i, i ^ bit) for i in range(count)])]
    unnamed x19 -> x23, local copies, waits for them, and re-layouts: 2.13 us -> 3.43 us
  transfers between devices with their start and end apart: 19 -> 16, of which waited for: 6 -> 6; matrix products, arithmetic and copies ran while one was open for 6% -> 6% of each run, Pallas kernels for 32% -> 30%
where the time goes in v7:
time: 131 us; the launch traced here: 130 us
  Pallas kernels  72.5 us (55%)
  starting transfers between devices  27.8 us (21%)
  waiting for transfers between devices  12.9 us (10%)
  local copies, waits for them, and re-layouts  8.18 us (6%)
  other arithmetic  7.87 us (6%)
    pallas_call x1, Pallas kernels, expand(): pl.pallas_call(expand_kernel, grid_spec=pltpu.PrefetchScalarGridSpec(num_...  33.5 us
    pallas_call x4, Pallas kernels, input_grad(): pl.pallas_call(functools.partial(input_grad_kernel, part * tall), grid=(1...  16.5 us
    ppermute x8, waiting for transfers between devices, swap(): return lax.ppermute(values, axis, [(i, i ^ bit) for i in range(count)])  12.9 us
    ppermute x8, starting transfers between devices, swap(): return lax.ppermute(values, axis, [(i, i ^ bit) for i in range(count)])  12 us
    ppermute x4, starting transfers between devices, end_halo(): return (lax.ppermute(tail, 'lat', ahead), lax.ppermute(head, 'lat', back))  11.5 us
    pallas_call x1, Pallas kernels, filter_grad(): pl.pallas_call(filter_grad_kernel, out_shape=jax.ShapeDtypeStruct((channe...  10.7 us
    pallas_call x1, Pallas kernels, conv_side(): pl.pallas_call(conv_side_kernel, out_shape=jax.ShapeDtypeStruct((rows, 16...  5.94 us
    pallas_call x1, Pallas kernels, conv_inner(): pl.pallas_call(conv_inner_kernel, out_shape=[jax.ShapeDtypeStruct((rows,...  5.81 us
  transfers between devices with their start and end apart: 16, of which 6 were waited for; matrix products, arithmetic and copies ran while one was open for 6% of the time, Pallas kernels for 30%

profile of v7, /device:TPU:0, one launch (start us, length us, event | category | flops | bytes accessed | tf_op | source)
XLA Modules:
  0.0 130.3 jit_solution(5350327144702636683)
XLA Ops:
  3.2 2.0 %collective-permute-start.1 = (bf16[32,3,512]{2,1,0:T(4,128)(2,1)S(1)}, bf16[32,3,512]{2,1,0:T(4,128)(2,1)S(1)}, u32[]{:S(2)}, u32[]{:S(2)}) collective-permute-start(bf16[32,3,512]{2,1,0:T(4,128)(2,1)S(1)} %get-tuple-element.98), channel_id=1, source_target_pairs={{4,0},{8,4},{12,8},{0,12},{5,1},{9,5},{13,9},{1,13},{6,2},{10,6},{... | collective-permute-start | bytes 294920 | tf_op jit(solution)/shard_map/ppermute | solution.py:506
  6.3 5.8 %conv_inner.1 = (f32[32,16,512]{2,1,0:T(8,128)}, bf16[3,32,512]{2,1,0:T(8,128)(2,1)}, bf16[3,32,512]{2,1,0:T(8,128)(2,1)}) custom-call(bf16[32,32,512]{2,1,0:T(8,128)(2,1)} %f_ref.4, f32[32,32,128]{2,1,0:T(8,128)} %broadcast_in_dim.4.m_ref, f32[7,7,512]{2,1,0:T(8,128)} %k_ref.13), custom_call_target="tpu_custom_call" | custom-call | flops 4600000000 | bytes 14400000 | tf_op jit(solution)/shard_map/conv_inner/pallas_call | solution.py:109
  13.7 4.2 %collective-permute-start.2 = (bf16[3,38,512]{2,1,0:T(8,128)(2,1)S(1)}, bf16[3,38,512]{2,1,0:T(8,128)(2,1)S(1)}, u32[]{:S(2)}, u32[]{:S(2)}) collective-permute-start(bf16[3,38,512]{2,1,0:T(8,128)(2,1)S(1)} %pad_maximum_fusion.4), channel_id=1, source_target_pairs={{0,1},{1,2},{2,3},{4,5},{5,6},{6,7},{8,9},{9,10},{10,11},{12,13},{... | collective-permute-start | bytes 350216 | tf_op jit(solution)/shard_map/ppermute | solution.py:521
  18.9 1.3 collective-permute-start.3
  20.2 5.9 %conv_side.1.side_ref = f32[32,16,512]{2,1,0:T(8,128)} custom-call(bf16[32,32,512]{2,1,0:T(8,128)(2,1)} %f_ref.4, f32[32,32,128]{2,1,0:T(8,128)} %broadcast_in_dim.4.m_ref, f32[7,7,512]{2,1,0:T(8,128)} %k_ref.13, bf16[32,3,512]{2,1,0:T(4,128)(2,1)} %copy-done.2, bf16[32,3,512]{2,1,0:T(4,128)(2,1)} %copy-done.3), custom_call_target="tpu_custom_call" | custom-call | flops 4600000000 | bytes 14400000 | tf_op jit(solution)/shard_map/conv_side/pallas_call | solution.py:125
  26.9 33.5 %expand.1 = (bf16[1024,512]{1,0:T(8,128)(2,1)}, bf16[1024,512]{1,0:T(8,128)(2,1)}, f32[4,8,512]{2,1,0:T(8,128)}, f32[1,2048]{1,0:T(1,128)}, bf16[2,2,4,512,128]{...) custom-call(s32[4]{0:T(128)} %pad_add_fusion.order_ref, f32[32,16,512]{2,1,0:T(8,128)} %get-tuple-element.46.inner_ref, ...), custom_call_target="tpu_custom_call" | custom-call | flops 23000000512 | bytes 72000000 | tf_op jit(solution)/shard_map/expand/pallas_call | solution.py:318
  64.8 1.3 %add_convert_fusion = bf16[2,1,4,384,128]{4,3,2,1,0:T(8,128)(2,1)S(1)} fusion(bf16[2,2,4,512,128]{4,3,2,1,0:T(8,128)(2,1)S(1)} %collective-permute-done.4, bf16[2,2,4,512,128]{4,3,2,1,0:T(8,128)(2,1)} %get-tuple-element.67), kind=kLoop, calls=%fused_computation.1 | loop fusion | flops 1572864 | bytes 2359296 | tf_op jit(solution)/shard_map/convert_element_type | solution.py:569
  66.2 1.6 %collective-permute-start.7 = (bf16[2,1,4,384,128]{4,3,2,1,0:T(8,128)(2,1)S(1)}, bf16[2,1,4,384,128]{4,3,2,1,0:T(8,128)(2,1)S(1)}, u32[]{:S(2)}, u32[]{:S(2)}) collective-permute-start(bf16[2,1,4,384,128]{4,3,2,1,0:T(8,128)(2,1)S(1)} %add_convert_fusion), channel_id=1, source_target_pairs={{0,8},{4,12},{8,0},{12,4},{1,9},{5,13},{9,1},{13,5},{2,10},{6,14},... | collective-permute-start | bytes 2359304 | tf_op jit(solution)/shard_map/ppermute | solution.py:482
  67.9 4.5 %collective-permute-start.8 = (bf16[3,38,512]{2,1,0:T(8,128)(2,1)S(1)}, bf16[3,38,512]{2,1,0:T(8,128)(2,1)S(1)}, u32[]{:S(2)}, u32[]{:S(2)}) collective-permute-start(bf16[3,38,512]{2,1,0:T(8,128)(2,1)S(1)} %pad_maximum_fusion.6), channel_id=1, source_target_pairs={{0,1},{1,2},{2,3},{4,5},{5,6},{6,7},{8,9},{9,10},{10,11},{12,13},{... | collective-permute-start | bytes 350216 | tf_op jit(solution)/shard_map/ppermute | solution.py:521
  72.5 1.5 %collective-permute-start.9 = (bf16[3,38,512]{2,1,0:T(8,128)(2,1)S(1)}, bf16[3,38,512]{2,1,0:T(8,128)(2,1)S(1)}, u32[]{:S(2)}, u32[]{:S(2)}) collective-permute-start(bf16[3,38,512]{2,1,0:T(8,128)(2,1)S(1)} %pad_maximum_fusion.7), channel_id=1, source_target_pairs={{1,0},{2,1},{3,2},{5,4},{6,5},{7,6},{9,8},{10,9},{11,10},{13,12},{... | collective-permute-start | bytes 350216 | tf_op jit(solution)/shard_map/ppermute | solution.py:521
  73.9 10.7 %filter_grad.1 = f32[4,64,128]{2,1,0:T(8,128)} custom-call(bf16[32,32,512]{2,1,0:T(8,128)(2,1)} %f_ref.4, f32[32,32,128]{2,1,0:T(8,128)} %broadcast_in_dim.4.m_ref, bf16[32,3,512]{2,1,0:T(4,128)(2,1)} %copy-done.2, bf16[32,3,512]{2,1,0:T(4,128)(2,1)} %copy-done.3, bf16[3,38,512]{2,1,0:T(8,128)(2,1)} %copy-done.6, bf16[3,38,512]{2,1,0:T(8,128)(2,1)} %copy-done.7, ...), custom_call_target="tpu_custom_call" | custom-call | flops 4600000000 | bytes 14400000 | tf_op jit(solution)/shard_map/filter_grad/pallas_call | solution.py:415
  86.4 2.7 %collective-permute-start.11 = (bf16[2,1,2,384,128]{4,3,0,2,1:T(8,128)(2,1)S(1)}, bf16[2,1,2,384,128]{4,3,0,2,1:T(8,128)(2,1)S(1)}, u32[]{:S(2)}, u32[]{:S(2)}) collective-permute-start(bf16[2,1,2,384,128]{4,3,0,2,1:T(8,128)(2,1)S(1)} %fusion), channel_id=1, source_target_pairs={{0,1},{1,0},{2,3},{3,2},{4,5},{5,4},{6,7},{7,6},{8,9},{9,8},{10,11... | collective-permute-start | bytes 1179656 | tf_op jit(solution)/shard_map/ppermute | solution.py:482
  90.4 4.1 %input_grad.4.rest_0_ = bf16[32,32,512]{2,1,0:T(8,128)(2,1)} custom-call(bf16[32,32,512]{2,1,0:T(8,128)(2,1)} %bitcast.109, bf16[32,3,512]{2,1,0:T(4,128)(2,1)} %copy-done.4, bf16[32,3,512]{2,1,0:T(4,128)(2,1)} %copy-done.5, bf16[3,38,512]{2,1,0:T(8,128)(2,1)} %copy-done.8, bf16[3,38,512]{2,1,0:T(8,128)(2,1)} %copy-done.9, f32[7,7,512]{2,1,0:T(8,128)} %k_ref.13, ...), custom_call_target="tpu_custom_call" | custom-call | flops 4600000000 | bytes 14400000 | tf_op jit(solution)/shard_map/input_grad/pallas_call | solution.py:461
  94.6 1.6 %collective-permute-start.12 = (bf16[1536,128]{1,0:T(8,128)(2,1)S(1)}, bf16[1536,128]{1,0:T(8,128)(2,1)S(1)}, u32[]{:S(2)}, u32[]{:S(2)}) collective-permute-start(bf16[1536,128]{1,0:T(8,128)(2,1)S(1)} %pad_maximum_fusion), channel_id=1, source_target_pairs={{0,8},{4,12},{8,0},{12,4},{1,9},{5,13},{9,1},{13,5},{2,10},{6,14},... | collective-permute-start | bytes 1179656 | tf_op jit(solution)/shard_map/ppermute | solution.py:482
  96.2 1.7 %collective-permute-done.11 = bf16[2,1,2,384,128]{4,3,0,2,1:T(8,128)(2,1)S(1)} collective-permute-done((bf16[2,1,2,384,128]{4,3,0,2,1:T(8,128)(2,1)S(1)}, bf16[2,1,2,384,128]{4,3,0,2,1:T(8,128)(2,1)S(1)}, u32[]{:S(2)}, u32[]{:S(2)}) %collective-permute-start.11) | collective-permute-done | bytes 393248 | tf_op jit(solution)/shard_map/ppermute | solution.py:482
  98.0 2.8 %collective-permute-start.15 = (bf16[2,1,1,384,128]{4,3,0,2,1:T(8,128)(2,1)S(1)}, bf16[2,1,1,384,128]{4,3,0,2,1:T(8,128)(2,1)S(1)}, u32[]{:S(2)}, u32[]{:S(2)}) collective-permute-start(bf16[2,1,1,384,128]{4,3,0,2,1:T(8,128)(2,1)S(1)} %fusion.5), channel_id=1, source_target_pairs={{0,2},{1,3},{2,0},{3,1},{4,6},{5,7},{6,4},{7,5},{8,10},{9,11},{10,... | collective-permute-start | bytes 589832 | tf_op jit(solution)/shard_map/ppermute | solution.py:482
  100.9 4.1 %input_grad.5.rest_0_ = bf16[32,32,512]{2,1,0:T(8,128)(2,1)} custom-call(bf16[32,32,512]{2,1,0:T(8,128)(2,1)} %bitcast.110, bf16[32,3,512]{2,1,0:T(4,128)(2,1)} %copy-done.4, bf16[32,3,512]{2,1,0:T(4,128)(2,1)} %copy-done.5, bf16[3,38,512]{2,1,0:T(8,128)(2,1)} %copy-done.8, bf16[3,38,512]{2,1,0:T(8,128)(2,1)} %copy-done.9, ...), custom_call_target="tpu_custom_call", output_to_operand_aliasing={{}: (8, {})} | custom-call | flops 4600000000 | bytes 14400000 | tf_op jit(solution)/shard_map/input_grad/pallas_call | solution.py:461
  105.3 1.6 %collective-permute-start.13 = (bf16[1024,128]{1,0:T(8,128)(2,1)S(1)}, bf16[1024,128]{1,0:T(8,128)(2,1)S(1)}, u32[]{:S(2)}, u32[]{:S(2)}) collective-permute-start(bf16[1024,128]{1,0:T(8,128)(2,1)S(1)} %pad_maximum_fusion.2), channel_id=1, source_target_pairs={{0,1},{1,0},{2,3},{3,2},{4,5},{5,4},{6,7},{7,6},{8,9},{9,8},{10,11... | collective-permute-start | bytes 786440 | tf_op jit(solution)/shard_map/ppermute | solution.py:482
  106.9 2.1 %collective-permute-done.15 = bf16[2,1,1,384,128]{4,3,0,2,1:T(8,128)(2,1)S(1)} collective-permute-done((bf16[2,1,1,384,128]{4,3,0,2,1:T(8,128)(2,1)S(1)}, bf16[2,1,1,384,128]{4,3,0,2,1:T(8,128)(2,1)S(1)}, u32[]{:S(2)}, u32[]{:S(2)}) %collective-permute-start.15) | collective-permute-done | bytes 196640 | tf_op jit(solution)/shard_map/ppermute | solution.py:482
  109.0 4.1 %input_grad.6.rest_0_ = bf16[32,32,512]{2,1,0:T(8,128)(2,1)} custom-call(bf16[32,32,512]{2,1,0:T(8,128)(2,1)} %bitcast.111, bf16[32,3,512]{2,1,0:T(4,128)(2,1)} %copy-done.4, bf16[32,3,512]{2,1,0:T(4,128)(2,1)} %copy-done.5, bf16[3,38,512]{2,1,0:T(8,128)(2,1)} %copy-done.8, bf16[3,38,512]{2,1,0:T(8,128)(2,1)} %copy-done.9, ...), custom_call_target="tpu_custom_call", output_to_operand_aliasing={{}: (8, {})} | custom-call | flops 4600000000 | bytes 14400000 | tf_op jit(solution)/shard_map/input_grad/pallas_call | solution.py:461
  113.1 1.3 %collective-permute-done.13 = bf16[1024,128]{1,0:T(8,128)(2,1)S(1)} collective-permute-done((bf16[1024,128]{1,0:T(8,128)(2,1)S(1)}, bf16[1024,128]{1,0:T(8,128)(2,1)S(1)}, u32[]{:S(2)}, u32[]{:S(2)}) %collective-permute-start.13) | collective-permute-done | bytes 262176 | tf_op jit(solution)/shard_map/ppermute | solution.py:482
  114.7 1.5 %collective-permute-start.14 = (bf16[768,128]{1,0:T(8,128)(2,1)S(1)}, bf16[768,128]{1,0:T(8,128)(2,1)S(1)}, u32[]{:S(2)}, u32[]{:S(2)}) collective-permute-start(bf16[768,128]{1,0:T(8,128)(2,1)S(1)} %pad_maximum_fusion.3), channel_id=1, source_target_pairs={{0,2},{1,3},{2,0},{3,1},{4,6},{5,7},{6,4},{7,5},{8,10},{9,11},{10,... | collective-permute-start | bytes 589832 | tf_op jit(solution)/shard_map/ppermute | solution.py:482
  116.2 4.1 %input_grad.7 = bf16[32,32,512]{2,1,0:T(8,128)(2,1)} custom-call(bf16[32,32,512]{2,1,0:T(8,128)(2,1)} %bitcast.112, bf16[32,3,512]{2,1,0:T(4,128)(2,1)} %copy-done.4, bf16[32,3,512]{2,1,0:T(4,128)(2,1)} %copy-done.5, bf16[3,38,512]{2,1,0:T(8,128)(2,1)} %copy-done.8, bf16[3,38,512]{2,1,0:T(8,128)(2,1)} %copy-done.9, ...), custom_call_target="tpu_custom_call", output_to_operand_aliasing={{}: (8, {})} | custom-call | flops 4600000000 | bytes 14400000 | tf_op jit(solution)/shard_map/input_grad/pallas_call | solution.py:461
  120.3 6.4 %collective-permute-done.14 = bf16[768,128]{1,0:T(8,128)(2,1)S(1)} collective-permute-done((bf16[768,128]{1,0:T(8,128)(2,1)S(1)}, bf16[768,128]{1,0:T(8,128)(2,1)S(1)}, u32[]{:S(2)}, u32[]{:S(2)}) %collective-permute-start.14) | collective-permute-done | bytes 196640 | tf_op jit(solution)/shard_map/ppermute | solution.py:482
  (88 shorter events, 18.6 us)
Async XLA Ops:
  2.7 10.0 %collective-permute-start = (bf16[32,3,512]{2,1,0:T(4,128)(2,1)S(1)}, bf16[32,3,512]{2,1,0:T(4,128)(2,1)S(1)}, u32[]{:S(2)}, u32[]{:S(2)}) collective-permute-start(bf16[32,3,512]{2,1,0:T(4,128)(2,1)S(1)} %get-tuple-element.99), channel_id=1, source_target_pairs={{0,4},{4,8},{8,12},{12,0},{1,5},{5,9},{9,13},{13,1},{2,6},{6,10},{... | collective-permute-start | bytes 294920 | tf_op jit(solution)/shard_map/ppermute | solution.py:506
  3.2 9.4 %collective-permute-start.1 = (bf16[32,3,512]{2,1,0:T(4,128)(2,1)S(1)}, bf16[32,3,512]{2,1,0:T(4,128)(2,1)S(1)}, u32[]{:S(2)}, u32[]{:S(2)}) collective-permute-start(bf16[32,3,512]{2,1,0:T(4,128)(2,1)S(1)} %get-tuple-element.98), channel_id=1, source_target_pairs={{4,0},{8,4},{12,8},{0,12},{5,1},{9,5},{13,9},{1,13},{6,2},{10,6},{... | collective-permute-start | bytes 294920 | tf_op jit(solution)/shard_map/ppermute | solution.py:506
  12.7 7.5 %copy-start.3 = (bf16[32,3,512]{2,1,0:T(4,128)(2,1)}, bf16[32,3,512]{2,1,0:T(4,128)(2,1)S(1)}, u32[]{:S(2)}) copy-start(bf16[32,3,512]{2,1,0:T(4,128)(2,1)S(1)} %collective-permute-done.1.r_ref) | copy-start | bytes 294916
  12.7 7.5 %copy-start.2 = (bf16[32,3,512]{2,1,0:T(4,128)(2,1)}, bf16[32,3,512]{2,1,0:T(4,128)(2,1)S(1)}, u32[]{:S(2)}) copy-start(bf16[32,3,512]{2,1,0:T(4,128)(2,1)S(1)} %collective-permute-done.l_ref) | copy-start | bytes 294916
  13.7 12.4 %collective-permute-start.2 = (bf16[3,38,512]{2,1,0:T(8,128)(2,1)S(1)}, bf16[3,38,512]{2,1,0:T(8,128)(2,1)S(1)}, u32[]{:S(2)}, u32[]{:S(2)}) collective-permute-start(bf16[3,38,512]{2,1,0:T(8,128)(2,1)S(1)} %pad_maximum_fusion.4), channel_id=1, source_target_pairs={{0,1},{1,2},{2,3},{4,5},{5,6},{6,7},{8,9},{9,10},{10,11},{12,13},{... | collective-permute-start | bytes 350216 | tf_op jit(solution)/shard_map/ppermute | solution.py:521
  18.9 7.3 %collective-permute-start.3 = (bf16[3,38,512]{2,1,0:T(8,128)(2,1)S(1)}, bf16[3,38,512]{2,1,0:T(8,128)(2,1)S(1)}, u32[]{:S(2)}, u32[]{:S(2)}) collective-permute-start(bf16[3,38,512]{2,1,0:T(8,128)(2,1)S(1)} %pad_maximum_fusion.5), channel_id=1, source_target_pairs={{1,0},{2,1},{3,2},{5,4},{6,5},{7,6},{9,8},{10,9},{11,10},{13,12},{... | collective-permute-start | bytes 350216 | tf_op jit(solution)/shard_map/ppermute | solution.py:521
  26.2 0.7 copy-start.7
  60.4 4.4 %collective-permute-start.4 = (bf16[2,2,4,512,128]{4,3,2,1,0:T(8,128)(2,1)}, bf16[2,2,4,512,128]{4,3,2,1,0:T(8,128)(2,1)S(1)}, u32[]{:S(2)}, u32[]{:S(2)}) collective-permute-start(bf16[2,2,4,512,128]{4,3,2,1,0:T(8,128)(2,1)} %get-tuple-element.52), channel_id=1, source_target_pairs={{0,4},{4,0},{8,12},{12,8},{1,5},{5,1},{9,13},{13,9},{2,6},{6,2},{1... | collective-permute-start | bytes 6291464 | tf_op jit(solution)/shard_map/ppermute | solution.py:482
  61.6 6.1 %collective-permute-start.5 = (bf16[32,3,512]{2,1,0:T(4,128)(2,1)S(1)}, bf16[32,3,512]{2,1,0:T(4,128)(2,1)S(1)}, u32[]{:S(2)}, u32[]{:S(2)}) collective-permute-start(bf16[32,3,512]{2,1,0:T(4,128)(2,1)S(1)} %get-tuple-element.96), channel_id=1, source_target_pairs={{0,4},{4,8},{8,12},{12,0},{1,5},{5,9},{9,13},{13,1},{2,6},{6,10},{... | collective-permute-start | bytes 294920 | tf_op jit(solution)/shard_map/ppermute | solution.py:506
  62.2 5.6 %collective-permute-start.6 = (bf16[32,3,512]{2,1,0:T(4,128)(2,1)S(1)}, bf16[32,3,512]{2,1,0:T(4,128)(2,1)S(1)}, u32[]{:S(2)}, u32[]{:S(2)}) collective-permute-start(bf16[32,3,512]{2,1,0:T(4,128)(2,1)S(1)} %get-tuple-element.97), channel_id=1, source_target_pairs={{4,0},{8,4},{12,8},{0,12},{5,1},{9,5},{13,9},{1,13},{6,2},{10,6},{... | collective-permute-start | bytes 294920 | tf_op jit(solution)/shard_map/ppermute | solution.py:506
  66.2 19.6 %collective-permute-start.7 = (bf16[2,1,4,384,128]{4,3,2,1,0:T(8,128)(2,1)S(1)}, bf16[2,1,4,384,128]{4,3,2,1,0:T(8,128)(2,1)S(1)}, u32[]{:S(2)}, u32[]{:S(2)}) collective-permute-start(bf16[2,1,4,384,128]{4,3,2,1,0:T(8,128)(2,1)S(1)} %add_convert_fusion), channel_id=1, source_target_pairs={{0,8},{4,12},{8,0},{12,4},{1,9},{5,13},{9,1},{13,5},{2,10},{6,14},... | collective-permute-start | bytes 2359304 | tf_op jit(solution)/shard_map/ppermute | solution.py:482
  67.8 16.9 %copy-start.4 = (bf16[32,3,512]{2,1,0:T(4,128)(2,1)}, bf16[32,3,512]{2,1,0:T(4,128)(2,1)S(1)}, u32[]{:S(2)}) copy-start(bf16[32,3,512]{2,1,0:T(4,128)(2,1)S(1)} %collective-permute-done.5.l_ref) | copy-start | bytes 294916
  67.8 16.9 %copy-start.5 = (bf16[32,3,512]{2,1,0:T(4,128)(2,1)}, bf16[32,3,512]{2,1,0:T(4,128)(2,1)S(1)}, u32[]{:S(2)}) copy-start(bf16[32,3,512]{2,1,0:T(4,128)(2,1)S(1)} %collective-permute-done.6.r_ref) | copy-start | bytes 294916
  67.9 21.2 %collective-permute-start.8 = (bf16[3,38,512]{2,1,0:T(8,128)(2,1)S(1)}, bf16[3,38,512]{2,1,0:T(8,128)(2,1)S(1)}, u32[]{:S(2)}, u32[]{:S(2)}) collective-permute-start(bf16[3,38,512]{2,1,0:T(8,128)(2,1)S(1)} %pad_maximum_fusion.6), channel_id=1, source_target_pairs={{0,1},{1,2},{2,3},{4,5},{5,6},{6,7},{8,9},{9,10},{10,11},{12,13},{... | collective-permute-start | bytes 350216 | tf_op jit(solution)/shard_map/ppermute | solution.py:521
  72.5 16.6 %collective-permute-start.9 = (bf16[3,38,512]{2,1,0:T(8,128)(2,1)S(1)}, bf16[3,38,512]{2,1,0:T(8,128)(2,1)S(1)}, u32[]{:S(2)}, u32[]{:S(2)}) collective-permute-start(bf16[3,38,512]{2,1,0:T(8,128)(2,1)S(1)} %pad_maximum_fusion.7), channel_id=1, source_target_pairs={{1,0},{2,1},{3,2},{5,4},{6,5},{7,6},{9,8},{10,9},{11,10},{13,12},{... | collective-permute-start | bytes 350216 | tf_op jit(solution)/shard_map/ppermute | solution.py:521
  73.9 10.8 %copy-start = (bf16[2,2,4,512,128]{4,3,2,1,0:T(8,128)(2,1)S(1)}, bf16[2,2,4,512,128]{4,3,2,1,0:T(8,128)(2,1)}, u32[]{:S(2)}) copy-start(bf16[2,2,4,512,128]{4,3,2,1,0:T(8,128)(2,1)} %get-tuple-element.67) | copy-start | bytes 6291460
  84.7 9.9 %collective-permute-start.10 = (f32[4,64,128]{2,1,0:T(8,128)}, f32[4,64,128]{2,1,0:T(8,128)S(1)}, u32[]{:S(2)}, u32[]{:S(2)}) collective-permute-start(f32[4,64,128]{2,1,0:T(8,128)} %filter_grad.1), channel_id=1, source_target_pairs={{0,4},{4,0},{8,12},{12,8},{1,5},{5,1},{9,13},{13,9},{2,6},{6,2},{1... | collective-permute-start | bytes 393224 | tf_op jit(solution)/shard_map/ppermute | solution.py:482
  86.4 8.1 %copy-start.1 = (f32[4,64,128]{2,1,0:T(8,128)S(1)}, f32[4,64,128]{2,1,0:T(8,128)}, u32[]{:S(2)}) copy-start(f32[4,64,128]{2,1,0:T(8,128)} %filter_grad.1) | copy-start | bytes 393220
  86.4 11.5 %collective-permute-start.11 = (bf16[2,1,2,384,128]{4,3,0,2,1:T(8,128)(2,1)S(1)}, bf16[2,1,2,384,128]{4,3,0,2,1:T(8,128)(2,1)S(1)}, u32[]{:S(2)}, u32[]{:S(2)}) collective-permute-start(bf16[2,1,2,384,128]{4,3,0,2,1:T(8,128)(2,1)S(1)} %fusion), channel_id=1, source_target_pairs={{0,1},{1,0},{2,3},{3,2},{4,5},{5,4},{6,7},{7,6},{8,9},{9,8},{10,11... | collective-permute-start | bytes 1179656 | tf_op jit(solution)/shard_map/ppermute | solution.py:482
  89.1 0.6 copy-start.8
  94.6 10.4 %collective-permute-start.12 = (bf16[1536,128]{1,0:T(8,128)(2,1)S(1)}, bf16[1536,128]{1,0:T(8,128)(2,1)S(1)}, u32[]{:S(2)}, u32[]{:S(2)}) collective-permute-start(bf16[1536,128]{1,0:T(8,128)(2,1)S(1)} %pad_maximum_fusion), channel_id=1, source_target_pairs={{0,8},{4,12},{8,0},{12,4},{1,9},{5,13},{9,1},{13,5},{2,10},{6,14},... | collective-permute-start | bytes 1179656 | tf_op jit(solution)/shard_map/ppermute | solution.py:482
  98.0 11.0 %collective-permute-start.15 = (bf16[2,1,1,384,128]{4,3,0,2,1:T(8,128)(2,1)S(1)}, bf16[2,1,1,384,128]{4,3,0,2,1:T(8,128)(2,1)S(1)}, u32[]{:S(2)}, u32[]{:S(2)}) collective-permute-start(bf16[2,1,1,384,128]{4,3,0,2,1:T(8,128)(2,1)S(1)} %fusion.5), channel_id=1, source_target_pairs={{0,2},{1,3},{2,0},{3,1},{4,6},{5,7},{6,4},{7,5},{8,10},{9,11},{10,... | collective-permute-start | bytes 589832 | tf_op jit(solution)/shard_map/ppermute | solution.py:482
  105.3 9.2 %collective-permute-start.13 = (bf16[1024,128]{1,0:T(8,128)(2,1)S(1)}, bf16[1024,128]{1,0:T(8,128)(2,1)S(1)}, u32[]{:S(2)}, u32[]{:S(2)}) collective-permute-start(bf16[1024,128]{1,0:T(8,128)(2,1)S(1)} %pad_maximum_fusion.2), channel_id=1, source_target_pairs={{0,1},{1,0},{2,3},{3,2},{4,5},{5,4},{6,7},{7,6},{8,9},{9,8},{10,11... | collective-permute-start | bytes 786440 | tf_op jit(solution)/shard_map/ppermute | solution.py:482
  114.7 12.0 %collective-permute-start.14 = (bf16[768,128]{1,0:T(8,128)(2,1)S(1)}, bf16[768,128]{1,0:T(8,128)(2,1)S(1)}, u32[]{:S(2)}, u32[]{:S(2)}) collective-permute-start(bf16[768,128]{1,0:T(8,128)(2,1)S(1)} %pad_maximum_fusion.3), channel_id=1, source_target_pairs={{0,2},{1,3},{2,0},{3,1},{4,6},{5,7},{6,4},{7,5},{8,10},{9,11},{10,... | collective-permute-start | bytes 589832 | tf_op jit(solution)/shard_map/ppermute | solution.py:482
  (2 other events, 1.3 us)

commit v8 on v7

--- a/solution.py
+++ b/solution.py
@@ -217,61 +217,60 @@
             normed_t[:, here] = normed[here, :].T
             dbr_t[:, here] = dbr[here, :].T
 
-    part = 256
-    count = cells // part
     block = act.shape[1]
     cut = min(block, 256)
+    count = block // cut
+    _, parts, _, width = sent_ref.shape
+    is_sent = step_now < pl.num_programs(0) // 2
 
     def products(index):
-        here = slice(index * part, (index + 1) * part)
-        pre_s[index % 2] = jnp.dot(normed[here, :], wi_ref[...], preferred_element_type=F32)
+        lanes = slice(index * cut, (index + 1) * cut)
+        pre_s[index % 2] = jnp.dot(normed[...], wi_ref[:, lanes], preferred_element_type=F32)
         dact_s[index % 2] = lax.dot_general(
-            dbr[here, :], wo_ref[...], (((1,), (1,)), ((), ())), preferred_element_type=F32
+            dbr[...], wo_ref[lanes, :], (((1,), (1,)), ((), ())), preferred_element_type=F32
         )
 
-    def project(index):
-        here = slice(index * part, (index + 1) * part)
-        branch[here, :] += jnp.dot(act[here, :], wo_ref[...], preferred_element_type=F32)
-        d_normed[here, :] += lax.dot_general(
-            dpre[here, :], wi_ref[...], (((1,), (1,)), ((), ())), preferred_element_type=F32
-        )
-
-    totals = [jnp.zeros((SUB, cut), F32) for _ in range(0, block, cut)]
+    def activate(index):
+        lanes = slice(index * cut, (index + 1) * cut)
+        bias = bi_ref[:, lanes]
+        total = jnp.zeros((SUB, cut), F32)
+        for at in range(0, cells, strip):
+            here = slice(at, at + strip)
+            value, slope = gelu_twice(pre_s[index % 2, here, :] + bias)
+            act[here, lanes] = value.astype(BF16)
+            d_pre = dact_s[index % 2, here, :] * slope
+            dpre[here, lanes] = d_pre.astype(BF16)
+            total = total + (d_pre[:SUB] + d_pre[SUB:])
+        gbi_ref[:, lanes] = jnp.sum(total, axis=0, keepdims=True)
+
+    def weight_grads(index):
+        left = index * cut
+        for which, (rows_t, source) in enumerate(((dbr_t, act), (normed_t, dpre))):
+            grad = jnp.dot(
+                rows_t[...], source[:, left : left + cut], preferred_element_type=F32
+            ).astype(BF16)
+
+            def store(ref):
+                size = min(width, cut)
+                for at in range(0, cut, size):
+                    lat, into = divmod(left + at, width)
+                    ref[which, lat, :, into : into + size] = grad[:, at : at + size]
+
+            pl.when(is_sent)(functools.partial(store, sent_ref))
+            pl.when(jnp.logical_not(is_sent))(functools.partial(store, kept_ref))
+
     products(0)
     for index in range(count):
         if index + 1 < count:
             products(index + 1)
-        for at in range(0, part, strip):
-            here = slice(index * part + at, index * part + at + strip)
-            for which, left in enumerate(range(0, block, cut)):
-                lanes = slice(left, left + cut)
-                x = pre_s[index % 2, at : at + strip, lanes] + bi_ref[:, lanes]
-                value, slope = gelu_twice(x)
-                act[here, lanes] = value.astype(BF16)
-                d_pre = dact_s[index % 2, at : at + strip, lanes] * slope
-                dpre[here, lanes] = d_pre.astype(BF16)
-                totals[which] = totals[which] + (d_pre[:SUB] + d_pre[SUB:])
+        activate(index)
         if index > 0:
-            project(index - 1)
-    project(count - 1)
-    for which, left in enumerate(range(0, block, cut)):
-        gbi_ref[:, left : left + cut] = jnp.sum(totals[which], axis=0, keepdims=True)
-    _, parts, _, width = sent_ref.shape
-    is_sent = step_now < pl.num_programs(0) // 2
-    for index, (rows_t, source) in enumerate(((dbr_t, act), (normed_t, dpre))):
-        for left in range(0, block, cut):
-            grad = jnp.dot(
-                rows_t[...], source[:, left : left + cut], preferred_element_type=F32
-            ).astype(BF16)
-
-            def store(ref):
-                for at in range(0, cut, min(width, cut)):
-                    lat, into = divmod(left + at, width)
-                    size = min(width, cut)
-                    ref[index, lat, :, into : into + size] = grad[:, at : at + size]
-
-            pl.when(is_sent)(functools.partial(store, sent_ref))
-            pl.when(jnp.logical_not(is_sent))(functools.partial(store, kept_ref))
+            weight_grads(index - 1)
+    weight_grads(count - 1)
+    branch[...] += jnp.dot(act[...], wo_ref[...], preferred_element_type=F32)
+    d_normed[...] += lax.dot_general(
+        dpre[...], wi_ref[...], (((1,), (1,)), ((), ())), preferred_element_type=F32
+    )
 
     @pl.when(step_now == pl.num_programs(0) - 1)
     def _():
@@ -346,8 +345,8 @@
                 pltpu.VMEM((cells, block), BF16),
                 pltpu.VMEM((cells, channels), F32),
                 pltpu.VMEM((cells, channels), F32),
-                pltpu.VMEM((2, 256, block), F32),
-                pltpu.VMEM((2, 256, block), F32),
+                pltpu.VMEM((2, cells, min(block, 256)), F32),
+                pltpu.VMEM((2, cells, min(block, 256)), F32),
             ],
         ),
         out_shape=[
@@ -425,14 +424,14 @@
     )(fields, mask, left, right, top, bot, d_conv, sums, gbi)
 
 
-def input_grad_kernel(first, d_ref, l_ref, r_ref, t_ref, b_ref, k_ref, m_ref, cot_ref, *rest):
+def input_grad_kernel(first_block, parts, d_ref, l_ref, r_ref, t_ref, b_ref, k_ref, m_ref, cot_ref, *rest):
     o_ref, window, grad = rest[-3:]
     rows, cols, channels = d_ref.shape
     tall = o_ref.shape[0]
-    low, high = max(0, first - 3), min(rows, first + tall + 3)
-    inside = slice(low - first + 3, high - first + 3)
-
-    def block(lanes):
+
+    def fill(first, lanes):
+        low, high = max(0, first - 3), min(rows, first + tall + 3)
+        inside = slice(low - first + 3, high - first + 3)
         if first < 3:
             window[0 : 3 - first, 5 : 11 + cols, :] = t_ref[first:3, :, lanes].astype(F32)
         if first + tall > rows - 3:
@@ -441,26 +440,30 @@
         window[inside, 5:8, :] = l_ref[low:high, :, lanes].astype(F32)
         window[inside, 8 : 8 + cols, :] = d_ref[low:high, :, lanes].astype(F32)
         window[inside, 8 + cols : 11 + cols, :] = r_ref[low:high, :, lanes].astype(F32)
-        for sums in [band_conv(window, k_ref, lanes, range(0, cols, SUB), tall, 3, True)]:
-            for (row, start), value in sums.items():
-                grad[row, start : start + SUB, :] = value
+
+    def block(lanes):
+        for at in range(parts):
+            pl.when(pl.program_id(0) == at)(functools.partial(fill, (first_block + at) * tall, lanes))
+        sums = band_conv(window, k_ref, lanes, range(0, cols, SUB), tall, 3, True)
+        for (row, start), value in sums.items():
+            grad[row, start : start + SUB, :] = value
         o_ref[:, :, lanes] = (cot_ref[:, :, lanes].astype(F32) + m_ref[...] * grad[...]).astype(BF16)
 
     each_lane_block(channels, block)
 
 
-def input_grad(d_conv, left, right, top, bot, kernel, mask, cot, part, parts, old=None):
+def input_grad(d_conv, left, right, top, bot, kernel, mask, cot, first, parts, old=None):
     rows, cols, channels = d_conv.shape
-    tall = rows // parts
+    tall = rows // 4
 
     def rows_of(width):
-        return pl.BlockSpec((tall, cols, width), lambda i: (part, 0, 0))
+        return pl.BlockSpec((tall, cols, width), lambda i: (first + i, 0, 0))
 
     whole = (d_conv, left, right, top, bot, kernel)
     more = [] if old is None else [old]
     return pl.pallas_call(
-        functools.partial(input_grad_kernel, part * tall),
-        grid=(1,),
+        functools.partial(input_grad_kernel, first, parts),
+        grid=(parts,),
         out_shape=jax.ShapeDtypeStruct((rows, cols, channels), BF16),
         in_specs=[once(x.shape) for x in whole]
         + [rows_of(LANES), rows_of(channels)]
@@ -563,71 +566,72 @@
     d_left, d_right = side_halo(d_conv[:, cols - 3 :], d_conv[:, :3])
 
     far = n_lon // 4
-    border = channels * 3 // 4
-    pieces = (slice(0, border), slice(border, channels))
-    far_sums = [
-        (kept[:, :far, :, piece].astype(F32) + got[:, :far, :, piece].astype(F32)).astype(BF16)
-        for piece in pieces
-    ]
+    border = channels * 5 // 8
+    lon_bits = [("lon", 1, bit) for bit in bits_of("lon")[2:]]
+    lat_bits = [("lat", 2, bit) for bit in bits_of("lat")]
+
+    def split_lat(x):
+        if x.shape[2] != n_lat:
+            x = x.reshape(x.shape[0], x.shape[1], x.shape[3], n_lat, -1).transpose(0, 1, 3, 2, 4)
+        return x
+
+    def pair(lons, piece, last=None):
+        a, b = (kept, got) if last is None else (after(kept, last), after(got, last))
+        return split_lat(a[:, lons, :, piece].astype(F32) + b[:, lons, :, piece].astype(F32))
+
+    def fold(mine, sent, axis, bit, last):
+        return after(mine, last) + after(swap(sent, axis, bit), last).astype(F32)
+
+    first, second = slice(0, border), slice(border, channels)
+    near_lons, far_lons = slice(far, 2 * far), slice(0, far)
+    far_first = pair(far_lons, first).astype(BF16)
+    got_first = swap(far_first, "lon", 2)
+    cut_b = halves(pair(slice(0, 2 * far), second), *lat_bits[0])
     d_tail, d_head = end_rows(
-        d_conv[:3], d_conv[rows - 3 :], after(d_left, far_sums[0]), after(d_right, far_sums[0])
+        d_conv[:3], d_conv[rows - 3 :],
+        after(d_left, far_first, cut_b[1]), after(d_right, far_first, cut_b[1]),
     )
     d_top, d_bot = end_halo(d_tail, d_head)
-    steps = [("lon", 1, bit) for bit in bits_of("lon")[2:]] + [("lat", 2, bit) for bit in bits_of("lat")]
-    got_far, owned, cut = [swap(far_sums[0], "lon", 2), None], [None, None], [None, None]
-
-    def begin(index, last):
-        here = pieces[index]
-        x = after(kept, last)[:, far:, :, here].astype(F32) + after(got, last)[:, far:, :, here].astype(F32)
-        x = x + after(got_far[index], last).astype(F32)
-        if x.shape[2] != n_lat:
-            x = x.reshape(2, far, x.shape[3], n_lat, -1).transpose(0, 1, 3, 2, 4)
-        cut[index] = halves(x, *steps[0])
-
-    def advance(index, step, last, came=None):
-        axis, dim, bit = steps[step]
-        mine, sent = cut[index]
-        if came is None:
-            came = after(swap(sent, axis, bit), last)
-        owned[index] = after(mine, last) + came.astype(F32)
-        if step + 1 < len(steps):
-            cut[index] = halves(owned[index], *steps[step + 1])
+    for (axis, _, bit), follow in zip(lat_bits[:-1], lat_bits[1:]):
+        cut_b = halves(fold(*cut_b, axis, bit, d_head), *follow)
 
     def pack(sent, small):
-        high = lax.reduce_precision(small, 8, 7)
-        low = lax.reduce_precision(small - high, 8, 7)
-        flat = [x.astype(BF16).reshape(-1, LANES) for x in (sent, high, low)]
-        return jnp.concatenate(flat), high + low
-
-    def ride(load, small, shape, axis, bit, last):
+        return jnp.concatenate([sent.reshape(-1, LANES), small.astype(BF16).reshape(-1, LANES)])
+
+    def ride(load, sent, small, axis, bit, last):
         came = after(swap(load, axis, bit), last)
-        size, more = math.prod(shape) // LANES, small.size // LANES
-        both = came[size : size + more].astype(F32) + came[size + more :].astype(F32)
-        return came[:size].reshape(shape), after(small, last) + both.reshape(small.shape)
+        size = sent.size // LANES
+        own = after(lax.reduce_precision(small, 8, 7), last)
+        return came[:size].reshape(sent.shape).astype(F32), own + came[size:].astype(F32).reshape(small.shape)
 
     small = filter_grad(
-        after(fields, d_tail, d_head, far_sums[0]), mask, left, right, top, bot, d_conv, sums, g_bi
-    )
-    begin(0, small)
-    for step in range(len(steps) - 2):
-        advance(0, step, small)
+        after(fields, d_tail, d_head, far_first, cut_b[1]),
+        mask, left, right, top, bot, d_conv, sums, g_bi,
+    )
+    small = small + swap(small, "lon", 1)
+    whole = pair(near_lons, first, small) + after(got_first, small).astype(F32)
     back = (d_left, d_right, d_top, d_bot, kernel, mask, cotangent)
-    grad_fields = input_grad(after(d_conv, small, cut[0][1]), *back, 0, 4)
-    small = after(small, grad_fields) + after(swap(small, "lon", 1), grad_fields)
-    advance(0, len(steps) - 2, grad_fields)
-    load, small = pack(far_sums[1], small)
-    grad_fields = input_grad(after(d_conv, load, cut[0][1]), *back, 1, 4, grad_fields)
-    got_far[1], small = ride(load, small, far_sums[1].shape, "lon", 2, grad_fields)
-    begin(1, grad_fields)
-    advance(0, len(steps) - 1, grad_fields)
-    for step, (axis, _, bit) in enumerate(steps):
-        shape = cut[1][1].shape
-        load, small = pack(cut[1][1], small)
-        if step >= len(steps) - 2:
-            part = step + 4 - len(steps)
-            grad_fields = input_grad(after(d_conv, load), *back, part, 4, grad_fields)
-        came, small = ride(load, small, shape, axis, bit, grad_fields)
-        advance(1, step, grad_fields, came)
+    grad_fields, block = None, 0
+    steps = lon_bits + lat_bits
+    for index, (axis, dim, bit) in enumerate(steps):
+        mine, sent = halves(whole, axis, dim, bit)
+        load = pack(sent, small)
+        last = load
+        if index >= len(steps) - 2:
+            count = 2 if grad_fields is None else 1
+            last = grad_fields = input_grad(after(d_conv, load), *back, block, count, grad_fields)
+            block += count
+        came, small = ride(load, sent, small, axis, bit, last)
+        whole = after(mine, last) + came
+    whole_b = fold(*cut_b, lat_bits[-1][0], lat_bits[-1][2], load)
+    far_second = whole_b[:, far_lons].astype(BF16)
+    load = pack(far_second, small)
+    last = grad_fields = input_grad(after(d_conv, load), *back, block, 1, grad_fields)
+    came, small = ride(load, far_second, small, "lon", 2, last)
+    whole_b = after(whole_b, last)[:, near_lons] + came
+    for axis, dim, bit in lon_bits:
+        whole_b = fold(*halves(whole_b, axis, dim, bit), axis, bit, last)
+    owned = (whole, whole_b)
     grad_w = jnp.concatenate([x[:, 0, 0] for x in owned], axis=1)
     small = small.transpose(1, 0, 2).reshape(8, 8, channels)
     return (

time: 131 us -> 131 us (level)
    pallas_call x4 -> x3, Pallas kernels: 16.5 us -> 15.2 us  [input_grad(): pl.pallas_call(functools.partial(input_grad_kernel, first, parts), grid=(...]
    unnamed x23 -> x21, local copies, waits for them, and re-layouts: 3.43 us -> 3.43 us
  transfers between devices with their start and end apart: 16 -> 16, of which waited for: 6 -> 5; matrix products, arithmetic and copies ran while one was open for 6% -> 6% of each run, Pallas kernels for 30% -> 29%
where the time goes in v8:
time: 131 us; the launch traced here: 130 us
  Pallas kernels  72 us (55%)
  starting transfers between devices  26.7 us (20%)
  waiting for transfers between devices  13.5 us (10%)
  other arithmetic  8.81 us (7%)
  local copies, waits for them, and re-layouts  8.22 us (6%)
    pallas_call x1, Pallas kernels, expand(): pl.pallas_call(expand_kernel, grid_spec=pltpu.PrefetchScalarGridSpec(num_...  34.5 us
    pallas_call x3, Pallas kernels, input_grad(): pl.pallas_call(functools.partial(input_grad_kernel, first, parts), grid=(...  15.2 us
    ppermute x8, waiting for transfers between devices, swap(): return lax.ppermute(values, axis, [(i, i ^ bit) for i in range(count)])  13.5 us
    ppermute x4, starting transfers between devices, end_halo(): return (lax.ppermute(tail, 'lat', ahead), lax.ppermute(head, 'lat', back))  11.5 us
    ppermute x8, starting transfers between devices, swap(): return lax.ppermute(values, axis, [(i, i ^ bit) for i in range(count)])  11 us
    pallas_call x1, Pallas kernels, filter_grad(): pl.pallas_call(filter_grad_kernel, out_shape=jax.ShapeDtypeStruct((channe...  10.6 us
    pallas_call x1, Pallas kernels, conv_side(): pl.pallas_call(conv_side_kernel, out_shape=jax.ShapeDtypeStruct((rows, 16...  5.95 us
    pallas_call x1, Pallas kernels, conv_inner(): pl.pallas_call(conv_inner_kernel, out_shape=[jax.ShapeDtypeStruct((rows,...  5.81 us
  transfers between devices with their start and end apart: 16, of which 5 were waited for; matrix products, arithmetic and copies ran while one was open for 6% of the time, Pallas kernels for 29%

profile of v8, /device:TPU:0, one launch (start us, length us, event | category | flops | bytes accessed | tf_op | source)
XLA Modules:
  0.0 130.4 jit_solution(6943813714466259353)
XLA Ops:
  1.5 1.2 slice_multiply_fusion
  3.2 2.0 %collective-permute-start.1 = (bf16[32,3,512]{2,1,0:T(4,128)(2,1)S(1)}, bf16[32,3,512]{2,1,0:T(4,128)(2,1)S(1)}, u32[]{:S(2)}, u32[]{:S(2)}) collective-permute-start(bf16[32,3,512]{2,1,0:T(4,128)(2,1)S(1)} %get-tuple-element.90), channel_id=1, source_target_pairs={{4,0},{8,4},{12,8},{0,12},{5,1},{9,5},{13,9},{1,13},{6,2},{10,6},{... | collective-permute-start | bytes 294920 | tf_op jit(solution)/shard_map/ppermute | solution.py:509
  6.3 5.8 %conv_inner.1 = (f32[32,16,512]{2,1,0:T(8,128)}, bf16[3,32,512]{2,1,0:T(8,128)(2,1)}, bf16[3,32,512]{2,1,0:T(8,128)(2,1)}) custom-call(bf16[32,32,512]{2,1,0:T(8,128)(2,1)} %f_ref.4, f32[32,32,128]{2,1,0:T(8,128)} %broadcast_in_dim.4.m_ref, f32[7,7,512]{2,1,0:T(8,128)} %k_ref.11), custom_call_target="tpu_custom_call" | custom-call | flops 4600000000 | bytes 14400000 | tf_op jit(solution)/shard_map/conv_inner/pallas_call | solution.py:109
  13.8 4.2 %collective-permute-start.2 = (bf16[3,38,512]{2,1,0:T(8,128)(2,1)S(1)}, bf16[3,38,512]{2,1,0:T(8,128)(2,1)S(1)}, u32[]{:S(2)}, u32[]{:S(2)}) collective-permute-start(bf16[3,38,512]{2,1,0:T(8,128)(2,1)S(1)} %pad_maximum_fusion.4), channel_id=1, source_target_pairs={{0,1},{1,2},{2,3},{4,5},{5,6},{6,7},{8,9},{9,10},{10,11},{12,13},{... | collective-permute-start | bytes 350216 | tf_op jit(solution)/shard_map/ppermute | solution.py:524
  18.9 1.3 collective-permute-start.3
  20.2 5.9 %conv_side.1.side_ref = f32[32,16,512]{2,1,0:T(8,128)} custom-call(bf16[32,32,512]{2,1,0:T(8,128)(2,1)} %f_ref.4, f32[32,32,128]{2,1,0:T(8,128)} %broadcast_in_dim.4.m_ref, f32[7,7,512]{2,1,0:T(8,128)} %k_ref.11, bf16[32,3,512]{2,1,0:T(4,128)(2,1)} %copy-done.1, bf16[32,3,512]{2,1,0:T(4,128)(2,1)} %copy-done.2), custom_call_target="tpu_custom_call" | custom-call | flops 4600000000 | bytes 14400000 | tf_op jit(solution)/shard_map/conv_side/pallas_call | solution.py:125
  26.9 34.5 %expand.1 = (bf16[1024,512]{1,0:T(8,128)(2,1)}, bf16[1024,512]{1,0:T(8,128)(2,1)}, f32[4,8,512]{2,1,0:T(8,128)}, f32[1,2048]{1,0:T(1,128)}, bf16[2,2,4,512,128]{...) custom-call(s32[4]{0:T(128)} %pad_add_fusion.order_ref, f32[32,16,512]{2,1,0:T(8,128)} %get-tuple-element.41.inner_ref, ...), custom_call_target="tpu_custom_call" | custom-call | flops 23000000512 | bytes 72000000 | tf_op jit(solution)/shard_map/expand/pallas_call | solution.py:317
  62.6 1.6 %collective-permute-start.6 = (bf16[32,3,512]{2,1,0:T(4,128)(2,1)S(1)}, bf16[32,3,512]{2,1,0:T(4,128)(2,1)S(1)}, u32[]{:S(2)}, u32[]{:S(2)}) collective-permute-start(bf16[32,3,512]{2,1,0:T(4,128)(2,1)S(1)} %get-tuple-element.89), channel_id=1, source_target_pairs={{4,0},{8,4},{12,8},{0,12},{5,1},{9,5},{13,9},{1,13},{6,2},{10,6},{... | collective-permute-start | bytes 294920 | tf_op jit(solution)/shard_map/ppermute | solution.py:509
  65.8 1.3 %convert_add_fusion = f32[2,2,4,192,128]{4,3,2,1,0:T(8,128)S(1)} fusion(bf16[2,2,4,512,128]{4,3,2,1,0:T(8,128)(2,1)S(1)} %collective-permute-done.4, bf16[2,2,4,512,128]{4,3,2,1,0:T(8,128)(2,1)} %get-tuple-element.55), kind=kLoop, calls=%fused_computation | loop fusion | flops 1179648 | bytes 3145728 | tf_op jit(solution)/shard_map/add | solution.py:580
  67.3 2.7 %collective-permute-start.7 = (bf16[2,2,2,192,128]{4,3,0,1,2:T(8,128)(2,1)S(1)}, bf16[2,2,2,192,128]{4,3,0,1,2:T(8,128)(2,1)S(1)}, u32[]{:S(2)}, u32[]{:S(2)}) collective-permute-start(bf16[2,2,2,192,128]{4,3,0,1,2:T(8,128)(2,1)S(1)} %fusion.1), channel_id=1, source_target_pairs={{0,1},{1,0},{2,3},{3,2},{4,5},{5,4},{6,7},{7,6},{8,9},{9,8},{10,11... | collective-permute-start | bytes 1179656 | tf_op jit(solution)/shard_map/ppermute | solution.py:485
  70.2 1.6 %collective-permute-start.9 = (bf16[2,1,4,320,128]{4,3,2,1,0:T(8,128)(2,1)S(1)}, bf16[2,1,4,320,128]{4,3,2,1,0:T(8,128)(2,1)S(1)}, u32[]{:S(2)}, u32[]{:S(2)}) collective-permute-start(bf16[2,1,4,320,128]{4,3,2,1,0:T(8,128)(2,1)S(1)} %add_convert_fusion), channel_id=1, source_target_pairs={{0,8},{4,12},{8,0},{12,4},{1,9},{5,13},{9,1},{13,5},{2,10},{6,14},... | collective-permute-start | bytes 1966088 | tf_op jit(solution)/shard_map/ppermute | solution.py:485
  71.9 1.3 collective-permute-start.11
  73.4 4.7 %collective-permute-start.10 = (bf16[3,38,512]{2,1,0:T(8,128)(2,1)S(1)}, bf16[3,38,512]{2,1,0:T(8,128)(2,1)S(1)}, u32[]{:S(2)}, u32[]{:S(2)}) collective-permute-start(bf16[3,38,512]{2,1,0:T(8,128)(2,1)S(1)} %pad_maximum_fusion.7), channel_id=1, source_target_pairs={{0,1},{1,2},{2,3},{4,5},{5,6},{6,7},{8,9},{9,10},{10,11},{12,13},{... | collective-permute-start | bytes 350216 | tf_op jit(solution)/shard_map/ppermute | solution.py:524
  78.1 1.8 %collective-permute-done.7 = bf16[2,2,2,192,128]{4,3,0,1,2:T(8,128)(2,1)S(1)} collective-permute-done((bf16[2,2,2,192,128]{4,3,0,1,2:T(8,128)(2,1)S(1)}, bf16[2,2,2,192,128]{4,3,0,1,2:T(8,128)(2,1)S(1)}, u32[]{:S(2)}, u32[]{:S(2)}) %collective-permute-start.7) | collective-permute-done | bytes 393248 | tf_op jit(solution)/shard_map/ppermute | solution.py:485
  80.1 3.1 %collective-permute-start.13 = (bf16[2,2,1,192,128]{4,3,0,2,1:T(8,128)(2,1)S(1)}, bf16[2,2,1,192,128]{4,3,0,2,1:T(8,128)(2,1)S(1)}, u32[]{:S(2)}, u32[]{:S(2)}) collective-permute-start(bf16[2,2,1,192,128]{4,3,0,2,1:T(8,128)(2,1)S(1)} %fusion.6), channel_id=1, source_target_pairs={{0,2},{1,3},{2,0},{3,1},{4,6},{5,7},{6,4},{7,5},{8,10},{9,11},{10,... | collective-permute-start | bytes 589832 | tf_op jit(solution)/shard_map/ppermute | solution.py:485
  83.2 10.6 %filter_grad.1 = f32[4,64,128]{2,1,0:T(8,128)} custom-call(bf16[32,32,512]{2,1,0:T(8,128)(2,1)} %f_ref.4, f32[32,32,128]{2,1,0:T(8,128)} %broadcast_in_dim.4.m_ref, bf16[32,3,512]{2,1,0:T(4,128)(2,1)} %copy-done.1, bf16[32,3,512]{2,1,0:T(4,128)(2,1)} %copy-done.2, bf16[3,38,512]{2,1,0:T(8,128)(2,1)} %copy-done.5, bf16[3,38,512]{2,1,0:T(8,128)(2,1)} %copy-done.6, ...), custom_call_target="tpu_custom_call" | custom-call | flops 4600000000 | bytes 14400000 | tf_op jit(solution)/shard_map/filter_grad/pallas_call | solution.py:414
  93.9 1.5 %collective-permute-done.8 = f32[4,64,128]{2,1,0:T(8,128)S(1)} collective-permute-done((f32[4,64,128]{2,1,0:T(8,128)}, f32[4,64,128]{2,1,0:T(8,128)S(1)}, u32[]{:S(2)}, u32[]{:S(2)}) %collective-permute-start.8) | collective-permute-done | bytes 131104 | tf_op jit(solution)/shard_map/ppermute | solution.py:485
  96.7 1.7 %collective-permute-start.12 = (bf16[1536,128]{1,0:T(8,128)(2,1)S(1)}, bf16[1536,128]{1,0:T(8,128)(2,1)S(1)}, u32[]{:S(2)}, u32[]{:S(2)}) collective-permute-start(bf16[1536,128]{1,0:T(8,128)(2,1)S(1)} %pad_maximum_fusion), channel_id=1, source_target_pairs={{0,1},{1,0},{2,3},{3,2},{4,5},{5,4},{6,7},{7,6},{8,9},{9,8},{10,11... | collective-permute-start | bytes 1179656 | tf_op jit(solution)/shard_map/ppermute | solution.py:485
  99.7 7.0 %input_grad.3.rest_0_ = bf16[32,32,512]{2,1,0:T(8,128)(2,1)} custom-call(bf16[32,32,512]{2,1,0:T(8,128)(2,1)} %bitcast.109, bf16[32,3,512]{2,1,0:T(4,128)(2,1)} %copy-done.4, bf16[32,3,512]{2,1,0:T(4,128)(2,1)} %copy-done.3, bf16[3,38,512]{2,1,0:T(8,128)(2,1)} %copy-done.8, bf16[3,38,512]{2,1,0:T(8,128)(2,1)} %copy-done.7, f32[7,7,512]{2,1,0:T(8,128)} %k_ref.11, ...), custom_call_target="tpu_custom_call" | custom-call | flops 4600000000 | bytes 14400000 | tf_op jit(solution)/shard_map/input_grad/pallas_call | solution.py:464
  106.6 1.3 %collective-permute-done.12 = bf16[1536,128]{1,0:T(8,128)(2,1)S(1)} collective-permute-done((bf16[1536,128]{1,0:T(8,128)(2,1)S(1)}, bf16[1536,128]{1,0:T(8,128)(2,1)S(1)}, u32[]{:S(2)}, u32[]{:S(2)}) %collective-permute-start.12) | collective-permute-done | bytes 393248 | tf_op jit(solution)/shard_map/ppermute | solution.py:485
  108.4 4.1 %input_grad.4.rest_0_ = bf16[32,32,512]{2,1,0:T(8,128)(2,1)} custom-call(bf16[32,32,512]{2,1,0:T(8,128)(2,1)} %bitcast.110, bf16[32,3,512]{2,1,0:T(4,128)(2,1)} %copy-done.4, bf16[32,3,512]{2,1,0:T(4,128)(2,1)} %copy-done.3, bf16[3,38,512]{2,1,0:T(8,128)(2,1)} %copy-done.8, bf16[3,38,512]{2,1,0:T(8,128)(2,1)} %copy-done.7, ...), custom_call_target="tpu_custom_call", output_to_operand_aliasing={{}: (8, {})} | custom-call | flops 4600000000 | bytes 14400000 | tf_op jit(solution)/shard_map/input_grad/pallas_call | solution.py:464
  112.7 8.2 %collective-permute-done.14 = bf16[896,128]{1,0:T(8,128)(2,1)S(1)} collective-permute-done((bf16[896,128]{1,0:T(8,128)(2,1)S(1)}, bf16[896,128]{1,0:T(8,128)(2,1)S(1)}, u32[]{:S(2)}, u32[]{:S(2)}) %collective-permute-start.14) | collective-permute-done | bytes 229408 | tf_op jit(solution)/shard_map/ppermute | solution.py:485
  121.0 1.6 %collective-permute-start.15 = (bf16[640,128]{1,0:T(8,128)(2,1)S(1)}, bf16[640,128]{1,0:T(8,128)(2,1)S(1)}, u32[]{:S(2)}, u32[]{:S(2)}) collective-permute-start(bf16[640,128]{1,0:T(8,128)(2,1)S(1)} %pad_maximum_fusion.3), channel_id=1, source_target_pairs={{0,8},{4,12},{8,0},{12,4},{1,9},{5,13},{9,1},{13,5},{2,10},{6,14},... | collective-permute-start | bytes 491528 | tf_op jit(solution)/shard_map/ppermute | solution.py:485
  122.5 4.1 %input_grad.5 = bf16[32,32,512]{2,1,0:T(8,128)(2,1)} custom-call(bf16[32,32,512]{2,1,0:T(8,128)(2,1)} %bitcast.111, bf16[32,3,512]{2,1,0:T(4,128)(2,1)} %copy-done.4, bf16[32,3,512]{2,1,0:T(4,128)(2,1)} %copy-done.3, bf16[3,38,512]{2,1,0:T(8,128)(2,1)} %copy-done.8, bf16[3,38,512]{2,1,0:T(8,128)(2,1)} %copy-done.7, ...), custom_call_target="tpu_custom_call", output_to_operand_aliasing={{}: (8, {})} | custom-call | flops 4600000000 | bytes 14400000 | tf_op jit(solution)/shard_map/input_grad/pallas_call | solution.py:464
  (87 shorter events, 15.9 us)
Async XLA Ops:
  2.7 10.0 %collective-permute-start = (bf16[32,3,512]{2,1,0:T(4,128)(2,1)S(1)}, bf16[32,3,512]{2,1,0:T(4,128)(2,1)S(1)}, u32[]{:S(2)}, u32[]{:S(2)}) collective-permute-start(bf16[32,3,512]{2,1,0:T(4,128)(2,1)S(1)} %get-tuple-element.91), channel_id=1, source_target_pairs={{0,4},{4,8},{8,12},{12,0},{1,5},{5,9},{9,13},{13,1},{2,6},{6,10},{... | collective-permute-start | bytes 294920 | tf_op jit(solution)/shard_map/ppermute | solution.py:509
  3.2 9.5 %collective-permute-start.1 = (bf16[32,3,512]{2,1,0:T(4,128)(2,1)S(1)}, bf16[32,3,512]{2,1,0:T(4,128)(2,1)S(1)}, u32[]{:S(2)}, u32[]{:S(2)}) collective-permute-start(bf16[32,3,512]{2,1,0:T(4,128)(2,1)S(1)} %get-tuple-element.90), channel_id=1, source_target_pairs={{4,0},{8,4},{12,8},{0,12},{5,1},{9,5},{13,9},{1,13},{6,2},{10,6},{... | collective-permute-start | bytes 294920 | tf_op jit(solution)/shard_map/ppermute | solution.py:509
  12.7 7.5 %copy-start.1 = (bf16[32,3,512]{2,1,0:T(4,128)(2,1)}, bf16[32,3,512]{2,1,0:T(4,128)(2,1)S(1)}, u32[]{:S(2)}) copy-start(bf16[32,3,512]{2,1,0:T(4,128)(2,1)S(1)} %collective-permute-done.l_ref) | copy-start | bytes 294916
  12.7 7.5 %copy-start.2 = (bf16[32,3,512]{2,1,0:T(4,128)(2,1)}, bf16[32,3,512]{2,1,0:T(4,128)(2,1)S(1)}, u32[]{:S(2)}) copy-start(bf16[32,3,512]{2,1,0:T(4,128)(2,1)S(1)} %collective-permute-done.1.r_ref) | copy-start | bytes 294916
  13.8 12.4 %collective-permute-start.2 = (bf16[3,38,512]{2,1,0:T(8,128)(2,1)S(1)}, bf16[3,38,512]{2,1,0:T(8,128)(2,1)S(1)}, u32[]{:S(2)}, u32[]{:S(2)}) collective-permute-start(bf16[3,38,512]{2,1,0:T(8,128)(2,1)S(1)} %pad_maximum_fusion.4), channel_id=1, source_target_pairs={{0,1},{1,2},{2,3},{4,5},{5,6},{6,7},{8,9},{9,10},{10,11},{12,13},{... | collective-permute-start | bytes 350216 | tf_op jit(solution)/shard_map/ppermute | solution.py:524
  18.9 7.3 %collective-permute-start.3 = (bf16[3,38,512]{2,1,0:T(8,128)(2,1)S(1)}, bf16[3,38,512]{2,1,0:T(8,128)(2,1)S(1)}, u32[]{:S(2)}, u32[]{:S(2)}) collective-permute-start(bf16[3,38,512]{2,1,0:T(8,128)(2,1)S(1)} %pad_maximum_fusion.5), channel_id=1, source_target_pairs={{1,0},{2,1},{3,2},{5,4},{6,5},{7,6},{9,8},{10,9},{11,10},{13,12},{... | collective-permute-start | bytes 350216 | tf_op jit(solution)/shard_map/ppermute | solution.py:524
  26.2 0.7 copy-start.5
  26.2 0.7 copy-start.6
  61.4 4.4 %collective-permute-start.4 = (bf16[2,2,4,512,128]{4,3,2,1,0:T(8,128)(2,1)}, bf16[2,2,4,512,128]{4,3,2,1,0:T(8,128)(2,1)S(1)}, u32[]{:S(2)}, u32[]{:S(2)}) collective-permute-start(bf16[2,2,4,512,128]{4,3,2,1,0:T(8,128)(2,1)} %get-tuple-element.47), channel_id=1, source_target_pairs={{0,4},{4,0},{8,12},{12,8},{1,5},{5,1},{9,13},{13,9},{2,6},{6,2},{1... | collective-permute-start | bytes 6291464 | tf_op jit(solution)/shard_map/ppermute | solution.py:485
  62.6 9.2 %collective-permute-start.6 = (bf16[32,3,512]{2,1,0:T(4,128)(2,1)S(1)}, bf16[32,3,512]{2,1,0:T(4,128)(2,1)S(1)}, u32[]{:S(2)}, u32[]{:S(2)}) collective-permute-start(bf16[32,3,512]{2,1,0:T(4,128)(2,1)S(1)} %get-tuple-element.89), channel_id=1, source_target_pairs={{4,0},{8,4},{12,8},{0,12},{5,1},{9,5},{13,9},{1,13},{6,2},{10,6},{... | collective-permute-start | bytes 294920 | tf_op jit(solution)/shard_map/ppermute | solution.py:509
  64.3 7.6 %collective-permute-start.5 = (bf16[32,3,512]{2,1,0:T(4,128)(2,1)S(1)}, bf16[32,3,512]{2,1,0:T(4,128)(2,1)S(1)}, u32[]{:S(2)}, u32[]{:S(2)}) collective-permute-start(bf16[32,3,512]{2,1,0:T(4,128)(2,1)S(1)} %get-tuple-element.88), channel_id=1, source_target_pairs={{0,4},{4,8},{8,12},{12,0},{1,5},{5,9},{9,13},{13,1},{2,6},{6,10},{... | collective-permute-start | bytes 294920 | tf_op jit(solution)/shard_map/ppermute | solution.py:509
  67.1 2.9 %copy-start = (bf16[2,2,4,512,128]{4,3,2,1,0:T(8,128)(2,1)S(1)}, bf16[2,2,4,512,128]{4,3,2,1,0:T(8,128)(2,1)}, u32[]{:S(2)}) copy-start(bf16[2,2,4,512,128]{4,3,2,1,0:T(8,128)(2,1)} %get-tuple-element.55) | copy-start | bytes 6291460
  67.3 12.6 %collective-permute-start.7 = (bf16[2,2,2,192,128]{4,3,0,1,2:T(8,128)(2,1)S(1)}, bf16[2,2,2,192,128]{4,3,0,1,2:T(8,128)(2,1)S(1)}, u32[]{:S(2)}, u32[]{:S(2)}) collective-permute-start(bf16[2,2,2,192,128]{4,3,0,1,2:T(8,128)(2,1)S(1)} %fusion.1), channel_id=1, source_target_pairs={{0,1},{1,0},{2,3},{3,2},{4,5},{5,4},{6,7},{7,6},{8,9},{9,8},{10,11... | collective-permute-start | bytes 1179656 | tf_op jit(solution)/shard_map/ppermute | solution.py:485
  70.2 26.1 %collective-permute-start.9 = (bf16[2,1,4,320,128]{4,3,2,1,0:T(8,128)(2,1)S(1)}, bf16[2,1,4,320,128]{4,3,2,1,0:T(8,128)(2,1)S(1)}, u32[]{:S(2)}, u32[]{:S(2)}) collective-permute-start(bf16[2,1,4,320,128]{4,3,2,1,0:T(8,128)(2,1)S(1)} %add_convert_fusion), channel_id=1, source_target_pairs={{0,8},{4,12},{8,0},{12,4},{1,9},{5,13},{9,1},{13,5},{2,10},{6,14},... | collective-permute-start | bytes 1966088 | tf_op jit(solution)/shard_map/ppermute | solution.py:485
  71.8 8.2 %copy-start.3 = (bf16[32,3,512]{2,1,0:T(4,128)(2,1)}, bf16[32,3,512]{2,1,0:T(4,128)(2,1)S(1)}, u32[]{:S(2)}) copy-start(bf16[32,3,512]{2,1,0:T(4,128)(2,1)S(1)} %collective-permute-done.6.r_ref) | copy-start | bytes 294916
  71.8 8.2 %copy-start.4 = (bf16[32,3,512]{2,1,0:T(4,128)(2,1)}, bf16[32,3,512]{2,1,0:T(4,128)(2,1)S(1)}, u32[]{:S(2)}) copy-start(bf16[32,3,512]{2,1,0:T(4,128)(2,1)S(1)} %collective-permute-done.5.l_ref) | copy-start | bytes 294916
  71.9 26.5 %collective-permute-start.11 = (bf16[3,38,512]{2,1,0:T(8,128)(2,1)S(1)}, bf16[3,38,512]{2,1,0:T(8,128)(2,1)S(1)}, u32[]{:S(2)}, u32[]{:S(2)}) collective-permute-start(bf16[3,38,512]{2,1,0:T(8,128)(2,1)S(1)} %pad_maximum_fusion.6), channel_id=1, source_target_pairs={{1,0},{2,1},{3,2},{5,4},{6,5},{7,6},{9,8},{10,9},{11,10},{13,12},{... | collective-permute-start | bytes 350216 | tf_op jit(solution)/shard_map/ppermute | solution.py:524
  73.4 25.0 %collective-permute-start.10 = (bf16[3,38,512]{2,1,0:T(8,128)(2,1)S(1)}, bf16[3,38,512]{2,1,0:T(8,128)(2,1)S(1)}, u32[]{:S(2)}, u32[]{:S(2)}) collective-permute-start(bf16[3,38,512]{2,1,0:T(8,128)(2,1)S(1)} %pad_maximum_fusion.7), channel_id=1, source_target_pairs={{0,1},{1,2},{2,3},{4,5},{5,6},{6,7},{8,9},{9,10},{10,11},{12,13},{... | collective-permute-start | bytes 350216 | tf_op jit(solution)/shard_map/ppermute | solution.py:524
  80.1 32.5 %collective-permute-start.13 = (bf16[2,2,1,192,128]{4,3,0,2,1:T(8,128)(2,1)S(1)}, bf16[2,2,1,192,128]{4,3,0,2,1:T(8,128)(2,1)S(1)}, u32[]{:S(2)}, u32[]{:S(2)}) collective-permute-start(bf16[2,2,1,192,128]{4,3,0,2,1:T(8,128)(2,1)S(1)} %fusion.6), channel_id=1, source_target_pairs={{0,2},{1,3},{2,0},{3,1},{4,6},{5,7},{6,4},{7,5},{8,10},{9,11},{10,... | collective-permute-start | bytes 589832 | tf_op jit(solution)/shard_map/ppermute | solution.py:485
  93.8 1.6 %collective-permute-start.8 = (f32[4,64,128]{2,1,0:T(8,128)}, f32[4,64,128]{2,1,0:T(8,128)S(1)}, u32[]{:S(2)}, u32[]{:S(2)}) collective-permute-start(f32[4,64,128]{2,1,0:T(8,128)} %filter_grad.1), channel_id=1, source_target_pairs={{0,4},{4,0},{8,12},{12,8},{1,5},{5,1},{9,13},{13,9},{2,6},{6,2},{1... | collective-permute-start | bytes 393224 | tf_op jit(solution)/shard_map/ppermute | solution.py:485
  96.7 11.2 %collective-permute-start.12 = (bf16[1536,128]{1,0:T(8,128)(2,1)S(1)}, bf16[1536,128]{1,0:T(8,128)(2,1)S(1)}, u32[]{:S(2)}, u32[]{:S(2)}) collective-permute-start(bf16[1536,128]{1,0:T(8,128)(2,1)S(1)} %pad_maximum_fusion), channel_id=1, source_target_pairs={{0,1},{1,0},{2,3},{3,2},{4,5},{5,4},{6,7},{7,6},{8,9},{9,8},{10,11... | collective-permute-start | bytes 1179656 | tf_op jit(solution)/shard_map/ppermute | solution.py:485
  98.4 0.6 copy-start.7
  108.2 12.7 %collective-permute-start.14 = (bf16[896,128]{1,0:T(8,128)(2,1)S(1)}, bf16[896,128]{1,0:T(8,128)(2,1)S(1)}, u32[]{:S(2)}, u32[]{:S(2)}) collective-permute-start(bf16[896,128]{1,0:T(8,128)(2,1)S(1)} %pad_maximum_fusion.2), channel_id=1, source_target_pairs={{0,2},{1,3},{2,0},{3,1},{4,6},{5,7},{6,4},{7,5},{8,10},{9,11},{10,... | collective-permute-start | bytes 688136 | tf_op jit(solution)/shard_map/ppermute | solution.py:485
  121.0 5.7 %collective-permute-start.15 = (bf16[640,128]{1,0:T(8,128)(2,1)S(1)}, bf16[640,128]{1,0:T(8,128)(2,1)S(1)}, u32[]{:S(2)}, u32[]{:S(2)}) collective-permute-start(bf16[640,128]{1,0:T(8,128)(2,1)S(1)} %pad_maximum_fusion.3), channel_id=1, source_target_pairs={{0,8},{4,12},{8,0},{12,4},{1,9},{5,13},{9,1},{13,5},{2,10},{6,14},... | collective-permute-start | bytes 491528 | tf_op jit(solution)/shard_map/ppermute | solution.py:485
  (1 other events, 0.6 us)

commit v9 on v8

--- a/solution.py
+++ b/solution.py
@@ -72,66 +72,6 @@
     return sums
 
 
-def conv_inner_kernel(f_ref, m_ref, k_ref, o_ref, head_ref, tail_ref, window):
-    rows, cols, channels = f_ref.shape
-
-    def block(lanes):
-        masked = f_ref[:, :, lanes].astype(F32) * m_ref[...]
-        window[:, 8 : 8 + cols, :] = masked
-        head_ref[:, :, lanes] = masked[:3].astype(BF16)
-        tail_ref[:, :, lanes] = masked[rows - 3 :].astype(BF16)
-        for start in range(8, cols - 8, 8):
-            sums = band_conv(window, k_ref, lanes, (start,), rows, 0, False)
-            for row in range(rows):
-                o_ref[row, start - 8 : start, lanes] = sums[row, start]
-
-    each_lane_block(channels, block)
-
-
-def conv_side_kernel(f_ref, m_ref, k_ref, l_ref, r_ref, o_ref, window):
-    rows, cols, channels = f_ref.shape
-
-    def block(lanes):
-        window[:, 5:8, :] = l_ref[:, :, lanes].astype(F32)
-        window[:, 8 : 8 + cols, :] = f_ref[:, :, lanes].astype(F32) * m_ref[...]
-        window[:, 8 + cols : 11 + cols, :] = r_ref[:, :, lanes].astype(F32)
-        for at, start in ((0, 0), (8, cols - 8)):
-            sums = band_conv(window, k_ref, lanes, (start,), rows, 0, False)
-            for row in range(rows):
-                o_ref[row, at : at + 8, lanes] = sums[row, start]
-
-    each_lane_block(channels, block)
-
-
-def conv_inner(fields, mask, kernel):
-    rows, cols, channels = fields.shape
-    ends = (3, cols, channels)
-    return pl.pallas_call(
-        conv_inner_kernel,
-        out_shape=[
-            jax.ShapeDtypeStruct((rows, cols - 16, channels), F32),
-            jax.ShapeDtypeStruct(ends, BF16),
-            jax.ShapeDtypeStruct(ends, BF16),
-        ],
-        scratch_shapes=[pltpu.VMEM((rows, cols + 16, LANES), F32)],
-        compiler_params=params(56),
-        cost_estimate=estimate(4),
-        name="conv_inner",
-    )(fields, mask, kernel)
-
-
-def conv_side(fields, mask, kernel, left, right):
-    rows, cols, channels = fields.shape
-    return pl.pallas_call(
-        conv_side_kernel,
-        out_shape=jax.ShapeDtypeStruct((rows, 16, channels), F32),
-        scratch_shapes=[pltpu.VMEM((rows, cols + 16, LANES), F32)],
-        compiler_params=params(56),
-        cost_estimate=estimate(4),
-        name="conv_side",
-    )(fields, mask, kernel, left, right)
-
-
 def gelu_twice(x):
     root = math.sqrt(2.0 / math.pi)
     inner = root + (root * 0.044715) * (x * x)
@@ -144,74 +84,71 @@
 
 def expand_kernel(
     order_ref,
-    inner_ref, side_ref, top_ref, bot_ref, k_ref, gain_ref, bias_ref, scale_ref, bo_ref, m_ref, cot_ref, f_ref,
+    l_ref, r_ref, t_ref, b_ref, k_ref, gain_ref, bias_ref, scale_ref, bo_ref, m_ref, cot_ref, f_ref,
     wi_ref, bi_ref, wo_ref,
     dconv_ref, mixed_ref, sums_ref, gbi_ref, sent_ref, kept_ref,
-    conv, halo, inv_s, normed, normed_t, dbr, dbr_t, act, dpre, d_normed, branch, pre_s, dact_s,
+    window, conv, xhat_s, inv_s, normed, normed_t, dbr, dbr_t, act, dpre, d_normed, branch, pre_s, dact_s,
 ):
-    rows, cols, channels = conv.shape
+    rows, cols, channels = f_ref.shape
     cells = rows * cols
     strip = 16
     chunk = 128
     step_now = pl.program_id(0)
     wide = channels // LANES
 
-    def strips(body):
-        def some(index, _):
-            for more in range(4):
-                row = index * 4 + more
-                for at in range(0, cols, strip):
-                    body(row, at, pl.ds(pl.multiple_of(row * cols + at, strip), strip))
-            return 0
-
-        lax.fori_loop(0, rows // 4, some, 0)
+    def strips(body, sums):
+        def some(index, sums):
+            places = [
+                (2 * index + more, at, pl.ds(pl.multiple_of((2 * index + more) * cols + at, strip), strip))
+                for more in range(2)
+                for at in range(0, cols, strip)
+            ]
+            return body(places, sums)
+
+        return lax.fori_loop(0, rows // 2, some, sums)
+
+    def folded(values):
+        return sum(value[:SUB] + value[SUB:] for value in values)
+
+    def mean(values):
+        return [jnp.mean(value, axis=-1, keepdims=True) for value in values]
+
+    def ocean(places):
+        return [jnp.concatenate([m_ref[row, at : at + strip, :]] * wide, axis=1) for row, at, _ in places]
+
+    zero = jnp.zeros((SUB, channels), F32)
 
     @pl.when(step_now == 0)
     def _():
-        conv[:, 0:8, :] = side_ref[:, 0:8, :]
-        conv[:, 8 : cols - 8, :] = inner_ref[...]
-        conv[:, cols - 8 : cols, :] = side_ref[:, 8:16, :]
-        halo[0:3, 5 : 11 + cols, :] = top_ref[...].astype(F32)
-        halo[3:6, 5 : 11 + cols, :] = bot_ref[...].astype(F32)
-        for block in range(wide):
-            lanes = slice(block * LANES, (block + 1) * LANES)
-            for start in range(0, cols, 8):
-                outs = list(range(3)) + list(range(rows - 3, rows))
-                sums = {out: conv[out, start : start + 8, lanes] for out in outs}
-                for col_off in range(7):
-                    for src in range(6):
-                        lat = src - 3 if src < 3 else rows + src - 3
-                        offset = (5 + col_off) % SUB
-                        base = start + (5 + col_off) // SUB * SUB
-                        pair = halo[src, base : base + 2 * SUB, lanes]
-                        cell = pltpu.roll(pair, 2 * SUB - offset, axis=0)[:SUB] if offset else pair[:SUB]
-                        for out in outs:
-                            row_off = lat - out + 3
-                            if 0 <= row_off < 7:
-                                tap = k_ref[row_off, col_off : col_off + 1, lanes]
-                                sums[out] = sums[out] + tap * cell
-                for out in outs:
-                    conv[out, start : start + 8, lanes] = sums[out]
-        sums_ref[...] = jnp.zeros_like(sums_ref)
         branch[...] = jnp.zeros_like(branch)
         d_normed[...] = jnp.zeros_like(d_normed)
 
-        def standardize(row, at, here):
-            x = conv[row, at : at + strip, :]
-            mean = jnp.mean(x, axis=-1, keepdims=True)
-            centered = x - mean
-            var = jnp.mean(centered * centered, axis=-1, keepdims=True)
-            inv = lax.rsqrt(var + 1e-06)
-            xhat = centered * inv
-            conv[row, at : at + strip, :] = xhat
-            inv_s[here, :] = jnp.broadcast_to(inv, (strip, LANES))
-            normed[here, :] = (xhat * gain_ref[...] + bias_ref[...]).astype(BF16)
-            ocean = jnp.concatenate([m_ref[row, at : at + strip, :]] * wide, axis=1)
-            grad = ocean * (scale_ref[...] * cot_ref[here, :].astype(F32))
-            sums_ref[0] += grad[:SUB] + grad[SUB:]
-            dbr[here, :] = (0.5 * grad).astype(BF16)
-
-        strips(standardize)
+        def convolve(lanes):
+            fill_window(window, f_ref[:, :, lanes].astype(F32) * m_ref[...], l_ref, r_ref, t_ref, b_ref, lanes)
+            for start in range(0, cols, SUB):
+                sums = band_conv(window, k_ref, lanes, (start,), rows, 3, False)
+                for row in range(rows):
+                    conv[row, start : start + SUB, lanes] = sums[row, start]
+
+        each_lane_block(channels, convolve)
+
+        def standardize(places, total):
+            xs = [conv[row, at : at + strip, :] for row, at, _ in places]
+            centered = [x - average for x, average in zip(xs, mean(xs))]
+            invs = [lax.rsqrt(var + 1e-06) for var in mean([x * x for x in centered])]
+            xhats = [x * inv for x, inv in zip(centered, invs)]
+            grads = [
+                mask * (scale_ref[...] * cot_ref[here, :].astype(F32))
+                for mask, (_, _, here) in zip(ocean(places), places)
+            ]
+            for (_, _, here), xhat, inv, grad in zip(places, xhats, invs, grads):
+                xhat_s[here, :] = xhat
+                inv_s[here, :] = jnp.broadcast_to(inv, (strip, LANES))
+                normed[here, :] = (xhat * gain_ref[...] + bias_ref[...]).astype(BF16)
+                dbr[here, :] = (0.5 * grad).astype(BF16)
+            return total + folded(grads)
+
+        sums_ref[0] = strips(standardize, zero)
         for at in range(0, cells, chunk):
             here = slice(at, at + chunk)
             normed_t[:, here] = normed[here, :].T
@@ -274,39 +211,39 @@
 
     @pl.when(step_now == pl.num_programs(0) - 1)
     def _():
-        def norm_back(row, at, here):
-            cot = cot_ref[here, :].astype(F32)
-            ocean = jnp.concatenate([m_ref[row, at : at + strip, :]] * wide, axis=1)
-            ocean = ocean * (0.5 * branch[here, :] + bo_ref[...])
-            mixed_ref[here, :] = (f_ref[here, :].astype(F32) + ocean * scale_ref[...]).astype(BF16)
-            term = ocean * cot
-            sums_ref[1] += term[:SUB] + term[SUB:]
-            grad = d_normed[here, :]
-            xhat = conv[row, at : at + strip, :]
-            term = grad * xhat
-            sums_ref[2] += term[:SUB] + term[SUB:]
-            sums_ref[3] += grad[:SUB] + grad[SUB:]
-            e = grad * gain_ref[...]
-            m1 = jnp.mean(e, axis=-1, keepdims=True)
-            m2 = jnp.mean(term * gain_ref[...], axis=-1, keepdims=True)
-            inv = jnp.concatenate([inv_s[here, :]] * wide, axis=1)
-            dconv_ref[here, :] = (inv * (e - m1 - xhat * m2)).astype(BF16)
-
-        strips(norm_back)
+        def norm_back(places, sums):
+            heres = [here for _, _, here in places]
+            branches = [
+                mask * (0.5 * branch[here, :] + bo_ref[...]) for mask, here in zip(ocean(places), heres)
+            ]
+            xhats = [xhat_s[here, :] for here in heres]
+            grads = [d_normed[here, :] for here in heres]
+            terms = [grad * xhat for grad, xhat in zip(grads, xhats)]
+            es = [grad * gain_ref[...] for grad in grads]
+            m1s = mean(es)
+            m2s = mean([e * xhat for e, xhat in zip(es, xhats)])
+            for (row, at, here), e, xhat, m1, m2, value in zip(places, es, xhats, m1s, m2s, branches):
+                inv = jnp.concatenate([inv_s[here, :]] * wide, axis=1)
+                dconv_ref[here, :] = (inv * (e - m1 - xhat * m2)).astype(BF16)
+                field = f_ref[row, at : at + strip, :].astype(F32)
+                mixed_ref[here, :] = (field + value * scale_ref[...]).astype(BF16)
+            products = [value * cot_ref[here, :].astype(F32) for value, here in zip(branches, heres)]
+            return tuple(total + folded(x) for total, x in zip(sums, (products, terms, grads)))
+
+        sums_ref[1], sums_ref[2], sums_ref[3] = strips(norm_back, (zero, zero, zero))
 
 
 def expand(
-    order, inner, side, top, bot, kernel, gain, bias, scale, b_out, mask, cot, fields, w_in, b_in, w_out, n_lon, n_lat
+    order, left, right, top, bot, kernel, gain, bias, scale, b_out, mask, cot, fields, w_in, b_in, w_out, n_lon, n_lat
 ):
-    rows, _, channels = inner.shape
+    rows, cols, channels = fields.shape
     hidden = w_in.shape[1]
-    cells, _ = cot.shape
-    cols = cells // rows
+    cells = rows * cols
     block = hidden // n_lon
     split = n_lat if (block // n_lat) % LANES == 0 else 1
     turn = n_lon // 2
     grads = (split, channels, block // split)
-    given = (inner, side, top, bot, kernel, gain, bias, scale, b_out, mask, cot, fields)
+    given = (left, right, top, bot, kernel, gain, bias, scale, b_out, mask, cot, fields)
 
     def sent_at(h, order):
         return (0, jnp.minimum(h, turn - 1), 0, 0, 0)
@@ -334,8 +271,9 @@
                 pl.BlockSpec((2, None) + grads, kept_at),
             ],
             scratch_shapes=[
+                pltpu.VMEM((rows + 6, cols + 16, LANES), F32),
                 pltpu.VMEM((rows, cols, channels), F32),
-                pltpu.VMEM((6, cols + 16, channels), F32),
+                pltpu.VMEM((cells, channels), F32),
                 pltpu.VMEM((cells, LANES), F32),
                 pltpu.VMEM((cells, channels), BF16),
                 pltpu.VMEM((channels, cells), BF16),
@@ -363,6 +301,15 @@
     )(order, *given, w_in, b_in, w_out)
 
 
+def fill_window(window, center, l_ref, r_ref, t_ref, b_ref, lanes):
+    rows, cols, _ = center.shape
+    window[0:3, 5 : 11 + cols, :] = t_ref[:, :, lanes].astype(F32)
+    window[3 : 3 + rows, 5:8, :] = l_ref[:, :, lanes].astype(F32)
+    window[3 : 3 + rows, 8 : 8 + cols, :] = center
+    window[3 : 3 + rows, 8 + cols : 11 + cols, :] = r_ref[:, :, lanes].astype(F32)
+    window[3 + rows : 6 + rows, 5 : 11 + cols, :] = b_ref[:, :, lanes].astype(F32)
+
+
 def filter_grad_kernel(
     f_ref, m_ref, l_ref, r_ref, t_ref, b_ref, d_ref, sums_ref, gbi_ref, o_ref, window, grad
 ):
@@ -371,11 +318,7 @@
 
     def block(index, _):
         lanes = lane_block(index)
-        window[0:3, 5 : 11 + cols, :] = t_ref[:, :, lanes].astype(F32)
-        window[3 : 3 + rows, 5:8, :] = l_ref[:, :, lanes].astype(F32)
-        window[3 : 3 + rows, 8 : 8 + cols, :] = f_ref[:, :, lanes].astype(F32) * m_ref[...]
-        window[3 : 3 + rows, 8 + cols : 11 + cols, :] = r_ref[:, :, lanes].astype(F32)
-        window[3 + rows : 6 + rows, 5 : 11 + cols, :] = b_ref[:, :, lanes].astype(F32)
+        fill_window(window, f_ref[:, :, lanes].astype(F32) * m_ref[...], l_ref, r_ref, t_ref, b_ref, lanes)
         grad[...] = d_ref[:, :, lanes].astype(F32)
         for col_off in range(7):
 
@@ -424,14 +367,15 @@
     )(fields, mask, left, right, top, bot, d_conv, sums, gbi)
 
 
-def input_grad_kernel(first_block, parts, d_ref, l_ref, r_ref, t_ref, b_ref, k_ref, m_ref, cot_ref, *rest):
+def input_grad_kernel(first, d_ref, l_ref, r_ref, t_ref, b_ref, k_ref, m_ref, cot_ref, *rest):
     o_ref, window, grad = rest[-3:]
     rows, cols, channels = d_ref.shape
     tall = o_ref.shape[0]
-
-    def fill(first, lanes):
-        low, high = max(0, first - 3), min(rows, first + tall + 3)
-        inside = slice(low - first + 3, high - first + 3)
+    low, high = max(0, first - 3), min(rows, first + tall + 3)
+    inside = slice(low - first + 3, high - first + 3)
+    group = 32 // tall * SUB
+
+    def block(lanes):
         if first < 3:
             window[0 : 3 - first, 5 : 11 + cols, :] = t_ref[first:3, :, lanes].astype(F32)
         if first + tall > rows - 3:
@@ -440,30 +384,28 @@
         window[inside, 5:8, :] = l_ref[low:high, :, lanes].astype(F32)
         window[inside, 8 : 8 + cols, :] = d_ref[low:high, :, lanes].astype(F32)
         window[inside, 8 + cols : 11 + cols, :] = r_ref[low:high, :, lanes].astype(F32)
-
-    def block(lanes):
-        for at in range(parts):
-            pl.when(pl.program_id(0) == at)(functools.partial(fill, (first_block + at) * tall, lanes))
-        sums = band_conv(window, k_ref, lanes, range(0, cols, SUB), tall, 3, True)
-        for (row, start), value in sums.items():
-            grad[row, start : start + SUB, :] = value
+        for left in range(0, cols, group):
+            starts = range(left, min(left + group, cols), SUB)
+            sums = band_conv(window, k_ref, lanes, starts, tall, 3, True)
+            for (row, start), value in sums.items():
+                grad[row, start : start + SUB, :] = value
         o_ref[:, :, lanes] = (cot_ref[:, :, lanes].astype(F32) + m_ref[...] * grad[...]).astype(BF16)
 
     each_lane_block(channels, block)
 
 
-def input_grad(d_conv, left, right, top, bot, kernel, mask, cot, first, parts, old=None):
+def input_grad(d_conv, left, right, top, bot, kernel, mask, cot, first, quarters, old=None):
     rows, cols, channels = d_conv.shape
-    tall = rows // 4
+    tall = rows // 4 * quarters
 
     def rows_of(width):
-        return pl.BlockSpec((tall, cols, width), lambda i: (first + i, 0, 0))
+        return pl.BlockSpec((tall, cols, width), lambda i: (first // quarters, 0, 0))
 
     whole = (d_conv, left, right, top, bot, kernel)
     more = [] if old is None else [old]
     return pl.pallas_call(
-        functools.partial(input_grad_kernel, first, parts),
-        grid=(parts,),
+        functools.partial(input_grad_kernel, rows // 4 * first),
+        grid=(1,),
         out_shape=jax.ShapeDtypeStruct((rows, cols, channels), BF16),
         in_specs=[once(x.shape) for x in whole]
         + [rows_of(LANES), rows_of(channels)]
@@ -547,19 +489,22 @@
     mask = jnp.broadcast_to(land_mask.astype(F32)[:, :, None], (rows, cols, LANES))
     ocean = land_mask.astype(BF16)[:, :, None]
     left, right = side_halo(fields[:, cols - 3 :] * ocean[:, cols - 3 :], fields[:, :3] * ocean[:, :3])
-    inner, head, tail = conv_inner(fields, mask, kernel)
-    top, bot = end_halo(*end_rows(head, tail, left, right))
-    side = conv_side(fields, mask, kernel, left, right)
-
     lon = lax.axis_index("lon")
     core, side_y = lon % 2, (lon // 2) % 2
     quads = 4 * jnp.arange(n_lon // 4, dtype=jnp.int32)
     order = jnp.concatenate(
         [quads + 2 * y + c for c in (1 - core, core) for y in (1 - side_y, side_y)]
     )
+    top, bot = end_halo(
+        *end_rows(
+            fields[:3] * ocean[:3], fields[rows - 3 :] * ocean[rows - 3 :],
+            after(left, mask, order), after(right, mask, order),
+        )
+    )
+
     d_conv, mixed, sums, g_bi, sent, kept = expand(
-        order, inner, side, top, bot, kernel, gain, bias, scale, b_out.reshape(1, -1), mask, cot_rows,
-        fields.reshape(cells, channels), w_in, b_in.reshape(1, -1), w_out, n_lon, n_lat,
+        order, left, right, top, bot, kernel, gain, bias, scale, b_out.reshape(1, -1), mask, cot_rows,
+        fields, w_in, b_in.reshape(1, -1), w_out, n_lon, n_lat,
     )
     got = swap(sent, "lon", 1)
     d_conv = d_conv.reshape(rows, cols, channels)

time: 131 us -> 131 us (level)
  Pallas kernels: 72 us -> 67 us
  waiting for transfers between devices: 13.5 us -> 17.9 us
    pallas_call x5 -> x3, Pallas kernels: 27 us -> 14.5 us  [input_grad(): pl.pallas_call(functools.partial(input_grad_kernel, rows // 4 * first), g...]
    pallas_call x1, Pallas kernels: 34.5 us -> 42 us  [expand(): pl.pallas_call(expand_kernel, grid_spec=pltpu.PrefetchScalarGridSpec(num_...]
    ppermute x4, waiting for transfers between devices: 0.01 us -> 3.53 us  [end_halo(): return (lax.ppermute(tail, 'lat', ahead), lax.ppermute(head, 'lat', back))]
  transfers between devices with their start and end apart: 16 -> 16, of which waited for: 5 -> 8; matrix products, arithmetic and copies ran while one was open for 6% -> 6% of each run, Pallas kernels for 29% -> 19%
where the time goes in v9:
time: 131 us; the launch traced here: 130 us
  Pallas kernels  67 us (51%)
  starting transfers between devices  27.9 us (21%)
  waiting for transfers between devices  17.9 us (14%)
  local copies, waits for them, and re-layouts  8.16 us (6%)
  other arithmetic  7.98 us (6%)
    pallas_call x1, Pallas kernels, expand(): pl.pallas_call(expand_kernel, grid_spec=pltpu.PrefetchScalarGridSpec(num_...  42 us
    pallas_call x3, Pallas kernels, input_grad(): pl.pallas_call(functools.partial(input_grad_kernel, rows // 4 * first), g...  14.5 us
    ppermute x8, waiting for transfers between devices, swap(): return lax.ppermute(values, axis, [(i, i ^ bit) for i in range(count)])  13.2 us
    ppermute x4, starting transfers between devices, end_halo(): return (lax.ppermute(tail, 'lat', ahead), lax.ppermute(head, 'lat', back))  12 us
    ppermute x8, starting transfers between devices, swap(): return lax.ppermute(values, axis, [(i, i ^ bit) for i in range(count)])  11 us
    pallas_call x1, Pallas kernels, filter_grad(): pl.pallas_call(filter_grad_kernel, out_shape=jax.ShapeDtypeStruct((channe...  10.6 us
    ppermute x4, starting transfers between devices, side_halo(): return (lax.ppermute(last, 'lon', ahead), lax.ppermute(first, 'lon', back))  4.88 us
    ppermute x4, waiting for transfers between devices, end_halo(): return (lax.ppermute(tail, 'lat', ahead), lax.ppermute(head, 'lat', back))  3.53 us
  transfers between devices with their start and end apart: 16, of which 8 were waited for; matrix products, arithmetic and copies ran while one was open for 6% of the time, Pallas kernels for 19%

profile of v9, /device:TPU:0, one launch (start us, length us, event | category | flops | bytes accessed | tf_op | source)
XLA Modules:
  0.0 130.1 jit_solution(2049632614198769807)
XLA Ops:
  1.5 1.2 slice_multiply_fusion
  3.2 2.0 %collective-permute-start.1 = (bf16[32,3,512]{2,1,0:T(4,128)(2,1)S(1)}, bf16[32,3,512]{2,1,0:T(4,128)(2,1)S(1)}, u32[]{:S(2)}, u32[]{:S(2)}) collective-permute-start(bf16[32,3,512]{2,1,0:T(4,128)(2,1)S(1)} %get-tuple-element.90), channel_id=1, source_target_pairs={{4,0},{8,4},{12,8},{0,12},{5,1},{9,5},{13,9},{1,13},{6,2},{10,6},{... | collective-permute-start | bytes 294920 | tf_op jit(solution)/shard_map/ppermute | solution.py:451
  9.2 1.3 collective-permute-start.3
  10.5 4.7 %collective-permute-start.2 = (bf16[3,38,512]{2,1,0:T(8,128)(2,1)S(1)}, bf16[3,38,512]{2,1,0:T(8,128)(2,1)S(1)}, u32[]{:S(2)}, u32[]{:S(2)}) collective-permute-start(bf16[3,38,512]{2,1,0:T(8,128)(2,1)S(1)} %pad_maximum_fusion.4), channel_id=1, source_target_pairs={{0,1},{1,2},{2,3},{4,5},{5,6},{6,7},{8,9},{9,10},{10,11},{12,13},{... | collective-permute-start | bytes 350216 | tf_op jit(solution)/shard_map/ppermute | solution.py:466
  15.2 2.1 %collective-permute-done.3.b_ref = bf16[3,38,512]{2,1,0:T(8,128)(2,1)S(1)} collective-permute-done((bf16[3,38,512]{2,1,0:T(8,128)(2,1)S(1)}, bf16[3,38,512]{2,1,0:T(8,128)(2,1)S(1)}, u32[]{:S(2)}, u32[]{:S(2)}) %collective-permute-start.3) | collective-permute-done | bytes 116768 | tf_op jit(solution)/shard_map/ppermute | solution.py:466
  17.2 1.5 %collective-permute-done.2.t_ref = bf16[3,38,512]{2,1,0:T(8,128)(2,1)S(1)} collective-permute-done((bf16[3,38,512]{2,1,0:T(8,128)(2,1)S(1)}, bf16[3,38,512]{2,1,0:T(8,128)(2,1)S(1)}, u32[]{:S(2)}, u32[]{:S(2)}) %collective-permute-start.2) | collective-permute-done | bytes 116768 | tf_op jit(solution)/shard_map/ppermute | solution.py:466
  19.4 42.0 %expand.1 = (bf16[1024,512]{1,0:T(8,128)(2,1)}, bf16[1024,512]{1,0:T(8,128)(2,1)}, f32[4,8,512]{2,1,0:T(8,128)}, f32[1,2048]{1,0:T(1,128)}, bf16[2,2,4,512,128]{...) custom-call(s32[4]{0:T(128)} %pad_add_fusion.order_ref, bf16[32,3,512]{2,1,0:T(4,128)(2,1)} %copy-done.3, ...), custom_call_target="tpu_custom_call" | custom-call | flops 23000000512 | bytes 72000000 | tf_op jit(solution)/shard_map/expand/pallas_call | solution.py:254
  63.1 1.8 %collective-permute-start.6 = (bf16[32,3,512]{2,1,0:T(4,128)(2,1)S(1)}, bf16[32,3,512]{2,1,0:T(4,128)(2,1)S(1)}, u32[]{:S(2)}, u32[]{:S(2)}) collective-permute-start(bf16[32,3,512]{2,1,0:T(4,128)(2,1)S(1)} %get-tuple-element.87), channel_id=1, source_target_pairs={{4,0},{8,4},{12,8},{0,12},{5,1},{9,5},{13,9},{1,13},{6,2},{10,6},{... | collective-permute-start | bytes 294920 | tf_op jit(solution)/shard_map/ppermute | solution.py:451
  65.9 1.3 %convert_add_fusion = f32[2,2,4,192,128]{4,3,2,1,0:T(8,128)S(1)} fusion(bf16[2,2,4,512,128]{4,3,2,1,0:T(8,128)(2,1)S(1)} %collective-permute-done.4, bf16[2,2,4,512,128]{4,3,2,1,0:T(8,128)(2,1)} %get-tuple-element.53), kind=kLoop, calls=%fused_computation | loop fusion | flops 1179648 | bytes 3145728 | tf_op jit(solution)/shard_map/add | solution.py:525
  67.5 2.5 %collective-permute-start.7 = (bf16[2,2,2,192,128]{4,3,0,1,2:T(8,128)(2,1)S(1)}, bf16[2,2,2,192,128]{4,3,0,1,2:T(8,128)(2,1)S(1)}, u32[]{:S(2)}, u32[]{:S(2)}) collective-permute-start(bf16[2,2,2,192,128]{4,3,0,1,2:T(8,128)(2,1)S(1)} %fusion.1), channel_id=1, source_target_pairs={{0,1},{1,0},{2,3},{3,2},{4,5},{5,4},{6,7},{7,6},{8,9},{9,8},{10,11... | collective-permute-start | bytes 1179656 | tf_op jit(solution)/shard_map/ppermute | solution.py:427
  70.2 2.1 %collective-permute-start.9 = (bf16[2,1,4,320,128]{4,3,2,1,0:T(8,128)(2,1)S(1)}, bf16[2,1,4,320,128]{4,3,2,1,0:T(8,128)(2,1)S(1)}, u32[]{:S(2)}, u32[]{:S(2)}) collective-permute-start(bf16[2,1,4,320,128]{4,3,2,1,0:T(8,128)(2,1)S(1)} %add_convert_fusion), channel_id=1, source_target_pairs={{0,8},{4,12},{8,0},{12,4},{1,9},{5,13},{9,1},{13,5},{2,10},{6,14},... | collective-permute-start | bytes 1966088 | tf_op jit(solution)/shard_map/ppermute | solution.py:427
  72.4 1.3 collective-permute-start.11
  73.8 4.7 %collective-permute-start.10 = (bf16[3,38,512]{2,1,0:T(8,128)(2,1)S(1)}, bf16[3,38,512]{2,1,0:T(8,128)(2,1)S(1)}, u32[]{:S(2)}, u32[]{:S(2)}) collective-permute-start(bf16[3,38,512]{2,1,0:T(8,128)(2,1)S(1)} %pad_maximum_fusion.7), channel_id=1, source_target_pairs={{0,1},{1,2},{2,3},{4,5},{5,6},{6,7},{8,9},{9,10},{10,11},{12,13},{... | collective-permute-start | bytes 350216 | tf_op jit(solution)/shard_map/ppermute | solution.py:466
  78.5 1.3 %collective-permute-done.7 = bf16[2,2,2,192,128]{4,3,0,1,2:T(8,128)(2,1)S(1)} collective-permute-done((bf16[2,2,2,192,128]{4,3,0,1,2:T(8,128)(2,1)S(1)}, bf16[2,2,2,192,128]{4,3,0,1,2:T(8,128)(2,1)S(1)}, u32[]{:S(2)}, u32[]{:S(2)}) %collective-permute-start.7) | collective-permute-done | bytes 393248 | tf_op jit(solution)/shard_map/ppermute | solution.py:427
  80.0 3.0 %collective-permute-start.13 = (bf16[2,2,1,192,128]{4,3,0,2,1:T(8,128)(2,1)S(1)}, bf16[2,2,1,192,128]{4,3,0,2,1:T(8,128)(2,1)S(1)}, u32[]{:S(2)}, u32[]{:S(2)}) collective-permute-start(bf16[2,2,1,192,128]{4,3,0,2,1:T(8,128)(2,1)S(1)} %fusion.6), channel_id=1, source_target_pairs={{0,2},{1,3},{2,0},{3,1},{4,6},{5,7},{6,4},{7,5},{8,10},{9,11},{10,... | collective-permute-start | bytes 589832 | tf_op jit(solution)/shard_map/ppermute | solution.py:427
  83.0 10.6 %filter_grad.1 = f32[4,64,128]{2,1,0:T(8,128)} custom-call(bf16[32,32,512]{2,1,0:T(8,128)(2,1)} %f_ref.2, f32[32,32,128]{2,1,0:T(8,128)} %broadcast_in_dim.10.m_ref, bf16[32,3,512]{2,1,0:T(4,128)(2,1)} %copy-done.3, bf16[32,3,512]{2,1,0:T(4,128)(2,1)} %copy-done.4, bf16[3,38,512]{2,1,0:T(8,128)(2,1)} %copy-done.6, bf16[3,38,512]{2,1,0:T(8,128)(2,1)} %copy-done.5, ...), custom_call_target="tpu_custom_call" | custom-call | flops 4600000000 | bytes 14400000 | tf_op jit(solution)/shard_map/filter_grad/pallas_call | solution.py:357
  93.7 1.5 %collective-permute-done.8 = f32[4,64,128]{2,1,0:T(8,128)S(1)} collective-permute-done((f32[4,64,128]{2,1,0:T(8,128)}, f32[4,64,128]{2,1,0:T(8,128)S(1)}, u32[]{:S(2)}, u32[]{:S(2)}) %collective-permute-start.8) | collective-permute-done | bytes 131104 | tf_op jit(solution)/shard_map/ppermute | solution.py:427
  96.5 1.7 %collective-permute-start.12 = (bf16[1536,128]{1,0:T(8,128)(2,1)S(1)}, bf16[1536,128]{1,0:T(8,128)(2,1)S(1)}, u32[]{:S(2)}, u32[]{:S(2)}) collective-permute-start(bf16[1536,128]{1,0:T(8,128)(2,1)S(1)} %pad_maximum_fusion), channel_id=1, source_target_pairs={{0,1},{1,0},{2,3},{3,2},{4,5},{5,4},{6,7},{7,6},{8,9},{9,8},{10,11... | collective-permute-start | bytes 1179656 | tf_op jit(solution)/shard_map/ppermute | solution.py:427
  99.5 6.2 %input_grad.3.rest_0_ = bf16[32,32,512]{2,1,0:T(8,128)(2,1)} custom-call(bf16[32,32,512]{2,1,0:T(8,128)(2,1)} %bitcast.107, bf16[32,3,512]{2,1,0:T(4,128)(2,1)} %copy-done.1, bf16[32,3,512]{2,1,0:T(4,128)(2,1)} %copy-done.2, bf16[3,38,512]{2,1,0:T(8,128)(2,1)} %copy-done.8, bf16[3,38,512]{2,1,0:T(8,128)(2,1)} %copy-done.7, f32[7,7,512]{2,1,0:T(8,128)} %k_ref.7, ...), custom_call_target="tpu_custom_call" | custom-call | flops 4600000000 | bytes 14400000 | tf_op jit(solution)/shard_map/input_grad/pallas_call | solution.py:406
  105.7 2.1 %collective-permute-done.12 = bf16[1536,128]{1,0:T(8,128)(2,1)S(1)} collective-permute-done((bf16[1536,128]{1,0:T(8,128)(2,1)S(1)}, bf16[1536,128]{1,0:T(8,128)(2,1)S(1)}, u32[]{:S(2)}, u32[]{:S(2)}) %collective-permute-start.12) | collective-permute-done | bytes 393248 | tf_op jit(solution)/shard_map/ppermute | solution.py:427
  108.2 4.1 %input_grad.4.rest_0_ = bf16[32,32,512]{2,1,0:T(8,128)(2,1)} custom-call(bf16[32,32,512]{2,1,0:T(8,128)(2,1)} %bitcast.108, bf16[32,3,512]{2,1,0:T(4,128)(2,1)} %copy-done.1, bf16[32,3,512]{2,1,0:T(4,128)(2,1)} %copy-done.2, bf16[3,38,512]{2,1,0:T(8,128)(2,1)} %copy-done.8, bf16[3,38,512]{2,1,0:T(8,128)(2,1)} %copy-done.7, ...), custom_call_target="tpu_custom_call", output_to_operand_aliasing={{}: (8, {})} | custom-call | flops 4600000000 | bytes 14400000 | tf_op jit(solution)/shard_map/input_grad/pallas_call | solution.py:406
  112.4 8.3 %collective-permute-done.14 = bf16[896,128]{1,0:T(8,128)(2,1)S(1)} collective-permute-done((bf16[896,128]{1,0:T(8,128)(2,1)S(1)}, bf16[896,128]{1,0:T(8,128)(2,1)S(1)}, u32[]{:S(2)}, u32[]{:S(2)}) %collective-permute-start.14) | collective-permute-done | bytes 229408 | tf_op jit(solution)/shard_map/ppermute | solution.py:427
  120.8 1.5 %collective-permute-start.15 = (bf16[640,128]{1,0:T(8,128)(2,1)S(1)}, bf16[640,128]{1,0:T(8,128)(2,1)S(1)}, u32[]{:S(2)}, u32[]{:S(2)}) collective-permute-start(bf16[640,128]{1,0:T(8,128)(2,1)S(1)} %pad_maximum_fusion.3), channel_id=1, source_target_pairs={{0,8},{4,12},{8,0},{12,4},{1,9},{5,13},{9,1},{13,5},{2,10},{6,14},... | collective-permute-start | bytes 491528 | tf_op jit(solution)/shard_map/ppermute | solution.py:427
  122.3 4.1 %input_grad.5 = bf16[32,32,512]{2,1,0:T(8,128)(2,1)} custom-call(bf16[32,32,512]{2,1,0:T(8,128)(2,1)} %bitcast.109, bf16[32,3,512]{2,1,0:T(4,128)(2,1)} %copy-done.1, bf16[32,3,512]{2,1,0:T(4,128)(2,1)} %copy-done.2, bf16[3,38,512]{2,1,0:T(8,128)(2,1)} %copy-done.8, bf16[3,38,512]{2,1,0:T(8,128)(2,1)} %copy-done.7, ...), custom_call_target="tpu_custom_call", output_to_operand_aliasing={{}: (8, {})} | custom-call | flops 4600000000 | bytes 14400000 | tf_op jit(solution)/shard_map/input_grad/pallas_call | solution.py:406
  (87 shorter events, 16.1 us)
Async XLA Ops:
  2.7 5.1 %collective-permute-start = (bf16[32,3,512]{2,1,0:T(4,128)(2,1)S(1)}, bf16[32,3,512]{2,1,0:T(4,128)(2,1)S(1)}, u32[]{:S(2)}, u32[]{:S(2)}) collective-permute-start(bf16[32,3,512]{2,1,0:T(4,128)(2,1)S(1)} %get-tuple-element.91), channel_id=1, source_target_pairs={{0,4},{4,8},{8,12},{12,0},{1,5},{5,9},{9,13},{13,1},{2,6},{6,10},{... | collective-permute-start | bytes 294920 | tf_op jit(solution)/shard_map/ppermute | solution.py:451
  3.2 5.8 %collective-permute-start.1 = (bf16[32,3,512]{2,1,0:T(4,128)(2,1)S(1)}, bf16[32,3,512]{2,1,0:T(4,128)(2,1)S(1)}, u32[]{:S(2)}, u32[]{:S(2)}) collective-permute-start(bf16[32,3,512]{2,1,0:T(4,128)(2,1)S(1)} %get-tuple-element.90), channel_id=1, source_target_pairs={{4,0},{8,4},{12,8},{0,12},{5,1},{9,5},{13,9},{1,13},{6,2},{10,6},{... | collective-permute-start | bytes 294920 | tf_op jit(solution)/shard_map/ppermute | solution.py:451
  7.9 10.9 %copy-start.3 = (bf16[32,3,512]{2,1,0:T(4,128)(2,1)}, bf16[32,3,512]{2,1,0:T(4,128)(2,1)S(1)}, u32[]{:S(2)}) copy-start(bf16[32,3,512]{2,1,0:T(4,128)(2,1)S(1)} %collective-permute-done.l_ref) | copy-start | bytes 294916
  9.1 9.6 %copy-start.4 = (bf16[32,3,512]{2,1,0:T(4,128)(2,1)}, bf16[32,3,512]{2,1,0:T(4,128)(2,1)S(1)}, u32[]{:S(2)}) copy-start(bf16[32,3,512]{2,1,0:T(4,128)(2,1)S(1)} %collective-permute-done.1.r_ref) | copy-start | bytes 294916
  9.2 8.1 %collective-permute-start.3 = (bf16[3,38,512]{2,1,0:T(8,128)(2,1)S(1)}, bf16[3,38,512]{2,1,0:T(8,128)(2,1)S(1)}, u32[]{:S(2)}, u32[]{:S(2)}) collective-permute-start(bf16[3,38,512]{2,1,0:T(8,128)(2,1)S(1)} %pad_maximum_fusion.5), channel_id=1, source_target_pairs={{1,0},{2,1},{3,2},{5,4},{6,5},{7,6},{9,8},{10,9},{11,10},{13,12},{... | collective-permute-start | bytes 350216 | tf_op jit(solution)/shard_map/ppermute | solution.py:466
  10.5 8.2 %collective-permute-start.2 = (bf16[3,38,512]{2,1,0:T(8,128)(2,1)S(1)}, bf16[3,38,512]{2,1,0:T(8,128)(2,1)S(1)}, u32[]{:S(2)}, u32[]{:S(2)}) collective-permute-start(bf16[3,38,512]{2,1,0:T(8,128)(2,1)S(1)} %pad_maximum_fusion.4), channel_id=1, source_target_pairs={{0,1},{1,2},{2,3},{4,5},{5,6},{6,7},{8,9},{9,10},{10,11},{12,13},{... | collective-permute-start | bytes 350216 | tf_op jit(solution)/shard_map/ppermute | solution.py:466
  17.2 1.5 %copy-start.5 = (bf16[3,38,512]{2,1,0:T(8,128)(2,1)}, bf16[3,38,512]{2,1,0:T(8,128)(2,1)S(1)}, u32[]{:S(2)}) copy-start(bf16[3,38,512]{2,1,0:T(8,128)(2,1)S(1)} %collective-permute-done.3.b_ref) | copy-start | bytes 350212
  18.7 0.7 copy-start.6
  61.4 4.6 %collective-permute-start.4 = (bf16[2,2,4,512,128]{4,3,2,1,0:T(8,128)(2,1)}, bf16[2,2,4,512,128]{4,3,2,1,0:T(8,128)(2,1)S(1)}, u32[]{:S(2)}, u32[]{:S(2)}) collective-permute-start(bf16[2,2,4,512,128]{4,3,2,1,0:T(8,128)(2,1)} %get-tuple-element.45), channel_id=1, source_target_pairs={{0,4},{4,0},{8,12},{12,8},{1,5},{5,1},{9,13},{13,9},{2,6},{6,2},{1... | collective-permute-start | bytes 6291464 | tf_op jit(solution)/shard_map/ppermute | solution.py:427
  62.6 9.6 %collective-permute-start.5 = (bf16[32,3,512]{2,1,0:T(4,128)(2,1)S(1)}, bf16[32,3,512]{2,1,0:T(4,128)(2,1)S(1)}, u32[]{:S(2)}, u32[]{:S(2)}) collective-permute-start(bf16[32,3,512]{2,1,0:T(4,128)(2,1)S(1)} %get-tuple-element.86), channel_id=1, source_target_pairs={{0,4},{4,8},{8,12},{12,0},{1,5},{5,9},{9,13},{13,1},{2,6},{6,10},{... | collective-permute-start | bytes 294920 | tf_op jit(solution)/shard_map/ppermute | solution.py:451
  63.1 9.1 %collective-permute-start.6 = (bf16[32,3,512]{2,1,0:T(4,128)(2,1)S(1)}, bf16[32,3,512]{2,1,0:T(4,128)(2,1)S(1)}, u32[]{:S(2)}, u32[]{:S(2)}) collective-permute-start(bf16[32,3,512]{2,1,0:T(4,128)(2,1)S(1)} %get-tuple-element.87), channel_id=1, source_target_pairs={{4,0},{8,4},{12,8},{0,12},{5,1},{9,5},{13,9},{1,13},{6,2},{10,6},{... | collective-permute-start | bytes 294920 | tf_op jit(solution)/shard_map/ppermute | solution.py:451
  67.3 2.7 %copy-start = (bf16[2,2,4,512,128]{4,3,2,1,0:T(8,128)(2,1)S(1)}, bf16[2,2,4,512,128]{4,3,2,1,0:T(8,128)(2,1)}, u32[]{:S(2)}) copy-start(bf16[2,2,4,512,128]{4,3,2,1,0:T(8,128)(2,1)} %get-tuple-element.53) | copy-start | bytes 6291460
  67.5 12.4 %collective-permute-start.7 = (bf16[2,2,2,192,128]{4,3,0,1,2:T(8,128)(2,1)S(1)}, bf16[2,2,2,192,128]{4,3,0,1,2:T(8,128)(2,1)S(1)}, u32[]{:S(2)}, u32[]{:S(2)}) collective-permute-start(bf16[2,2,2,192,128]{4,3,0,1,2:T(8,128)(2,1)S(1)} %fusion.1), channel_id=1, source_target_pairs={{0,1},{1,0},{2,3},{3,2},{4,5},{5,4},{6,7},{7,6},{8,9},{9,8},{10,11... | collective-permute-start | bytes 1179656 | tf_op jit(solution)/shard_map/ppermute | solution.py:427
  70.2 26.0 %collective-permute-start.9 = (bf16[2,1,4,320,128]{4,3,2,1,0:T(8,128)(2,1)S(1)}, bf16[2,1,4,320,128]{4,3,2,1,0:T(8,128)(2,1)S(1)}, u32[]{:S(2)}, u32[]{:S(2)}) collective-permute-start(bf16[2,1,4,320,128]{4,3,2,1,0:T(8,128)(2,1)S(1)} %add_convert_fusion), channel_id=1, source_target_pairs={{0,8},{4,12},{8,0},{12,4},{1,9},{5,13},{9,1},{13,5},{2,10},{6,14},... | collective-permute-start | bytes 1966088 | tf_op jit(solution)/shard_map/ppermute | solution.py:427
  72.2 7.7 %copy-start.1 = (bf16[32,3,512]{2,1,0:T(4,128)(2,1)}, bf16[32,3,512]{2,1,0:T(4,128)(2,1)S(1)}, u32[]{:S(2)}) copy-start(bf16[32,3,512]{2,1,0:T(4,128)(2,1)S(1)} %collective-permute-done.5.l_ref) | copy-start | bytes 294916
  72.3 7.7 %copy-start.2 = (bf16[32,3,512]{2,1,0:T(4,128)(2,1)}, bf16[32,3,512]{2,1,0:T(4,128)(2,1)S(1)}, u32[]{:S(2)}) copy-start(bf16[32,3,512]{2,1,0:T(4,128)(2,1)S(1)} %collective-permute-done.6.r_ref) | copy-start | bytes 294916
  72.4 25.8 %collective-permute-start.11 = (bf16[3,38,512]{2,1,0:T(8,128)(2,1)S(1)}, bf16[3,38,512]{2,1,0:T(8,128)(2,1)S(1)}, u32[]{:S(2)}, u32[]{:S(2)}) collective-permute-start(bf16[3,38,512]{2,1,0:T(8,128)(2,1)S(1)} %pad_maximum_fusion.6), channel_id=1, source_target_pairs={{1,0},{2,1},{3,2},{5,4},{6,5},{7,6},{9,8},{10,9},{11,10},{13,12},{... | collective-permute-start | bytes 350216 | tf_op jit(solution)/shard_map/ppermute | solution.py:466
  73.8 24.4 %collective-permute-start.10 = (bf16[3,38,512]{2,1,0:T(8,128)(2,1)S(1)}, bf16[3,38,512]{2,1,0:T(8,128)(2,1)S(1)}, u32[]{:S(2)}, u32[]{:S(2)}) collective-permute-start(bf16[3,38,512]{2,1,0:T(8,128)(2,1)S(1)} %pad_maximum_fusion.7), channel_id=1, source_target_pairs={{0,1},{1,2},{2,3},{4,5},{5,6},{6,7},{8,9},{9,10},{10,11},{12,13},{... | collective-permute-start | bytes 350216 | tf_op jit(solution)/shard_map/ppermute | solution.py:466
  80.0 32.3 %collective-permute-start.13 = (bf16[2,2,1,192,128]{4,3,0,2,1:T(8,128)(2,1)S(1)}, bf16[2,2,1,192,128]{4,3,0,2,1:T(8,128)(2,1)S(1)}, u32[]{:S(2)}, u32[]{:S(2)}) collective-permute-start(bf16[2,2,1,192,128]{4,3,0,2,1:T(8,128)(2,1)S(1)} %fusion.6), channel_id=1, source_target_pairs={{0,2},{1,3},{2,0},{3,1},{4,6},{5,7},{6,4},{7,5},{8,10},{9,11},{10,... | collective-permute-start | bytes 589832 | tf_op jit(solution)/shard_map/ppermute | solution.py:427
  93.6 1.6 %collective-permute-start.8 = (f32[4,64,128]{2,1,0:T(8,128)}, f32[4,64,128]{2,1,0:T(8,128)S(1)}, u32[]{:S(2)}, u32[]{:S(2)}) collective-permute-start(f32[4,64,128]{2,1,0:T(8,128)} %filter_grad.1), channel_id=1, source_target_pairs={{0,4},{4,0},{8,12},{12,8},{1,5},{5,1},{9,13},{13,9},{2,6},{6,2},{1... | collective-permute-start | bytes 393224 | tf_op jit(solution)/shard_map/ppermute | solution.py:427
  96.5 11.2 %collective-permute-start.12 = (bf16[1536,128]{1,0:T(8,128)(2,1)S(1)}, bf16[1536,128]{1,0:T(8,128)(2,1)S(1)}, u32[]{:S(2)}, u32[]{:S(2)}) collective-permute-start(bf16[1536,128]{1,0:T(8,128)(2,1)S(1)} %pad_maximum_fusion), channel_id=1, source_target_pairs={{0,1},{1,0},{2,3},{3,2},{4,5},{5,4},{6,7},{7,6},{8,9},{9,8},{10,11... | collective-permute-start | bytes 1179656 | tf_op jit(solution)/shard_map/ppermute | solution.py:427
  98.2 0.6 copy-start.7
  108.0 12.7 %collective-permute-start.14 = (bf16[896,128]{1,0:T(8,128)(2,1)S(1)}, bf16[896,128]{1,0:T(8,128)(2,1)S(1)}, u32[]{:S(2)}, u32[]{:S(2)}) collective-permute-start(bf16[896,128]{1,0:T(8,128)(2,1)S(1)} %pad_maximum_fusion.2), channel_id=1, source_target_pairs={{0,2},{1,3},{2,0},{3,1},{4,6},{5,7},{6,4},{7,5},{8,10},{9,11},{10,... | collective-permute-start | bytes 688136 | tf_op jit(solution)/shard_map/ppermute | solution.py:427
  120.8 5.7 %collective-permute-start.15 = (bf16[640,128]{1,0:T(8,128)(2,1)S(1)}, bf16[640,128]{1,0:T(8,128)(2,1)S(1)}, u32[]{:S(2)}, u32[]{:S(2)}) collective-permute-start(bf16[640,128]{1,0:T(8,128)(2,1)S(1)} %pad_maximum_fusion.3), channel_id=1, source_target_pairs={{0,8},{4,12},{8,0},{12,4},{1,9},{5,13},{9,1},{13,5},{2,10},{6,14},... | collective-permute-start | bytes 491528 | tf_op jit(solution)/shard_map/ppermute | solution.py:427
  (1 other events, 0.6 us)

commit v10 on v9

--- a/solution.py
+++ b/solution.py
@@ -187,14 +187,13 @@
                 rows_t[...], source[:, left : left + cut], preferred_element_type=F32
             ).astype(BF16)
 
-            def store(ref):
-                size = min(width, cut)
-                for at in range(0, cut, size):
-                    lat, into = divmod(left + at, width)
-                    ref[which, lat, :, into : into + size] = grad[:, at : at + size]
-
-            pl.when(is_sent)(functools.partial(store, sent_ref))
-            pl.when(jnp.logical_not(is_sent))(functools.partial(store, kept_ref))
+            size = min(width, cut)
+            for at in range(0, cut, size):
+                lat, into = divmod(left + at, width)
+                spot = (which, lat, slice(None), slice(into, into + size))
+                value = grad[:, at : at + size]
+                kept_ref[spot] = value
+                sent_ref[spot] = jnp.where(is_sent, value, sent_ref[spot])
 
     products(0)
     for index in range(count):
@@ -422,6 +421,46 @@
     )(*whole, mask, cot, *more)
 
 
+def finish_kernel(a_ref, b_ref, load_ref, small_ref, wo_ref, wi_ref, gk_ref, vec_ref, gbi_ref):
+    channels = wi_ref.shape[0]
+    border = a_ref.shape[1]
+    rest = channels - border
+    blocks = channels // LANES
+    for index, ref in ((0, wo_ref), (1, wi_ref)):
+        came = load_ref[index * rest : (index + 1) * rest, :].astype(F32)
+        grad = jnp.concatenate([a_ref[index], b_ref[index] + came], axis=0)
+        ref[...] = grad.T if index == 0 else grad
+    for block in range(blocks):
+        at = 2 * rest + block * 64
+        total = small_ref[block] + load_ref[at : at + 64, :].astype(F32)
+        lanes = slice(block * LANES, (block + 1) * LANES)
+        for row in range(7):
+            gk_ref[row, :, lanes] = total[row * 8 : row * 8 + 7]
+        for row in range(4):
+            vec_ref[row, :, lanes] = total[56 + row : 57 + row]
+            gbi_ref[:, slice(row * channels + block * LANES, row * channels + (block + 1) * LANES)] = total[
+                60 + row : 61 + row
+            ]
+
+
+def finish(first, second, load, small, hidden):
+    channels = first.shape[1] + second.shape[1]
+    width = first.shape[2]
+    return pl.pallas_call(
+        finish_kernel,
+        out_shape=[
+            jax.ShapeDtypeStruct((width, channels), F32),
+            jax.ShapeDtypeStruct((channels, width), F32),
+            jax.ShapeDtypeStruct((7, 7, channels), F32),
+            jax.ShapeDtypeStruct((4, 1, channels), F32),
+            jax.ShapeDtypeStruct((1, hidden), F32),
+        ],
+        compiler_params=params(56),
+        cost_estimate=estimate(2),
+        name="finish",
+    )(first, second, load, small)
+
+
 def swap(values, axis, bit):
     count = lax.axis_size(axis)
     return lax.ppermute(values, axis, [(i, i ^ bit) for i in range(count)])
@@ -553,43 +592,57 @@
         after(fields, d_tail, d_head, far_first, cut_b[1]),
         mask, left, right, top, bot, d_conv, sums, g_bi,
     )
-    small = small + swap(small, "lon", 1)
-    whole = pair(near_lons, first, small) + after(got_first, small).astype(F32)
+    alone = small
+    whole = pair(near_lons, first, alone) + after(got_first, alone).astype(F32)
+    whole_b = fold(*cut_b, lat_bits[-1][0], lat_bits[-1][2], alone)
+    far_second = whole_b[:, far_lons].astype(BF16)
     back = (d_left, d_right, d_top, d_bot, kernel, mask, cotangent)
     grad_fields, block = None, 0
     steps = lon_bits + lat_bits
+    early = halves(whole, *steps[0])[1]
+    small = after(alone, early, far_second) + after(swap(alone, "lon", 1), early, far_second)
     for index, (axis, dim, bit) in enumerate(steps):
         mine, sent = halves(whole, axis, dim, bit)
         load = pack(sent, small)
         last = load
         if index >= len(steps) - 2:
             count = 2 if grad_fields is None else 1
-            last = grad_fields = input_grad(after(d_conv, load), *back, block, count, grad_fields)
+            last = grad_fields = input_grad(
+                after(d_conv, load, far_second), *back, block, count, grad_fields
+            )
             block += count
         came, small = ride(load, sent, small, axis, bit, last)
         whole = after(mine, last) + came
-    whole_b = fold(*cut_b, lat_bits[-1][0], lat_bits[-1][2], load)
-    far_second = whole_b[:, far_lons].astype(BF16)
     load = pack(far_second, small)
     last = grad_fields = input_grad(after(d_conv, load), *back, block, 1, grad_fields)
-    came, small = ride(load, far_second, small, "lon", 2, last)
-    whole_b = after(whole_b, last)[:, near_lons] + came
-    for axis, dim, bit in lon_bits:
-        whole_b = fold(*halves(whole_b, axis, dim, bit), axis, bit, last)
-    owned = (whole, whole_b)
-    grad_w = jnp.concatenate([x[:, 0, 0] for x in owned], axis=1)
-    small = small.transpose(1, 0, 2).reshape(8, 8, channels)
+    if not lon_bits and whole.shape[-1] == LANES:
+        load = after(swap(load, "lon", 2), last)
+        near = after(whole_b, last)[:, near_lons]
+        grad_wo, grad_wi, grad_k, vectors, g_bi = finish(
+            whole[:, 0, 0], near[:, 0, 0], load, after(lax.reduce_precision(small, 8, 7), last), hidden
+        )
+        g_scale, g_gain, g_shift, g_bo = (vectors[i, 0] for i in range(4))
+    else:
+        came, small = ride(load, far_second, small, "lon", 2, last)
+        whole_b = after(whole_b, last)[:, near_lons] + came
+        for axis, dim, bit in lon_bits:
+            whole_b = fold(*halves(whole_b, axis, dim, bit), axis, bit, last)
+        grad_w = jnp.concatenate([x[:, 0, 0] for x in (whole, whole_b)], axis=1)
+        grad_wo, grad_wi = grad_w[0].T, grad_w[1]
+        small = small.transpose(1, 0, 2).reshape(8, 8, channels)
+        grad_k, g_bi = small[:7, :7], small[7, 4:]
+        g_scale, g_gain, g_shift, g_bo = (small[7, i] for i in range(4))
     return (
         mixed.reshape(rows, cols, channels),
         grad_fields,
-        small[:7, :7],
-        small[7, 1],
-        small[7, 2],
-        grad_w[1],
-        small[7, 4:].reshape(hidden),
-        grad_w[0].T,
-        small[7, 3],
-        small[7, 0],
+        grad_k,
+        g_gain,
+        g_shift,
+        grad_wi,
+        g_bi.reshape(hidden),
+        grad_wo,
+        g_bo,
+        g_scale,
     )
 
 

time: 131 us -> 125 us (0.954)
  Pallas kernels: 67 us -> 61.7 us
    pallas_call x1, Pallas kernels: 42 us -> 34.6 us  [expand(): pl.pallas_call(expand_kernel, grid_spec=pltpu.PrefetchScalarGridSpec(num_...]
    pallas_call x0 -> x1, Pallas kernels: none -> 2.06 us  [finish(): pl.pallas_call(finish_kernel, out_shape=[jax.ShapeDtypeStruct((width, cha...]
    unnamed x21 -> x22, local copies, waits for them, and re-layouts: 3.4 us -> 2.61 us
  transfers between devices with their start and end apart: 16 -> 16, of which waited for: 8 -> 8; matrix products, arithmetic and copies ran while one was open for 6% -> 7% of each run, Pallas kernels for 19% -> 20%
where the time goes in v10:
time: 125 us; the launch traced here: 124 us
  Pallas kernels  61.7 us (49%)
  starting transfers between devices  27.9 us (22%)
  waiting for transfers between devices  17.8 us (14%)
  local copies, waits for them, and re-layouts  8.12 us (6%)
  other arithmetic  7.69 us (6%)
    pallas_call x1, Pallas kernels, expand(): pl.pallas_call(expand_kernel, grid_spec=pltpu.PrefetchScalarGridSpec(num_...  34.6 us
    pallas_call x3, Pallas kernels, input_grad(): pl.pallas_call(functools.partial(input_grad_kernel, rows // 4 * first), g...  14.5 us
    ppermute x8, waiting for transfers between devices, swap(): return lax.ppermute(values, axis, [(i, i ^ bit) for i in range(count)])  13.1 us
    ppermute x4, starting transfers between devices, end_halo(): return (lax.ppermute(tail, 'lat', ahead), lax.ppermute(head, 'lat', back))  12 us
    ppermute x8, starting transfers between devices, swap(): return lax.ppermute(values, axis, [(i, i ^ bit) for i in range(count)])  11 us
    pallas_call x1, Pallas kernels, filter_grad(): pl.pallas_call(filter_grad_kernel, out_shape=jax.ShapeDtypeStruct((channe...  10.6 us
    ppermute x4, starting transfers between devices, side_halo(): return (lax.ppermute(last, 'lon', ahead), lax.ppermute(first, 'lon', back))  4.89 us
    ppermute x4, waiting for transfers between devices, end_halo(): return (lax.ppermute(tail, 'lat', ahead), lax.ppermute(head, 'lat', back))  3.51 us
  transfers between devices with their start and end apart: 16, of which 8 were waited for; matrix products, arithmetic and copies ran while one was open for 7% of the time, Pallas kernels for 20%

profile of v10, /device:TPU:0, one launch (start us, length us, event | category | flops | bytes accessed | tf_op | source)
XLA Modules:
  0.0 124.3 jit_solution(2501556884731340)
XLA Ops:
  3.2 2.0 %collective-permute-start.1 = (bf16[32,3,512]{2,1,0:T(4,128)(2,1)S(1)}, bf16[32,3,512]{2,1,0:T(4,128)(2,1)S(1)}, u32[]{:S(2)}, u32[]{:S(2)}) collective-permute-start(bf16[32,3,512]{2,1,0:T(4,128)(2,1)S(1)} %get-tuple-element.94), channel_id=1, source_target_pairs={{4,0},{8,4},{12,8},{0,12},{5,1},{9,5},{13,9},{1,13},{6,2},{10,6},{... | collective-permute-start | bytes 294920 | tf_op jit(solution)/shard_map/ppermute | solution.py:490
  9.2 1.3 %collective-permute-start.3 = (bf16[3,38,512]{2,1,0:T(8,128)(2,1)S(1)}, bf16[3,38,512]{2,1,0:T(8,128)(2,1)S(1)}, u32[]{:S(2)}, u32[]{:S(2)}) collective-permute-start(bf16[3,38,512]{2,1,0:T(8,128)(2,1)S(1)} %pad_maximum_fusion.4), channel_id=1, source_target_pairs={{1,0},{2,1},{3,2},{5,4},{6,5},{7,6},{9,8},{10,9},{11,10},{13,12},{... | collective-permute-start | bytes 350216 | tf_op jit(solution)/shard_map/ppermute | solution.py:505
  10.5 4.7 %collective-permute-start.2 = (bf16[3,38,512]{2,1,0:T(8,128)(2,1)S(1)}, bf16[3,38,512]{2,1,0:T(8,128)(2,1)S(1)}, u32[]{:S(2)}, u32[]{:S(2)}) collective-permute-start(bf16[3,38,512]{2,1,0:T(8,128)(2,1)S(1)} %pad_maximum_fusion.3), channel_id=1, source_target_pairs={{0,1},{1,2},{2,3},{4,5},{5,6},{6,7},{8,9},{9,10},{10,11},{12,13},{... | collective-permute-start | bytes 350216 | tf_op jit(solution)/shard_map/ppermute | solution.py:505
  15.2 2.1 %collective-permute-done.3.b_ref = bf16[3,38,512]{2,1,0:T(8,128)(2,1)S(1)} collective-permute-done((bf16[3,38,512]{2,1,0:T(8,128)(2,1)S(1)}, bf16[3,38,512]{2,1,0:T(8,128)(2,1)S(1)}, u32[]{:S(2)}, u32[]{:S(2)}) %collective-permute-start.3) | collective-permute-done | bytes 116768 | tf_op jit(solution)/shard_map/ppermute | solution.py:505
  17.3 1.4 %collective-permute-done.2.t_ref = bf16[3,38,512]{2,1,0:T(8,128)(2,1)S(1)} collective-permute-done((bf16[3,38,512]{2,1,0:T(8,128)(2,1)S(1)}, bf16[3,38,512]{2,1,0:T(8,128)(2,1)S(1)}, u32[]{:S(2)}, u32[]{:S(2)}) %collective-permute-start.2) | collective-permute-done | bytes 116768 | tf_op jit(solution)/shard_map/ppermute | solution.py:505
  19.3 34.6 %expand.1 = (bf16[1024,512]{1,0:T(8,128)(2,1)}, bf16[1024,512]{1,0:T(8,128)(2,1)}, f32[4,8,512]{2,1,0:T(8,128)}, f32[1,2048]{1,0:T(1,128)}, bf16[2,2,4,512,128]{...) custom-call(s32[4]{0:T(128)} %pad_add_fusion.order_ref, bf16[32,3,512]{2,1,0:T(4,128)(2,1)} %copy-done.4, ...), custom_call_target="tpu_custom_call" | custom-call | flops 23000000512 | bytes 72000000 | tf_op jit(solution)/shard_map/expand/pallas_call | solution.py:253
  55.7 1.9 %collective-permute-start.6 = (bf16[32,3,512]{2,1,0:T(4,128)(2,1)S(1)}, bf16[32,3,512]{2,1,0:T(4,128)(2,1)S(1)}, u32[]{:S(2)}, u32[]{:S(2)}) collective-permute-start(bf16[32,3,512]{2,1,0:T(4,128)(2,1)S(1)} %get-tuple-element.91), channel_id=1, source_target_pairs={{4,0},{8,4},{12,8},{0,12},{5,1},{9,5},{13,9},{1,13},{6,2},{10,6},{... | collective-permute-start | bytes 294920 | tf_op jit(solution)/shard_map/ppermute | solution.py:490
  58.5 1.3 %convert_add_fusion = f32[2,2,4,192,128]{4,3,2,1,0:T(8,128)S(1)} fusion(bf16[2,2,4,512,128]{4,3,2,1,0:T(8,128)(2,1)S(1)} %collective-permute-done.4, bf16[2,2,4,512,128]{4,3,2,1,0:T(8,128)(2,1)} %get-tuple-element.62), kind=kLoop, calls=%fused_computation | loop fusion | flops 1179648 | bytes 3145728 | tf_op jit(solution)/shard_map/add | solution.py:564
  60.1 2.5 %collective-permute-start.7 = (bf16[2,2,2,192,128]{4,3,0,1,2:T(8,128)(2,1)S(1)}, bf16[2,2,2,192,128]{4,3,0,1,2:T(8,128)(2,1)S(1)}, u32[]{:S(2)}, u32[]{:S(2)}) collective-permute-start(bf16[2,2,2,192,128]{4,3,0,1,2:T(8,128)(2,1)S(1)} %fusion.1), channel_id=1, source_target_pairs={{0,1},{1,0},{2,3},{3,2},{4,5},{5,4},{6,7},{7,6},{8,9},{9,8},{10,11... | collective-permute-start | bytes 1179656 | tf_op jit(solution)/shard_map/ppermute | solution.py:466
  62.8 2.1 %collective-permute-start.9 = (bf16[2,1,4,320,128]{4,3,2,1,0:T(8,128)(2,1)S(1)}, bf16[2,1,4,320,128]{4,3,2,1,0:T(8,128)(2,1)S(1)}, u32[]{:S(2)}, u32[]{:S(2)}) collective-permute-start(bf16[2,1,4,320,128]{4,3,2,1,0:T(8,128)(2,1)S(1)} %add_convert_fusion), channel_id=1, source_target_pairs={{0,8},{4,12},{8,0},{12,4},{1,9},{5,13},{9,1},{13,5},{2,10},{6,14},... | collective-permute-start | bytes 1966088 | tf_op jit(solution)/shard_map/ppermute | solution.py:466
  65.0 1.3 %collective-permute-start.12 = (bf16[3,38,512]{2,1,0:T(8,128)(2,1)S(1)}, bf16[3,38,512]{2,1,0:T(8,128)(2,1)S(1)}, u32[]{:S(2)}, u32[]{:S(2)}) collective-permute-start(bf16[3,38,512]{2,1,0:T(8,128)(2,1)S(1)} %pad_maximum_fusion.5), channel_id=1, source_target_pairs={{1,0},{2,1},{3,2},{5,4},{6,5},{7,6},{9,8},{10,9},{11,10},{13,12},{... | collective-permute-start | bytes 350216 | tf_op jit(solution)/shard_map/ppermute | solution.py:505
  66.4 4.7 %collective-permute-start.11 = (bf16[3,38,512]{2,1,0:T(8,128)(2,1)S(1)}, bf16[3,38,512]{2,1,0:T(8,128)(2,1)S(1)}, u32[]{:S(2)}, u32[]{:S(2)}) collective-permute-start(bf16[3,38,512]{2,1,0:T(8,128)(2,1)S(1)} %pad_maximum_fusion.6), channel_id=1, source_target_pairs={{0,1},{1,2},{2,3},{4,5},{5,6},{6,7},{8,9},{9,10},{10,11},{12,13},{... | collective-permute-start | bytes 350216 | tf_op jit(solution)/shard_map/ppermute | solution.py:505
  71.2 1.3 %collective-permute-done.7 = bf16[2,2,2,192,128]{4,3,0,1,2:T(8,128)(2,1)S(1)} collective-permute-done((bf16[2,2,2,192,128]{4,3,0,1,2:T(8,128)(2,1)S(1)}, bf16[2,2,2,192,128]{4,3,0,1,2:T(8,128)(2,1)S(1)}, u32[]{:S(2)}, u32[]{:S(2)}) %collective-permute-start.7) | collective-permute-done | bytes 393248 | tf_op jit(solution)/shard_map/ppermute | solution.py:466
  72.7 3.0 %collective-permute-start.8 = (bf16[2,2,1,192,128]{4,3,0,2,1:T(8,128)(2,1)S(1)}, bf16[2,2,1,192,128]{4,3,0,2,1:T(8,128)(2,1)S(1)}, u32[]{:S(2)}, u32[]{:S(2)}) collective-permute-start(bf16[2,2,1,192,128]{4,3,0,2,1:T(8,128)(2,1)S(1)} %fusion.3), channel_id=1, source_target_pairs={{0,2},{1,3},{2,0},{3,1},{4,6},{5,7},{6,4},{7,5},{8,10},{9,11},{10,... | collective-permute-start | bytes 589832 | tf_op jit(solution)/shard_map/ppermute | solution.py:466
  75.7 10.6 %filter_grad.1 = f32[4,64,128]{2,1,0:T(8,128)} custom-call(bf16[32,32,512]{2,1,0:T(8,128)(2,1)} %f_ref.2, f32[32,32,128]{2,1,0:T(8,128)} %broadcast_in_dim.10.m_ref, bf16[32,3,512]{2,1,0:T(4,128)(2,1)} %copy-done.4, bf16[32,3,512]{2,1,0:T(4,128)(2,1)} %copy-done.5, bf16[3,38,512]{2,1,0:T(8,128)(2,1)} %copy-done.8, bf16[3,38,512]{2,1,0:T(8,128)(2,1)} %copy-done.7, ...), custom_call_target="tpu_custom_call" | custom-call | flops 4600000000 | bytes 14400000 | tf_op jit(solution)/shard_map/filter_grad/pallas_call | solution.py:356
  87.9 1.7 %collective-permute-start.13 = (bf16[1536,128]{1,0:T(8,128)(2,1)S(1)}, bf16[1536,128]{1,0:T(8,128)(2,1)S(1)}, u32[]{:S(2)}, u32[]{:S(2)}) collective-permute-start(bf16[1536,128]{1,0:T(8,128)(2,1)S(1)} %pad_maximum_fusion), channel_id=1, source_target_pairs={{0,1},{1,0},{2,3},{3,2},{4,5},{5,4},{6,7},{7,6},{8,9},{9,8},{10,11... | collective-permute-start | bytes 1179656 | tf_op jit(solution)/shard_map/ppermute | solution.py:466
  90.9 6.2 %input_grad.3.rest_0_ = bf16[32,32,512]{2,1,0:T(8,128)(2,1)} custom-call(bf16[32,32,512]{2,1,0:T(8,128)(2,1)} %bitcast.79, bf16[32,3,512]{2,1,0:T(4,128)(2,1)} %copy-done.2, bf16[32,3,512]{2,1,0:T(4,128)(2,1)} %copy-done.3, bf16[3,38,512]{2,1,0:T(8,128)(2,1)} %copy-done.10, bf16[3,38,512]{2,1,0:T(8,128)(2,1)} %copy-done.9, f32[7,7,512]{2,1,0:T(8,128)} %k_ref.7, ...), custom_call_target="tpu_custom_call" | custom-call | flops 4600000000 | bytes 14400000 | tf_op jit(solution)/shard_map/input_grad/pallas_call | solution.py:405
  97.1 2.3 %collective-permute-done.13 = bf16[1536,128]{1,0:T(8,128)(2,1)S(1)} collective-permute-done((bf16[1536,128]{1,0:T(8,128)(2,1)S(1)}, bf16[1536,128]{1,0:T(8,128)(2,1)S(1)}, u32[]{:S(2)}, u32[]{:S(2)}) %collective-permute-start.13) | collective-permute-done | bytes 393248 | tf_op jit(solution)/shard_map/ppermute | solution.py:466
  99.8 4.1 %input_grad.4.rest_0_ = bf16[32,32,512]{2,1,0:T(8,128)(2,1)} custom-call(bf16[32,32,512]{2,1,0:T(8,128)(2,1)} %bitcast.80, bf16[32,3,512]{2,1,0:T(4,128)(2,1)} %copy-done.2, bf16[32,3,512]{2,1,0:T(4,128)(2,1)} %copy-done.3, bf16[3,38,512]{2,1,0:T(8,128)(2,1)} %copy-done.10, bf16[3,38,512]{2,1,0:T(8,128)(2,1)} %copy-done.9, ...), custom_call_target="tpu_custom_call", output_to_operand_aliasing={{}: (8, {})} | custom-call | flops 4600000000 | bytes 14400000 | tf_op jit(solution)/shard_map/input_grad/pallas_call | solution.py:405
  103.9 8.6 %collective-permute-done.14 = bf16[896,128]{1,0:T(8,128)(2,1)S(1)} collective-permute-done((bf16[896,128]{1,0:T(8,128)(2,1)S(1)}, bf16[896,128]{1,0:T(8,128)(2,1)S(1)}, u32[]{:S(2)}, u32[]{:S(2)}) %collective-permute-start.14) | collective-permute-done | bytes 229408 | tf_op jit(solution)/shard_map/ppermute | solution.py:466
  113.2 1.5 %collective-permute-start.15 = (bf16[640,128]{1,0:T(8,128)(2,1)S(1)}, bf16[640,128]{1,0:T(8,128)(2,1)S(1)}, u32[]{:S(2)}, u32[]{:S(2)}) collective-permute-start(bf16[640,128]{1,0:T(8,128)(2,1)S(1)} %pad_maximum_fusion.2), channel_id=1, source_target_pairs={{0,8},{4,12},{8,0},{12,4},{1,9},{5,13},{9,1},{13,5},{2,10},{6,14},... | collective-permute-start | bytes 491528 | tf_op jit(solution)/shard_map/ppermute | solution.py:466
  114.7 4.1 %input_grad.5 = bf16[32,32,512]{2,1,0:T(8,128)(2,1)} custom-call(bf16[32,32,512]{2,1,0:T(8,128)(2,1)} %bitcast.81, bf16[32,3,512]{2,1,0:T(4,128)(2,1)} %copy-done.2, bf16[32,3,512]{2,1,0:T(4,128)(2,1)} %copy-done.3, bf16[3,38,512]{2,1,0:T(8,128)(2,1)} %copy-done.10, bf16[3,38,512]{2,1,0:T(8,128)(2,1)} %copy-done.9, ...), custom_call_target="tpu_custom_call", output_to_operand_aliasing={{}: (8, {})} | custom-call | flops 4600000000 | bytes 14400000 | tf_op jit(solution)/shard_map/input_grad/pallas_call | solution.py:405
  121.0 2.1 %finish.1 = (f32[128,512]{1,0:T(8,128)}, f32[512,128]{1,0:T(8,128)}, f32[7,7,512]{2,1,0:T(8,128)}, f32[4,1,512]{2,1,0:T(1,128)}, f32[1,2048]{1,0:T(1,128)}) custom-call(f32[2,320,128]{2,1,0:T(8,128)} %fusion.2.a_ref, f32[2,192,128]{2,1,0:T(8,128)} %slice_bitcast_fusion.b_ref, bf16[640,128]{1,0:T(8,128)(2,1)} %copy-done.6, ...), custom_call_target="tpu_custom_call" | custom-call | flops 2300000000 | bytes 7200000 | tf_op jit(solution)/shard_map/finish/pallas_call | solution.py:449
  123.1 1.3 %fusion.17 = (f32[1,1,512]{2,1,0:T(1,128)}, f32[1,1,512]{2,1,0:T(1,128)}, f32[1,1,512]{2,1,0:T(1,128)}, f32[1,1,512]{2,1,0:T(1,128)}) fusion(f32[4,1,512]{2,1,0:T(1,128)} %get-tuple-element.80), kind=kLoop, calls=%fused_computation.52 | loop fusion | bytes 16384 | tf_op jit(solution)/shard_map/slice | solution.py:624
  (83 shorter events, 16.6 us)
Async XLA Ops:
  2.7 5.1 %collective-permute-start = (bf16[32,3,512]{2,1,0:T(4,128)(2,1)S(1)}, bf16[32,3,512]{2,1,0:T(4,128)(2,1)S(1)}, u32[]{:S(2)}, u32[]{:S(2)}) collective-permute-start(bf16[32,3,512]{2,1,0:T(4,128)(2,1)S(1)} %get-tuple-element.95), channel_id=1, source_target_pairs={{0,4},{4,8},{8,12},{12,0},{1,5},{5,9},{9,13},{13,1},{2,6},{6,10},{... | collective-permute-start | bytes 294920 | tf_op jit(solution)/shard_map/ppermute | solution.py:490
  3.2 5.8 %collective-permute-start.1 = (bf16[32,3,512]{2,1,0:T(4,128)(2,1)S(1)}, bf16[32,3,512]{2,1,0:T(4,128)(2,1)S(1)}, u32[]{:S(2)}, u32[]{:S(2)}) collective-permute-start(bf16[32,3,512]{2,1,0:T(4,128)(2,1)S(1)} %get-tuple-element.94), channel_id=1, source_target_pairs={{4,0},{8,4},{12,8},{0,12},{5,1},{9,5},{13,9},{1,13},{6,2},{10,6},{... | collective-permute-start | bytes 294920 | tf_op jit(solution)/shard_map/ppermute | solution.py:490
  7.9 10.9 %copy-start.4 = (bf16[32,3,512]{2,1,0:T(4,128)(2,1)}, bf16[32,3,512]{2,1,0:T(4,128)(2,1)S(1)}, u32[]{:S(2)}) copy-start(bf16[32,3,512]{2,1,0:T(4,128)(2,1)S(1)} %collective-permute-done.l_ref) | copy-start | bytes 294916
  9.1 9.6 %copy-start.5 = (bf16[32,3,512]{2,1,0:T(4,128)(2,1)}, bf16[32,3,512]{2,1,0:T(4,128)(2,1)S(1)}, u32[]{:S(2)}) copy-start(bf16[32,3,512]{2,1,0:T(4,128)(2,1)S(1)} %collective-permute-done.1.r_ref) | copy-start | bytes 294916
  9.2 8.1 %collective-permute-start.3 = (bf16[3,38,512]{2,1,0:T(8,128)(2,1)S(1)}, bf16[3,38,512]{2,1,0:T(8,128)(2,1)S(1)}, u32[]{:S(2)}, u32[]{:S(2)}) collective-permute-start(bf16[3,38,512]{2,1,0:T(8,128)(2,1)S(1)} %pad_maximum_fusion.4), channel_id=1, source_target_pairs={{1,0},{2,1},{3,2},{5,4},{6,5},{7,6},{9,8},{10,9},{11,10},{13,12},{... | collective-permute-start | bytes 350216 | tf_op jit(solution)/shard_map/ppermute | solution.py:505
  10.5 8.2 %collective-permute-start.2 = (bf16[3,38,512]{2,1,0:T(8,128)(2,1)S(1)}, bf16[3,38,512]{2,1,0:T(8,128)(2,1)S(1)}, u32[]{:S(2)}, u32[]{:S(2)}) collective-permute-start(bf16[3,38,512]{2,1,0:T(8,128)(2,1)S(1)} %pad_maximum_fusion.3), channel_id=1, source_target_pairs={{0,1},{1,2},{2,3},{4,5},{5,6},{6,7},{8,9},{9,10},{10,11},{12,13},{... | collective-permute-start | bytes 350216 | tf_op jit(solution)/shard_map/ppermute | solution.py:505
  17.3 1.4 %copy-start.7 = (bf16[3,38,512]{2,1,0:T(8,128)(2,1)}, bf16[3,38,512]{2,1,0:T(8,128)(2,1)S(1)}, u32[]{:S(2)}) copy-start(bf16[3,38,512]{2,1,0:T(8,128)(2,1)S(1)} %collective-permute-done.3.b_ref) | copy-start | bytes 350212
  53.9 4.6 %collective-permute-start.4 = (bf16[2,2,4,512,128]{4,3,2,1,0:T(8,128)(2,1)}, bf16[2,2,4,512,128]{4,3,2,1,0:T(8,128)(2,1)S(1)}, u32[]{:S(2)}, u32[]{:S(2)}) collective-permute-start(bf16[2,2,4,512,128]{4,3,2,1,0:T(8,128)(2,1)} %get-tuple-element.52), channel_id=1, source_target_pairs={{0,4},{4,0},{8,12},{12,8},{1,5},{5,1},{9,13},{13,9},{2,6},{6,2},{1... | collective-permute-start | bytes 6291464 | tf_op jit(solution)/shard_map/ppermute | solution.py:466
  55.2 9.7 %collective-permute-start.5 = (bf16[32,3,512]{2,1,0:T(4,128)(2,1)S(1)}, bf16[32,3,512]{2,1,0:T(4,128)(2,1)S(1)}, u32[]{:S(2)}, u32[]{:S(2)}) collective-permute-start(bf16[32,3,512]{2,1,0:T(4,128)(2,1)S(1)} %get-tuple-element.90), channel_id=1, source_target_pairs={{0,4},{4,8},{8,12},{12,0},{1,5},{5,9},{9,13},{13,1},{2,6},{6,10},{... | collective-permute-start | bytes 294920 | tf_op jit(solution)/shard_map/ppermute | solution.py:490
  55.7 9.2 %collective-permute-start.6 = (bf16[32,3,512]{2,1,0:T(4,128)(2,1)S(1)}, bf16[32,3,512]{2,1,0:T(4,128)(2,1)S(1)}, u32[]{:S(2)}, u32[]{:S(2)}) collective-permute-start(bf16[32,3,512]{2,1,0:T(4,128)(2,1)S(1)} %get-tuple-element.91), channel_id=1, source_target_pairs={{4,0},{8,4},{12,8},{0,12},{5,1},{9,5},{13,9},{1,13},{6,2},{10,6},{... | collective-permute-start | bytes 294920 | tf_op jit(solution)/shard_map/ppermute | solution.py:490
  59.9 2.7 %copy-start = (bf16[2,2,4,512,128]{4,3,2,1,0:T(8,128)(2,1)S(1)}, bf16[2,2,4,512,128]{4,3,2,1,0:T(8,128)(2,1)}, u32[]{:S(2)}) copy-start(bf16[2,2,4,512,128]{4,3,2,1,0:T(8,128)(2,1)} %get-tuple-element.62) | copy-start | bytes 6291460
  60.1 12.4 %collective-permute-start.7 = (bf16[2,2,2,192,128]{4,3,0,1,2:T(8,128)(2,1)S(1)}, bf16[2,2,2,192,128]{4,3,0,1,2:T(8,128)(2,1)S(1)}, u32[]{:S(2)}, u32[]{:S(2)}) collective-permute-start(bf16[2,2,2,192,128]{4,3,0,1,2:T(8,128)(2,1)S(1)} %fusion.1), channel_id=1, source_target_pairs={{0,1},{1,0},{2,3},{3,2},{4,5},{5,4},{6,7},{7,6},{8,9},{9,8},{10,11... | collective-permute-start | bytes 1179656 | tf_op jit(solution)/shard_map/ppermute | solution.py:466
  62.8 23.6 %collective-permute-start.9 = (bf16[2,1,4,320,128]{4,3,2,1,0:T(8,128)(2,1)S(1)}, bf16[2,1,4,320,128]{4,3,2,1,0:T(8,128)(2,1)S(1)}, u32[]{:S(2)}, u32[]{:S(2)}) collective-permute-start(bf16[2,1,4,320,128]{4,3,2,1,0:T(8,128)(2,1)S(1)} %add_convert_fusion), channel_id=1, source_target_pairs={{0,8},{4,12},{8,0},{12,4},{1,9},{5,13},{9,1},{13,5},{2,10},{6,14},... | collective-permute-start | bytes 1966088 | tf_op jit(solution)/shard_map/ppermute | solution.py:466
  64.9 7.7 %copy-start.2 = (bf16[32,3,512]{2,1,0:T(4,128)(2,1)}, bf16[32,3,512]{2,1,0:T(4,128)(2,1)S(1)}, u32[]{:S(2)}) copy-start(bf16[32,3,512]{2,1,0:T(4,128)(2,1)S(1)} %collective-permute-done.5.l_ref) | copy-start | bytes 294916
  64.9 7.7 %copy-start.3 = (bf16[32,3,512]{2,1,0:T(4,128)(2,1)}, bf16[32,3,512]{2,1,0:T(4,128)(2,1)S(1)}, u32[]{:S(2)}) copy-start(bf16[32,3,512]{2,1,0:T(4,128)(2,1)S(1)} %collective-permute-done.6.r_ref) | copy-start | bytes 294916
  65.0 24.6 %collective-permute-start.12 = (bf16[3,38,512]{2,1,0:T(8,128)(2,1)S(1)}, bf16[3,38,512]{2,1,0:T(8,128)(2,1)S(1)}, u32[]{:S(2)}, u32[]{:S(2)}) collective-permute-start(bf16[3,38,512]{2,1,0:T(8,128)(2,1)S(1)} %pad_maximum_fusion.5), channel_id=1, source_target_pairs={{1,0},{2,1},{3,2},{5,4},{6,5},{7,6},{9,8},{10,9},{11,10},{13,12},{... | collective-permute-start | bytes 350216 | tf_op jit(solution)/shard_map/ppermute | solution.py:505
  66.4 23.1 %collective-permute-start.11 = (bf16[3,38,512]{2,1,0:T(8,128)(2,1)S(1)}, bf16[3,38,512]{2,1,0:T(8,128)(2,1)S(1)}, u32[]{:S(2)}, u32[]{:S(2)}) collective-permute-start(bf16[3,38,512]{2,1,0:T(8,128)(2,1)S(1)} %pad_maximum_fusion.6), channel_id=1, source_target_pairs={{0,1},{1,2},{2,3},{4,5},{5,6},{6,7},{8,9},{9,10},{10,11},{12,13},{... | collective-permute-start | bytes 350216 | tf_op jit(solution)/shard_map/ppermute | solution.py:505
  72.7 13.6 %collective-permute-start.8 = (bf16[2,2,1,192,128]{4,3,0,2,1:T(8,128)(2,1)S(1)}, bf16[2,2,1,192,128]{4,3,0,2,1:T(8,128)(2,1)S(1)}, u32[]{:S(2)}, u32[]{:S(2)}) collective-permute-start(bf16[2,2,1,192,128]{4,3,0,2,1:T(8,128)(2,1)S(1)} %fusion.3), channel_id=1, source_target_pairs={{0,2},{1,3},{2,0},{3,1},{4,6},{5,7},{6,4},{7,5},{8,10},{9,11},{10,... | collective-permute-start | bytes 589832 | tf_op jit(solution)/shard_map/ppermute | solution.py:466
  86.3 1.6 %collective-permute-start.10 = (f32[4,64,128]{2,1,0:T(8,128)}, f32[4,64,128]{2,1,0:T(8,128)S(1)}, u32[]{:S(2)}, u32[]{:S(2)}) collective-permute-start(f32[4,64,128]{2,1,0:T(8,128)} %filter_grad.1), channel_id=1, source_target_pairs={{0,4},{4,0},{8,12},{12,8},{1,5},{5,1},{9,13},{13,9},{2,6},{6,2},{1... | collective-permute-start | bytes 393224 | tf_op jit(solution)/shard_map/ppermute | solution.py:466
  86.8 1.0 copy-start.1
  87.9 11.5 %collective-permute-start.13 = (bf16[1536,128]{1,0:T(8,128)(2,1)S(1)}, bf16[1536,128]{1,0:T(8,128)(2,1)S(1)}, u32[]{:S(2)}, u32[]{:S(2)}) collective-permute-start(bf16[1536,128]{1,0:T(8,128)(2,1)S(1)} %pad_maximum_fusion), channel_id=1, source_target_pairs={{0,1},{1,0},{2,3},{3,2},{4,5},{5,4},{6,7},{7,6},{8,9},{9,8},{10,11... | collective-permute-start | bytes 1179656 | tf_op jit(solution)/shard_map/ppermute | solution.py:466
  99.6 12.9 %collective-permute-start.14 = (bf16[896,128]{1,0:T(8,128)(2,1)S(1)}, bf16[896,128]{1,0:T(8,128)(2,1)S(1)}, u32[]{:S(2)}, u32[]{:S(2)}) collective-permute-start(bf16[896,128]{1,0:T(8,128)(2,1)S(1)} %pad_maximum_fusion.1), channel_id=1, source_target_pairs={{0,2},{1,3},{2,0},{3,1},{4,6},{5,7},{6,4},{7,5},{8,10},{9,11},{10,... | collective-permute-start | bytes 688136 | tf_op jit(solution)/shard_map/ppermute | solution.py:466
  113.2 7.1 %collective-permute-start.15 = (bf16[640,128]{1,0:T(8,128)(2,1)S(1)}, bf16[640,128]{1,0:T(8,128)(2,1)S(1)}, u32[]{:S(2)}, u32[]{:S(2)}) collective-permute-start(bf16[640,128]{1,0:T(8,128)(2,1)S(1)} %pad_maximum_fusion.2), channel_id=1, source_target_pairs={{0,8},{4,12},{8,0},{12,4},{1,9},{5,13},{9,1},{13,5},{2,10},{6,14},... | collective-permute-start | bytes 491528 | tf_op jit(solution)/shard_map/ppermute | solution.py:466
  120.3 0.7 copy-start.6
  (3 other events, 1.9 us)

commit v11 on v10

--- a/solution.py
+++ b/solution.py
@@ -87,7 +87,7 @@
     l_ref, r_ref, t_ref, b_ref, k_ref, gain_ref, bias_ref, scale_ref, bo_ref, m_ref, cot_ref, f_ref,
     wi_ref, bi_ref, wo_ref,
     dconv_ref, mixed_ref, sums_ref, gbi_ref, sent_ref, kept_ref,
-    window, conv, xhat_s, inv_s, normed, normed_t, dbr, dbr_t, act, dpre, d_normed, branch, pre_s, dact_s,
+    window, conv, xhat_s, inv_s, normed, normed_t, dbr, dbr_t, act, dpre, d_normed, branch, pre_s, d_act,
 ):
     rows, cols, channels = f_ref.shape
     cells = rows * cols
@@ -123,59 +123,74 @@
         branch[...] = jnp.zeros_like(branch)
         d_normed[...] = jnp.zeros_like(d_normed)
 
-        def convolve(lanes):
-            fill_window(window, f_ref[:, :, lanes].astype(F32) * m_ref[...], l_ref, r_ref, t_ref, b_ref, lanes)
-            for start in range(0, cols, SUB):
-                sums = band_conv(window, k_ref, lanes, (start,), rows, 3, False)
-                for row in range(rows):
-                    conv[row, start : start + SUB, lanes] = sums[row, start]
-
-        each_lane_block(channels, convolve)
-
-        def standardize(places, total):
-            xs = [conv[row, at : at + strip, :] for row, at, _ in places]
-            centered = [x - average for x, average in zip(xs, mean(xs))]
-            invs = [lax.rsqrt(var + 1e-06) for var in mean([x * x for x in centered])]
-            xhats = [x * inv for x, inv in zip(centered, invs)]
+        def cotangents(places, total):
             grads = [
                 mask * (scale_ref[...] * cot_ref[here, :].astype(F32))
                 for mask, (_, _, here) in zip(ocean(places), places)
             ]
-            for (_, _, here), xhat, inv, grad in zip(places, xhats, invs, grads):
+            for (_, _, here), grad in zip(places, grads):
+                dbr[here, :] = (0.5 * grad).astype(BF16)
+            return total + folded(grads)
+
+        sums_ref[0] = strips(cotangents, zero)
+        for at in range(0, cells, chunk):
+            here = slice(at, at + chunk)
+            dbr_t[:, here] = dbr[here, :].T
+        share = wo_ref.shape[0] // wide
+
+        def convolve(index, _):
+            lanes = lane_block(index)
+            units = pl.ds(pl.multiple_of(index * share, LANES), share)
+            fill_window(window, f_ref[:, :, lanes].astype(F32) * m_ref[...], l_ref, r_ref, t_ref, b_ref, lanes)
+            for start in range(0, cols, SUB):
+                here = slice(start * rows, (start + SUB) * rows)
+                d_act[here, units] = lax.dot_general(
+                    dbr[here, :], wo_ref[units, :], (((1,), (1,)), ((), ())), preferred_element_type=F32
+                )
+                sums = band_conv(window, k_ref, lanes, (start,), rows, 3, False)
+                for row in range(rows):
+                    conv[row, start : start + SUB, lanes] = sums[row, start]
+            return 0
+
+        lax.fori_loop(0, wide, convolve, 0)
+
+        def standardize(places, _):
+            xs = [conv[row, at : at + strip, :] for row, at, _ in places]
+            centered = [x - average for x, average in zip(xs, mean(xs))]
+            invs = [lax.rsqrt(var + 1e-06) for var in mean([x * x for x in centered])]
+            for (_, _, here), x, inv in zip(places, centered, invs):
+                xhat = x * inv
                 xhat_s[here, :] = xhat
                 inv_s[here, :] = jnp.broadcast_to(inv, (strip, LANES))
                 normed[here, :] = (xhat * gain_ref[...] + bias_ref[...]).astype(BF16)
-                dbr[here, :] = (0.5 * grad).astype(BF16)
-            return total + folded(grads)
-
-        sums_ref[0] = strips(standardize, zero)
+            return 0
+
+        strips(standardize, 0)
         for at in range(0, cells, chunk):
             here = slice(at, at + chunk)
             normed_t[:, here] = normed[here, :].T
-            dbr_t[:, here] = dbr[here, :].T
 
     block = act.shape[1]
     cut = min(block, 256)
     count = block // cut
     _, parts, _, width = sent_ref.shape
     is_sent = step_now < pl.num_programs(0) // 2
+    base = pl.multiple_of(order_ref[step_now] * block, LANES)
 
     def products(index):
         lanes = slice(index * cut, (index + 1) * cut)
         pre_s[index % 2] = jnp.dot(normed[...], wi_ref[:, lanes], preferred_element_type=F32)
-        dact_s[index % 2] = lax.dot_general(
-            dbr[...], wo_ref[lanes, :], (((1,), (1,)), ((), ())), preferred_element_type=F32
-        )
 
     def activate(index):
         lanes = slice(index * cut, (index + 1) * cut)
+        units = pl.ds(pl.multiple_of(base + index * cut, LANES), cut)
         bias = bi_ref[:, lanes]
         total = jnp.zeros((SUB, cut), F32)
         for at in range(0, cells, strip):
             here = slice(at, at + strip)
             value, slope = gelu_twice(pre_s[index % 2, here, :] + bias)
             act[here, lanes] = value.astype(BF16)
-            d_pre = dact_s[index % 2, here, :] * slope
+            d_pre = d_act[here, units] * slope
             dpre[here, lanes] = d_pre.astype(BF16)
             total = total + (d_pre[:SUB] + d_pre[SUB:])
         gbi_ref[:, lanes] = jnp.sum(total, axis=0, keepdims=True)
@@ -203,7 +218,7 @@
         if index > 0:
             weight_grads(index - 1)
     weight_grads(count - 1)
-    branch[...] += jnp.dot(act[...], wo_ref[...], preferred_element_type=F32)
+    branch[...] += jnp.dot(act[...], wo_ref[pl.ds(base, block), :], preferred_element_type=F32)
     d_normed[...] += lax.dot_general(
         dpre[...], wi_ref[...], (((1,), (1,)), ((), ())), preferred_element_type=F32
     )
@@ -259,7 +274,7 @@
             + [
                 pl.BlockSpec((channels, block), lambda h, order: (0, order[h])),
                 pl.BlockSpec((1, block), lambda h, order: (0, order[h])),
-                pl.BlockSpec((block, channels), lambda h, order: (order[h], 0)),
+                once(w_out.shape),
             ],
             out_specs=[
                 once((cells, channels)),
@@ -283,7 +298,7 @@
                 pltpu.VMEM((cells, channels), F32),
                 pltpu.VMEM((cells, channels), F32),
                 pltpu.VMEM((2, cells, min(block, 256)), F32),
-                pltpu.VMEM((2, cells, min(block, 256)), F32),
+                pltpu.VMEM((cells, hidden), F32),
             ],
         ),
         out_shape=[
@@ -309,14 +324,13 @@
     window[3 + rows : 6 + rows, 5 : 11 + cols, :] = b_ref[:, :, lanes].astype(F32)
 
 
-def filter_grad_kernel(
-    f_ref, m_ref, l_ref, r_ref, t_ref, b_ref, d_ref, sums_ref, gbi_ref, o_ref, window, grad
-):
+def filter_grad_kernel(first, f_ref, m_ref, l_ref, r_ref, t_ref, b_ref, d_ref, sums_ref, gbi_ref, *rest):
+    o_ref, window, grad = rest[-3:]
     rows, cols, channels = f_ref.shape
     blocks = channels // LANES
 
     def block(index, _):
-        lanes = lane_block(index)
+        lanes = lane_block(first + index)
         fill_window(window, f_ref[:, :, lanes].astype(F32) * m_ref[...], l_ref, r_ref, t_ref, b_ref, lanes)
         grad[...] = d_ref[:, :, lanes].astype(F32)
         for col_off in range(7):
@@ -345,25 +359,32 @@
         for at, source in enumerate((1, 2, 3, 0)):
             o_ref[index, 56 + at : 57 + at, :] = jnp.sum(sums_ref[source, :, lanes], axis=0, keepdims=True)
         for at in range(4):
-            o_ref[index, 60 + at : 61 + at, :] = gbi_ref[:, lane_block(at * blocks + index)]
+            o_ref[index, 60 + at : 61 + at, :] = gbi_ref[:, lane_block(at * blocks + first + index)]
         return 0
 
-    lax.fori_loop(0, blocks, block, 0)
-
-
-def filter_grad(fields, mask, left, right, top, bot, d_conv, sums, gbi):
+    lax.fori_loop(0, o_ref.shape[0], block, 0)
+
+
+def filter_grad(fields, mask, left, right, top, bot, d_conv, sums, gbi, half, old=None):
     rows, cols, channels = fields.shape
+    blocks = channels // LANES
+    whole = (fields, mask, left, right, top, bot, d_conv, sums, gbi)
+    more = [] if old is None else [old]
     return pl.pallas_call(
-        filter_grad_kernel,
-        out_shape=jax.ShapeDtypeStruct((channels // LANES, 64, LANES), F32),
+        functools.partial(filter_grad_kernel, half * (blocks // 2)),
+        grid=(1,),
+        out_shape=jax.ShapeDtypeStruct((blocks, 64, LANES), F32),
+        in_specs=[once(x.shape) for x in whole] + [UNUSED] * len(more),
+        out_specs=pl.BlockSpec((blocks // 2, 64, LANES), lambda i: (half, 0, 0)),
         scratch_shapes=[
             pltpu.VMEM((rows + 6, cols + 16, LANES), F32),
             pltpu.VMEM((rows, cols, LANES), F32),
         ],
+        input_output_aliases={9: 0} if more else {},
         compiler_params=params(56),
         cost_estimate=estimate(4),
         name="filter_grad",
-    )(fields, mask, left, right, top, bot, d_conv, sums, gbi)
+    )(*whole, *more)
 
 
 def input_grad_kernel(first, d_ref, l_ref, r_ref, t_ref, b_ref, k_ref, m_ref, cot_ref, *rest):
@@ -421,14 +442,17 @@
     )(*whole, mask, cot, *more)
 
 
-def finish_kernel(a_ref, b_ref, load_ref, small_ref, wo_ref, wi_ref, gk_ref, vec_ref, gbi_ref):
+def finish_kernel(
+    a_ref, load_a_ref, b_ref, load_ref, small_ref, wo_ref, wi_ref, gk_ref, gsc_ref, gga_ref, gsh_ref, gbo_ref, gbi_ref
+):
     channels = wi_ref.shape[0]
-    border = a_ref.shape[1]
+    border = a_ref.shape[3]
     rest = channels - border
     blocks = channels // LANES
     for index, ref in ((0, wo_ref), (1, wi_ref)):
-        came = load_ref[index * rest : (index + 1) * rest, :].astype(F32)
-        grad = jnp.concatenate([a_ref[index], b_ref[index] + came], axis=0)
+        came_a = load_a_ref[index * border : (index + 1) * border, :].astype(F32)
+        came_b = load_ref[index * rest : (index + 1) * rest, :].astype(F32)
+        grad = jnp.concatenate([a_ref[index, 0, 0] + came_a, b_ref[index, 1, 0] + came_b], axis=0)
         ref[...] = grad.T if index == 0 else grad
     for block in range(blocks):
         at = 2 * rest + block * 64
@@ -436,29 +460,33 @@
         lanes = slice(block * LANES, (block + 1) * LANES)
         for row in range(7):
             gk_ref[row, :, lanes] = total[row * 8 : row * 8 + 7]
+        for row, ref in enumerate((gsc_ref, gga_ref, gsh_ref, gbo_ref)):
+            ref[:, lanes] = total[56 + row : 57 + row]
         for row in range(4):
-            vec_ref[row, :, lanes] = total[56 + row : 57 + row]
-            gbi_ref[:, slice(row * channels + block * LANES, row * channels + (block + 1) * LANES)] = total[
-                60 + row : 61 + row
-            ]
-
-
-def finish(first, second, load, small, hidden):
-    channels = first.shape[1] + second.shape[1]
-    width = first.shape[2]
+            to = slice(row * channels + block * LANES, row * channels + (block + 1) * LANES)
+            gbi_ref[:, to] = total[60 + row : 61 + row]
+
+
+def finish(first, load_first, second, load, small, hidden):
+    channels = first.shape[3] + second.shape[3]
+    width = first.shape[4]
+    line = jax.ShapeDtypeStruct((1, channels), F32)
     return pl.pallas_call(
         finish_kernel,
         out_shape=[
             jax.ShapeDtypeStruct((width, channels), F32),
             jax.ShapeDtypeStruct((channels, width), F32),
             jax.ShapeDtypeStruct((7, 7, channels), F32),
-            jax.ShapeDtypeStruct((4, 1, channels), F32),
+            line,
+            line,
+            line,
+            line,
             jax.ShapeDtypeStruct((1, hidden), F32),
         ],
         compiler_params=params(56),
         cost_estimate=estimate(2),
         name="finish",
-    )(first, second, load, small)
+    )(first, load_first, second, load, small)
 
 
 def swap(values, axis, bit):
@@ -550,7 +578,7 @@
     d_left, d_right = side_halo(d_conv[:, cols - 3 :], d_conv[:, :3])
 
     far = n_lon // 4
-    border = channels * 5 // 8
+    border = channels // 2
     lon_bits = [("lon", 1, bit) for bit in bits_of("lon")[2:]]
     lat_bits = [("lat", 2, bit) for bit in bits_of("lat")]
 
@@ -571,27 +599,24 @@
     far_first = pair(far_lons, first).astype(BF16)
     got_first = swap(far_first, "lon", 2)
     cut_b = halves(pair(slice(0, 2 * far), second), *lat_bits[0])
+    rest = (mask, left, right, top, bot, d_conv, sums, g_bi)
+    small = filter_grad(after(fields, far_first, cut_b[1]), *rest, 0)
     d_tail, d_head = end_rows(
-        d_conv[:3], d_conv[rows - 3 :],
-        after(d_left, far_first, cut_b[1]), after(d_right, far_first, cut_b[1]),
+        d_conv[:3], d_conv[rows - 3 :], after(d_left, small), after(d_right, small)
     )
     d_top, d_bot = end_halo(d_tail, d_head)
     for (axis, _, bit), follow in zip(lat_bits[:-1], lat_bits[1:]):
-        cut_b = halves(fold(*cut_b, axis, bit, d_head), *follow)
+        cut_b = halves(fold(*cut_b, axis, bit, small), *follow)
 
     def pack(sent, small):
         return jnp.concatenate([sent.reshape(-1, LANES), small.astype(BF16).reshape(-1, LANES)])
 
-    def ride(load, sent, small, axis, bit, last):
-        came = after(swap(load, axis, bit), last)
+    def ride(came, sent, small, last):
         size = sent.size // LANES
         own = after(lax.reduce_precision(small, 8, 7), last)
         return came[:size].reshape(sent.shape).astype(F32), own + came[size:].astype(F32).reshape(small.shape)
 
-    small = filter_grad(
-        after(fields, d_tail, d_head, far_first, cut_b[1]),
-        mask, left, right, top, bot, d_conv, sums, g_bi,
-    )
+    small = filter_grad(after(fields, d_tail, d_head, cut_b[1]), *rest, 1, small)
     alone = small
     whole = pair(near_lons, first, alone) + after(got_first, alone).astype(F32)
     whole_b = fold(*cut_b, lat_bits[-1][0], lat_bits[-1][2], alone)
@@ -611,19 +636,19 @@
                 after(d_conv, load, far_second), *back, block, count, grad_fields
             )
             block += count
-        came, small = ride(load, sent, small, axis, bit, last)
-        whole = after(mine, last) + came
+        load_a, mine_a = after(swap(load, axis, bit), last), after(mine, last)
+        came, small = ride(load_a, sent, small, last)
+        whole = mine_a + came
     load = pack(far_second, small)
     last = grad_fields = input_grad(after(d_conv, load), *back, block, 1, grad_fields)
     if not lon_bits and whole.shape[-1] == LANES:
         load = after(swap(load, "lon", 2), last)
-        near = after(whole_b, last)[:, near_lons]
-        grad_wo, grad_wi, grad_k, vectors, g_bi = finish(
-            whole[:, 0, 0], near[:, 0, 0], load, after(lax.reduce_precision(small, 8, 7), last), hidden
+        grad_wo, grad_wi, grad_k, *lines, g_bi = finish(
+            mine_a, load_a, after(whole_b, last), load, after(lax.reduce_precision(small, 8, 7), last), hidden
         )
-        g_scale, g_gain, g_shift, g_bo = (vectors[i, 0] for i in range(4))
+        g_scale, g_gain, g_shift, g_bo = (line.reshape(channels) for line in lines)
     else:
-        came, small = ride(load, far_second, small, "lon", 2, last)
+        came, small = ride(after(swap(load, "lon", 2), last), far_second, small, last)
         whole_b = after(whole_b, last)[:, near_lons] + came
         for axis, dim, bit in lon_bits:
             whole_b = fold(*halves(whole_b, axis, dim, bit), axis, bit, last)

time: 125 us -> 123 us (0.984)
  local copies, waits for them, and re-layouts: 8.12 us -> 5.51 us
  Pallas kernels: 61.7 us -> 64.3 us
  starting transfers between devices: 27.9 us -> 26.5 us
    pallas_call x1 -> x2, Pallas kernels: 10.6 us -> 13.1 us  [filter_grad(): pl.pallas_call(functools.partial(filter_grad_kernel, half * (blocks // 2)...]
    ppermute x8, starting transfers between devices: 11 us -> 9.14 us  [swap(): return lax.ppermute(values, axis, [(i, i ^ bit) for i in range(count)])]
    slice x1 -> x0, local copies, waits for them, and re-layouts: 1.28 us -> none  [per_device(): g_scale, g_gain, g_shift, g_bo = (vectors[i, 0] for i in range(4))]
  transfers between devices with their start and end apart: 16 -> 16, of which waited for: 8 -> 8; matrix products, arithmetic and copies ran while one was open for 7% -> 7% of each run, Pallas kernels for 20% -> 23%
where the time goes in v11:
time: 123 us; the launch traced here: 122 us
  Pallas kernels  64.3 us (52%)
  starting transfers between devices  26.5 us (22%)
  waiting for transfers between devices  17.2 us (14%)
  other arithmetic  7.81 us (6%)
  local copies, waits for them, and re-layouts  5.51 us (4%)
    pallas_call x1, Pallas kernels, expand(): pl.pallas_call(expand_kernel, grid_spec=pltpu.PrefetchScalarGridSpec(num_...  34.5 us
    pallas_call x3, Pallas kernels, input_grad(): pl.pallas_call(functools.partial(input_grad_kernel, rows // 4 * first), g...  14.5 us
    pallas_call x2, Pallas kernels, filter_grad(): pl.pallas_call(functools.partial(filter_grad_kernel, half * (blocks // 2)...  13.1 us
    ppermute x8, waiting for transfers between devices, swap(): return lax.ppermute(values, axis, [(i, i ^ bit) for i in range(count)])  12.5 us
    ppermute x4, starting transfers between devices, end_halo(): return (lax.ppermute(tail, 'lat', ahead), lax.ppermute(head, 'lat', back))  12.5 us
    ppermute x8, starting transfers between devices, swap(): return lax.ppermute(values, axis, [(i, i ^ bit) for i in range(count)])  9.14 us
    ppermute x4, starting transfers between devices, side_halo(): return (lax.ppermute(last, 'lon', ahead), lax.ppermute(first, 'lon', back))  4.88 us
    ppermute x4, waiting for transfers between devices, end_halo(): return (lax.ppermute(tail, 'lat', ahead), lax.ppermute(head, 'lat', back))  3.53 us
  transfers between devices with their start and end apart: 16, of which 8 were waited for; matrix products, arithmetic and copies ran while one was open for 7% of the time, Pallas kernels for 23%

profile of v11, /device:TPU:0, one launch (start us, length us, event | category | flops | bytes accessed | tf_op | source)
XLA Modules:
  0.0 122.3 jit_solution(11486754153611930259)
XLA Ops:
  3.2 2.0 %collective-permute-start.1 = (bf16[32,3,512]{2,1,0:T(4,128)(2,1)S(1)}, bf16[32,3,512]{2,1,0:T(4,128)(2,1)S(1)}, u32[]{:S(2)}, u32[]{:S(2)}) collective-permute-start(bf16[32,3,512]{2,1,0:T(4,128)(2,1)S(1)} %get-tuple-element.102), channel_id=1, source_target_pairs={{4,0},{8,4},{12,8},{0,12},{5,1},{9,5},{13,9},{1,13},{6,2},{10,6},{... | collective-permute-start | bytes 294920 | tf_op jit(solution)/shard_map/ppermute | solution.py:518
  9.2 1.3 %collective-permute-start.3 = (bf16[3,38,512]{2,1,0:T(8,128)(2,1)S(1)}, bf16[3,38,512]{2,1,0:T(8,128)(2,1)S(1)}, u32[]{:S(2)}, u32[]{:S(2)}) collective-permute-start(bf16[3,38,512]{2,1,0:T(8,128)(2,1)S(1)} %pad_maximum_fusion.4), channel_id=1, source_target_pairs={{1,0},{2,1},{3,2},{5,4},{6,5},{7,6},{9,8},{10,9},{11,10},{13,12},{... | collective-permute-start | bytes 350216 | tf_op jit(solution)/shard_map/ppermute | solution.py:533
  10.5 4.7 %collective-permute-start.2 = (bf16[3,38,512]{2,1,0:T(8,128)(2,1)S(1)}, bf16[3,38,512]{2,1,0:T(8,128)(2,1)S(1)}, u32[]{:S(2)}, u32[]{:S(2)}) collective-permute-start(bf16[3,38,512]{2,1,0:T(8,128)(2,1)S(1)} %pad_maximum_fusion.3), channel_id=1, source_target_pairs={{0,1},{1,2},{2,3},{4,5},{5,6},{6,7},{8,9},{9,10},{10,11},{12,13},{... | collective-permute-start | bytes 350216 | tf_op jit(solution)/shard_map/ppermute | solution.py:533
  15.2 2.1 %collective-permute-done.3.b_ref = bf16[3,38,512]{2,1,0:T(8,128)(2,1)S(1)} collective-permute-done((bf16[3,38,512]{2,1,0:T(8,128)(2,1)S(1)}, bf16[3,38,512]{2,1,0:T(8,128)(2,1)S(1)}, u32[]{:S(2)}, u32[]{:S(2)}) %collective-permute-start.3) | collective-permute-done | bytes 116768 | tf_op jit(solution)/shard_map/ppermute | solution.py:533
  17.2 1.5 %collective-permute-done.2.t_ref = bf16[3,38,512]{2,1,0:T(8,128)(2,1)S(1)} collective-permute-done((bf16[3,38,512]{2,1,0:T(8,128)(2,1)S(1)}, bf16[3,38,512]{2,1,0:T(8,128)(2,1)S(1)}, u32[]{:S(2)}, u32[]{:S(2)}) %collective-permute-start.2) | collective-permute-done | bytes 116768 | tf_op jit(solution)/shard_map/ppermute | solution.py:533
  19.3 34.5 %expand.1 = (bf16[1024,512]{1,0:T(8,128)(2,1)}, bf16[1024,512]{1,0:T(8,128)(2,1)}, f32[4,8,512]{2,1,0:T(8,128)}, f32[1,2048]{1,0:T(1,128)}, bf16[2,2,4,512,128]{...) custom-call(s32[4]{0:T(128)} %pad_add_fusion.order_ref, bf16[32,3,512]{2,1,0:T(4,128)(2,1)} %copy-done.6, ...), custom_call_target="tpu_custom_call" | custom-call | flops 23000000512 | bytes 72000000 | tf_op jit(solution)/shard_map/expand/pallas_call | solution.py:268
  55.6 1.8 %collective-permute-start.7 = (bf16[32,3,512]{2,1,0:T(4,128)(2,1)S(1)}, bf16[32,3,512]{2,1,0:T(4,128)(2,1)S(1)}, u32[]{:S(2)}, u32[]{:S(2)}) collective-permute-start(bf16[32,3,512]{2,1,0:T(4,128)(2,1)S(1)} %get-tuple-element.99), channel_id=1, source_target_pairs={{4,0},{8,4},{12,8},{0,12},{5,1},{9,5},{13,9},{1,13},{6,2},{10,6},{... | collective-permute-start | bytes 294920 | tf_op jit(solution)/shard_map/ppermute | solution.py:518
  58.4 1.5 %convert_add_fusion = f32[2,2,4,256,128]{4,3,2,1,0:T(8,128)S(1)} fusion(bf16[2,2,4,512,128]{4,3,2,1,0:T(8,128)(2,1)S(1)} %collective-permute-done.4, bf16[2,2,4,512,128]{4,3,2,1,0:T(8,128)(2,1)} %get-tuple-element.67), kind=kLoop, calls=%fused_computation | loop fusion | flops 1572864 | bytes 4194304 | tf_op jit(solution)/shard_map/add | solution.py:592
  60.3 2.5 %collective-permute-start.5 = (bf16[2,2,2,256,128]{4,3,1,0,2:T(8,128)(2,1)S(1)}, bf16[2,2,2,256,128]{4,3,1,0,2:T(8,128)(2,1)S(1)}, u32[]{:S(2)}, u32[]{:S(2)}) collective-permute-start(bf16[2,2,2,256,128]{4,3,1,0,2:T(8,128)(2,1)S(1)} %fusion), channel_id=1, source_target_pairs={{0,1},{1,0},{2,3},{3,2},{4,5},{5,4},{6,7},{7,6},{8,9},{9,8},{10,11... | collective-permute-start | bytes 1572872 | tf_op jit(solution)/shard_map/ppermute | solution.py:494
  63.0 2.1 %collective-permute-start.9 = (bf16[2,1,4,256,128]{4,3,2,1,0:T(8,128)(2,1)S(1)}, bf16[2,1,4,256,128]{4,3,2,1,0:T(8,128)(2,1)S(1)}, u32[]{:S(2)}, u32[]{:S(2)}) collective-permute-start(bf16[2,1,4,256,128]{4,3,2,1,0:T(8,128)(2,1)S(1)} %add_convert_fusion), channel_id=1, source_target_pairs={{0,8},{4,12},{8,0},{12,4},{1,9},{5,13},{9,1},{13,5},{2,10},{6,14},... | collective-permute-start | bytes 1572872 | tf_op jit(solution)/shard_map/ppermute | solution.py:494
  65.1 6.5 %filter_grad.2.rest_0_ = f32[4,64,128]{2,1,0:T(8,128)} custom-call(bf16[32,32,512]{2,1,0:T(8,128)(2,1)} %f_ref.3, f32[32,32,128]{2,1,0:T(8,128)} %broadcast_in_dim.10.m_ref, bf16[32,3,512]{2,1,0:T(4,128)(2,1)} %copy-done.6, bf16[32,3,512]{2,1,0:T(4,128)(2,1)} %copy-done.7, bf16[3,38,512]{2,1,0:T(8,128)(2,1)} %copy-done.10, bf16[3,38,512]{2,1,0:T(8,128)(2,1)} %copy-done.9, ...), custom_call_target="tpu_custom_call" | custom-call | flops 4600000000 | bytes 14400000 | tf_op jit(solution)/shard_map/filter_grad/pallas_call | solution.py:373
  72.3 1.3 %collective-permute-start.12 = (bf16[3,38,512]{2,1,0:T(8,128)(2,1)S(1)}, bf16[3,38,512]{2,1,0:T(8,128)(2,1)}, u32[]{:S(2)}, u32[]{:S(2)}) collective-permute-start(bf16[3,38,512]{2,1,0:T(8,128)(2,1)S(1)} %pad_maximum_fusion.6), channel_id=1, source_target_pairs={{1,0},{2,1},{3,2},{5,4},{6,5},{7,6},{9,8},{10,9},{11,10},{13,12},{... | collective-permute-start | bytes 350216 | tf_op jit(solution)/shard_map/ppermute | solution.py:533
  73.7 5.2 %collective-permute-start.11 = (bf16[3,38,512]{2,1,0:T(8,128)(2,1)S(1)}, bf16[3,38,512]{2,1,0:T(8,128)(2,1)}, u32[]{:S(2)}, u32[]{:S(2)}) collective-permute-start(bf16[3,38,512]{2,1,0:T(8,128)(2,1)S(1)} %pad_maximum_fusion.5), channel_id=1, source_target_pairs={{0,1},{1,2},{2,3},{4,5},{5,6},{6,7},{8,9},{9,10},{10,11},{12,13},{... | collective-permute-start | bytes 350216 | tf_op jit(solution)/shard_map/ppermute | solution.py:533
  79.0 2.1 %collective-permute-start.8 = (bf16[2,2,1,256,128]{4,3,2,1,0:T(8,128)(2,1)S(1)}, bf16[2,2,1,256,128]{4,3,2,1,0:T(8,128)(2,1)S(1)}, u32[]{:S(2)}, u32[]{:S(2)}) collective-permute-start(bf16[2,2,1,256,128]{4,3,2,1,0:T(8,128)(2,1)S(1)} %fusion.2), channel_id=1, source_target_pairs={{0,2},{1,3},{2,0},{3,1},{4,6},{5,7},{6,4},{7,5},{8,10},{9,11},{10,... | collective-permute-start | bytes 786440 | tf_op jit(solution)/shard_map/ppermute | solution.py:494
  81.2 6.6 %filter_grad.3 = f32[4,64,128]{2,1,0:T(8,128)} custom-call(bf16[32,32,512]{2,1,0:T(8,128)(2,1)} %f_ref.3, f32[32,32,128]{2,1,0:T(8,128)} %broadcast_in_dim.10.m_ref, bf16[32,3,512]{2,1,0:T(4,128)(2,1)} %copy-done.6, bf16[32,3,512]{2,1,0:T(4,128)(2,1)} %copy-done.7, bf16[3,38,512]{2,1,0:T(8,128)(2,1)} %copy-done.10, ...), custom_call_target="tpu_custom_call", output_to_operand_aliasing={{}: (9, {})} | custom-call | flops 4600000000 | bytes 14400000 | tf_op jit(solution)/shard_map/filter_grad/pallas_call | solution.py:373
  88.2 4.6 %collective-permute-done.8 = bf16[2,2,1,256,128]{4,3,2,1,0:T(8,128)(2,1)S(1)} collective-permute-done((bf16[2,2,1,256,128]{4,3,2,1,0:T(8,128)(2,1)S(1)}, bf16[2,2,1,256,128]{4,3,2,1,0:T(8,128)(2,1)S(1)}, u32[]{:S(2)}, u32[]{:S(2)}) %collective-permute-start.8) | collective-permute-done | bytes 262176 | tf_op jit(solution)/shard_map/ppermute | solution.py:494
  93.4 6.2 %input_grad.3.rest_0_ = bf16[32,32,512]{2,1,0:T(8,128)(2,1)} custom-call(bf16[32,32,512]{2,1,0:T(8,128)(2,1)} %bitcast.73, bf16[32,3,512]{2,1,0:T(4,128)(2,1)} %copy-done.4, bf16[32,3,512]{2,1,0:T(4,128)(2,1)} %copy-done.5, bf16[3,38,512]{2,1,0:T(8,128)(2,1)} %collective-permute-done.11.t_ref, bf16[3,38,512]{2,1,0:T(8,128)(2,1)} %collective-permute-done.12.b_ref, ...), custom_call_target="tpu_custom_call" | custom-call | flops 4600000000 | bytes 14400000 | tf_op jit(solution)/shard_map/input_grad/pallas_call | solution.py:426
  99.6 2.4 %collective-permute-done.13 = bf16[1280,128]{1,0:T(8,128)(2,1)S(1)} collective-permute-done((bf16[1280,128]{1,0:T(8,128)(2,1)S(1)}, bf16[1280,128]{1,0:T(8,128)(2,1)S(1)}, u32[]{:S(2)}, u32[]{:S(2)}) %collective-permute-start.13) | collective-permute-done | bytes 327712 | tf_op jit(solution)/shard_map/ppermute | solution.py:494
  102.2 1.4 %collective-permute-start.14 = (bf16[768,128]{1,0:T(8,128)(2,1)S(1)}, bf16[768,128]{1,0:T(8,128)(2,1)S(1)}, u32[]{:S(2)}, u32[]{:S(2)}) collective-permute-start(bf16[768,128]{1,0:T(8,128)(2,1)S(1)} %pad_maximum_fusion.1), channel_id=1, source_target_pairs={{0,2},{1,3},{2,0},{3,1},{4,6},{5,7},{6,4},{7,5},{8,10},{9,11},{10,... | collective-permute-start | bytes 589832 | tf_op jit(solution)/shard_map/ppermute | solution.py:494
  103.6 4.1 %input_grad.4.rest_0_ = bf16[32,32,512]{2,1,0:T(8,128)(2,1)} custom-call(bf16[32,32,512]{2,1,0:T(8,128)(2,1)} %bitcast.74, bf16[32,3,512]{2,1,0:T(4,128)(2,1)} %copy-done.4, bf16[32,3,512]{2,1,0:T(4,128)(2,1)} %copy-done.5, bf16[3,38,512]{2,1,0:T(8,128)(2,1)} %collective-permute-done.11.t_ref, ...), custom_call_target="tpu_custom_call", output_to_operand_aliasing={{}: (8, {})} | custom-call | flops 4600000000 | bytes 14400000 | tf_op jit(solution)/shard_map/input_grad/pallas_call | solution.py:426
  108.4 3.8 %collective-permute-done.14.load_a_ref = bf16[768,128]{1,0:T(8,128)(2,1)S(1)} collective-permute-done((bf16[768,128]{1,0:T(8,128)(2,1)S(1)}, bf16[768,128]{1,0:T(8,128)(2,1)S(1)}, u32[]{:S(2)}, u32[]{:S(2)}) %collective-permute-start.14) | collective-permute-done | bytes 196640 | tf_op jit(solution)/shard_map/ppermute | solution.py:494
  113.5 4.1 %input_grad.5 = bf16[32,32,512]{2,1,0:T(8,128)(2,1)} custom-call(bf16[32,32,512]{2,1,0:T(8,128)(2,1)} %bitcast.75, bf16[32,3,512]{2,1,0:T(4,128)(2,1)} %copy-done.4, bf16[32,3,512]{2,1,0:T(4,128)(2,1)} %copy-done.5, bf16[3,38,512]{2,1,0:T(8,128)(2,1)} %collective-permute-done.11.t_ref, ...), custom_call_target="tpu_custom_call", output_to_operand_aliasing={{}: (8, {})} | custom-call | flops 4600000000 | bytes 14400000 | tf_op jit(solution)/shard_map/input_grad/pallas_call | solution.py:426
  117.7 1.7 %collective-permute-done.15.load_ref = bf16[768,128]{1,0:T(8,128)(2,1)S(1)} collective-permute-done((bf16[768,128]{1,0:T(8,128)(2,1)S(1)}, bf16[768,128]{1,0:T(8,128)(2,1)S(1)}, u32[]{:S(2)}, u32[]{:S(2)}) %collective-permute-start.15) | collective-permute-done | bytes 196640 | tf_op jit(solution)/shard_map/ppermute | solution.py:494
  120.1 2.3 %finish.1 = (f32[128,512]{1,0:T(8,128)}, f32[512,128]{1,0:T(8,128)}, f32[7,7,512]{2,1,0:T(8,128)}, f32[1,512]{1,0:T(1,128)}, f32[1,512]{1,0:T(1,128)}, /*index=5...) custom-call(f32[2,1,1,256,128]{4,3,2,1,0:T(8,128)} %select_bitcast_fusion.3.a_ref, bf16[768,128]{1,0:T(8,128)(2,1)} %copy-done.3, ...), custom_call_target="tpu_custom_call" | custom-call | flops 2300000000 | bytes 7200000 | tf_op jit(solution)/shard_map/finish/pallas_call | solution.py:474
  (80 shorter events, 15.1 us)
Async XLA Ops:
  2.7 5.1 %collective-permute-start = (bf16[32,3,512]{2,1,0:T(4,128)(2,1)S(1)}, bf16[32,3,512]{2,1,0:T(4,128)(2,1)S(1)}, u32[]{:S(2)}, u32[]{:S(2)}) collective-permute-start(bf16[32,3,512]{2,1,0:T(4,128)(2,1)S(1)} %get-tuple-element.103), channel_id=1, source_target_pairs={{0,4},{4,8},{8,12},{12,0},{1,5},{5,9},{9,13},{13,1},{2,6},{6,10},{... | collective-permute-start | bytes 294920 | tf_op jit(solution)/shard_map/ppermute | solution.py:518
  3.2 5.8 %collective-permute-start.1 = (bf16[32,3,512]{2,1,0:T(4,128)(2,1)S(1)}, bf16[32,3,512]{2,1,0:T(4,128)(2,1)S(1)}, u32[]{:S(2)}, u32[]{:S(2)}) collective-permute-start(bf16[32,3,512]{2,1,0:T(4,128)(2,1)S(1)} %get-tuple-element.102), channel_id=1, source_target_pairs={{4,0},{8,4},{12,8},{0,12},{5,1},{9,5},{13,9},{1,13},{6,2},{10,6},{... | collective-permute-start | bytes 294920 | tf_op jit(solution)/shard_map/ppermute | solution.py:518
  7.9 10.9 %copy-start.6 = (bf16[32,3,512]{2,1,0:T(4,128)(2,1)}, bf16[32,3,512]{2,1,0:T(4,128)(2,1)S(1)}, u32[]{:S(2)}) copy-start(bf16[32,3,512]{2,1,0:T(4,128)(2,1)S(1)} %collective-permute-done.l_ref) | copy-start | bytes 294916
  9.1 9.6 %copy-start.7 = (bf16[32,3,512]{2,1,0:T(4,128)(2,1)}, bf16[32,3,512]{2,1,0:T(4,128)(2,1)S(1)}, u32[]{:S(2)}) copy-start(bf16[32,3,512]{2,1,0:T(4,128)(2,1)S(1)} %collective-permute-done.1.r_ref) | copy-start | bytes 294916
  9.2 8.1 %collective-permute-start.3 = (bf16[3,38,512]{2,1,0:T(8,128)(2,1)S(1)}, bf16[3,38,512]{2,1,0:T(8,128)(2,1)S(1)}, u32[]{:S(2)}, u32[]{:S(2)}) collective-permute-start(bf16[3,38,512]{2,1,0:T(8,128)(2,1)S(1)} %pad_maximum_fusion.4), channel_id=1, source_target_pairs={{1,0},{2,1},{3,2},{5,4},{6,5},{7,6},{9,8},{10,9},{11,10},{13,12},{... | collective-permute-start | bytes 350216 | tf_op jit(solution)/shard_map/ppermute | solution.py:533
  10.5 8.2 %collective-permute-start.2 = (bf16[3,38,512]{2,1,0:T(8,128)(2,1)S(1)}, bf16[3,38,512]{2,1,0:T(8,128)(2,1)S(1)}, u32[]{:S(2)}, u32[]{:S(2)}) collective-permute-start(bf16[3,38,512]{2,1,0:T(8,128)(2,1)S(1)} %pad_maximum_fusion.3), channel_id=1, source_target_pairs={{0,1},{1,2},{2,3},{4,5},{5,6},{6,7},{8,9},{9,10},{10,11},{12,13},{... | collective-permute-start | bytes 350216 | tf_op jit(solution)/shard_map/ppermute | solution.py:533
  17.2 1.5 %copy-start.9 = (bf16[3,38,512]{2,1,0:T(8,128)(2,1)}, bf16[3,38,512]{2,1,0:T(8,128)(2,1)S(1)}, u32[]{:S(2)}) copy-start(bf16[3,38,512]{2,1,0:T(8,128)(2,1)S(1)} %collective-permute-done.3.b_ref) | copy-start | bytes 350212
  53.8 4.6 %collective-permute-start.4 = (bf16[2,2,4,512,128]{4,3,2,1,0:T(8,128)(2,1)}, bf16[2,2,4,512,128]{4,3,2,1,0:T(8,128)(2,1)S(1)}, u32[]{:S(2)}, u32[]{:S(2)}) collective-permute-start(bf16[2,2,4,512,128]{4,3,2,1,0:T(8,128)(2,1)} %get-tuple-element.56), channel_id=1, source_target_pairs={{0,4},{4,0},{8,12},{12,8},{1,5},{5,1},{9,13},{13,9},{2,6},{6,2},{1... | collective-permute-start | bytes 6291464 | tf_op jit(solution)/shard_map/ppermute | solution.py:494
  55.1 16.5 %collective-permute-start.6 = (bf16[32,3,512]{2,1,0:T(4,128)(2,1)S(1)}, bf16[32,3,512]{2,1,0:T(4,128)(2,1)S(1)}, u32[]{:S(2)}, u32[]{:S(2)}) collective-permute-start(bf16[32,3,512]{2,1,0:T(4,128)(2,1)S(1)} %get-tuple-element.98), channel_id=1, source_target_pairs={{0,4},{4,8},{8,12},{12,0},{1,5},{5,9},{9,13},{13,1},{2,6},{6,10},{... | collective-permute-start | bytes 294920 | tf_op jit(solution)/shard_map/ppermute | solution.py:518
  55.6 16.0 %collective-permute-start.7 = (bf16[32,3,512]{2,1,0:T(4,128)(2,1)S(1)}, bf16[32,3,512]{2,1,0:T(4,128)(2,1)S(1)}, u32[]{:S(2)}, u32[]{:S(2)}) collective-permute-start(bf16[32,3,512]{2,1,0:T(4,128)(2,1)S(1)} %get-tuple-element.99), channel_id=1, source_target_pairs={{4,0},{8,4},{12,8},{0,12},{5,1},{9,5},{13,9},{1,13},{6,2},{10,6},{... | collective-permute-start | bytes 294920 | tf_op jit(solution)/shard_map/ppermute | solution.py:518
  60.2 2.6 %copy-start = (bf16[2,2,4,512,128]{4,3,2,1,0:T(8,128)(2,1)S(1)}, bf16[2,2,4,512,128]{4,3,2,1,0:T(8,128)(2,1)}, u32[]{:S(2)}) copy-start(bf16[2,2,4,512,128]{4,3,2,1,0:T(8,128)(2,1)} %get-tuple-element.67) | copy-start | bytes 6291460
  60.3 18.5 %collective-permute-start.5 = (bf16[2,2,2,256,128]{4,3,1,0,2:T(8,128)(2,1)S(1)}, bf16[2,2,2,256,128]{4,3,1,0,2:T(8,128)(2,1)S(1)}, u32[]{:S(2)}, u32[]{:S(2)}) collective-permute-start(bf16[2,2,2,256,128]{4,3,1,0,2:T(8,128)(2,1)S(1)} %fusion), channel_id=1, source_target_pairs={{0,1},{1,0},{2,3},{3,2},{4,5},{5,4},{6,7},{7,6},{8,9},{9,8},{10,11... | collective-permute-start | bytes 1572872 | tf_op jit(solution)/shard_map/ppermute | solution.py:494
  63.0 24.8 %collective-permute-start.9 = (bf16[2,1,4,256,128]{4,3,2,1,0:T(8,128)(2,1)S(1)}, bf16[2,1,4,256,128]{4,3,2,1,0:T(8,128)(2,1)S(1)}, u32[]{:S(2)}, u32[]{:S(2)}) collective-permute-start(bf16[2,1,4,256,128]{4,3,2,1,0:T(8,128)(2,1)S(1)} %add_convert_fusion), channel_id=1, source_target_pairs={{0,8},{4,12},{8,0},{12,4},{1,9},{5,13},{9,1},{13,5},{2,10},{6,14},... | collective-permute-start | bytes 1572872 | tf_op jit(solution)/shard_map/ppermute | solution.py:494
  71.6 16.2 %copy-start.4 = (bf16[32,3,512]{2,1,0:T(4,128)(2,1)}, bf16[32,3,512]{2,1,0:T(4,128)(2,1)S(1)}, u32[]{:S(2)}) copy-start(bf16[32,3,512]{2,1,0:T(4,128)(2,1)S(1)} %collective-permute-done.6.l_ref) | copy-start | bytes 294916
  72.3 21.1 %collective-permute-start.12 = (bf16[3,38,512]{2,1,0:T(8,128)(2,1)S(1)}, bf16[3,38,512]{2,1,0:T(8,128)(2,1)}, u32[]{:S(2)}, u32[]{:S(2)}) collective-permute-start(bf16[3,38,512]{2,1,0:T(8,128)(2,1)S(1)} %pad_maximum_fusion.6), channel_id=1, source_target_pairs={{1,0},{2,1},{3,2},{5,4},{6,5},{7,6},{9,8},{10,9},{11,10},{13,12},{... | collective-permute-start | bytes 350216 | tf_op jit(solution)/shard_map/ppermute | solution.py:533
  73.7 19.7 %collective-permute-start.11 = (bf16[3,38,512]{2,1,0:T(8,128)(2,1)S(1)}, bf16[3,38,512]{2,1,0:T(8,128)(2,1)}, u32[]{:S(2)}, u32[]{:S(2)}) collective-permute-start(bf16[3,38,512]{2,1,0:T(8,128)(2,1)S(1)} %pad_maximum_fusion.5), channel_id=1, source_target_pairs={{0,1},{1,2},{2,3},{4,5},{5,6},{6,7},{8,9},{9,10},{10,11},{12,13},{... | collective-permute-start | bytes 350216 | tf_op jit(solution)/shard_map/ppermute | solution.py:533
  79.0 13.8 %collective-permute-start.8 = (bf16[2,2,1,256,128]{4,3,2,1,0:T(8,128)(2,1)S(1)}, bf16[2,2,1,256,128]{4,3,2,1,0:T(8,128)(2,1)S(1)}, u32[]{:S(2)}, u32[]{:S(2)}) collective-permute-start(bf16[2,2,1,256,128]{4,3,2,1,0:T(8,128)(2,1)S(1)} %fusion.2), channel_id=1, source_target_pairs={{0,2},{1,3},{2,0},{3,1},{4,6},{5,7},{6,4},{7,5},{8,10},{9,11},{10,... | collective-permute-start | bytes 786440 | tf_op jit(solution)/shard_map/ppermute | solution.py:494
  87.7 5.2 %collective-permute-start.10 = (f32[4,64,128]{2,1,0:T(8,128)}, f32[4,64,128]{2,1,0:T(8,128)S(1)}, u32[]{:S(2)}, u32[]{:S(2)}) collective-permute-start(f32[4,64,128]{2,1,0:T(8,128)} %filter_grad.3), channel_id=1, source_target_pairs={{0,4},{4,0},{8,12},{12,8},{1,5},{5,1},{9,13},{13,9},{2,6},{6,2},{1... | collective-permute-start | bytes 393224 | tf_op jit(solution)/shard_map/ppermute | solution.py:494
  88.1 4.8 %copy-start.2 = (f32[4,64,128]{2,1,0:T(8,128)S(1)}, f32[4,64,128]{2,1,0:T(8,128)}, u32[]{:S(2)}) copy-start(f32[4,64,128]{2,1,0:T(8,128)} %filter_grad.3) | copy-start | bytes 393220
  92.9 6.7 %copy-start.1 = (f32[2,2,1,256,128]{4,3,2,1,0:T(8,128)}, f32[2,2,1,256,128]{4,3,2,1,0:T(8,128)S(1)}, u32[]{:S(2)}) copy-start(f32[2,2,1,256,128]{4,3,2,1,0:T(8,128)S(1)} %bitcast_add_fusion.b_ref) | copy-start | bytes 1572868
  93.0 9.0 %collective-permute-start.13 = (bf16[1280,128]{1,0:T(8,128)(2,1)S(1)}, bf16[1280,128]{1,0:T(8,128)(2,1)S(1)}, u32[]{:S(2)}, u32[]{:S(2)}) collective-permute-start(bf16[1280,128]{1,0:T(8,128)(2,1)S(1)} %pad_maximum_fusion), channel_id=1, source_target_pairs={{0,1},{1,0},{2,3},{3,2},{4,5},{5,4},{6,7},{7,6},{8,9},{9,8},{10,11... | collective-permute-start | bytes 983048 | tf_op jit(solution)/shard_map/ppermute | solution.py:494
  102.2 10.0 %collective-permute-start.14 = (bf16[768,128]{1,0:T(8,128)(2,1)S(1)}, bf16[768,128]{1,0:T(8,128)(2,1)S(1)}, u32[]{:S(2)}, u32[]{:S(2)}) collective-permute-start(bf16[768,128]{1,0:T(8,128)(2,1)S(1)} %pad_maximum_fusion.1), channel_id=1, source_target_pairs={{0,2},{1,3},{2,0},{3,1},{4,6},{5,7},{6,4},{7,5},{8,10},{9,11},{10,... | collective-permute-start | bytes 589832 | tf_op jit(solution)/shard_map/ppermute | solution.py:494
  112.2 5.4 %copy-start.3 = (bf16[768,128]{1,0:T(8,128)(2,1)}, bf16[768,128]{1,0:T(8,128)(2,1)S(1)}, u32[]{:S(2)}) copy-start(bf16[768,128]{1,0:T(8,128)(2,1)S(1)} %collective-permute-done.14.load_a_ref) | copy-start | bytes 589828
  113.0 6.4 %collective-permute-start.15 = (bf16[768,128]{1,0:T(8,128)(2,1)S(1)}, bf16[768,128]{1,0:T(8,128)(2,1)S(1)}, u32[]{:S(2)}, u32[]{:S(2)}) collective-permute-start(bf16[768,128]{1,0:T(8,128)(2,1)S(1)} %pad_maximum_fusion.2), channel_id=1, source_target_pairs={{0,8},{4,12},{8,0},{12,4},{1,9},{5,13},{9,1},{13,5},{2,10},{6,14},... | collective-permute-start | bytes 589832 | tf_op jit(solution)/shard_map/ppermute | solution.py:494
  (3 other events, 2.0 us)

commit v12 on v11

--- a/solution.py
+++ b/solution.py
@@ -86,7 +86,7 @@
     order_ref,
     l_ref, r_ref, t_ref, b_ref, k_ref, gain_ref, bias_ref, scale_ref, bo_ref, m_ref, cot_ref, f_ref,
     wi_ref, bi_ref, wo_ref,
-    dconv_ref, mixed_ref, sums_ref, gbi_ref, sent_ref, kept_ref,
+    dconv_ref, first_ref, last_ref, mixed_ref, sums_ref, gbi_ref, sent_ref, kept_ref,
     window, conv, xhat_s, inv_s, normed, normed_t, dbr, dbr_t, act, dpre, d_normed, branch, pre_s, d_act,
 ):
     rows, cols, channels = f_ref.shape
@@ -238,7 +238,12 @@
             m2s = mean([e * xhat for e, xhat in zip(es, xhats)])
             for (row, at, here), e, xhat, m1, m2, value in zip(places, es, xhats, m1s, m2s, branches):
                 inv = jnp.concatenate([inv_s[here, :]] * wide, axis=1)
-                dconv_ref[here, :] = (inv * (e - m1 - xhat * m2)).astype(BF16)
+                d_conv = inv * (e - m1 - xhat * m2)
+                dconv_ref[here, :] = d_conv.astype(BF16)
+                if at == 0:
+                    first_ref[row] = d_conv[:3].astype(BF16)
+                if at == cols - strip:
+                    last_ref[row] = d_conv[strip - 3 :].astype(BF16)
                 field = f_ref[row, at : at + strip, :].astype(F32)
                 mixed_ref[here, :] = (field + value * scale_ref[...]).astype(BF16)
             products = [value * cot_ref[here, :].astype(F32) for value, here in zip(branches, heres)]
@@ -278,6 +283,8 @@
             ],
             out_specs=[
                 once((cells, channels)),
+                once((rows, 3, channels)),
+                once((rows, 3, channels)),
                 once((cells, channels)),
                 once((4, SUB, channels)),
                 pl.BlockSpec((1, block), lambda h, order: (0, order[h])),
@@ -303,6 +310,8 @@
         ),
         out_shape=[
             jax.ShapeDtypeStruct((cells, channels), BF16),
+            jax.ShapeDtypeStruct((rows, 3, channels), BF16),
+            jax.ShapeDtypeStruct((rows, 3, channels), BF16),
             jax.ShapeDtypeStruct((cells, channels), BF16),
             jax.ShapeDtypeStruct((4, SUB, channels), F32),
             jax.ShapeDtypeStruct((1, hidden), F32),
@@ -381,7 +390,7 @@
             pltpu.VMEM((rows, cols, LANES), F32),
         ],
         input_output_aliases={9: 0} if more else {},
-        compiler_params=params(56),
+        compiler_params=params(16),
         cost_estimate=estimate(4),
         name="filter_grad",
     )(*whole, *more)
@@ -436,7 +445,7 @@
             pltpu.VMEM((tall, cols, LANES), F32),
         ],
         input_output_aliases={8: 0} if more else {},
-        compiler_params=params(56),
+        compiler_params=params(16),
         cost_estimate=estimate(4),
         name="input_grad",
     )(*whole, mask, cot, *more)
@@ -483,7 +492,7 @@
             line,
             jax.ShapeDtypeStruct((1, hidden), F32),
         ],
-        compiler_params=params(56),
+        compiler_params=params(16),
         cost_estimate=estimate(2),
         name="finish",
     )(first, load_first, second, load, small)
@@ -569,13 +578,13 @@
         )
     )
 
-    d_conv, mixed, sums, g_bi, sent, kept = expand(
+    d_conv, d_first, d_last, mixed, sums, g_bi, sent, kept = expand(
         order, left, right, top, bot, kernel, gain, bias, scale, b_out.reshape(1, -1), mask, cot_rows,
         fields, w_in, b_in.reshape(1, -1), w_out, n_lon, n_lat,
     )
     got = swap(sent, "lon", 1)
     d_conv = d_conv.reshape(rows, cols, channels)
-    d_left, d_right = side_halo(d_conv[:, cols - 3 :], d_conv[:, :3])
+    d_left, d_right = side_halo(d_last, d_first)
 
     far = n_lon // 4
     border = channels // 2

time: 123 us -> 118 us (0.959)
  Pallas kernels: 64.3 us -> 53.1 us
  waiting for transfers between devices: 17.2 us -> 23 us
  starting transfers between devices: 26.5 us -> 30.6 us
  local copies, waits for them, and re-layouts: 5.51 us -> 3.08 us
  other arithmetic: 7.81 us -> 6.43 us
    ppermute x8, waiting for transfers between devices: 12.5 us -> 18.3 us  [swap(): return lax.ppermute(values, axis, [(i, i ^ bit) for i in range(count)])]
    pallas_call x2, Pallas kernels: 13.1 us -> 8.03 us  [filter_grad(): pl.pallas_call(functools.partial(filter_grad_kernel, half * (blocks // 2)...]
    pallas_call x3, Pallas kernels: 14.5 us -> 9.62 us  [input_grad(): pl.pallas_call(functools.partial(input_grad_kernel, rows // 4 * first), g...]
    ppermute x8, starting transfers between devices: 9.14 us -> 13.7 us  [swap(): return lax.ppermute(values, axis, [(i, i ^ bit) for i in range(count)])]
    pallas_call x1, Pallas kernels: 2.28 us -> 0.95 us  [finish(): pl.pallas_call(finish_kernel, out_shape=[jax.ShapeDtypeStruct((width, cha...]
    unnamed x22 -> x32, local copies, waits for them, and re-layouts: 1.98 us -> 0.72 us
  transfers between devices with their start and end apart: 16 -> 16, of which waited for: 8 -> 10; matrix products, arithmetic and copies ran while one was open for 7% -> 5% of each run, Pallas kernels for 23% -> 15%
where the time goes in v12:
time: 118 us; the launch traced here: 117 us
  Pallas kernels  53.1 us (45%)
  starting transfers between devices  30.6 us (26%)
  waiting for transfers between devices  23 us (19%)
  other arithmetic  6.43 us (5%)
  local copies, waits for them, and re-layouts  3.08 us (3%)
  between operations  1.18 us (1%)
    pallas_call x1, Pallas kernels, expand(): pl.pallas_call(expand_kernel, grid_spec=pltpu.PrefetchScalarGridSpec(num_...  34.5 us
    ppermute x8, waiting for transfers between devices, swap(): return lax.ppermute(values, axis, [(i, i ^ bit) for i in range(count)])  18.3 us
    ppermute x8, starting transfers between devices, swap(): return lax.ppermute(values, axis, [(i, i ^ bit) for i in range(count)])  13.7 us
    ppermute x4, starting transfers between devices, end_halo(): return (lax.ppermute(tail, 'lat', ahead), lax.ppermute(head, 'lat', back))  12 us
    pallas_call x3, Pallas kernels, input_grad(): pl.pallas_call(functools.partial(input_grad_kernel, rows // 4 * first), g...  9.62 us
    pallas_call x2, Pallas kernels, filter_grad(): pl.pallas_call(functools.partial(filter_grad_kernel, half * (blocks // 2)...  8.03 us
    ppermute x4, starting transfers between devices, side_halo(): return (lax.ppermute(last, 'lon', ahead), lax.ppermute(first, 'lon', back))  4.8 us
    ppermute x4, waiting for transfers between devices, end_halo(): return (lax.ppermute(tail, 'lat', ahead), lax.ppermute(head, 'lat', back))  3.51 us
  transfers between devices with their start and end apart: 16, of which 10 were waited for; matrix products, arithmetic and copies ran while one was open for 5% of the time, Pallas kernels for 15%

profile of v12, /device:TPU:0, one launch (start us, length us, event | category | flops | bytes accessed | tf_op | source)
XLA Modules:
  0.0 117.4 jit_solution(842726921225904466)
XLA Ops:
  3.2 2.0 %collective-permute-start.1 = (bf16[32,3,512]{2,1,0:T(4,128)(2,1)S(1)}, bf16[32,3,512]{2,1,0:T(4,128)(2,1)S(1)}, u32[]{:S(2)}, u32[]{:S(2)}) collective-permute-start(bf16[32,3,512]{2,1,0:T(4,128)(2,1)S(1)} %get-tuple-element.104), channel_id=1, source_target_pairs={{4,0},{8,4},{12,8},{0,12},{5,1},{9,5},{13,9},{1,13},{6,2},{10,6},{... | collective-permute-start | bytes 294920 | tf_op jit(solution)/shard_map/ppermute | solution.py:527
  9.2 1.3 %collective-permute-start.3 = (bf16[3,38,512]{2,1,0:T(8,128)(2,1)S(1)}, bf16[3,38,512]{2,1,0:T(8,128)(2,1)S(1)}, u32[]{:S(2)}, u32[]{:S(2)}) collective-permute-start(bf16[3,38,512]{2,1,0:T(8,128)(2,1)S(1)} %pad_maximum_fusion.4), channel_id=1, source_target_pairs={{1,0},{2,1},{3,2},{5,4},{6,5},{7,6},{9,8},{10,9},{11,10},{13,12},{... | collective-permute-start | bytes 350216 | tf_op jit(solution)/shard_map/ppermute | solution.py:542
  10.5 4.7 %collective-permute-start.2 = (bf16[3,38,512]{2,1,0:T(8,128)(2,1)S(1)}, bf16[3,38,512]{2,1,0:T(8,128)(2,1)S(1)}, u32[]{:S(2)}, u32[]{:S(2)}) collective-permute-start(bf16[3,38,512]{2,1,0:T(8,128)(2,1)S(1)} %pad_maximum_fusion.3), channel_id=1, source_target_pairs={{0,1},{1,2},{2,3},{4,5},{5,6},{6,7},{8,9},{9,10},{10,11},{12,13},{... | collective-permute-start | bytes 350216 | tf_op jit(solution)/shard_map/ppermute | solution.py:542
  15.2 2.1 %collective-permute-done.3.b_ref = bf16[3,38,512]{2,1,0:T(8,128)(2,1)S(1)} collective-permute-done((bf16[3,38,512]{2,1,0:T(8,128)(2,1)S(1)}, bf16[3,38,512]{2,1,0:T(8,128)(2,1)S(1)}, u32[]{:S(2)}, u32[]{:S(2)}) %collective-permute-start.3) | collective-permute-done | bytes 116768 | tf_op jit(solution)/shard_map/ppermute | solution.py:542
  17.3 1.4 %collective-permute-done.2.t_ref = bf16[3,38,512]{2,1,0:T(8,128)(2,1)S(1)} collective-permute-done((bf16[3,38,512]{2,1,0:T(8,128)(2,1)S(1)}, bf16[3,38,512]{2,1,0:T(8,128)(2,1)S(1)}, u32[]{:S(2)}, u32[]{:S(2)}) %collective-permute-start.2) | collective-permute-done | bytes 116768 | tf_op jit(solution)/shard_map/ppermute | solution.py:542
  19.4 34.5 %expand.1 = (bf16[1024,512]{1,0:T(8,128)(2,1)}, bf16[32,3,512]{2,1,0:T(4,128)(2,1)}, bf16[32,3,512]{2,1,0:T(4,128)(2,1)}, bf16[1024,512]{1,0:T(8,128)(2,1)}, f32...) custom-call(s32[4]{0:T(128)} %pad_add_fusion.order_ref, ...), custom_call_target="tpu_custom_call" | custom-call | flops 23000000512 | bytes 72000000 | tf_op jit(solution)/shard_map/expand/pallas_call | solution.py:273
  54.5 1.8 %collective-permute-start.7 = (bf16[32,3,512]{2,1,0:T(4,128)(2,1)}, bf16[32,3,512]{2,1,0:T(4,128)(2,1)S(1)}, u32[]{:S(2)}, u32[]{:S(2)}) collective-permute-start(bf16[32,3,512]{2,1,0:T(4,128)(2,1)} %get-tuple-element.66), channel_id=1, source_target_pairs={{4,0},{8,4},{12,8},{0,12},{5,1},{9,5},{13,9},{1,13},{6,2},{10,6},{... | collective-permute-start | bytes 294920 | tf_op jit(solution)/shard_map/ppermute | solution.py:527
  58.3 1.5 %convert_add_fusion = f32[2,2,4,256,128]{4,3,2,1,0:T(8,128)S(1)} fusion(bf16[2,2,4,512,128]{4,3,2,1,0:T(8,128)(2,1)S(1)} %collective-permute-done.4, bf16[2,2,4,512,128]{4,3,2,1,0:T(8,128)(2,1)} %get-tuple-element.71), kind=kLoop, calls=%fused_computation | loop fusion | flops 1572864 | bytes 4194304 | tf_op jit(solution)/shard_map/add | solution.py:601
  60.3 2.5 %collective-permute-start.5 = (bf16[2,2,2,256,128]{4,3,1,0,2:T(8,128)(2,1)S(1)}, bf16[2,2,2,256,128]{4,3,1,0,2:T(8,128)(2,1)S(1)}, u32[]{:S(2)}, u32[]{:S(2)}) collective-permute-start(bf16[2,2,2,256,128]{4,3,1,0,2:T(8,128)(2,1)S(1)} %fusion), channel_id=1, source_target_pairs={{0,1},{1,0},{2,3},{3,2},{4,5},{5,4},{6,7},{7,6},{8,9},{9,8},{10,11... | collective-permute-start | bytes 1572872 | tf_op jit(solution)/shard_map/ppermute | solution.py:503
  63.0 2.2 %collective-permute-start.9 = (bf16[2,1,4,256,128]{4,3,2,1,0:T(8,128)(2,1)S(1)}, bf16[2,1,4,256,128]{4,3,2,1,0:T(8,128)(2,1)S(1)}, u32[]{:S(2)}, u32[]{:S(2)}) collective-permute-start(bf16[2,1,4,256,128]{4,3,2,1,0:T(8,128)(2,1)S(1)} %add_convert_fusion), channel_id=1, source_target_pairs={{0,8},{4,12},{8,0},{12,4},{1,9},{5,13},{9,1},{13,5},{2,10},{6,14},... | collective-permute-start | bytes 1572872 | tf_op jit(solution)/shard_map/ppermute | solution.py:503
  65.2 4.0 %filter_grad.2.rest_0_ = f32[4,64,128]{2,1,0:T(8,128)S(1)} custom-call(bf16[32,32,512]{2,1,0:T(8,128)(2,1)S(1)} %copy-done.1, f32[32,32,128]{2,1,0:T(8,128)S(1)} %copy-done, bf16[32,3,512]{2,1,0:T(4,128)(2,1)S(1)} %copy-done.4, bf16[32,3,512]{2,1,0:T(4,128)(2,1)S(1)} %copy-done.6, bf16[3,38,512]{2,1,0:T(8,128)(2,1)S(1)} %copy-done.11, ...), custom_call_target="tpu_custom_call" | custom-call | flops 4600000000 | bytes 14400000 | tf_op jit(solution)/shard_map/filter_grad/pallas_call | solution.py:382
  69.4 1.3 %collective-permute-start.12 = (bf16[3,38,512]{2,1,0:T(8,128)(2,1)S(1)}, bf16[3,38,512]{2,1,0:T(8,128)(2,1)S(1)}, u32[]{:S(2)}, u32[]{:S(2)}) collective-permute-start(bf16[3,38,512]{2,1,0:T(8,128)(2,1)S(1)} %pad_maximum_fusion.6), channel_id=1, source_target_pairs={{1,0},{2,1},{3,2},{5,4},{6,5},{7,6},{9,8},{10,9},{11,10},{13,12},{... | collective-permute-start | bytes 350216 | tf_op jit(solution)/shard_map/ppermute | solution.py:542
  70.7 4.7 %collective-permute-start.11 = (bf16[3,38,512]{2,1,0:T(8,128)(2,1)S(1)}, bf16[3,38,512]{2,1,0:T(8,128)(2,1)S(1)}, u32[]{:S(2)}, u32[]{:S(2)}) collective-permute-start(bf16[3,38,512]{2,1,0:T(8,128)(2,1)S(1)} %pad_maximum_fusion.5), channel_id=1, source_target_pairs={{0,1},{1,2},{2,3},{4,5},{5,6},{6,7},{8,9},{9,10},{10,11},{12,13},{... | collective-permute-start | bytes 350216 | tf_op jit(solution)/shard_map/ppermute | solution.py:542
  75.7 3.1 %collective-permute-start.8 = (bf16[2,2,1,256,128]{4,3,2,1,0:T(8,128)(2,1)S(1)}, bf16[2,2,1,256,128]{4,3,2,1,0:T(8,128)(2,1)S(1)}, u32[]{:S(2)}, u32[]{:S(2)}) collective-permute-start(bf16[2,2,1,256,128]{4,3,2,1,0:T(8,128)(2,1)S(1)} %fusion.2), channel_id=1, source_target_pairs={{0,2},{1,3},{2,0},{3,1},{4,6},{5,7},{6,4},{7,5},{8,10},{9,11},{10,... | collective-permute-start | bytes 786440 | tf_op jit(solution)/shard_map/ppermute | solution.py:503
  78.8 4.0 %filter_grad.3 = f32[4,64,128]{2,1,0:T(8,128)S(1)} custom-call(bf16[32,32,512]{2,1,0:T(8,128)(2,1)S(1)} %copy-done.1, f32[32,32,128]{2,1,0:T(8,128)S(1)} %copy-done, bf16[32,3,512]{2,1,0:T(4,128)(2,1)S(1)} %copy-done.4, bf16[32,3,512]{2,1,0:T(4,128)(2,1)S(1)} %copy-done.6, bf16[3,38,512]{2,1,0:T(8,128)(2,1)S(1)} %copy-done.11, ...), custom_call_target="tpu_custom_call", output_to_operand_aliasing={{}: (9, {})} | custom-call | flops 4600000000 | bytes 14400000 | tf_op jit(solution)/shard_map/filter_grad/pallas_call | solution.py:382
  83.5 6.2 %collective-permute-done.8 = bf16[2,2,1,256,128]{4,3,2,1,0:T(8,128)(2,1)S(1)} collective-permute-done((bf16[2,2,1,256,128]{4,3,2,1,0:T(8,128)(2,1)S(1)}, bf16[2,2,1,256,128]{4,3,2,1,0:T(8,128)(2,1)S(1)}, u32[]{:S(2)}, u32[]{:S(2)}) %collective-permute-start.8) | collective-permute-done | bytes 262176 | tf_op jit(solution)/shard_map/ppermute | solution.py:503
  90.4 4.5 %input_grad.3.rest_0_ = bf16[32,32,512]{2,1,0:T(8,128)(2,1)} custom-call(bf16[32,32,512]{2,1,0:T(8,128)(2,1)S(1)} %bitcast.59, bf16[32,3,512]{2,1,0:T(4,128)(2,1)S(1)} %collective-permute-done.6.l_ref, bf16[32,3,512]{2,1,0:T(4,128)(2,1)S(1)} %collective-permute-done.7.r_ref, bf16[3,38,512]{2,1,0:T(8,128)(2,1)S(1)} %collective-permute-done.11.t_ref, ...), custom_call_target="tpu_custom_call" | custom-call | flops 4600000000 | bytes 14400000 | tf_op jit(solution)/shard_map/input_grad/pallas_call | solution.py:435
  94.9 3.2 %collective-permute-done.13 = bf16[1280,128]{1,0:T(8,128)(2,1)S(1)} collective-permute-done((bf16[1280,128]{1,0:T(8,128)(2,1)S(1)}, bf16[1280,128]{1,0:T(8,128)(2,1)S(1)}, u32[]{:S(2)}, u32[]{:S(2)}) %collective-permute-start.13) | collective-permute-done | bytes 327712 | tf_op jit(solution)/shard_map/ppermute | solution.py:503
  98.4 3.4 %collective-permute-start.14 = (bf16[768,128]{1,0:T(8,128)(2,1)S(1)}, bf16[768,128]{1,0:T(8,128)(2,1)S(1)}, u32[]{:S(2)}, u32[]{:S(2)}) collective-permute-start(bf16[768,128]{1,0:T(8,128)(2,1)S(1)} %pad_maximum_fusion.1), channel_id=1, source_target_pairs={{0,2},{1,3},{2,0},{3,1},{4,6},{5,7},{6,4},{7,5},{8,10},{9,11},{10,... | collective-permute-start | bytes 589832 | tf_op jit(solution)/shard_map/ppermute | solution.py:503
  101.8 2.6 %input_grad.4.rest_0_ = bf16[32,32,512]{2,1,0:T(8,128)(2,1)} custom-call(bf16[32,32,512]{2,1,0:T(8,128)(2,1)S(1)} %bitcast.60, bf16[32,3,512]{2,1,0:T(4,128)(2,1)S(1)} %collective-permute-done.6.l_ref, bf16[32,3,512]{2,1,0:T(4,128)(2,1)S(1)} %collective-permute-done.7.r_ref, ...), custom_call_target="tpu_custom_call", output_to_operand_aliasing={{}: (8, {})} | custom-call | flops 4600000000 | bytes 14400000 | tf_op jit(solution)/shard_map/input_grad/pallas_call | solution.py:435
  104.4 6.0 %collective-permute-done.14.load_a_ref = bf16[768,128]{1,0:T(8,128)(2,1)S(1)} collective-permute-done((bf16[768,128]{1,0:T(8,128)(2,1)S(1)}, bf16[768,128]{1,0:T(8,128)(2,1)S(1)}, u32[]{:S(2)}, u32[]{:S(2)}) %collective-permute-start.14) | collective-permute-done | bytes 196640 | tf_op jit(solution)/shard_map/ppermute | solution.py:503
  110.5 1.6 %collective-permute-start.15 = (bf16[768,128]{1,0:T(8,128)(2,1)S(1)}, bf16[768,128]{1,0:T(8,128)(2,1)S(1)}, u32[]{:S(2)}, u32[]{:S(2)}) collective-permute-start(bf16[768,128]{1,0:T(8,128)(2,1)S(1)} %pad_maximum_fusion.2), channel_id=1, source_target_pairs={{0,8},{4,12},{8,0},{12,4},{1,9},{5,13},{9,1},{13,5},{2,10},{6,14},... | collective-permute-start | bytes 589832 | tf_op jit(solution)/shard_map/ppermute | solution.py:503
  112.1 2.6 %input_grad.5 = bf16[32,32,512]{2,1,0:T(8,128)(2,1)} custom-call(bf16[32,32,512]{2,1,0:T(8,128)(2,1)S(1)} %bitcast.61, bf16[32,3,512]{2,1,0:T(4,128)(2,1)S(1)} %collective-permute-done.6.l_ref, bf16[32,3,512]{2,1,0:T(4,128)(2,1)S(1)} %collective-permute-done.7.r_ref, ...), custom_call_target="tpu_custom_call", output_to_operand_aliasing={{}: (8, {})} | custom-call | flops 4600000000 | bytes 14400000 | tf_op jit(solution)/shard_map/input_grad/pallas_call | solution.py:435
  114.7 1.8 %collective-permute-done.15.load_ref = bf16[768,128]{1,0:T(8,128)(2,1)S(1)} collective-permute-done((bf16[768,128]{1,0:T(8,128)(2,1)S(1)}, bf16[768,128]{1,0:T(8,128)(2,1)S(1)}, u32[]{:S(2)}, u32[]{:S(2)}) %collective-permute-start.15) | collective-permute-done | bytes 196640 | tf_op jit(solution)/shard_map/ppermute | solution.py:503
  (89 shorter events, 13.1 us)
Async XLA Ops:
  2.7 5.1 %collective-permute-start = (bf16[32,3,512]{2,1,0:T(4,128)(2,1)S(1)}, bf16[32,3,512]{2,1,0:T(4,128)(2,1)S(1)}, u32[]{:S(2)}, u32[]{:S(2)}) collective-permute-start(bf16[32,3,512]{2,1,0:T(4,128)(2,1)S(1)} %get-tuple-element.105), channel_id=1, source_target_pairs={{0,4},{4,8},{8,12},{12,0},{1,5},{5,9},{9,13},{13,1},{2,6},{6,10},{... | collective-permute-start | bytes 294920 | tf_op jit(solution)/shard_map/ppermute | solution.py:527
  3.2 5.8 %collective-permute-start.1 = (bf16[32,3,512]{2,1,0:T(4,128)(2,1)S(1)}, bf16[32,3,512]{2,1,0:T(4,128)(2,1)S(1)}, u32[]{:S(2)}, u32[]{:S(2)}) collective-permute-start(bf16[32,3,512]{2,1,0:T(4,128)(2,1)S(1)} %get-tuple-element.104), channel_id=1, source_target_pairs={{4,0},{8,4},{12,8},{0,12},{5,1},{9,5},{13,9},{1,13},{6,2},{10,6},{... | collective-permute-start | bytes 294920 | tf_op jit(solution)/shard_map/ppermute | solution.py:527
  7.9 10.9 %copy-start.3 = (bf16[32,3,512]{2,1,0:T(4,128)(2,1)}, bf16[32,3,512]{2,1,0:T(4,128)(2,1)S(1)}, u32[]{:S(2)}) copy-start(bf16[32,3,512]{2,1,0:T(4,128)(2,1)S(1)} %collective-permute-done.l_ref) | copy-start | bytes 294916
  9.1 9.6 %copy-start.5 = (bf16[32,3,512]{2,1,0:T(4,128)(2,1)}, bf16[32,3,512]{2,1,0:T(4,128)(2,1)S(1)}, u32[]{:S(2)}) copy-start(bf16[32,3,512]{2,1,0:T(4,128)(2,1)S(1)} %collective-permute-done.1.r_ref) | copy-start | bytes 294916
  9.2 8.1 %collective-permute-start.3 = (bf16[3,38,512]{2,1,0:T(8,128)(2,1)S(1)}, bf16[3,38,512]{2,1,0:T(8,128)(2,1)S(1)}, u32[]{:S(2)}, u32[]{:S(2)}) collective-permute-start(bf16[3,38,512]{2,1,0:T(8,128)(2,1)S(1)} %pad_maximum_fusion.4), channel_id=1, source_target_pairs={{1,0},{2,1},{3,2},{5,4},{6,5},{7,6},{9,8},{10,9},{11,10},{13,12},{... | collective-permute-start | bytes 350216 | tf_op jit(solution)/shard_map/ppermute | solution.py:542
  10.5 8.2 %collective-permute-start.2 = (bf16[3,38,512]{2,1,0:T(8,128)(2,1)S(1)}, bf16[3,38,512]{2,1,0:T(8,128)(2,1)S(1)}, u32[]{:S(2)}, u32[]{:S(2)}) collective-permute-start(bf16[3,38,512]{2,1,0:T(8,128)(2,1)S(1)} %pad_maximum_fusion.3), channel_id=1, source_target_pairs={{0,1},{1,2},{2,3},{4,5},{5,6},{6,7},{8,9},{9,10},{10,11},{12,13},{... | collective-permute-start | bytes 350216 | tf_op jit(solution)/shard_map/ppermute | solution.py:542
  53.9 4.4 %collective-permute-start.4 = (bf16[2,2,4,512,128]{4,3,2,1,0:T(8,128)(2,1)}, bf16[2,2,4,512,128]{4,3,2,1,0:T(8,128)(2,1)S(1)}, u32[]{:S(2)}, u32[]{:S(2)}) collective-permute-start(bf16[2,2,4,512,128]{4,3,2,1,0:T(8,128)(2,1)} %get-tuple-element.58), channel_id=1, source_target_pairs={{0,4},{4,0},{8,12},{12,8},{1,5},{5,1},{9,13},{13,9},{2,6},{6,2},{1... | collective-permute-start | bytes 6291464 | tf_op jit(solution)/shard_map/ppermute | solution.py:503
  54.0 15.2 %collective-permute-start.6 = (bf16[32,3,512]{2,1,0:T(4,128)(2,1)}, bf16[32,3,512]{2,1,0:T(4,128)(2,1)S(1)}, u32[]{:S(2)}, u32[]{:S(2)}) collective-permute-start(bf16[32,3,512]{2,1,0:T(4,128)(2,1)} %get-tuple-element.64), channel_id=1, source_target_pairs={{0,4},{4,8},{8,12},{12,0},{1,5},{5,9},{9,13},{13,1},{2,6},{6,10},{... | collective-permute-start | bytes 294920 | tf_op jit(solution)/shard_map/ppermute | solution.py:527
  54.5 14.8 %collective-permute-start.7 = (bf16[32,3,512]{2,1,0:T(4,128)(2,1)}, bf16[32,3,512]{2,1,0:T(4,128)(2,1)S(1)}, u32[]{:S(2)}, u32[]{:S(2)}) collective-permute-start(bf16[32,3,512]{2,1,0:T(4,128)(2,1)} %get-tuple-element.66), channel_id=1, source_target_pairs={{4,0},{8,4},{12,8},{0,12},{5,1},{9,5},{13,9},{1,13},{6,2},{10,6},{... | collective-permute-start | bytes 294920 | tf_op jit(solution)/shard_map/ppermute | solution.py:527
  60.1 5.1 %copy-start = (f32[32,32,128]{2,1,0:T(8,128)S(1)}, f32[32,32,128]{2,1,0:T(8,128)}, u32[]{:S(2)}) copy-start(f32[32,32,128]{2,1,0:T(8,128)} %broadcast_in_dim.10.m_ref) | copy-start | bytes 1572868
  60.1 5.1 %copy-start.1 = (bf16[32,32,512]{2,1,0:T(8,128)(2,1)S(1)}, bf16[32,32,512]{2,1,0:T(8,128)(2,1)}, u32[]{:S(2)}) copy-start(bf16[32,32,512]{2,1,0:T(8,128)(2,1)} %f_ref.3) | copy-start | bytes 3145732
  60.1 5.1 %copy-start.2 = (bf16[1024,512]{1,0:T(8,128)(2,1)S(1)}, bf16[1024,512]{1,0:T(8,128)(2,1)}, u32[]{:S(2)}) copy-start(bf16[1024,512]{1,0:T(8,128)(2,1)} %get-tuple-element.56) | copy-start | bytes 3145732
  60.1 5.1 %copy-start.4 = (bf16[32,3,512]{2,1,0:T(4,128)(2,1)S(1)}, bf16[32,3,512]{2,1,0:T(4,128)(2,1)}, u32[]{:S(2)}) copy-start(bf16[32,3,512]{2,1,0:T(4,128)(2,1)} %copy-done.3) | copy-start | bytes 294916
  60.3 15.3 %collective-permute-start.5 = (bf16[2,2,2,256,128]{4,3,1,0,2:T(8,128)(2,1)S(1)}, bf16[2,2,2,256,128]{4,3,1,0,2:T(8,128)(2,1)S(1)}, u32[]{:S(2)}, u32[]{:S(2)}) collective-permute-start(bf16[2,2,2,256,128]{4,3,1,0,2:T(8,128)(2,1)S(1)} %fusion), channel_id=1, source_target_pairs={{0,1},{1,0},{2,3},{3,2},{4,5},{5,4},{6,7},{7,6},{8,9},{9,8},{10,11... | collective-permute-start | bytes 1572872 | tf_op jit(solution)/shard_map/ppermute | solution.py:503
  63.0 20.0 %collective-permute-start.9 = (bf16[2,1,4,256,128]{4,3,2,1,0:T(8,128)(2,1)S(1)}, bf16[2,1,4,256,128]{4,3,2,1,0:T(8,128)(2,1)S(1)}, u32[]{:S(2)}, u32[]{:S(2)}) collective-permute-start(bf16[2,1,4,256,128]{4,3,2,1,0:T(8,128)(2,1)S(1)} %add_convert_fusion), channel_id=1, source_target_pairs={{0,8},{4,12},{8,0},{12,4},{1,9},{5,13},{9,1},{13,5},{2,10},{6,14},... | collective-permute-start | bytes 1572872 | tf_op jit(solution)/shard_map/ppermute | solution.py:503
  69.4 21.1 %collective-permute-start.12 = (bf16[3,38,512]{2,1,0:T(8,128)(2,1)S(1)}, bf16[3,38,512]{2,1,0:T(8,128)(2,1)S(1)}, u32[]{:S(2)}, u32[]{:S(2)}) collective-permute-start(bf16[3,38,512]{2,1,0:T(8,128)(2,1)S(1)} %pad_maximum_fusion.6), channel_id=1, source_target_pairs={{1,0},{2,1},{3,2},{5,4},{6,5},{7,6},{9,8},{10,9},{11,10},{13,12},{... | collective-permute-start | bytes 350216 | tf_op jit(solution)/shard_map/ppermute | solution.py:542
  70.7 19.7 %collective-permute-start.11 = (bf16[3,38,512]{2,1,0:T(8,128)(2,1)S(1)}, bf16[3,38,512]{2,1,0:T(8,128)(2,1)S(1)}, u32[]{:S(2)}, u32[]{:S(2)}) collective-permute-start(bf16[3,38,512]{2,1,0:T(8,128)(2,1)S(1)} %pad_maximum_fusion.5), channel_id=1, source_target_pairs={{0,1},{1,2},{2,3},{4,5},{5,6},{6,7},{8,9},{9,10},{10,11},{12,13},{... | collective-permute-start | bytes 350216 | tf_op jit(solution)/shard_map/ppermute | solution.py:542
  75.7 13.9 %collective-permute-start.8 = (bf16[2,2,1,256,128]{4,3,2,1,0:T(8,128)(2,1)S(1)}, bf16[2,2,1,256,128]{4,3,2,1,0:T(8,128)(2,1)S(1)}, u32[]{:S(2)}, u32[]{:S(2)}) collective-permute-start(bf16[2,2,1,256,128]{4,3,2,1,0:T(8,128)(2,1)S(1)} %fusion.2), channel_id=1, source_target_pairs={{0,2},{1,3},{2,0},{3,1},{4,6},{5,7},{6,4},{7,5},{8,10},{9,11},{10,... | collective-permute-start | bytes 786440 | tf_op jit(solution)/shard_map/ppermute | solution.py:503
  82.9 6.8 %collective-permute-start.10 = (f32[4,64,128]{2,1,0:T(8,128)S(1)}, f32[4,64,128]{2,1,0:T(8,128)S(1)}, u32[]{:S(2)}, u32[]{:S(2)}) collective-permute-start(f32[4,64,128]{2,1,0:T(8,128)S(1)} %filter_grad.3), channel_id=1, source_target_pairs={{0,4},{4,0},{8,12},{12,8},{1,5},{5,1},{9,13},{13,9},{2,6},{6,2},{1... | collective-permute-start | bytes 393224 | tf_op jit(solution)/shard_map/ppermute | solution.py:503
  83.4 7.1 %copy-start.7 = (bf16[32,32,512]{2,1,0:T(8,128)(2,1)S(1)}, bf16[32,32,512]{2,1,0:T(8,128)(2,1)}, u32[]{:S(2)}) copy-start(bf16[32,32,512]{2,1,0:T(8,128)(2,1)} %cot_ref.5) | copy-start | bytes 3145732
  83.4 7.1 %copy-start.12 = (f32[7,7,512]{2,1,0:T(8,128)S(1)}, f32[7,7,512]{2,1,0:T(8,128)}, u32[]{:S(2)}) copy-start(f32[7,7,512]{2,1,0:T(8,128)} %k_ref.7) | copy-start | bytes 301060
  89.8 8.4 %collective-permute-start.13 = (bf16[1280,128]{1,0:T(8,128)(2,1)S(1)}, bf16[1280,128]{1,0:T(8,128)(2,1)S(1)}, u32[]{:S(2)}, u32[]{:S(2)}) collective-permute-start(bf16[1280,128]{1,0:T(8,128)(2,1)S(1)} %pad_maximum_fusion), channel_id=1, source_target_pairs={{0,1},{1,0},{2,3},{3,2},{4,5},{5,4},{6,7},{7,6},{8,9},{9,8},{10,11... | collective-permute-start | bytes 983048 | tf_op jit(solution)/shard_map/ppermute | solution.py:503
  98.4 12.1 %collective-permute-start.14 = (bf16[768,128]{1,0:T(8,128)(2,1)S(1)}, bf16[768,128]{1,0:T(8,128)(2,1)S(1)}, u32[]{:S(2)}, u32[]{:S(2)}) collective-permute-start(bf16[768,128]{1,0:T(8,128)(2,1)S(1)} %pad_maximum_fusion.1), channel_id=1, source_target_pairs={{0,2},{1,3},{2,0},{3,1},{4,6},{5,7},{6,4},{7,5},{8,10},{9,11},{10,... | collective-permute-start | bytes 589832 | tf_op jit(solution)/shard_map/ppermute | solution.py:503
  110.5 6.0 %collective-permute-start.15 = (bf16[768,128]{1,0:T(8,128)(2,1)S(1)}, bf16[768,128]{1,0:T(8,128)(2,1)S(1)}, u32[]{:S(2)}, u32[]{:S(2)}) collective-permute-start(bf16[768,128]{1,0:T(8,128)(2,1)S(1)} %pad_maximum_fusion.2), channel_id=1, source_target_pairs={{0,8},{4,12},{8,0},{12,4},{1,9},{5,13},{9,1},{13,5},{2,10},{6,14},... | collective-permute-start | bytes 589832 | tf_op jit(solution)/shard_map/ppermute | solution.py:503
  (8 other events, 30.4 us)

commit v13 on v12

--- a/solution.py
+++ b/solution.py
@@ -587,7 +587,7 @@
     d_left, d_right = side_halo(d_last, d_first)
 
     far = n_lon // 4
-    border = channels // 2
+    border = channels * 3 // 4
     lon_bits = [("lon", 1, bit) for bit in bits_of("lon")[2:]]
     lat_bits = [("lat", 2, bit) for bit in bits_of("lat")]
 
@@ -607,7 +607,7 @@
     near_lons, far_lons = slice(far, 2 * far), slice(0, far)
     far_first = pair(far_lons, first).astype(BF16)
     got_first = swap(far_first, "lon", 2)
-    cut_b = halves(pair(slice(0, 2 * far), second), *lat_bits[0])
+    cut_b = halves(pair(slice(0, 2 * far), second, far_first), *lat_bits[0])
     rest = (mask, left, right, top, bot, d_conv, sums, g_bi)
     small = filter_grad(after(fields, far_first, cut_b[1]), *rest, 0)
     d_tail, d_head = end_rows(

time: 118 us -> 120 us (1.017)
  starting transfers between devices: 30.6 us -> 24.3 us
  waiting for transfers between devices: 23 us -> 27.6 us
  other arithmetic: 6.43 us -> 8.88 us
    ppermute x8, starting transfers between devices: 13.7 us -> 7.53 us  [swap(): return lax.ppermute(values, axis, [(i, i ^ bit) for i in range(count)])]
    ppermute x8, waiting for transfers between devices: 18.3 us -> 23 us  [swap(): return lax.ppermute(values, axis, [(i, i ^ bit) for i in range(count)])]
    convert_element_type x1, other arithmetic: 0.14 us -> 1.58 us  [per_device(): far_first = pair(far_lons, first).astype(BF16)]
    add x1, other arithmetic: 0.18 us -> 1.4 us  [per_device(): whole = pair(near_lons, first, alone) + after(got_first, alone).astype(F32)]
  transfers between devices with their start and end apart: 16 -> 16, of which waited for: 10 -> 9; matrix products, arithmetic and copies ran while one was open for 5% -> 7% of each run, Pallas kernels for 15% -> 15%
where the time goes in v13:
time: 120 us; the launch traced here: 119 us
  Pallas kernels  53.2 us (44%)
  waiting for transfers between devices  27.6 us (23%)
  starting transfers between devices  24.3 us (20%)
  other arithmetic  8.88 us (7%)
  local copies, waits for them, and re-layouts  3.9 us (3%)
    pallas_call x1, Pallas kernels, expand(): pl.pallas_call(expand_kernel, grid_spec=pltpu.PrefetchScalarGridSpec(num_...  34.6 us
    ppermute x8, waiting for transfers between devices, swap(): return lax.ppermute(values, axis, [(i, i ^ bit) for i in range(count)])  23 us
    ppermute x4, starting transfers between devices, end_halo(): return (lax.ppermute(tail, 'lat', ahead), lax.ppermute(head, 'lat', back))  12 us
    pallas_call x3, Pallas kernels, input_grad(): pl.pallas_call(functools.partial(input_grad_kernel, rows // 4 * first), g...  9.65 us
    pallas_call x2, Pallas kernels, filter_grad(): pl.pallas_call(functools.partial(filter_grad_kernel, half * (blocks // 2)...  8.03 us
    ppermute x8, starting transfers between devices, swap(): return lax.ppermute(values, axis, [(i, i ^ bit) for i in range(count)])  7.53 us
    ppermute x4, starting transfers between devices, side_halo(): return (lax.ppermute(last, 'lon', ahead), lax.ppermute(first, 'lon', back))  4.78 us
    ppermute x4, waiting for transfers between devices, end_halo(): return (lax.ppermute(tail, 'lat', ahead), lax.ppermute(head, 'lat', back))  3.52 us
  transfers between devices with their start and end apart: 16, of which 9 were waited for; matrix products, arithmetic and copies ran while one was open for 7% of the time, Pallas kernels for 15%

profile of v13, /device:TPU:0, one launch (start us, length us, event | category | flops | bytes accessed | tf_op | source)
XLA Modules:
  0.0 119.1 jit_solution(15948036062537571690)
XLA Ops:
  3.2 2.0 %collective-permute-start.1 = (bf16[32,3,512]{2,1,0:T(4,128)(2,1)S(1)}, bf16[32,3,512]{2,1,0:T(4,128)(2,1)S(1)}, u32[]{:S(2)}, u32[]{:S(2)}) collective-permute-start(bf16[32,3,512]{2,1,0:T(4,128)(2,1)S(1)} %get-tuple-element.108), channel_id=1, source_target_pairs={{4,0},{8,4},{12,8},{0,12},{5,1},{9,5},{13,9},{1,13},{6,2},{10,6},{... | collective-permute-start | bytes 294920 | tf_op jit(solution)/shard_map/ppermute | solution.py:527
  9.2 1.3 %collective-permute-start.3 = (bf16[3,38,512]{2,1,0:T(8,128)(2,1)S(1)}, bf16[3,38,512]{2,1,0:T(8,128)(2,1)S(1)}, u32[]{:S(2)}, u32[]{:S(2)}) collective-permute-start(bf16[3,38,512]{2,1,0:T(8,128)(2,1)S(1)} %pad_maximum_fusion.4), channel_id=1, source_target_pairs={{1,0},{2,1},{3,2},{5,4},{6,5},{7,6},{9,8},{10,9},{11,10},{13,12},{... | collective-permute-start | bytes 350216 | tf_op jit(solution)/shard_map/ppermute | solution.py:542
  10.5 4.7 %collective-permute-start.2 = (bf16[3,38,512]{2,1,0:T(8,128)(2,1)S(1)}, bf16[3,38,512]{2,1,0:T(8,128)(2,1)S(1)}, u32[]{:S(2)}, u32[]{:S(2)}) collective-permute-start(bf16[3,38,512]{2,1,0:T(8,128)(2,1)S(1)} %pad_maximum_fusion.3), channel_id=1, source_target_pairs={{0,1},{1,2},{2,3},{4,5},{5,6},{6,7},{8,9},{9,10},{10,11},{12,13},{... | collective-permute-start | bytes 350216 | tf_op jit(solution)/shard_map/ppermute | solution.py:542
  15.2 2.1 %collective-permute-done.3.b_ref = bf16[3,38,512]{2,1,0:T(8,128)(2,1)S(1)} collective-permute-done((bf16[3,38,512]{2,1,0:T(8,128)(2,1)S(1)}, bf16[3,38,512]{2,1,0:T(8,128)(2,1)S(1)}, u32[]{:S(2)}, u32[]{:S(2)}) %collective-permute-start.3) | collective-permute-done | bytes 116768 | tf_op jit(solution)/shard_map/ppermute | solution.py:542
  17.3 1.4 %collective-permute-done.2.t_ref = bf16[3,38,512]{2,1,0:T(8,128)(2,1)S(1)} collective-permute-done((bf16[3,38,512]{2,1,0:T(8,128)(2,1)S(1)}, bf16[3,38,512]{2,1,0:T(8,128)(2,1)S(1)}, u32[]{:S(2)}, u32[]{:S(2)}) %collective-permute-start.2) | collective-permute-done | bytes 116768 | tf_op jit(solution)/shard_map/ppermute | solution.py:542
  19.3 34.6 %expand.1 = (bf16[1024,512]{1,0:T(8,128)(2,1)}, bf16[32,3,512]{2,1,0:T(4,128)(2,1)}, bf16[32,3,512]{2,1,0:T(4,128)(2,1)}, bf16[1024,512]{1,0:T(8,128)(2,1)}, f32...) custom-call(s32[4]{0:T(128)} %pad_add_fusion.order_ref, ...), custom_call_target="tpu_custom_call" | custom-call | flops 23000000512 | bytes 72000000 | tf_op jit(solution)/shard_map/expand/pallas_call | solution.py:273
  54.5 1.8 %collective-permute-start.7 = (bf16[32,3,512]{2,1,0:T(4,128)(2,1)}, bf16[32,3,512]{2,1,0:T(4,128)(2,1)S(1)}, u32[]{:S(2)}, u32[]{:S(2)}) collective-permute-start(bf16[32,3,512]{2,1,0:T(4,128)(2,1)} %get-tuple-element.70), channel_id=1, source_target_pairs={{4,0},{8,4},{12,8},{0,12},{5,1},{9,5},{13,9},{1,13},{6,2},{10,6},{... | collective-permute-start | bytes 294920 | tf_op jit(solution)/shard_map/ppermute | solution.py:527
  57.2 1.2 %collective-permute-done.4 = bf16[2,2,4,512,128]{4,3,2,1,0:T(8,128)(2,1)} collective-permute-done((bf16[2,2,4,512,128]{4,3,2,1,0:T(8,128)(2,1)}, bf16[2,2,4,512,128]{4,3,2,1,0:T(8,128)(2,1)}, u32[]{:S(2)}, u32[]{:S(2)}) %collective-permute-start.4) | collective-permute-done | bytes 2097184 | tf_op jit(solution)/shard_map/ppermute | solution.py:503
  58.5 1.6 %add_convert_fusion = bf16[2,1,4,384,128]{4,3,2,1,0:T(8,128)(2,1)S(1)} fusion(bf16[2,2,4,512,128]{4,3,2,1,0:T(8,128)(2,1)} %collective-permute-done.4, bf16[2,2,4,512,128]{4,3,2,1,0:T(8,128)(2,1)} %get-tuple-element.75), kind=kLoop, calls=%fused_computation.1 | loop fusion | flops 1572864 | bytes 2359296 | tf_op jit(solution)/shard_map/convert_element_type | solution.py:608
  61.5 2.5 %collective-permute-start.5 = (bf16[2,2,2,128,128]{4,3,1,0,2:T(8,128)(2,1)S(1)}, bf16[2,2,2,128,128]{4,3,1,0,2:T(8,128)(2,1)S(1)}, u32[]{:S(2)}, u32[]{:S(2)}) collective-permute-start(bf16[2,2,2,128,128]{4,3,1,0,2:T(8,128)(2,1)S(1)} %fusion.1), channel_id=1, source_target_pairs={{0,1},{1,0},{2,3},{3,2},{4,5},{5,4},{6,7},{7,6},{8,9},{9,8},{10,11... | collective-permute-start | bytes 786440 | tf_op jit(solution)/shard_map/ppermute | solution.py:503
  64.1 2.2 %collective-permute-start.9 = (bf16[2,1,4,384,128]{4,3,2,1,0:T(8,128)(2,1)S(1)}, bf16[2,1,4,384,128]{4,3,2,1,0:T(8,128)(2,1)S(1)}, u32[]{:S(2)}, u32[]{:S(2)}) collective-permute-start(bf16[2,1,4,384,128]{4,3,2,1,0:T(8,128)(2,1)S(1)} %add_convert_fusion), channel_id=1, source_target_pairs={{0,8},{4,12},{8,0},{12,4},{1,9},{5,13},{9,1},{13,5},{2,10},{6,14},... | collective-permute-start | bytes 2359304 | tf_op jit(solution)/shard_map/ppermute | solution.py:503
  66.4 4.0 %filter_grad.2.rest_0_ = f32[4,64,128]{2,1,0:T(8,128)S(1)} custom-call(bf16[32,32,512]{2,1,0:T(8,128)(2,1)S(1)} %copy-done.1, f32[32,32,128]{2,1,0:T(8,128)S(1)} %copy-done, bf16[32,3,512]{2,1,0:T(4,128)(2,1)S(1)} %copy-done.4, bf16[32,3,512]{2,1,0:T(4,128)(2,1)S(1)} %copy-done.6, bf16[3,38,512]{2,1,0:T(8,128)(2,1)S(1)} %copy-done.11, ...), custom_call_target="tpu_custom_call" | custom-call | flops 4600000000 | bytes 14400000 | tf_op jit(solution)/shard_map/filter_grad/pallas_call | solution.py:382
  70.5 1.3 %collective-permute-start.12 = (bf16[3,38,512]{2,1,0:T(8,128)(2,1)S(1)}, bf16[3,38,512]{2,1,0:T(8,128)(2,1)S(1)}, u32[]{:S(2)}, u32[]{:S(2)}) collective-permute-start(bf16[3,38,512]{2,1,0:T(8,128)(2,1)S(1)} %pad_maximum_fusion.6), channel_id=1, source_target_pairs={{1,0},{2,1},{3,2},{5,4},{6,5},{7,6},{9,8},{10,9},{11,10},{13,12},{... | collective-permute-start | bytes 350216 | tf_op jit(solution)/shard_map/ppermute | solution.py:542
  71.9 4.7 %collective-permute-start.11 = (bf16[3,38,512]{2,1,0:T(8,128)(2,1)S(1)}, bf16[3,38,512]{2,1,0:T(8,128)(2,1)S(1)}, u32[]{:S(2)}, u32[]{:S(2)}) collective-permute-start(bf16[3,38,512]{2,1,0:T(8,128)(2,1)S(1)} %pad_maximum_fusion.5), channel_id=1, source_target_pairs={{0,1},{1,2},{2,3},{4,5},{5,6},{6,7},{8,9},{9,10},{10,11},{12,13},{... | collective-permute-start | bytes 350216 | tf_op jit(solution)/shard_map/ppermute | solution.py:542
  76.7 2.0 %collective-permute-start.8 = (bf16[2,2,1,128,128]{4,3,2,1,0:T(8,128)(2,1)S(1)}, bf16[2,2,1,128,128]{4,3,2,1,0:T(8,128)(2,1)S(1)}, u32[]{:S(2)}, u32[]{:S(2)}) collective-permute-start(bf16[2,2,1,128,128]{4,3,2,1,0:T(8,128)(2,1)S(1)} %fusion.2), channel_id=1, source_target_pairs={{0,2},{1,3},{2,0},{3,1},{4,6},{5,7},{6,4},{7,5},{8,10},{9,11},{10,... | collective-permute-start | bytes 393224 | tf_op jit(solution)/shard_map/ppermute | solution.py:503
  78.7 4.0 %filter_grad.3 = f32[4,64,128]{2,1,0:T(8,128)S(1)} custom-call(bf16[32,32,512]{2,1,0:T(8,128)(2,1)S(1)} %copy-done.1, f32[32,32,128]{2,1,0:T(8,128)S(1)} %copy-done, bf16[32,3,512]{2,1,0:T(4,128)(2,1)S(1)} %copy-done.4, bf16[32,3,512]{2,1,0:T(4,128)(2,1)S(1)} %copy-done.6, bf16[3,38,512]{2,1,0:T(8,128)(2,1)S(1)} %copy-done.11, ...), custom_call_target="tpu_custom_call", output_to_operand_aliasing={{}: (9, {})} | custom-call | flops 4600000000 | bytes 14400000 | tf_op jit(solution)/shard_map/filter_grad/pallas_call | solution.py:382
  82.8 2.1 %collective-permute-done.8 = bf16[2,2,1,128,128]{4,3,2,1,0:T(8,128)(2,1)S(1)} collective-permute-done((bf16[2,2,1,128,128]{4,3,2,1,0:T(8,128)(2,1)S(1)}, bf16[2,2,1,128,128]{4,3,2,1,0:T(8,128)(2,1)S(1)}, u32[]{:S(2)}, u32[]{:S(2)}) %collective-permute-start.8) | collective-permute-done | bytes 131104 | tf_op jit(solution)/shard_map/ppermute | solution.py:503
  85.0 1.4 %convert_add_fusion = f32[2,1,4,384,128]{4,3,2,1,0:T(8,128)S(1)} fusion(bf16[2,1,4,384,128]{4,3,2,1,0:T(8,128)(2,1)S(1)} %collective-permute-done.9, bf16[2,2,4,512,128]{4,3,2,1,0:T(8,128)(2,1)} %collective-permute-done.4, bf16[2,2,4,512,128]{4,3,2,1,0:T(8,128)(2,1)S(1)} %copy-done.15), kind=kLoop, calls=%fused_computation | loop fusion | flops 1966080 | bytes 3932160 | tf_op jit(solution)/shard_map/add | solution.py:630
  87.8 4.5 %input_grad.3.rest_0_ = bf16[32,32,512]{2,1,0:T(8,128)(2,1)} custom-call(bf16[32,32,512]{2,1,0:T(8,128)(2,1)S(1)} %bitcast.59, bf16[32,3,512]{2,1,0:T(4,128)(2,1)S(1)} %collective-permute-done.6.l_ref, bf16[32,3,512]{2,1,0:T(4,128)(2,1)S(1)} %collective-permute-done.7.r_ref, bf16[3,38,512]{2,1,0:T(8,128)(2,1)S(1)} %collective-permute-done.11.t_ref, ...), custom_call_target="tpu_custom_call" | custom-call | flops 4600000000 | bytes 14400000 | tf_op jit(solution)/shard_map/input_grad/pallas_call | solution.py:435
  92.4 6.5 %collective-permute-done.13 = bf16[1792,128]{1,0:T(8,128)(2,1)S(1)} collective-permute-done((bf16[1792,128]{1,0:T(8,128)(2,1)S(1)}, bf16[1792,128]{1,0:T(8,128)(2,1)S(1)}, u32[]{:S(2)}, u32[]{:S(2)}) %collective-permute-start.13) | collective-permute-done | bytes 458784 | tf_op jit(solution)/shard_map/ppermute | solution.py:503
  99.6 2.6 %input_grad.4.rest_0_ = bf16[32,32,512]{2,1,0:T(8,128)(2,1)} custom-call(bf16[32,32,512]{2,1,0:T(8,128)(2,1)S(1)} %bitcast.60, bf16[32,3,512]{2,1,0:T(4,128)(2,1)S(1)} %collective-permute-done.6.l_ref, bf16[32,3,512]{2,1,0:T(4,128)(2,1)S(1)} %collective-permute-done.7.r_ref, ...), custom_call_target="tpu_custom_call", output_to_operand_aliasing={{}: (8, {})} | custom-call | flops 4600000000 | bytes 14400000 | tf_op jit(solution)/shard_map/input_grad/pallas_call | solution.py:435
  102.2 10.4 %collective-permute-done.14.load_a_ref = bf16[1024,128]{1,0:T(8,128)(2,1)S(1)} collective-permute-done((bf16[1024,128]{1,0:T(8,128)(2,1)S(1)}, bf16[1024,128]{1,0:T(8,128)(2,1)S(1)}, u32[]{:S(2)}, u32[]{:S(2)}) %collective-permute-start.14) | collective-permute-done | bytes 262176 | tf_op jit(solution)/shard_map/ppermute | solution.py:503
  112.8 2.6 %input_grad.5 = bf16[32,32,512]{2,1,0:T(8,128)(2,1)} custom-call(bf16[32,32,512]{2,1,0:T(8,128)(2,1)S(1)} %bitcast.61, bf16[32,3,512]{2,1,0:T(4,128)(2,1)S(1)} %collective-permute-done.6.l_ref, bf16[32,3,512]{2,1,0:T(4,128)(2,1)S(1)} %collective-permute-done.7.r_ref, ...), custom_call_target="tpu_custom_call", output_to_operand_aliasing={{}: (8, {})} | custom-call | flops 4600000000 | bytes 14400000 | tf_op jit(solution)/shard_map/input_grad/pallas_call | solution.py:435
  115.3 2.8 %collective-permute-done.15.load_ref = bf16[512,128]{1,0:T(8,128)(2,1)S(1)} collective-permute-done((bf16[512,128]{1,0:T(8,128)(2,1)S(1)}, bf16[512,128]{1,0:T(8,128)(2,1)S(1)}, u32[]{:S(2)}, u32[]{:S(2)}) %collective-permute-start.15) | collective-permute-done | bytes 131104 | tf_op jit(solution)/shard_map/ppermute | solution.py:503
  (89 shorter events, 13.7 us)
Async XLA Ops:
  2.7 5.1 %collective-permute-start = (bf16[32,3,512]{2,1,0:T(4,128)(2,1)S(1)}, bf16[32,3,512]{2,1,0:T(4,128)(2,1)S(1)}, u32[]{:S(2)}, u32[]{:S(2)}) collective-permute-start(bf16[32,3,512]{2,1,0:T(4,128)(2,1)S(1)} %get-tuple-element.109), channel_id=1, source_target_pairs={{0,4},{4,8},{8,12},{12,0},{1,5},{5,9},{9,13},{13,1},{2,6},{6,10},{... | collective-permute-start | bytes 294920 | tf_op jit(solution)/shard_map/ppermute | solution.py:527
  3.2 5.8 %collective-permute-start.1 = (bf16[32,3,512]{2,1,0:T(4,128)(2,1)S(1)}, bf16[32,3,512]{2,1,0:T(4,128)(2,1)S(1)}, u32[]{:S(2)}, u32[]{:S(2)}) collective-permute-start(bf16[32,3,512]{2,1,0:T(4,128)(2,1)S(1)} %get-tuple-element.108), channel_id=1, source_target_pairs={{4,0},{8,4},{12,8},{0,12},{5,1},{9,5},{13,9},{1,13},{6,2},{10,6},{... | collective-permute-start | bytes 294920 | tf_op jit(solution)/shard_map/ppermute | solution.py:527
  7.9 10.9 %copy-start.3 = (bf16[32,3,512]{2,1,0:T(4,128)(2,1)}, bf16[32,3,512]{2,1,0:T(4,128)(2,1)S(1)}, u32[]{:S(2)}) copy-start(bf16[32,3,512]{2,1,0:T(4,128)(2,1)S(1)} %collective-permute-done.l_ref) | copy-start | bytes 294916
  9.1 9.6 %copy-start.5 = (bf16[32,3,512]{2,1,0:T(4,128)(2,1)}, bf16[32,3,512]{2,1,0:T(4,128)(2,1)S(1)}, u32[]{:S(2)}) copy-start(bf16[32,3,512]{2,1,0:T(4,128)(2,1)S(1)} %collective-permute-done.1.r_ref) | copy-start | bytes 294916
  9.2 8.1 %collective-permute-start.3 = (bf16[3,38,512]{2,1,0:T(8,128)(2,1)S(1)}, bf16[3,38,512]{2,1,0:T(8,128)(2,1)S(1)}, u32[]{:S(2)}, u32[]{:S(2)}) collective-permute-start(bf16[3,38,512]{2,1,0:T(8,128)(2,1)S(1)} %pad_maximum_fusion.4), channel_id=1, source_target_pairs={{1,0},{2,1},{3,2},{5,4},{6,5},{7,6},{9,8},{10,9},{11,10},{13,12},{... | collective-permute-start | bytes 350216 | tf_op jit(solution)/shard_map/ppermute | solution.py:542
  10.5 8.2 %collective-permute-start.2 = (bf16[3,38,512]{2,1,0:T(8,128)(2,1)S(1)}, bf16[3,38,512]{2,1,0:T(8,128)(2,1)S(1)}, u32[]{:S(2)}, u32[]{:S(2)}) collective-permute-start(bf16[3,38,512]{2,1,0:T(8,128)(2,1)S(1)} %pad_maximum_fusion.3), channel_id=1, source_target_pairs={{0,1},{1,2},{2,3},{4,5},{5,6},{6,7},{8,9},{9,10},{10,11},{12,13},{... | collective-permute-start | bytes 350216 | tf_op jit(solution)/shard_map/ppermute | solution.py:542
  53.9 6.2 %copy-start.15 = (bf16[2,2,4,512,128]{4,3,2,1,0:T(8,128)(2,1)S(1)}, bf16[2,2,4,512,128]{4,3,2,1,0:T(8,128)(2,1)}, u32[]{:S(2)}) copy-start(bf16[2,2,4,512,128]{4,3,2,1,0:T(8,128)(2,1)} %get-tuple-element.75) | copy-start | bytes 6291460
  53.9 4.6 %collective-permute-start.4 = (bf16[2,2,4,512,128]{4,3,2,1,0:T(8,128)(2,1)}, bf16[2,2,4,512,128]{4,3,2,1,0:T(8,128)(2,1)}, u32[]{:S(2)}, u32[]{:S(2)}) collective-permute-start(bf16[2,2,4,512,128]{4,3,2,1,0:T(8,128)(2,1)} %get-tuple-element.60), channel_id=1, source_target_pairs={{0,4},{4,0},{8,12},{12,8},{1,5},{5,1},{9,13},{13,9},{2,6},{6,2},{1... | collective-permute-start | bytes 6291464 | tf_op jit(solution)/shard_map/ppermute | solution.py:503
  54.0 16.4 %collective-permute-start.6 = (bf16[32,3,512]{2,1,0:T(4,128)(2,1)}, bf16[32,3,512]{2,1,0:T(4,128)(2,1)S(1)}, u32[]{:S(2)}, u32[]{:S(2)}) collective-permute-start(bf16[32,3,512]{2,1,0:T(4,128)(2,1)} %get-tuple-element.68), channel_id=1, source_target_pairs={{0,4},{4,8},{8,12},{12,0},{1,5},{5,9},{9,13},{13,1},{2,6},{6,10},{... | collective-permute-start | bytes 294920 | tf_op jit(solution)/shard_map/ppermute | solution.py:527
  54.5 15.9 %collective-permute-start.7 = (bf16[32,3,512]{2,1,0:T(4,128)(2,1)}, bf16[32,3,512]{2,1,0:T(4,128)(2,1)S(1)}, u32[]{:S(2)}, u32[]{:S(2)}) collective-permute-start(bf16[32,3,512]{2,1,0:T(4,128)(2,1)} %get-tuple-element.70), channel_id=1, source_target_pairs={{4,0},{8,4},{12,8},{0,12},{5,1},{9,5},{13,9},{1,13},{6,2},{10,6},{... | collective-permute-start | bytes 294920 | tf_op jit(solution)/shard_map/ppermute | solution.py:527
  61.2 5.1 %copy-start = (f32[32,32,128]{2,1,0:T(8,128)S(1)}, f32[32,32,128]{2,1,0:T(8,128)}, u32[]{:S(2)}) copy-start(f32[32,32,128]{2,1,0:T(8,128)} %broadcast_in_dim.10.m_ref) | copy-start | bytes 1572868
  61.3 5.1 %copy-start.1 = (bf16[32,32,512]{2,1,0:T(8,128)(2,1)S(1)}, bf16[32,32,512]{2,1,0:T(8,128)(2,1)}, u32[]{:S(2)}) copy-start(bf16[32,32,512]{2,1,0:T(8,128)(2,1)} %f_ref.3) | copy-start | bytes 3145732
  61.3 5.1 %copy-start.2 = (bf16[1024,512]{1,0:T(8,128)(2,1)S(1)}, bf16[1024,512]{1,0:T(8,128)(2,1)}, u32[]{:S(2)}) copy-start(bf16[1024,512]{1,0:T(8,128)(2,1)} %get-tuple-element.58) | copy-start | bytes 3145732
  61.3 5.1 %copy-start.4 = (bf16[32,3,512]{2,1,0:T(4,128)(2,1)S(1)}, bf16[32,3,512]{2,1,0:T(4,128)(2,1)}, u32[]{:S(2)}) copy-start(bf16[32,3,512]{2,1,0:T(4,128)(2,1)} %copy-done.3) | copy-start | bytes 294916
  61.3 5.1 %copy-start.6 = (bf16[32,3,512]{2,1,0:T(4,128)(2,1)S(1)}, bf16[32,3,512]{2,1,0:T(4,128)(2,1)}, u32[]{:S(2)}) copy-start(bf16[32,3,512]{2,1,0:T(4,128)(2,1)} %copy-done.5) | copy-start | bytes 294916
  61.5 15.1 %collective-permute-start.5 = (bf16[2,2,2,128,128]{4,3,1,0,2:T(8,128)(2,1)S(1)}, bf16[2,2,2,128,128]{4,3,1,0,2:T(8,128)(2,1)S(1)}, u32[]{:S(2)}, u32[]{:S(2)}) collective-permute-start(bf16[2,2,2,128,128]{4,3,1,0,2:T(8,128)(2,1)S(1)} %fusion.1), channel_id=1, source_target_pairs={{0,1},{1,0},{2,3},{3,2},{4,5},{5,4},{6,7},{7,6},{8,9},{9,8},{10,11... | collective-permute-start | bytes 786440 | tf_op jit(solution)/shard_map/ppermute | solution.py:503
  64.1 20.8 %collective-permute-start.9 = (bf16[2,1,4,384,128]{4,3,2,1,0:T(8,128)(2,1)S(1)}, bf16[2,1,4,384,128]{4,3,2,1,0:T(8,128)(2,1)S(1)}, u32[]{:S(2)}, u32[]{:S(2)}) collective-permute-start(bf16[2,1,4,384,128]{4,3,2,1,0:T(8,128)(2,1)S(1)} %add_convert_fusion), channel_id=1, source_target_pairs={{0,8},{4,12},{8,0},{12,4},{1,9},{5,13},{9,1},{13,5},{2,10},{6,14},... | collective-permute-start | bytes 2359304 | tf_op jit(solution)/shard_map/ppermute | solution.py:503
  70.5 16.4 %collective-permute-start.12 = (bf16[3,38,512]{2,1,0:T(8,128)(2,1)S(1)}, bf16[3,38,512]{2,1,0:T(8,128)(2,1)S(1)}, u32[]{:S(2)}, u32[]{:S(2)}) collective-permute-start(bf16[3,38,512]{2,1,0:T(8,128)(2,1)S(1)} %pad_maximum_fusion.6), channel_id=1, source_target_pairs={{1,0},{2,1},{3,2},{5,4},{6,5},{7,6},{9,8},{10,9},{11,10},{13,12},{... | collective-permute-start | bytes 350216 | tf_op jit(solution)/shard_map/ppermute | solution.py:542
  71.9 15.1 %collective-permute-start.11 = (bf16[3,38,512]{2,1,0:T(8,128)(2,1)S(1)}, bf16[3,38,512]{2,1,0:T(8,128)(2,1)S(1)}, u32[]{:S(2)}, u32[]{:S(2)}) collective-permute-start(bf16[3,38,512]{2,1,0:T(8,128)(2,1)S(1)} %pad_maximum_fusion.5), channel_id=1, source_target_pairs={{0,1},{1,2},{2,3},{4,5},{5,6},{6,7},{8,9},{9,10},{10,11},{12,13},{... | collective-permute-start | bytes 350216 | tf_op jit(solution)/shard_map/ppermute | solution.py:542
  76.7 8.2 %collective-permute-start.8 = (bf16[2,2,1,128,128]{4,3,2,1,0:T(8,128)(2,1)S(1)}, bf16[2,2,1,128,128]{4,3,2,1,0:T(8,128)(2,1)S(1)}, u32[]{:S(2)}, u32[]{:S(2)}) collective-permute-start(bf16[2,2,1,128,128]{4,3,2,1,0:T(8,128)(2,1)S(1)} %fusion.2), channel_id=1, source_target_pairs={{0,2},{1,3},{2,0},{3,1},{4,6},{5,7},{6,4},{7,5},{8,10},{9,11},{10,... | collective-permute-start | bytes 393224 | tf_op jit(solution)/shard_map/ppermute | solution.py:503
  82.7 4.0 %collective-permute-start.10 = (f32[4,64,128]{2,1,0:T(8,128)S(1)}, f32[4,64,128]{2,1,0:T(8,128)S(1)}, u32[]{:S(2)}, u32[]{:S(2)}) collective-permute-start(f32[4,64,128]{2,1,0:T(8,128)S(1)} %filter_grad.3), channel_id=1, source_target_pairs={{0,4},{4,0},{8,12},{12,8},{1,5},{5,1},{9,13},{13,9},{2,6},{6,2},{1... | collective-permute-start | bytes 393224 | tf_op jit(solution)/shard_map/ppermute | solution.py:503
  86.8 12.1 %collective-permute-start.13 = (bf16[1792,128]{1,0:T(8,128)(2,1)S(1)}, bf16[1792,128]{1,0:T(8,128)(2,1)S(1)}, u32[]{:S(2)}, u32[]{:S(2)}) collective-permute-start(bf16[1792,128]{1,0:T(8,128)(2,1)S(1)} %pad_maximum_fusion), channel_id=1, source_target_pairs={{0,1},{1,0},{2,3},{3,2},{4,5},{5,4},{6,7},{7,6},{8,9},{9,8},{10,11... | collective-permute-start | bytes 1376264 | tf_op jit(solution)/shard_map/ppermute | solution.py:503
  99.1 13.5 %collective-permute-start.14 = (bf16[1024,128]{1,0:T(8,128)(2,1)S(1)}, bf16[1024,128]{1,0:T(8,128)(2,1)S(1)}, u32[]{:S(2)}, u32[]{:S(2)}) collective-permute-start(bf16[1024,128]{1,0:T(8,128)(2,1)S(1)} %pad_maximum_fusion.1), channel_id=1, source_target_pairs={{0,2},{1,3},{2,0},{3,1},{4,6},{5,7},{6,4},{7,5},{8,10},{9,11},{10,... | collective-permute-start | bytes 786440 | tf_op jit(solution)/shard_map/ppermute | solution.py:503
  112.7 5.4 %collective-permute-start.15 = (bf16[512,128]{1,0:T(8,128)(2,1)S(1)}, bf16[512,128]{1,0:T(8,128)(2,1)S(1)}, u32[]{:S(2)}, u32[]{:S(2)}) collective-permute-start(bf16[512,128]{1,0:T(8,128)(2,1)S(1)} %pad_maximum_fusion.2), channel_id=1, source_target_pairs={{0,8},{4,12},{8,0},{12,4},{1,9},{5,13},{9,1},{13,5},{2,10},{6,14},... | collective-permute-start | bytes 393224 | tf_op jit(solution)/shard_map/ppermute | solution.py:503
  (8 other events, 24.7 us)

commit v14 on v12

--- a/solution.py
+++ b/solution.py
@@ -318,7 +318,7 @@
             jax.ShapeDtypeStruct((2, turn) + grads, BF16),
             jax.ShapeDtypeStruct((2, turn) + grads, BF16),
         ],
-        compiler_params=params(56),
+        compiler_params=params(42),
         cost_estimate=estimate(20),
         name="expand",
     )(order, *given, w_in, b_in, w_out)

time: 118 us -> 120 us (1.017)
  local copies, waits for them, and re-layouts: 3.08 us -> 7.23 us
  Pallas kernels: 53.1 us -> 50.7 us
  other arithmetic: 6.43 us -> 7.97 us
  starting transfers between devices: 30.6 us -> 29.1 us
    unnamed x32 -> x30, local copies, waits for them, and re-layouts: 0.72 us -> 5.68 us
    pallas_call x1, Pallas kernels: 34.5 us -> 32.1 us  [expand(): pl.pallas_call(expand_kernel, grid_spec=pltpu.PrefetchScalarGridSpec(num_...]
    ppermute x4, waiting for transfers between devices: 1.16 us -> 2.49 us  [side_halo(): return (lax.ppermute(last, 'lon', ahead), lax.ppermute(first, 'lon', back))]
  transfers between devices with their start and end apart: 16 -> 16, of which waited for: 10 -> 9; matrix products, arithmetic and copies ran while one was open for 5% -> 6% of each run, Pallas kernels for 15% -> 15%
where the time goes in v14:
time: 120 us
  Pallas kernels  50.7 us (42%)
  starting transfers between devices  29.1 us (24%)
  waiting for transfers between devices  23.5 us (20%)
  other arithmetic  7.97 us (7%)
  local copies, waits for them, and re-layouts  7.23 us (6%)
    pallas_call x1, Pallas kernels, expand(): pl.pallas_call(expand_kernel, grid_spec=pltpu.PrefetchScalarGridSpec(num_...  32.1 us
    ppermute x8, waiting for transfers between devices, swap(): return lax.ppermute(values, axis, [(i, i ^ bit) for i in range(count)])  17.4 us
    ppermute x8, starting transfers between devices, swap(): return lax.ppermute(values, axis, [(i, i ^ bit) for i in range(count)])  13 us
    ppermute x4, starting transfers between devices, end_halo(): return (lax.ppermute(tail, 'lat', ahead), lax.ppermute(head, 'lat', back))  11.9 us
    pallas_call x3, Pallas kernels, input_grad(): pl.pallas_call(functools.partial(input_grad_kernel, rows // 4 * first), g...  9.62 us
    pallas_call x2, Pallas kernels, filter_grad(): pl.pallas_call(functools.partial(filter_grad_kernel, half * (blocks // 2)...  8.02 us
    unnamed x30, local copies, waits for them, and re-layouts  5.68 us
    ppermute x4, starting transfers between devices, side_halo(): return (lax.ppermute(last, 'lon', ahead), lax.ppermute(first, 'lon', back))  4.27 us
  transfers between devices with their start and end apart: 16, of which 9 were waited for; matrix products, arithmetic and copies ran while one was open for 6% of the time, Pallas kernels for 15%

profile of v14, /device:TPU:0, one launch (start us, length us, event | category | flops | bytes accessed | tf_op | source)
XLA Modules:
  0.0 119.7 jit_solution(10901038372098450441)
XLA Ops:
  3.3 2.0 %collective-permute-start.1 = (bf16[32,3,512]{2,1,0:T(4,128)(2,1)S(1)}, bf16[32,3,512]{2,1,0:T(4,128)(2,1)S(1)}, u32[]{:S(2)}, u32[]{:S(2)}) collective-permute-start(bf16[32,3,512]{2,1,0:T(4,128)(2,1)S(1)} %get-tuple-element.104), channel_id=1, source_target_pairs={{4,0},{8,4},{12,8},{0,12},{5,1},{9,5},{13,9},{1,13},{6,2},{10,6},{... | collective-permute-start | bytes 294920 | tf_op jit(solution)/shard_map/ppermute | solution.py:527
  6.5 1.5 %collective-permute-done.l_ref = bf16[32,3,512]{2,1,0:T(4,128)(2,1)S(1)} collective-permute-done((bf16[32,3,512]{2,1,0:T(4,128)(2,1)S(1)}, bf16[32,3,512]{2,1,0:T(4,128)(2,1)S(1)}, u32[]{:S(2)}, u32[]{:S(2)}) %collective-permute-start) | collective-permute-done | bytes 98336 | tf_op jit(solution)/shard_map/ppermute | solution.py:527
  10.6 4.6 %collective-permute-start.2 = (bf16[3,38,512]{2,1,0:T(8,128)(2,1)S(1)}, bf16[3,38,512]{2,1,0:T(8,128)(2,1)S(1)}, u32[]{:S(2)}, u32[]{:S(2)}) collective-permute-start(bf16[3,38,512]{2,1,0:T(8,128)(2,1)S(1)} %pad_maximum_fusion.3), channel_id=1, source_target_pairs={{0,1},{1,2},{2,3},{4,5},{5,6},{6,7},{8,9},{9,10},{10,11},{12,13},{... | collective-permute-start | bytes 350216 | tf_op jit(solution)/shard_map/ppermute | solution.py:542
  15.1 2.0 %collective-permute-done.3.b_ref = bf16[3,38,512]{2,1,0:T(8,128)(2,1)S(1)} collective-permute-done((bf16[3,38,512]{2,1,0:T(8,128)(2,1)S(1)}, bf16[3,38,512]{2,1,0:T(8,128)(2,1)S(1)}, u32[]{:S(2)}, u32[]{:S(2)}) %collective-permute-start.3) | collective-permute-done | bytes 116768 | tf_op jit(solution)/shard_map/ppermute | solution.py:542
  17.1 1.7 %collective-permute-done.2.t_ref = bf16[3,38,512]{2,1,0:T(8,128)(2,1)S(1)} collective-permute-done((bf16[3,38,512]{2,1,0:T(8,128)(2,1)S(1)}, bf16[3,38,512]{2,1,0:T(8,128)(2,1)S(1)}, u32[]{:S(2)}, u32[]{:S(2)}) %collective-permute-start.2) | collective-permute-done | bytes 116768 | tf_op jit(solution)/shard_map/ppermute | solution.py:542
  20.0 1.6 %copy-done.4 = bf16[512,2048]{1,0:T(8,128)(2,1)S(1)} copy-done((bf16[512,2048]{1,0:T(8,128)(2,1)S(1)}, bf16[512,2048]{1,0:T(8,128)(2,1)}, u32[]{:S(2)}) %copy-start.4) | copy-done | bytes 2097176
  22.9 32.1 %expand.1 = (bf16[1024,512]{1,0:T(8,128)(2,1)S(1)}, bf16[32,3,512]{2,1,0:T(4,128)(2,1)S(1)}, bf16[32,3,512]{2,1,0:T(4,128)(2,1)S(1)}, bf16[1024,512]{1,0:T(8,128...) custom-call(s32[4]{0:T(128)S(1)} %pad_add_fusion.order_ref, ...), custom_call_target="tpu_custom_call" | custom-call | flops 23000000512 | bytes 72000000 | tf_op jit(solution)/shard_map/expand/pallas_call | solution.py:273
  59.3 1.8 %collective-permute-done.4 = bf16[2,2,4,512,128]{4,3,2,1,0:T(8,128)(2,1)} collective-permute-done((bf16[2,2,4,512,128]{4,3,2,1,0:T(8,128)(2,1)}, bf16[2,2,4,512,128]{4,3,2,1,0:T(8,128)(2,1)}, u32[]{:S(2)}, u32[]{:S(2)}) %collective-permute-start.4) | collective-permute-done | bytes 2097184 | tf_op jit(solution)/shard_map/ppermute | solution.py:503
  61.1 1.5 %convert_add_fusion = f32[2,2,4,256,128]{4,3,2,1,0:T(8,128)S(1)} fusion(bf16[2,2,4,512,128]{4,3,2,1,0:T(8,128)(2,1)} %collective-permute-done.4, bf16[2,2,4,512,128]{4,3,2,1,0:T(8,128)(2,1)S(1)} %get-tuple-element.71), kind=kLoop, calls=%fused_computation | loop fusion | flops 1572864 | bytes 4194304 | tf_op jit(solution)/shard_map/add | solution.py:601
  63.0 2.5 %collective-permute-start.5 = (bf16[2,2,2,256,128]{4,3,1,0,2:T(8,128)(2,1)S(1)}, bf16[2,2,2,256,128]{4,3,1,0,2:T(8,128)(2,1)S(1)}, u32[]{:S(2)}, u32[]{:S(2)}) collective-permute-start(bf16[2,2,2,256,128]{4,3,1,0,2:T(8,128)(2,1)S(1)} %fusion), channel_id=1, source_target_pairs={{0,1},{1,0},{2,3},{3,2},{4,5},{5,4},{6,7},{7,6},{8,9},{9,8},{10,11... | collective-permute-start | bytes 1572872 | tf_op jit(solution)/shard_map/ppermute | solution.py:503
  66.7 1.4 %collective-permute-start.9 = (bf16[2,1,4,256,128]{4,3,2,1,0:T(8,128)(2,1)S(1)}, bf16[2,1,4,256,128]{4,3,2,1,0:T(8,128)(2,1)S(1)}, u32[]{:S(2)}, u32[]{:S(2)}) collective-permute-start(bf16[2,1,4,256,128]{4,3,2,1,0:T(8,128)(2,1)S(1)} %add_convert_fusion), channel_id=1, source_target_pairs={{0,8},{4,12},{8,0},{12,4},{1,9},{5,13},{9,1},{13,5},{2,10},{6,14},... | collective-permute-start | bytes 1572872 | tf_op jit(solution)/shard_map/ppermute | solution.py:503
  68.1 4.0 %filter_grad.2.rest_0_ = f32[4,64,128]{2,1,0:T(8,128)S(1)} custom-call(bf16[32,32,512]{2,1,0:T(8,128)(2,1)S(1)} %copy-done.1, f32[32,32,128]{2,1,0:T(8,128)S(1)} %broadcast_in_dim.10.m_ref, bf16[32,3,512]{2,1,0:T(4,128)(2,1)S(1)} %collective-permute-done.l_ref, bf16[32,3,512]{2,1,0:T(4,128)(2,1)S(1)} %collective-permute-done.1.r_ref, ...), custom_call_target="tpu_custom_call" | custom-call | flops 4600000000 | bytes 14400000 | tf_op jit(solution)/shard_map/filter_grad/pallas_call | solution.py:382
  73.6 4.7 %collective-permute-start.11 = (bf16[3,38,512]{2,1,0:T(8,128)(2,1)S(1)}, bf16[3,38,512]{2,1,0:T(8,128)(2,1)S(1)}, u32[]{:S(2)}, u32[]{:S(2)}) collective-permute-start(bf16[3,38,512]{2,1,0:T(8,128)(2,1)S(1)} %pad_maximum_fusion.5), channel_id=1, source_target_pairs={{0,1},{1,2},{2,3},{4,5},{5,6},{6,7},{8,9},{9,10},{10,11},{12,13},{... | collective-permute-start | bytes 350216 | tf_op jit(solution)/shard_map/ppermute | solution.py:542
  78.5 3.0 %collective-permute-start.8 = (bf16[2,2,1,256,128]{4,3,2,1,0:T(8,128)(2,1)S(1)}, bf16[2,2,1,256,128]{4,3,2,1,0:T(8,128)(2,1)S(1)}, u32[]{:S(2)}, u32[]{:S(2)}) collective-permute-start(bf16[2,2,1,256,128]{4,3,2,1,0:T(8,128)(2,1)S(1)} %fusion.2), channel_id=1, source_target_pairs={{0,2},{1,3},{2,0},{3,1},{4,6},{5,7},{6,4},{7,5},{8,10},{9,11},{10,... | collective-permute-start | bytes 786440 | tf_op jit(solution)/shard_map/ppermute | solution.py:503
  81.5 4.0 %filter_grad.3 = f32[4,64,128]{2,1,0:T(8,128)S(1)} custom-call(bf16[32,32,512]{2,1,0:T(8,128)(2,1)S(1)} %copy-done.1, f32[32,32,128]{2,1,0:T(8,128)S(1)} %broadcast_in_dim.10.m_ref, bf16[32,3,512]{2,1,0:T(4,128)(2,1)S(1)} %collective-permute-done.l_ref, bf16[32,3,512]{2,1,0:T(4,128)(2,1)S(1)} %collective-permute-done.1.r_ref, ...), custom_call_target="tpu_custom_call", output_to_operand_aliasing={{}: (9, {})} | custom-call | flops 4600000000 | bytes 14400000 | tf_op jit(solution)/shard_map/filter_grad/pallas_call | solution.py:382
  87.2 5.1 %collective-permute-done.8 = bf16[2,2,1,256,128]{4,3,2,1,0:T(8,128)(2,1)S(1)} collective-permute-done((bf16[2,2,1,256,128]{4,3,2,1,0:T(8,128)(2,1)S(1)}, bf16[2,2,1,256,128]{4,3,2,1,0:T(8,128)(2,1)S(1)}, u32[]{:S(2)}, u32[]{:S(2)}) %collective-permute-start.8) | collective-permute-done | bytes 262176 | tf_op jit(solution)/shard_map/ppermute | solution.py:503
  93.1 4.5 %input_grad.3.rest_0_ = bf16[32,32,512]{2,1,0:T(8,128)(2,1)} custom-call(bf16[32,32,512]{2,1,0:T(8,128)(2,1)S(1)} %bitcast.59, bf16[32,3,512]{2,1,0:T(4,128)(2,1)S(1)} %collective-permute-done.6.l_ref, bf16[32,3,512]{2,1,0:T(4,128)(2,1)S(1)} %collective-permute-done.7.r_ref, bf16[3,38,512]{2,1,0:T(8,128)(2,1)S(1)} %collective-permute-done.11.t_ref, ...), custom_call_target="tpu_custom_call" | custom-call | flops 4600000000 | bytes 14400000 | tf_op jit(solution)/shard_map/input_grad/pallas_call | solution.py:435
  97.6 3.1 %collective-permute-done.13 = bf16[1280,128]{1,0:T(8,128)(2,1)S(1)} collective-permute-done((bf16[1280,128]{1,0:T(8,128)(2,1)S(1)}, bf16[1280,128]{1,0:T(8,128)(2,1)S(1)}, u32[]{:S(2)}, u32[]{:S(2)}) %collective-permute-start.13) | collective-permute-done | bytes 327712 | tf_op jit(solution)/shard_map/ppermute | solution.py:503
  100.9 3.3 %collective-permute-start.14 = (bf16[768,128]{1,0:T(8,128)(2,1)S(1)}, bf16[768,128]{1,0:T(8,128)(2,1)S(1)}, u32[]{:S(2)}, u32[]{:S(2)}) collective-permute-start(bf16[768,128]{1,0:T(8,128)(2,1)S(1)} %pad_maximum_fusion.1), channel_id=1, source_target_pairs={{0,2},{1,3},{2,0},{3,1},{4,6},{5,7},{6,4},{7,5},{8,10},{9,11},{10,... | collective-permute-start | bytes 589832 | tf_op jit(solution)/shard_map/ppermute | solution.py:503
  104.2 2.6 %input_grad.4.rest_0_ = bf16[32,32,512]{2,1,0:T(8,128)(2,1)} custom-call(bf16[32,32,512]{2,1,0:T(8,128)(2,1)S(1)} %bitcast.60, bf16[32,3,512]{2,1,0:T(4,128)(2,1)S(1)} %collective-permute-done.6.l_ref, bf16[32,3,512]{2,1,0:T(4,128)(2,1)S(1)} %collective-permute-done.7.r_ref, ...), custom_call_target="tpu_custom_call", output_to_operand_aliasing={{}: (8, {})} | custom-call | flops 4600000000 | bytes 14400000 | tf_op jit(solution)/shard_map/input_grad/pallas_call | solution.py:435
  106.8 5.7 %collective-permute-done.14.load_a_ref = bf16[768,128]{1,0:T(8,128)(2,1)S(1)} collective-permute-done((bf16[768,128]{1,0:T(8,128)(2,1)S(1)}, bf16[768,128]{1,0:T(8,128)(2,1)S(1)}, u32[]{:S(2)}, u32[]{:S(2)}) %collective-permute-start.14) | collective-permute-done | bytes 196640 | tf_op jit(solution)/shard_map/ppermute | solution.py:503
  112.6 2.0 %collective-permute-start.15 = (bf16[768,128]{1,0:T(8,128)(2,1)S(1)}, bf16[768,128]{1,0:T(8,128)(2,1)S(1)}, u32[]{:S(2)}, u32[]{:S(2)}) collective-permute-start(bf16[768,128]{1,0:T(8,128)(2,1)S(1)} %pad_maximum_fusion.2), channel_id=1, source_target_pairs={{0,8},{4,12},{8,0},{12,4},{1,9},{5,13},{9,1},{13,5},{2,10},{6,14},... | collective-permute-start | bytes 589832 | tf_op jit(solution)/shard_map/ppermute | solution.py:503
  114.5 2.6 %input_grad.5 = bf16[32,32,512]{2,1,0:T(8,128)(2,1)} custom-call(bf16[32,32,512]{2,1,0:T(8,128)(2,1)S(1)} %bitcast.61, bf16[32,3,512]{2,1,0:T(4,128)(2,1)S(1)} %collective-permute-done.6.l_ref, bf16[32,3,512]{2,1,0:T(4,128)(2,1)S(1)} %collective-permute-done.7.r_ref, ...), custom_call_target="tpu_custom_call", output_to_operand_aliasing={{}: (8, {})} | custom-call | flops 4600000000 | bytes 14400000 | tf_op jit(solution)/shard_map/input_grad/pallas_call | solution.py:435
  117.1 1.6 %collective-permute-done.15.load_ref = bf16[768,128]{1,0:T(8,128)(2,1)S(1)} collective-permute-done((bf16[768,128]{1,0:T(8,128)(2,1)S(1)}, bf16[768,128]{1,0:T(8,128)(2,1)S(1)}, u32[]{:S(2)}, u32[]{:S(2)}) %collective-permute-start.15) | collective-permute-done | bytes 196640 | tf_op jit(solution)/shard_map/ppermute | solution.py:503
  (87 shorter events, 19.7 us)
Async XLA Ops:
  0.6 18.1 %copy-start.12 = (f32[512]{0:T(512)S(1)}, f32[512]{0:T(512)}, u32[]{:S(2)}) copy-start(f32[512]{0:T(512)} %param.20) | copy-start | bytes 6148
  0.7 18.1 %copy-start.8 = (f32[2048]{0:T(1024)S(1)}, f32[2048]{0:T(1024)}, u32[]{:S(2)}) copy-start(f32[2048]{0:T(1024)} %param.18) | copy-start | bytes 24580
  0.7 18.1 %copy-start.9 = (f32[512]{0:T(512)S(1)}, f32[512]{0:T(512)}, u32[]{:S(2)}) copy-start(f32[512]{0:T(512)} %param.15) | copy-start | bytes 6148
  0.7 18.1 %copy-start.10 = (f32[512]{0:T(512)S(1)}, f32[512]{0:T(512)}, u32[]{:S(2)}) copy-start(f32[512]{0:T(512)} %param.16) | copy-start | bytes 6148
  0.7 18.1 %copy-start.11 = (f32[512]{0:T(512)S(1)}, f32[512]{0:T(512)}, u32[]{:S(2)}) copy-start(f32[512]{0:T(512)} %param.21) | copy-start | bytes 6148
  0.7 18.1 %copy-start.7 = (f32[7,7,512]{2,1,0:T(8,128)S(1)}, f32[7,7,512]{2,1,0:T(8,128)}, u32[]{:S(2)}) copy-start(f32[7,7,512]{2,1,0:T(8,128)} %k_ref.7) | copy-start | bytes 301060
  2.8 5.1 %collective-permute-start = (bf16[32,3,512]{2,1,0:T(4,128)(2,1)S(1)}, bf16[32,3,512]{2,1,0:T(4,128)(2,1)S(1)}, u32[]{:S(2)}, u32[]{:S(2)}) collective-permute-start(bf16[32,3,512]{2,1,0:T(4,128)(2,1)S(1)} %get-tuple-element.105), channel_id=1, source_target_pairs={{0,4},{4,8},{8,12},{12,0},{1,5},{5,9},{9,13},{13,1},{2,6},{6,10},{... | collective-permute-start | bytes 294920 | tf_op jit(solution)/shard_map/ppermute | solution.py:527
  3.3 5.8 %collective-permute-start.1 = (bf16[32,3,512]{2,1,0:T(4,128)(2,1)S(1)}, bf16[32,3,512]{2,1,0:T(4,128)(2,1)S(1)}, u32[]{:S(2)}, u32[]{:S(2)}) collective-permute-start(bf16[32,3,512]{2,1,0:T(4,128)(2,1)S(1)} %get-tuple-element.104), channel_id=1, source_target_pairs={{4,0},{8,4},{12,8},{0,12},{5,1},{9,5},{13,9},{1,13},{6,2},{10,6},{... | collective-permute-start | bytes 294920 | tf_op jit(solution)/shard_map/ppermute | solution.py:527
  9.2 7.9 %collective-permute-start.3 = (bf16[3,38,512]{2,1,0:T(8,128)(2,1)S(1)}, bf16[3,38,512]{2,1,0:T(8,128)(2,1)S(1)}, u32[]{:S(2)}, u32[]{:S(2)}) collective-permute-start(bf16[3,38,512]{2,1,0:T(8,128)(2,1)S(1)} %pad_maximum_fusion.4), channel_id=1, source_target_pairs={{1,0},{2,1},{3,2},{5,4},{6,5},{7,6},{9,8},{10,9},{11,10},{13,12},{... | collective-permute-start | bytes 350216 | tf_op jit(solution)/shard_map/ppermute | solution.py:542
  10.6 8.2 %collective-permute-start.2 = (bf16[3,38,512]{2,1,0:T(8,128)(2,1)S(1)}, bf16[3,38,512]{2,1,0:T(8,128)(2,1)S(1)}, u32[]{:S(2)}, u32[]{:S(2)}) collective-permute-start(bf16[3,38,512]{2,1,0:T(8,128)(2,1)S(1)} %pad_maximum_fusion.3), channel_id=1, source_target_pairs={{0,1},{1,2},{2,3},{4,5},{5,6},{6,7},{8,9},{9,10},{10,11},{12,13},{... | collective-permute-start | bytes 350216 | tf_op jit(solution)/shard_map/ppermute | solution.py:542
  56.6 4.5 %collective-permute-start.4 = (bf16[2,2,4,512,128]{4,3,2,1,0:T(8,128)(2,1)}, bf16[2,2,4,512,128]{4,3,2,1,0:T(8,128)(2,1)}, u32[]{:S(2)}, u32[]{:S(2)}) collective-permute-start(bf16[2,2,4,512,128]{4,3,2,1,0:T(8,128)(2,1)} %get-tuple-element.58), channel_id=1, source_target_pairs={{0,4},{4,0},{8,12},{12,8},{1,5},{5,1},{9,13},{13,9},{2,6},{6,2},{1... | collective-permute-start | bytes 6291464 | tf_op jit(solution)/shard_map/ppermute | solution.py:503
  56.6 15.5 %collective-permute-start.6 = (bf16[32,3,512]{2,1,0:T(4,128)(2,1)S(1)}, bf16[32,3,512]{2,1,0:T(4,128)(2,1)S(1)}, u32[]{:S(2)}, u32[]{:S(2)}) collective-permute-start(bf16[32,3,512]{2,1,0:T(4,128)(2,1)S(1)} %get-tuple-element.64), channel_id=1, source_target_pairs={{0,4},{4,8},{8,12},{12,0},{1,5},{5,9},{9,13},{13,1},{2,6},{6,10},{... | collective-permute-start | bytes 294920 | tf_op jit(solution)/shard_map/ppermute | solution.py:527
  57.1 15.0 %collective-permute-start.7 = (bf16[32,3,512]{2,1,0:T(4,128)(2,1)S(1)}, bf16[32,3,512]{2,1,0:T(4,128)(2,1)S(1)}, u32[]{:S(2)}, u32[]{:S(2)}) collective-permute-start(bf16[32,3,512]{2,1,0:T(4,128)(2,1)S(1)} %get-tuple-element.66), channel_id=1, source_target_pairs={{4,0},{8,4},{12,8},{0,12},{5,1},{9,5},{13,9},{1,13},{6,2},{10,6},{... | collective-permute-start | bytes 294920 | tf_op jit(solution)/shard_map/ppermute | solution.py:527
  62.8 5.3 %copy-start.1 = (bf16[32,32,512]{2,1,0:T(8,128)(2,1)S(1)}, bf16[32,32,512]{2,1,0:T(8,128)(2,1)}, u32[]{:S(2)}) copy-start(bf16[32,32,512]{2,1,0:T(8,128)(2,1)} %f_ref.3) | copy-start | bytes 3145732
  63.0 15.3 %collective-permute-start.5 = (bf16[2,2,2,256,128]{4,3,1,0,2:T(8,128)(2,1)S(1)}, bf16[2,2,2,256,128]{4,3,1,0,2:T(8,128)(2,1)S(1)}, u32[]{:S(2)}, u32[]{:S(2)}) collective-permute-start(bf16[2,2,2,256,128]{4,3,1,0,2:T(8,128)(2,1)S(1)} %fusion), channel_id=1, source_target_pairs={{0,1},{1,0},{2,3},{3,2},{4,5},{5,4},{6,7},{7,6},{8,9},{9,8},{10,11... | collective-permute-start | bytes 1572872 | tf_op jit(solution)/shard_map/ppermute | solution.py:503
  66.7 19.0 %collective-permute-start.9 = (bf16[2,1,4,256,128]{4,3,2,1,0:T(8,128)(2,1)S(1)}, bf16[2,1,4,256,128]{4,3,2,1,0:T(8,128)(2,1)S(1)}, u32[]{:S(2)}, u32[]{:S(2)}) collective-permute-start(bf16[2,1,4,256,128]{4,3,2,1,0:T(8,128)(2,1)S(1)} %add_convert_fusion), channel_id=1, source_target_pairs={{0,8},{4,12},{8,0},{12,4},{1,9},{5,13},{9,1},{13,5},{2,10},{6,14},... | collective-permute-start | bytes 1572872 | tf_op jit(solution)/shard_map/ppermute | solution.py:503
  72.2 20.9 %collective-permute-start.12 = (bf16[3,38,512]{2,1,0:T(8,128)(2,1)S(1)}, bf16[3,38,512]{2,1,0:T(8,128)(2,1)S(1)}, u32[]{:S(2)}, u32[]{:S(2)}) collective-permute-start(bf16[3,38,512]{2,1,0:T(8,128)(2,1)S(1)} %pad_maximum_fusion.6), channel_id=1, source_target_pairs={{1,0},{2,1},{3,2},{5,4},{6,5},{7,6},{9,8},{10,9},{11,10},{13,12},{... | collective-permute-start | bytes 350216 | tf_op jit(solution)/shard_map/ppermute | solution.py:542
  73.6 19.5 %collective-permute-start.11 = (bf16[3,38,512]{2,1,0:T(8,128)(2,1)S(1)}, bf16[3,38,512]{2,1,0:T(8,128)(2,1)S(1)}, u32[]{:S(2)}, u32[]{:S(2)}) collective-permute-start(bf16[3,38,512]{2,1,0:T(8,128)(2,1)S(1)} %pad_maximum_fusion.5), channel_id=1, source_target_pairs={{0,1},{1,2},{2,3},{4,5},{5,6},{6,7},{8,9},{9,10},{10,11},{12,13},{... | collective-permute-start | bytes 350216 | tf_op jit(solution)/shard_map/ppermute | solution.py:542
  78.5 13.8 %collective-permute-start.8 = (bf16[2,2,1,256,128]{4,3,2,1,0:T(8,128)(2,1)S(1)}, bf16[2,2,1,256,128]{4,3,2,1,0:T(8,128)(2,1)S(1)}, u32[]{:S(2)}, u32[]{:S(2)}) collective-permute-start(bf16[2,2,1,256,128]{4,3,2,1,0:T(8,128)(2,1)S(1)} %fusion.2), channel_id=1, source_target_pairs={{0,2},{1,3},{2,0},{3,1},{4,6},{5,7},{6,4},{7,5},{8,10},{9,11},{10,... | collective-permute-start | bytes 786440 | tf_op jit(solution)/shard_map/ppermute | solution.py:503
  85.5 6.8 %collective-permute-start.10 = (f32[4,64,128]{2,1,0:T(8,128)S(1)}, f32[4,64,128]{2,1,0:T(8,128)S(1)}, u32[]{:S(2)}, u32[]{:S(2)}) collective-permute-start(f32[4,64,128]{2,1,0:T(8,128)S(1)} %filter_grad.3), channel_id=1, source_target_pairs={{0,4},{4,0},{8,12},{12,8},{1,5},{5,1},{9,13},{13,9},{2,6},{6,2},{1... | collective-permute-start | bytes 393224 | tf_op jit(solution)/shard_map/ppermute | solution.py:503
  87.1 6.0 %copy-start.6 = (bf16[32,32,512]{2,1,0:T(8,128)(2,1)S(1)}, bf16[32,32,512]{2,1,0:T(8,128)(2,1)}, u32[]{:S(2)}) copy-start(bf16[32,32,512]{2,1,0:T(8,128)(2,1)} %cot_ref.5) | copy-start | bytes 3145732
  92.4 8.3 %collective-permute-start.13 = (bf16[1280,128]{1,0:T(8,128)(2,1)S(1)}, bf16[1280,128]{1,0:T(8,128)(2,1)S(1)}, u32[]{:S(2)}, u32[]{:S(2)}) collective-permute-start(bf16[1280,128]{1,0:T(8,128)(2,1)S(1)} %pad_maximum_fusion), channel_id=1, source_target_pairs={{0,1},{1,0},{2,3},{3,2},{4,5},{5,4},{6,7},{7,6},{8,9},{9,8},{10,11... | collective-permute-start | bytes 983048 | tf_op jit(solution)/shard_map/ppermute | solution.py:503
  100.9 11.6 %collective-permute-start.14 = (bf16[768,128]{1,0:T(8,128)(2,1)S(1)}, bf16[768,128]{1,0:T(8,128)(2,1)S(1)}, u32[]{:S(2)}, u32[]{:S(2)}) collective-permute-start(bf16[768,128]{1,0:T(8,128)(2,1)S(1)} %pad_maximum_fusion.1), channel_id=1, source_target_pairs={{0,2},{1,3},{2,0},{3,1},{4,6},{5,7},{6,4},{7,5},{8,10},{9,11},{10,... | collective-permute-start | bytes 589832 | tf_op jit(solution)/shard_map/ppermute | solution.py:503
  112.6 6.2 %collective-permute-start.15 = (bf16[768,128]{1,0:T(8,128)(2,1)S(1)}, bf16[768,128]{1,0:T(8,128)(2,1)S(1)}, u32[]{:S(2)}, u32[]{:S(2)}) collective-permute-start(bf16[768,128]{1,0:T(8,128)(2,1)S(1)} %pad_maximum_fusion.2), channel_id=1, source_target_pairs={{0,8},{4,12},{8,0},{12,4},{1,9},{5,13},{9,1},{13,5},{2,10},{6,14},... | collective-permute-start | bytes 589832 | tf_op jit(solution)/shard_map/ppermute | solution.py:503
  (7 other events, 16.2 us)

commit v15 on v12

--- a/solution.py
+++ b/solution.py
@@ -587,7 +587,7 @@
     d_left, d_right = side_halo(d_last, d_first)
 
     far = n_lon // 4
-    border = channels // 2
+    border = channels * 9 // 16
     lon_bits = [("lon", 1, bit) for bit in bits_of("lon")[2:]]
     lat_bits = [("lat", 2, bit) for bit in bits_of("lat")]
 

time: 118 us -> 116 us (0.983)
  starting transfers between devices: 30.6 us -> 28.3 us
    ppermute x8, starting transfers between devices: 13.7 us -> 11.5 us  [swap(): return lax.ppermute(values, axis, [(i, i ^ bit) for i in range(count)])]
  transfers between devices with their start and end apart: 16 -> 16, of which waited for: 10 -> 9; matrix products, arithmetic and copies ran while one was open for 5% -> 6% of each run, Pallas kernels for 15% -> 15%
where the time goes in v15:
time: 116 us; the launch traced here: 115 us
  Pallas kernels  53.1 us (46%)
  starting transfers between devices  28.3 us (24%)
  waiting for transfers between devices  23.3 us (20%)
  other arithmetic  6.41 us (6%)
  local copies, waits for them, and re-layouts  3.07 us (3%)
  between operations  1.19 us (1%)
    pallas_call x1, Pallas kernels, expand(): pl.pallas_call(expand_kernel, grid_spec=pltpu.PrefetchScalarGridSpec(num_...  34.5 us
    ppermute x8, waiting for transfers between devices, swap(): return lax.ppermute(values, axis, [(i, i ^ bit) for i in range(count)])  18.7 us
    ppermute x4, starting transfers between devices, end_halo(): return (lax.ppermute(tail, 'lat', ahead), lax.ppermute(head, 'lat', back))  12 us
    ppermute x8, starting transfers between devices, swap(): return lax.ppermute(values, axis, [(i, i ^ bit) for i in range(count)])  11.5 us
    pallas_call x3, Pallas kernels, input_grad(): pl.pallas_call(functools.partial(input_grad_kernel, rows // 4 * first), g...  9.62 us
    pallas_call x2, Pallas kernels, filter_grad(): pl.pallas_call(functools.partial(filter_grad_kernel, half * (blocks // 2)...  8.03 us
    ppermute x4, starting transfers between devices, side_halo(): return (lax.ppermute(last, 'lon', ahead), lax.ppermute(first, 'lon', back))  4.8 us
    ppermute x4, waiting for transfers between devices, end_halo(): return (lax.ppermute(tail, 'lat', ahead), lax.ppermute(head, 'lat', back))  3.51 us
  transfers between devices with their start and end apart: 16, of which 9 were waited for; matrix products, arithmetic and copies ran while one was open for 6% of the time, Pallas kernels for 15%

profile of v15, /device:TPU:0, one launch (start us, length us, event | category | flops | bytes accessed | tf_op | source)
XLA Modules:
  0.0 115.4 jit_solution(12151923456572915615)
XLA Ops:
  3.2 2.0 %collective-permute-start.1 = (bf16[32,3,512]{2,1,0:T(4,128)(2,1)S(1)}, bf16[32,3,512]{2,1,0:T(4,128)(2,1)S(1)}, u32[]{:S(2)}, u32[]{:S(2)}) collective-permute-start(bf16[32,3,512]{2,1,0:T(4,128)(2,1)S(1)} %get-tuple-element.104), channel_id=1, source_target_pairs={{4,0},{8,4},{12,8},{0,12},{5,1},{9,5},{13,9},{1,13},{6,2},{10,6},{... | collective-permute-start | bytes 294920 | tf_op jit(solution)/shard_map/ppermute | solution.py:527
  9.2 1.3 %collective-permute-start.3 = (bf16[3,38,512]{2,1,0:T(8,128)(2,1)S(1)}, bf16[3,38,512]{2,1,0:T(8,128)(2,1)S(1)}, u32[]{:S(2)}, u32[]{:S(2)}) collective-permute-start(bf16[3,38,512]{2,1,0:T(8,128)(2,1)S(1)} %pad_maximum_fusion.4), channel_id=1, source_target_pairs={{1,0},{2,1},{3,2},{5,4},{6,5},{7,6},{9,8},{10,9},{11,10},{13,12},{... | collective-permute-start | bytes 350216 | tf_op jit(solution)/shard_map/ppermute | solution.py:542
  10.5 4.7 %collective-permute-start.2 = (bf16[3,38,512]{2,1,0:T(8,128)(2,1)S(1)}, bf16[3,38,512]{2,1,0:T(8,128)(2,1)S(1)}, u32[]{:S(2)}, u32[]{:S(2)}) collective-permute-start(bf16[3,38,512]{2,1,0:T(8,128)(2,1)S(1)} %pad_maximum_fusion.3), channel_id=1, source_target_pairs={{0,1},{1,2},{2,3},{4,5},{5,6},{6,7},{8,9},{9,10},{10,11},{12,13},{... | collective-permute-start | bytes 350216 | tf_op jit(solution)/shard_map/ppermute | solution.py:542
  15.2 2.1 %collective-permute-done.3.b_ref = bf16[3,38,512]{2,1,0:T(8,128)(2,1)S(1)} collective-permute-done((bf16[3,38,512]{2,1,0:T(8,128)(2,1)S(1)}, bf16[3,38,512]{2,1,0:T(8,128)(2,1)S(1)}, u32[]{:S(2)}, u32[]{:S(2)}) %collective-permute-start.3) | collective-permute-done | bytes 116768 | tf_op jit(solution)/shard_map/ppermute | solution.py:542
  17.3 1.4 %collective-permute-done.2.t_ref = bf16[3,38,512]{2,1,0:T(8,128)(2,1)S(1)} collective-permute-done((bf16[3,38,512]{2,1,0:T(8,128)(2,1)S(1)}, bf16[3,38,512]{2,1,0:T(8,128)(2,1)S(1)}, u32[]{:S(2)}, u32[]{:S(2)}) %collective-permute-start.2) | collective-permute-done | bytes 116768 | tf_op jit(solution)/shard_map/ppermute | solution.py:542
  19.4 34.5 %expand.1 = (bf16[1024,512]{1,0:T(8,128)(2,1)}, bf16[32,3,512]{2,1,0:T(4,128)(2,1)}, bf16[32,3,512]{2,1,0:T(4,128)(2,1)}, bf16[1024,512]{1,0:T(8,128)(2,1)}, f32...) custom-call(s32[4]{0:T(128)} %pad_add_fusion.order_ref, ...), custom_call_target="tpu_custom_call" | custom-call | flops 23000000512 | bytes 72000000 | tf_op jit(solution)/shard_map/expand/pallas_call | solution.py:273
  54.5 1.8 %collective-permute-start.7 = (bf16[32,3,512]{2,1,0:T(4,128)(2,1)}, bf16[32,3,512]{2,1,0:T(4,128)(2,1)S(1)}, u32[]{:S(2)}, u32[]{:S(2)}) collective-permute-start(bf16[32,3,512]{2,1,0:T(4,128)(2,1)} %get-tuple-element.66), channel_id=1, source_target_pairs={{4,0},{8,4},{12,8},{0,12},{5,1},{9,5},{13,9},{1,13},{6,2},{10,6},{... | collective-permute-start | bytes 294920 | tf_op jit(solution)/shard_map/ppermute | solution.py:527
  58.3 1.4 %convert_add_fusion = f32[2,2,4,224,128]{4,3,2,1,0:T(8,128)S(1)} fusion(bf16[2,2,4,512,128]{4,3,2,1,0:T(8,128)(2,1)S(1)} %collective-permute-done.4, bf16[2,2,4,512,128]{4,3,2,1,0:T(8,128)(2,1)} %get-tuple-element.71), kind=kLoop, calls=%fused_computation | loop fusion | flops 1376256 | bytes 3670016 | tf_op jit(solution)/shard_map/add | solution.py:601
  60.2 2.5 %collective-permute-start.5 = (bf16[2,2,2,224,128]{4,3,1,0,2:T(8,128)(2,1)S(1)}, bf16[2,2,2,224,128]{4,3,1,0,2:T(8,128)(2,1)S(1)}, u32[]{:S(2)}, u32[]{:S(2)}) collective-permute-start(bf16[2,2,2,224,128]{4,3,1,0,2:T(8,128)(2,1)S(1)} %fusion.1), channel_id=1, source_target_pairs={{0,1},{1,0},{2,3},{3,2},{4,5},{5,4},{6,7},{7,6},{8,9},{9,8},{10,11... | collective-permute-start | bytes 1376264 | tf_op jit(solution)/shard_map/ppermute | solution.py:503
  62.9 2.2 %collective-permute-start.9 = (bf16[2,1,4,288,128]{4,3,2,1,0:T(8,128)(2,1)S(1)}, bf16[2,1,4,288,128]{4,3,2,1,0:T(8,128)(2,1)S(1)}, u32[]{:S(2)}, u32[]{:S(2)}) collective-permute-start(bf16[2,1,4,288,128]{4,3,2,1,0:T(8,128)(2,1)S(1)} %add_convert_fusion), channel_id=1, source_target_pairs={{0,8},{4,12},{8,0},{12,4},{1,9},{5,13},{9,1},{13,5},{2,10},{6,14},... | collective-permute-start | bytes 1769480 | tf_op jit(solution)/shard_map/ppermute | solution.py:503
  65.2 4.0 %filter_grad.2.rest_0_ = f32[4,64,128]{2,1,0:T(8,128)S(1)} custom-call(bf16[32,32,512]{2,1,0:T(8,128)(2,1)S(1)} %copy-done.1, f32[32,32,128]{2,1,0:T(8,128)S(1)} %copy-done, bf16[32,3,512]{2,1,0:T(4,128)(2,1)S(1)} %copy-done.4, bf16[32,3,512]{2,1,0:T(4,128)(2,1)S(1)} %copy-done.6, bf16[3,38,512]{2,1,0:T(8,128)(2,1)S(1)} %copy-done.11, ...), custom_call_target="tpu_custom_call" | custom-call | flops 4600000000 | bytes 14400000 | tf_op jit(solution)/shard_map/filter_grad/pallas_call | solution.py:382
  69.3 1.3 %collective-permute-start.12 = (bf16[3,38,512]{2,1,0:T(8,128)(2,1)S(1)}, bf16[3,38,512]{2,1,0:T(8,128)(2,1)S(1)}, u32[]{:S(2)}, u32[]{:S(2)}) collective-permute-start(bf16[3,38,512]{2,1,0:T(8,128)(2,1)S(1)} %pad_maximum_fusion.6), channel_id=1, source_target_pairs={{1,0},{2,1},{3,2},{5,4},{6,5},{7,6},{9,8},{10,9},{11,10},{13,12},{... | collective-permute-start | bytes 350216 | tf_op jit(solution)/shard_map/ppermute | solution.py:542
  70.6 4.7 %collective-permute-start.11 = (bf16[3,38,512]{2,1,0:T(8,128)(2,1)S(1)}, bf16[3,38,512]{2,1,0:T(8,128)(2,1)S(1)}, u32[]{:S(2)}, u32[]{:S(2)}) collective-permute-start(bf16[3,38,512]{2,1,0:T(8,128)(2,1)S(1)} %pad_maximum_fusion.5), channel_id=1, source_target_pairs={{0,1},{1,2},{2,3},{4,5},{5,6},{6,7},{8,9},{9,10},{10,11},{12,13},{... | collective-permute-start | bytes 350216 | tf_op jit(solution)/shard_map/ppermute | solution.py:542
  75.5 2.0 %collective-permute-start.8 = (bf16[2,2,1,224,128]{4,3,2,1,0:T(8,128)(2,1)S(1)}, bf16[2,2,1,224,128]{4,3,2,1,0:T(8,128)(2,1)S(1)}, u32[]{:S(2)}, u32[]{:S(2)}) collective-permute-start(bf16[2,2,1,224,128]{4,3,2,1,0:T(8,128)(2,1)S(1)} %fusion.2), channel_id=1, source_target_pairs={{0,2},{1,3},{2,0},{3,1},{4,6},{5,7},{6,4},{7,5},{8,10},{9,11},{10,... | collective-permute-start | bytes 688136 | tf_op jit(solution)/shard_map/ppermute | solution.py:503
  77.5 4.0 %filter_grad.3 = f32[4,64,128]{2,1,0:T(8,128)S(1)} custom-call(bf16[32,32,512]{2,1,0:T(8,128)(2,1)S(1)} %copy-done.1, f32[32,32,128]{2,1,0:T(8,128)S(1)} %copy-done, bf16[32,3,512]{2,1,0:T(4,128)(2,1)S(1)} %copy-done.4, bf16[32,3,512]{2,1,0:T(4,128)(2,1)S(1)} %copy-done.6, bf16[3,38,512]{2,1,0:T(8,128)(2,1)S(1)} %copy-done.11, ...), custom_call_target="tpu_custom_call", output_to_operand_aliasing={{}: (9, {})} | custom-call | flops 4600000000 | bytes 14400000 | tf_op jit(solution)/shard_map/filter_grad/pallas_call | solution.py:382
  82.2 5.7 %collective-permute-done.8 = bf16[2,2,1,224,128]{4,3,2,1,0:T(8,128)(2,1)S(1)} collective-permute-done((bf16[2,2,1,224,128]{4,3,2,1,0:T(8,128)(2,1)S(1)}, bf16[2,2,1,224,128]{4,3,2,1,0:T(8,128)(2,1)S(1)}, u32[]{:S(2)}, u32[]{:S(2)}) %collective-permute-start.8) | collective-permute-done | bytes 229408 | tf_op jit(solution)/shard_map/ppermute | solution.py:503
  88.8 4.5 %input_grad.3.rest_0_ = bf16[32,32,512]{2,1,0:T(8,128)(2,1)} custom-call(bf16[32,32,512]{2,1,0:T(8,128)(2,1)S(1)} %bitcast.59, bf16[32,3,512]{2,1,0:T(4,128)(2,1)S(1)} %collective-permute-done.6.l_ref, bf16[32,3,512]{2,1,0:T(4,128)(2,1)S(1)} %collective-permute-done.7.r_ref, bf16[3,38,512]{2,1,0:T(8,128)(2,1)S(1)} %collective-permute-done.11.t_ref, ...), custom_call_target="tpu_custom_call" | custom-call | flops 4600000000 | bytes 14400000 | tf_op jit(solution)/shard_map/input_grad/pallas_call | solution.py:435
  93.3 4.1 %collective-permute-done.13 = bf16[1408,128]{1,0:T(8,128)(2,1)S(1)} collective-permute-done((bf16[1408,128]{1,0:T(8,128)(2,1)S(1)}, bf16[1408,128]{1,0:T(8,128)(2,1)S(1)}, u32[]{:S(2)}, u32[]{:S(2)}) %collective-permute-start.13) | collective-permute-done | bytes 360480 | tf_op jit(solution)/shard_map/ppermute | solution.py:503
  97.7 2.2 %collective-permute-start.14 = (bf16[832,128]{1,0:T(8,128)(2,1)S(1)}, bf16[832,128]{1,0:T(8,128)(2,1)S(1)}, u32[]{:S(2)}, u32[]{:S(2)}) collective-permute-start(bf16[832,128]{1,0:T(8,128)(2,1)S(1)} %pad_maximum_fusion.1), channel_id=1, source_target_pairs={{0,2},{1,3},{2,0},{3,1},{4,6},{5,7},{6,4},{7,5},{8,10},{9,11},{10,... | collective-permute-start | bytes 638984 | tf_op jit(solution)/shard_map/ppermute | solution.py:503
  99.9 2.6 %input_grad.4.rest_0_ = bf16[32,32,512]{2,1,0:T(8,128)(2,1)} custom-call(bf16[32,32,512]{2,1,0:T(8,128)(2,1)S(1)} %bitcast.60, bf16[32,3,512]{2,1,0:T(4,128)(2,1)S(1)} %collective-permute-done.6.l_ref, bf16[32,3,512]{2,1,0:T(4,128)(2,1)S(1)} %collective-permute-done.7.r_ref, ...), custom_call_target="tpu_custom_call", output_to_operand_aliasing={{}: (8, {})} | custom-call | flops 4600000000 | bytes 14400000 | tf_op jit(solution)/shard_map/input_grad/pallas_call | solution.py:435
  102.5 6.0 %collective-permute-done.14.load_a_ref = bf16[832,128]{1,0:T(8,128)(2,1)S(1)} collective-permute-done((bf16[832,128]{1,0:T(8,128)(2,1)S(1)}, bf16[832,128]{1,0:T(8,128)(2,1)S(1)}, u32[]{:S(2)}, u32[]{:S(2)}) %collective-permute-start.14) | collective-permute-done | bytes 213024 | tf_op jit(solution)/shard_map/ppermute | solution.py:503
  108.5 1.7 %collective-permute-start.15 = (bf16[704,128]{1,0:T(8,128)(2,1)S(1)}, bf16[704,128]{1,0:T(8,128)(2,1)S(1)}, u32[]{:S(2)}, u32[]{:S(2)}) collective-permute-start(bf16[704,128]{1,0:T(8,128)(2,1)S(1)} %pad_maximum_fusion.2), channel_id=1, source_target_pairs={{0,8},{4,12},{8,0},{12,4},{1,9},{5,13},{9,1},{13,5},{2,10},{6,14},... | collective-permute-start | bytes 540680 | tf_op jit(solution)/shard_map/ppermute | solution.py:503
  110.2 2.6 %input_grad.5 = bf16[32,32,512]{2,1,0:T(8,128)(2,1)} custom-call(bf16[32,32,512]{2,1,0:T(8,128)(2,1)S(1)} %bitcast.61, bf16[32,3,512]{2,1,0:T(4,128)(2,1)S(1)} %collective-permute-done.6.l_ref, bf16[32,3,512]{2,1,0:T(4,128)(2,1)S(1)} %collective-permute-done.7.r_ref, ...), custom_call_target="tpu_custom_call", output_to_operand_aliasing={{}: (8, {})} | custom-call | flops 4600000000 | bytes 14400000 | tf_op jit(solution)/shard_map/input_grad/pallas_call | solution.py:435
  112.8 1.7 %collective-permute-done.15.load_ref = bf16[704,128]{1,0:T(8,128)(2,1)S(1)} collective-permute-done((bf16[704,128]{1,0:T(8,128)(2,1)S(1)}, bf16[704,128]{1,0:T(8,128)(2,1)S(1)}, u32[]{:S(2)}, u32[]{:S(2)}) %collective-permute-start.15) | collective-permute-done | bytes 180256 | tf_op jit(solution)/shard_map/ppermute | solution.py:503
  (89 shorter events, 13.1 us)
Async XLA Ops:
  2.7 5.1 %collective-permute-start = (bf16[32,3,512]{2,1,0:T(4,128)(2,1)S(1)}, bf16[32,3,512]{2,1,0:T(4,128)(2,1)S(1)}, u32[]{:S(2)}, u32[]{:S(2)}) collective-permute-start(bf16[32,3,512]{2,1,0:T(4,128)(2,1)S(1)} %get-tuple-element.105), channel_id=1, source_target_pairs={{0,4},{4,8},{8,12},{12,0},{1,5},{5,9},{9,13},{13,1},{2,6},{6,10},{... | collective-permute-start | bytes 294920 | tf_op jit(solution)/shard_map/ppermute | solution.py:527
  3.2 5.8 %collective-permute-start.1 = (bf16[32,3,512]{2,1,0:T(4,128)(2,1)S(1)}, bf16[32,3,512]{2,1,0:T(4,128)(2,1)S(1)}, u32[]{:S(2)}, u32[]{:S(2)}) collective-permute-start(bf16[32,3,512]{2,1,0:T(4,128)(2,1)S(1)} %get-tuple-element.104), channel_id=1, source_target_pairs={{4,0},{8,4},{12,8},{0,12},{5,1},{9,5},{13,9},{1,13},{6,2},{10,6},{... | collective-permute-start | bytes 294920 | tf_op jit(solution)/shard_map/ppermute | solution.py:527
  7.9 10.9 %copy-start.3 = (bf16[32,3,512]{2,1,0:T(4,128)(2,1)}, bf16[32,3,512]{2,1,0:T(4,128)(2,1)S(1)}, u32[]{:S(2)}) copy-start(bf16[32,3,512]{2,1,0:T(4,128)(2,1)S(1)} %collective-permute-done.l_ref) | copy-start | bytes 294916
  9.1 9.6 %copy-start.5 = (bf16[32,3,512]{2,1,0:T(4,128)(2,1)}, bf16[32,3,512]{2,1,0:T(4,128)(2,1)S(1)}, u32[]{:S(2)}) copy-start(bf16[32,3,512]{2,1,0:T(4,128)(2,1)S(1)} %collective-permute-done.1.r_ref) | copy-start | bytes 294916
  9.2 8.1 %collective-permute-start.3 = (bf16[3,38,512]{2,1,0:T(8,128)(2,1)S(1)}, bf16[3,38,512]{2,1,0:T(8,128)(2,1)S(1)}, u32[]{:S(2)}, u32[]{:S(2)}) collective-permute-start(bf16[3,38,512]{2,1,0:T(8,128)(2,1)S(1)} %pad_maximum_fusion.4), channel_id=1, source_target_pairs={{1,0},{2,1},{3,2},{5,4},{6,5},{7,6},{9,8},{10,9},{11,10},{13,12},{... | collective-permute-start | bytes 350216 | tf_op jit(solution)/shard_map/ppermute | solution.py:542
  10.5 8.2 %collective-permute-start.2 = (bf16[3,38,512]{2,1,0:T(8,128)(2,1)S(1)}, bf16[3,38,512]{2,1,0:T(8,128)(2,1)S(1)}, u32[]{:S(2)}, u32[]{:S(2)}) collective-permute-start(bf16[3,38,512]{2,1,0:T(8,128)(2,1)S(1)} %pad_maximum_fusion.3), channel_id=1, source_target_pairs={{0,1},{1,2},{2,3},{4,5},{5,6},{6,7},{8,9},{9,10},{10,11},{12,13},{... | collective-permute-start | bytes 350216 | tf_op jit(solution)/shard_map/ppermute | solution.py:542
  53.9 4.4 %collective-permute-start.4 = (bf16[2,2,4,512,128]{4,3,2,1,0:T(8,128)(2,1)}, bf16[2,2,4,512,128]{4,3,2,1,0:T(8,128)(2,1)S(1)}, u32[]{:S(2)}, u32[]{:S(2)}) collective-permute-start(bf16[2,2,4,512,128]{4,3,2,1,0:T(8,128)(2,1)} %get-tuple-element.58), channel_id=1, source_target_pairs={{0,4},{4,0},{8,12},{12,8},{1,5},{5,1},{9,13},{13,9},{2,6},{6,2},{1... | collective-permute-start | bytes 6291464 | tf_op jit(solution)/shard_map/ppermute | solution.py:503
  54.0 15.2 %collective-permute-start.6 = (bf16[32,3,512]{2,1,0:T(4,128)(2,1)}, bf16[32,3,512]{2,1,0:T(4,128)(2,1)S(1)}, u32[]{:S(2)}, u32[]{:S(2)}) collective-permute-start(bf16[32,3,512]{2,1,0:T(4,128)(2,1)} %get-tuple-element.64), channel_id=1, source_target_pairs={{0,4},{4,8},{8,12},{12,0},{1,5},{5,9},{9,13},{13,1},{2,6},{6,10},{... | collective-permute-start | bytes 294920 | tf_op jit(solution)/shard_map/ppermute | solution.py:527
  54.5 14.7 %collective-permute-start.7 = (bf16[32,3,512]{2,1,0:T(4,128)(2,1)}, bf16[32,3,512]{2,1,0:T(4,128)(2,1)S(1)}, u32[]{:S(2)}, u32[]{:S(2)}) collective-permute-start(bf16[32,3,512]{2,1,0:T(4,128)(2,1)} %get-tuple-element.66), channel_id=1, source_target_pairs={{4,0},{8,4},{12,8},{0,12},{5,1},{9,5},{13,9},{1,13},{6,2},{10,6},{... | collective-permute-start | bytes 294920 | tf_op jit(solution)/shard_map/ppermute | solution.py:527
  60.0 5.1 %copy-start = (f32[32,32,128]{2,1,0:T(8,128)S(1)}, f32[32,32,128]{2,1,0:T(8,128)}, u32[]{:S(2)}) copy-start(f32[32,32,128]{2,1,0:T(8,128)} %broadcast_in_dim.10.m_ref) | copy-start | bytes 1572868
  60.0 5.1 %copy-start.1 = (bf16[32,32,512]{2,1,0:T(8,128)(2,1)S(1)}, bf16[32,32,512]{2,1,0:T(8,128)(2,1)}, u32[]{:S(2)}) copy-start(bf16[32,32,512]{2,1,0:T(8,128)(2,1)} %f_ref.3) | copy-start | bytes 3145732
  60.0 5.1 %copy-start.2 = (bf16[1024,512]{1,0:T(8,128)(2,1)S(1)}, bf16[1024,512]{1,0:T(8,128)(2,1)}, u32[]{:S(2)}) copy-start(bf16[1024,512]{1,0:T(8,128)(2,1)} %get-tuple-element.56) | copy-start | bytes 3145732
  60.0 5.1 %copy-start.4 = (bf16[32,3,512]{2,1,0:T(4,128)(2,1)S(1)}, bf16[32,3,512]{2,1,0:T(4,128)(2,1)}, u32[]{:S(2)}) copy-start(bf16[32,3,512]{2,1,0:T(4,128)(2,1)} %copy-done.3) | copy-start | bytes 294916
  60.2 15.2 %collective-permute-start.5 = (bf16[2,2,2,224,128]{4,3,1,0,2:T(8,128)(2,1)S(1)}, bf16[2,2,2,224,128]{4,3,1,0,2:T(8,128)(2,1)S(1)}, u32[]{:S(2)}, u32[]{:S(2)}) collective-permute-start(bf16[2,2,2,224,128]{4,3,1,0,2:T(8,128)(2,1)S(1)} %fusion.1), channel_id=1, source_target_pairs={{0,1},{1,0},{2,3},{3,2},{4,5},{5,4},{6,7},{7,6},{8,9},{9,8},{10,11... | collective-permute-start | bytes 1376264 | tf_op jit(solution)/shard_map/ppermute | solution.py:503
  62.9 18.8 %collective-permute-start.9 = (bf16[2,1,4,288,128]{4,3,2,1,0:T(8,128)(2,1)S(1)}, bf16[2,1,4,288,128]{4,3,2,1,0:T(8,128)(2,1)S(1)}, u32[]{:S(2)}, u32[]{:S(2)}) collective-permute-start(bf16[2,1,4,288,128]{4,3,2,1,0:T(8,128)(2,1)S(1)} %add_convert_fusion), channel_id=1, source_target_pairs={{0,8},{4,12},{8,0},{12,4},{1,9},{5,13},{9,1},{13,5},{2,10},{6,14},... | collective-permute-start | bytes 1769480 | tf_op jit(solution)/shard_map/ppermute | solution.py:503
  69.3 19.5 %collective-permute-start.12 = (bf16[3,38,512]{2,1,0:T(8,128)(2,1)S(1)}, bf16[3,38,512]{2,1,0:T(8,128)(2,1)S(1)}, u32[]{:S(2)}, u32[]{:S(2)}) collective-permute-start(bf16[3,38,512]{2,1,0:T(8,128)(2,1)S(1)} %pad_maximum_fusion.6), channel_id=1, source_target_pairs={{1,0},{2,1},{3,2},{5,4},{6,5},{7,6},{9,8},{10,9},{11,10},{13,12},{... | collective-permute-start | bytes 350216 | tf_op jit(solution)/shard_map/ppermute | solution.py:542
  70.6 18.2 %collective-permute-start.11 = (bf16[3,38,512]{2,1,0:T(8,128)(2,1)S(1)}, bf16[3,38,512]{2,1,0:T(8,128)(2,1)S(1)}, u32[]{:S(2)}, u32[]{:S(2)}) collective-permute-start(bf16[3,38,512]{2,1,0:T(8,128)(2,1)S(1)} %pad_maximum_fusion.5), channel_id=1, source_target_pairs={{0,1},{1,2},{2,3},{4,5},{5,6},{6,7},{8,9},{9,10},{10,11},{12,13},{... | collective-permute-start | bytes 350216 | tf_op jit(solution)/shard_map/ppermute | solution.py:542
  75.5 12.4 %collective-permute-start.8 = (bf16[2,2,1,224,128]{4,3,2,1,0:T(8,128)(2,1)S(1)}, bf16[2,2,1,224,128]{4,3,2,1,0:T(8,128)(2,1)S(1)}, u32[]{:S(2)}, u32[]{:S(2)}) collective-permute-start(bf16[2,2,1,224,128]{4,3,2,1,0:T(8,128)(2,1)S(1)} %fusion.2), channel_id=1, source_target_pairs={{0,2},{1,3},{2,0},{3,1},{4,6},{5,7},{6,4},{7,5},{8,10},{9,11},{10,... | collective-permute-start | bytes 688136 | tf_op jit(solution)/shard_map/ppermute | solution.py:503
  81.5 6.5 %collective-permute-start.10 = (f32[4,64,128]{2,1,0:T(8,128)S(1)}, f32[4,64,128]{2,1,0:T(8,128)S(1)}, u32[]{:S(2)}, u32[]{:S(2)}) collective-permute-start(f32[4,64,128]{2,1,0:T(8,128)S(1)} %filter_grad.3), channel_id=1, source_target_pairs={{0,4},{4,0},{8,12},{12,8},{1,5},{5,1},{9,13},{13,9},{2,6},{6,2},{1... | collective-permute-start | bytes 393224 | tf_op jit(solution)/shard_map/ppermute | solution.py:503
  82.1 6.7 %copy-start.7 = (bf16[32,32,512]{2,1,0:T(8,128)(2,1)S(1)}, bf16[32,32,512]{2,1,0:T(8,128)(2,1)}, u32[]{:S(2)}) copy-start(bf16[32,32,512]{2,1,0:T(8,128)(2,1)} %cot_ref.5) | copy-start | bytes 3145732
  82.1 6.7 %copy-start.12 = (f32[7,7,512]{2,1,0:T(8,128)S(1)}, f32[7,7,512]{2,1,0:T(8,128)}, u32[]{:S(2)}) copy-start(f32[7,7,512]{2,1,0:T(8,128)} %k_ref.7) | copy-start | bytes 301060
  88.1 9.4 %collective-permute-start.13 = (bf16[1408,128]{1,0:T(8,128)(2,1)S(1)}, bf16[1408,128]{1,0:T(8,128)(2,1)S(1)}, u32[]{:S(2)}, u32[]{:S(2)}) collective-permute-start(bf16[1408,128]{1,0:T(8,128)(2,1)S(1)} %pad_maximum_fusion), channel_id=1, source_target_pairs={{0,1},{1,0},{2,3},{3,2},{4,5},{5,4},{6,7},{7,6},{8,9},{9,8},{10,11... | collective-permute-start | bytes 1081352 | tf_op jit(solution)/shard_map/ppermute | solution.py:503
  97.7 10.8 %collective-permute-start.14 = (bf16[832,128]{1,0:T(8,128)(2,1)S(1)}, bf16[832,128]{1,0:T(8,128)(2,1)S(1)}, u32[]{:S(2)}, u32[]{:S(2)}) collective-permute-start(bf16[832,128]{1,0:T(8,128)(2,1)S(1)} %pad_maximum_fusion.1), channel_id=1, source_target_pairs={{0,2},{1,3},{2,0},{3,1},{4,6},{5,7},{6,4},{7,5},{8,10},{9,11},{10,... | collective-permute-start | bytes 638984 | tf_op jit(solution)/shard_map/ppermute | solution.py:503
  108.5 6.0 %collective-permute-start.15 = (bf16[704,128]{1,0:T(8,128)(2,1)S(1)}, bf16[704,128]{1,0:T(8,128)(2,1)S(1)}, u32[]{:S(2)}, u32[]{:S(2)}) collective-permute-start(bf16[704,128]{1,0:T(8,128)(2,1)S(1)} %pad_maximum_fusion.2), channel_id=1, source_target_pairs={{0,8},{4,12},{8,0},{12,4},{1,9},{5,13},{9,1},{13,5},{2,10},{6,14},... | collective-permute-start | bytes 540680 | tf_op jit(solution)/shard_map/ppermute | solution.py:503
  (8 other events, 30.4 us)
